TPU v7x, 32 devices: a whole 2x2x4 slice. The times are simulated.
32 devices in a mesh: seq: 8 (over z, y), exp: 4 (over x, core).
Axes of the slice: x: 2, y: 2, z: 4, core: 2. Of those that a mesh axis runs over, the one named last changes fastest.
Arguments:
- query_in: bfloat16 [4096, 2048], P('seq', 'exp'), may hold values from -0.52734375 to 0.52734375
- key_in: bfloat16 [4096, 2048], P('seq', 'exp'), may hold values from -0.52734375 to 0.52734375
- value_in: bfloat16 [4096, 2048], P('seq', 'exp'), may hold values from -0.52734375 to 0.52734375
- out_grad: bfloat16 [4096, 2048], P('seq', 'exp'), may hold values from -1.0546875 to 1.0546875
- inputs: bfloat16 [4096, 1024], P('seq'), may hold values from -0.13183594 to 0.13183594
- expert_ids: int32 [4096, 2], P('seq'), may hold values from 0 to 3, all different within a row; in each aligned block of 512 rows (0 to 511, 512 to 1023, ...) at most 384 rows name the same one
- route_gates: float32 [4096, 2], P('seq'), may hold values from 0.2 to 1
- expert_weight: bfloat16 [4, 1024, 4096], P('exp'), may hold values from -0.09375 to 0.09375
Outputs:
- gradient_of_queries: bfloat16 [4096, 2048], P('seq', 'exp')
- gradient_of_keys: bfloat16 [4096, 2048], P('seq', 'exp')
- value_grad: bfloat16 [4096, 2048], P('seq', 'exp')
- input_grad: bfloat16 [4096, 1024], P('seq', 'exp')
- weight_grad: float32 [4, 1024, 4096], P('exp', 'seq')
Inputs may be any that keep to these rules, and one draw needn't show every extreme that they name: `expert_ids`: each token names two different experts. Among the 512 tokens of one index of seq no expert is named more than 384 times, a bound that some block reaches in some of them.
All inputs are finite; a program needn't handle non-finite values.
Results may differ from a plain program's by a relative error of at most 0.013.
Values may be sent and summed in bfloat16 or wider, within the bound.
No kernel may reach another device: no remote copies, remote signals or barrier semaphores. Data moves between devices by JAX's collectives and lax.ppermute only.
A program may use at most 128 MiB of HBM per device.

v0:
```python
import jax
import jax.numpy as jnp
from jax import lax
from jax.sharding import PartitionSpec as P

DH = 128
CAP = 384


highest_accuracy = lax.Precision.HIGHEST


def prefix(array, axis, join, neutral, backward):
    count = lax.axis_size(axis)
    place = lax.axis_index(axis)
    ahead = count - 1 - place if backward else place
    gathered = lax.all_gather(array.astype(jnp.bfloat16), axis)
    state = jnp.zeros_like(array) + jnp.asarray(neutral, array.dtype)

    def one(hop, state):
        source = count - 1 - hop if backward else hop
        return join(state, lax.dynamic_index_in_dim(gathered, source, 0, False).astype(array.dtype))

    return lax.fori_loop(0, ahead, one, state)


def block_grads(
    backward_query, backward_key, backward_value, backward_gradient, leading_sum, trailing_sum
):
    length = backward_query.shape[0]
    places = jnp.arange(length, dtype=jnp.int32)
    lower_triangle = (places[:, None] >= places[None, :])[None]
    upper_triangle = (places[:, None] <= places[None, :])[None]
    first_scores = jnp.where(
        lower_triangle,
        jnp.einsum(
            "qnc,onc->nqo", backward_gradient, backward_value, preferred_element_type=jnp.float32
        ),
        0.0,
    ).astype(jnp.bfloat16)
    middle_scores = jnp.where(
        upper_triangle,
        jnp.einsum(
            "qnc,onc->nqo", backward_key, backward_query, preferred_element_type=jnp.float32
        ),
        0.0,
    ).astype(jnp.bfloat16)
    third_scores = jnp.where(
        upper_triangle,
        jnp.einsum(
            "qnc,onc->nqo", backward_value, backward_gradient, preferred_element_type=jnp.float32
        ),
        0.0,
    ).astype(jnp.bfloat16)
    forward_gradient = backward_gradient.astype(jnp.float32)
    forward_value = backward_value.astype(jnp.float32)
    forward_key = backward_key.astype(jnp.float32)
    gradient_of_queries = jnp.einsum(
        "wgq,qwn->gwn", first_scores, backward_key, preferred_element_type=jnp.float32
    ) + jnp.einsum("iok,osk->ios", forward_gradient, leading_sum, precision=highest_accuracy)
    gradient_of_keys = jnp.einsum(
        "wgq,qwn->gwn", third_scores, backward_query, preferred_element_type=jnp.float32
    ) + jnp.einsum("iok,osk->ios", forward_value, trailing_sum, precision=highest_accuracy)
    value_grad = jnp.einsum(
        "hlm,mhe->lhe", middle_scores, backward_gradient, preferred_element_type=jnp.float32
    ) + jnp.einsum("lhd,hde->lhe", forward_key, trailing_sum, precision=highest_accuracy)
    return (
        gradient_of_queries.astype(jnp.bfloat16),
        gradient_of_keys.astype(jnp.bfloat16),
        value_grad.astype(jnp.bfloat16),
    )


def add_states(earlier, later):
    return earlier + later


def per_device(
    query_in, key_in, value_in, out_grad, inputs, expert_ids, route_gates, expert_weight
):
    tok_rows = query_in.shape[0]
    head_local = query_in.shape[1] // DH
    backward_query = query_in.reshape(tok_rows, head_local, DH)
    backward_key = key_in.reshape(tok_rows, head_local, DH)
    backward_value = value_in.reshape(tok_rows, head_local, DH)
    backward_gradient = out_grad.reshape(tok_rows, head_local, DH)
    kv_own = jnp.einsum(
        "lhd,lhe->hde", backward_key, backward_value, preferred_element_type=jnp.float32
    )
    qo_own = jnp.einsum(
        "lhd,lhe->hde", backward_query, backward_gradient, preferred_element_type=jnp.float32
    )
    zeros_state = jnp.zeros_like(kv_own)
    prefix_state = prefix(kv_own, "seq", add_states, zeros_state, False)
    suffix_state = prefix(qo_own, "seq", add_states, zeros_state, True)
    gradient_of_queries, gradient_of_keys, value_grad = block_grads(
        backward_query, backward_key, backward_value, backward_gradient, prefix_state, suffix_state
    )
    key_flat = gradient_of_keys.reshape(tok_rows, -1)
    value_flat = value_grad.reshape(tok_rows, -1)
    experts = lax.axis_size("exp")
    expert_iota = jnp.arange(experts, dtype=jnp.int32)
    flat_ids = expert_ids.reshape(-1)
    onehot_ids = (flat_ids[:, None] == expert_iota[None, :]).astype(jnp.int32)
    earlier_hits = jnp.cumsum(onehot_ids, axis=0) - onehot_ids
    slot_ids = jnp.sum(earlier_hits * onehot_ids, axis=1).reshape(tok_rows, 2)
    slot_iota = jnp.arange(CAP, dtype=jnp.int32)
    placed = (expert_ids[None, None] == expert_iota[:, None, None, None]) & (
        slot_ids[None, None] == slot_iota[None, :, None, None]
    )
    dispatch_f = jnp.sum(placed.astype(jnp.float32), axis=3)
    slot_gate = jnp.sum(jnp.where(placed, route_gates[None, None], 0.0), axis=(2, 3))
    dispatch_b = dispatch_f.astype(jnp.bfloat16)
    stacked = jnp.stack([key_flat, value_flat], axis=1)
    outgoing = jnp.einsum(
        "ect,tkd->eckd", dispatch_b, stacked, preferred_element_type=jnp.float32
    ).astype(jnp.bfloat16)
    incoming = lax.all_to_all(outgoing, "exp", split_axis=0, concat_axis=3, tiled=True)
    slot_grads = incoming.reshape(CAP, -1)
    owner = lax.axis_index("exp")
    mine_f = lax.dynamic_index_in_dim(dispatch_f, owner, 0, keepdims=False)
    mine_gate = lax.dynamic_index_in_dim(slot_gate, owner, 0, keepdims=False)
    slot_inputs = jnp.dot(mine_f.astype(jnp.bfloat16), inputs, preferred_element_type=jnp.float32)
    weighted = (mine_gate[:, None] * slot_inputs).astype(jnp.bfloat16)
    weight_part = lax.psum_scatter(
        lax.dot_general(
            weighted, slot_grads, (((0,), (0,)), ((), ())), preferred_element_type=jnp.float32
        ),
        "seq",
        scatter_dimension=0,
        tiled=True,
    )
    back_proj = lax.dot_general(
        slot_grads, expert_weight[0], (((1,), (1,)), ((), ())), preferred_element_type=jnp.float32
    )
    back_proj = mine_gate[:, None] * back_proj
    split_back = back_proj.reshape(1, CAP, experts, back_proj.shape[1] // experts)
    returned = lax.all_to_all(
        split_back.astype(jnp.bfloat16), "exp", split_axis=2, concat_axis=0, tiled=True
    ).astype(split_back.dtype)
    input_grad = jnp.einsum(
        "ect,ecd->td", dispatch_f, returned[:, :, 0, :], precision=highest_accuracy
    )
    return (
        gradient_of_queries.reshape(tok_rows, -1),
        key_flat,
        value_flat,
        input_grad.astype(jnp.bfloat16),
        weight_part[None],
    )


def solution(mesh):
    return jax.shard_map(
        per_device,
        mesh=mesh,
        in_specs=(
            P("seq", "exp"),
            P("seq", "exp"),
            P("seq", "exp"),
            P("seq", "exp"),
            P("seq", None),
            P("seq", None),
            P("seq", None),
            P("exp", None, None),
        ),
        out_specs=(
            P("seq", "exp"),
            P("seq", "exp"),
            P("seq", "exp"),
            P("seq", "exp"),
            P("exp", "seq", None),
        ),
        check_vma=False,
    )
```

profile of v0, /device:TPU:0, one launch (start us, length us, event | category | flops | bytes accessed | tf_op | source)
XLA Modules:
  0.0 417.9 jit_solution(16865783569932284489)
XLA Ops:
  7.2 0.0 copy-start
  7.2 0.0 copy-start.4
  7.2 0.0 copy-start.5
  7.2 0.0 all-gather.7.cloned.1.call-start
  7.3 1.3 copy.116
  8.6 2.1 convolution_convert_fusion.1
  10.6 0.0 all-gather.7.cloned.1.call-update
  10.7 0.8 copy.102
  11.5 0.2 eq.70
  11.7 0.2 eq.66
  11.9 1.1 reduce-window.6
  13.0 0.2 slice_reduce_fusion
  13.2 0.2 reduce-window.9
  13.4 0.1 add_bitcast_fusion
  13.5 0.2 eq.74
  13.7 0.1 copy.104
  13.8 0.8 iota_compare_fusion.1
  14.6 0.0 copy-done.4
  14.6 0.2 iota_compare_fusion
  14.9 0.0 copy-done.5
  14.9 0.0 copy-start.3
  14.9 3.1 fusion.3
  17.9 35.8 %all-gather.7.cloned.1.call-done = bf16[32,128,128]{2,1,0:T(8,128)(2,1)} async-done(((bf16[4,128,128]{2,1,0:T(8,128)(2,1)}), bf16[32,128,128]{2,1,0:T(8,128)(2,1)}) %all-gather.7.cloned.1.call-update) | async-done | bytes 1048592 | tf_op jit(solution)/shard_map/all_gather | solution.py:17
  53.8 6.9 %while.23 = (s32[]{:T(128)}, f32[4,128,128]{2,1,0:T(8,128)S(1)}, s32[]{:T(128)}, bf16[8,4,128,128]{3,2,1,0:T(8,128)(2,1)}, s32[]{:T(128)}, /*index=5*/s32[]{:T(128)}, s32[]{:T(128)}, s32[]{:T(128)}) while((s32[]{:T(128)}, f32[4,128,128]{2,1,0:T(8,128)S(1)}, s32[]{:T(128)}, bf16[8,4,128,128]{3,2,1,0:T(8,128)(2,1)}, s32[]{:T(128)}, ...), condition=%wide.region_3.4_spmd, body=%wide.region_2.3_spmd.sunk | while | flops 131078 | bytes 655503 | solution.py:24
  53.8 1.0 convert_add_fusion.5
  54.8 1.0 convert_add_fusion.5
  55.8 1.0 convert_add_fusion.5
  56.7 1.0 convert_add_fusion.5
  57.7 1.0 convert_add_fusion.5
  58.7 1.0 convert_add_fusion.5
  59.7 1.0 convert_add_fusion.5
  60.7 0.0 copy-done.3
  60.7 0.6 convolution_bitcast_fusion.1
  61.3 2.6 fusion.18
  63.9 0.2 copy.105
  64.1 2.6 convolution_bitcast_fusion
  66.8 3.0 fusion.19
  69.7 0.0 copy-start.1
  69.7 1.0 copy.106
  70.7 5.5 %convolution_convert_fusion = bf16[4,384,2,512]{3,1,2,0:T(8,128)(2,1)} fusion(f32[4,384,512]{2,1,0:T(8,128)} %get-tuple-element.107, bf16[512,1,512]{2,0,1:T(8,128)(2,1)} %copy.106, bf16[512,1,512]{2,0,1:T(8,128)(2,1)S(1)} %copy.105), kind=kOutput, calls=%fused_computation.11 | convolution fusion | flops 1615069184 | bytes 7340032 | tf_op jit(solution)/shard_map/ect,tkd->eckd/dot_general | solution.py:115
  76.2 0.0 copy-done.1
  76.2 4.8 %all-to-all-start = ((bf16[4,384,2,512]{3,1,2,0:T(8,128)(2,1)}), bf16[4,384,2,512]{3,1,2,0:T(8,128)(2,1)}, u32[]{:S(2)}, u32[]{:S(2)}) async-start(bf16[4,384,2,512]{3,1,2,0:T(8,128)(2,1)} %convolution_convert_fusion), calls=%async_computation | async-start | bytes 6291456 | tf_op jit(solution)/shard_map/all_to_all | solution.py:118
  81.0 0.0 all-gather.5.cloned.1.call-start
  81.1 2.0 convolution_convert_fusion.2
  83.1 0.0 all-gather.5.cloned.1.call-update
  83.1 0.2 reduce-scatter.2.cloned.1.call-start
  83.4 34.6 %all-to-all-done = bf16[4,384,2,512]{3,1,2,0:T(8,128)(2,1)} async-done(((bf16[4,384,2,512]{3,1,2,0:T(8,128)(2,1)}), bf16[4,384,2,512]{3,1,2,0:T(8,128)(2,1)}, u32[]{:S(2)}, u32[]{:S(2)}) %all-to-all-start) | async-done | bytes 3145760 | tf_op jit(solution)/shard_map/all_to_all | solution.py:118
  118.0 4.7 %copy.107 = bf16[1,384,2,4,512]{1,4,3,2,0:T(8,128)(2,1)} copy(bf16[1,384,2,4,512]{4,1,2,3,0:T(8,128)(2,1)} %bitcast.20) | data formatting | bytes 6291456 | tf_op jit(solution)/shard_map/all_to_all | solution.py:118
  122.7 10.4 %fusion.20 = f32[1024,4096]{1,0:T(8,128)} fusion(bf16[384,4096]{0,1:T(8,128)(2,1)} %bitcast.175, bf16[512,1024]{1,0:T(8,128)(2,1)S(1)} %copy-done, f32[384]{0:T(512)S(1)} %dynamic-slice_reduce_fusion, f32[4,384,512]{2,1,0:T(8,128)} %get-tuple-element.107, s32[]{:T(128)S(6)} %select_n.35), kind=kOutput, calls=%fused_computation.32 | convolution fusion | flops 3624665088 | bytes 21366276 | tf_op jit(solution)/shard_map/dot_general | solution.py:126
  133.1 0.0 reduce-scatter.2.cloned.1.call-update
  133.1 0.1 iota_compare_fusion.2
  133.2 0.0 all-gather.5.cloned.1.call-done
  133.2 9.4 %multiply_convert_fusion.1 = bf16[384,1024]{1,0:T(8,128)(2,1)} fusion(bf16[384,4096]{0,1:T(8,128)(2,1)} %bitcast.176, bf16[1,1024,4096]{2,1,0:T(8,128)(2,1)} %param.19, f32[384]{0:T(512)S(1)} %dynamic-slice_reduce_fusion), kind=kOutput, calls=%fused_computation.17 | convolution fusion | flops 3222011904 | bytes 12322304 | tf_op jit(solution)/shard_map/dot_general | solution.py:133
  142.7 1.9 convert_element_type.99
  144.6 1.0 copy.108
  145.6 3.7 all-to-all-start.1
  149.3 1.6 convolution_bitcast_fusion.2
  150.9 3.7 fusion.17
  154.6 2.1 copy.110
  156.7 1.0 copy.111
  157.7 2.1 copy.112
  159.8 1.0 all-to-all-done.1
  160.7 5.2 %fusion.21 = bf16[512,256]{1,0:T(8,128)(2,1)} fusion(f32[4,384,512]{2,1,0:T(8,128)} %get-tuple-element.107, bf16[1,384,4,256]{3,1,0,2:T(8,128)(2,1)S(1)} %all-to-all-done.1), kind=kOutput, calls=%fused_computation.34 | convolution fusion | flops 2416050176 | bytes 4194304 | tf_op jit(solution)/shard_map/ect,ecd->td/dot_general | solution.py:141
  166.0 245.4 %reduce-scatter.2.cloned.1.call-done = f32[128,4096]{1,0:T(8,128)} async-done(((f32[1024,4096]{1,0:T(8,128)}), f32[128,4096]{1,0:T(8,128)}) %reduce-scatter.2.cloned.1.call-update) | async-done | bytes 2097168 | tf_op jit(solution)/shard_map/reduce_scatter | solution.py:125
  (10 shorter events, 0.1 us)
Async XLA Ops:
  7.2 115.5 %copy-start = (bf16[512,1024]{1,0:T(8,128)(2,1)S(1)}, bf16[512,1024]{1,0:T(8,128)(2,1)}, u32[]{:S(2)}) copy-start(bf16[512,1024]{1,0:T(8,128)(2,1)} %param.16) | copy-start | bytes 3145732
  7.2 7.4 %copy-start.4 = (s32[512,2]{0,1:T(2,128)S(1)}, s32[512,2]{0,1:T(2,128)}, u32[]{:S(2)}) copy-start(s32[512,2]{0,1:T(2,128)} %param.17) | copy-start | bytes 12292
  7.2 7.7 %copy-start.5 = (f32[512,2]{0,1:T(2,128)S(1)}, f32[512,2]{0,1:T(2,128)}, u32[]{:S(2)}) copy-start(f32[512,2]{0,1:T(2,128)} %param.18) | copy-start | bytes 12292
  7.2 46.5 %all-gather.7.cloned.1.call-start = ((), (), s32[]{:S(2)}) async-start(), calls=%async_computation.5 | async-start | bytes 1179648 | tf_op jit(solution)/shard_map/all_gather | solution.py:17
  14.9 45.8 %copy-start.3 = (bf16[512,512]{1,0:T(8,128)(2,1)S(1)}, bf16[512,512]{1,0:T(8,128)(2,1)}, u32[]{:S(2)}) copy-start(bf16[512,512]{1,0:T(8,128)(2,1)} %param.14) | copy-start | bytes 1572868
  69.7 6.5 %copy-start.1 = (bf16[512,4,128]{0,2,1:T(8,128)(2,1)}, bf16[512,4,128]{0,2,1:T(8,128)(2,1)S(1)}, u32[]{:S(2)}) copy-start(bf16[512,4,128]{0,2,1:T(8,128)(2,1)S(1)} %fusion.19) | copy-start | bytes 1572868
  76.2 4.8 %copy-start.2 = (bf16[512,512]{1,0:T(8,128)(2,1)S(1)}, bf16[512,512]{1,0:T(8,128)(2,1)}, u32[]{:S(2)}) copy-start(bf16[512,512]{1,0:T(8,128)(2,1)} %param.13) | copy-start | bytes 1572868
  76.2 41.8 %all-to-all-start = ((bf16[4,384,2,512]{3,1,2,0:T(8,128)(2,1)}), bf16[4,384,2,512]{3,1,2,0:T(8,128)(2,1)}, u32[]{:S(2)}, u32[]{:S(2)}) async-start(bf16[4,384,2,512]{3,1,2,0:T(8,128)(2,1)} %convolution_convert_fusion), calls=%async_computation | async-start | bytes 6291456 | tf_op jit(solution)/shard_map/all_to_all | solution.py:118
  81.0 52.2 %all-gather.5.cloned.1.call-start = ((), (), s32[]{:S(2)}) async-start(), calls=%async_computation.4 | async-start | bytes 1179648 | tf_op jit(solution)/shard_map/all_gather | solution.py:17
  83.1 328.2 %reduce-scatter.2.cloned.1.call-start = ((), (), s32[]{:S(2)}) async-start(), calls=%async_computation.3 | async-start | bytes 18874368 | tf_op jit(solution)/shard_map/reduce_scatter | solution.py:125
  145.6 15.1 %all-to-all-start.1 = ((bf16[1,384,4,256]{3,1,0,2:T(8,128)(2,1)}), bf16[1,384,4,256]{3,1,0,2:T(8,128)(2,1)S(1)}, u32[]{:S(2)}, u32[]{:S(2)}) async-start(bf16[1,384,4,256]{3,1,0,2:T(8,128)(2,1)} %copy.108), calls=%async_computation.1 | async-start | bytes 1572864 | tf_op jit(solution)/shard_map/all_to_all | solution.py:138
Sparse Core Ops, SparseCore 0:
  10.8 42.9 all-gather.6
  84.6 37.7 all-gather.4
  133.2 278.0 reduce-scatter.1
where the time goes:
time: 419 us; the launch traced here: 418 us
  waiting for transfers between devices  317 us (76%)
  matrix products  48.7 us (12%)
  local copies, waits for them, and re-layouts  17.1 us (4%)
  between operations  14 us (3%)
  other arithmetic  12.3 us (3%)
  starting transfers between devices  8.78 us (2%)
    reduce_scatter x1, waiting for transfers between devices, per_device(): lax.psum_scatter(lax.dot_general(weighted, slot_grads, (((0,), (0,)), (()...  245 us
    all_gather x2, waiting for transfers between devices, prefix(): gathered = lax.all_gather(array.astype(jnp.bfloat16), axis)  35.8 us
    all_to_all x1, waiting for transfers between devices, per_device(): lax.all_to_all(outgoing, 'exp', split_axis=0, concat_axis=3, tiled=True)  34.6 us
    dot_general x1, matrix products, per_device(): lax.dot_general(weighted, slot_grads, (((0,), (0,)), ((), ())), preferred...  10.4 us
    dot_general x1, matrix products, per_device(): lax.dot_general(slot_grads, expert_weight[0], (((1,), (1,)), ((), ())), p...  9.43 us
  transfers between devices with their start and end apart: 5, of which 4 were waited for; matrix products, arithmetic and copies ran while one was open for 13% of the time, Pallas kernels for 0%

commit v1 on v0

v1 whole, which is shorter than its diff:
```python
import functools

import jax
import jax.numpy as jnp
from jax import lax
from jax.experimental import pallas as pl
from jax.experimental.pallas import tpu as pltpu
from jax.sharding import PartitionSpec as P

DH = 128
PAD = 16
MIB = 1 << 20
BF16 = jnp.bfloat16
F32 = jnp.float32


def struct(shape, dtype):
    return jax.ShapeDtypeStruct(shape, dtype)


def call(kernel, out_shape, flops=0, moved=0, limit=16, **options):
    return pl.pallas_call(
        kernel,
        out_shape=out_shape,
        cost_estimate=pl.CostEstimate(flops=flops, bytes_accessed=moved, transcendentals=0),
        compiler_params=pltpu.CompilerParams(vmem_limit_bytes=limit * MIB),
        **options,
    )


def swap(array, axis, mask):
    count = lax.axis_size(axis)
    return lax.ppermute(array, axis, [(place, place ^ mask) for place in range(count)])


def shift(array, axis, step):
    count = lax.axis_size(axis)
    return lax.ppermute(array, axis, [(place, (place + step) % count) for place in range(count)])


def dot(a, b, left, right):
    return lax.dot_general(a, b, (((left,), (right,)), ((), ())), preferred_element_type=F32)


def head(ref, number):
    return ref[:, number * DH : (number + 1) * DH]


def own_states(first, second):
    rows, width = first.shape
    heads = width // DH

    def kernel(a_ref, b_ref, wide_ref, narrow_ref):
        for number in range(heads):
            state = dot(head(a_ref, number), head(b_ref, number), 0, 0)
            wide_ref[number] = state
            narrow_ref[number] = state.astype(BF16)

    return call(
        kernel,
        (struct((heads, DH, DH), F32), struct((heads, DH, DH), BF16)),
        flops=2 * rows * width * DH,
        moved=4 * rows * width,
    )(first, second)


def scan_states(total, sent, backward):
    count = lax.axis_size("seq")
    place = lax.axis_index("seq")
    state = jnp.zeros_like(total)
    mask = 1
    while mask < count:
        received = swap(sent, "seq", mask).astype(F32)
        lower = (place & mask) == 0
        state = state + jnp.where(lower == backward, received, 0.0)
        total = total + received
        sent = total.astype(BF16)
        mask *= 2
    return state


def triangle(size, lower):
    down = lax.broadcasted_iota(jnp.int32, (size, size), 0)
    across = lax.broadcasted_iota(jnp.int32, (size, size), 1)
    return down >= across if lower else down <= across


def intra_keys_values(query, key, value, grad):
    rows, width = query.shape
    heads = width // DH
    tile = rows // 2

    def kernel(q_ref, k_ref, v_ref, g_ref, out_ref):
        keep = triangle(tile, False)
        for down in range(2):
            here = pl.ds(down * tile, tile)
            rest = pl.ds(down * tile, rows - down * tile)
            for left, right, other, place in ((v_ref, g_ref, q_ref, 0), (k_ref, q_ref, g_ref, DH)):
                scores = dot(left[here, :], right[rest, :], 1, 1)
                first = jnp.where(keep, scores[:, :tile], 0.0).astype(BF16)
                if down == 0:
                    first = jnp.concatenate([first, scores[:, tile:].astype(BF16)], axis=1)
                out_ref[0, here, place : place + DH] = dot(first, other[rest, :], 1, 0)

    column = pl.BlockSpec((rows, DH), lambda number: (0, number))
    return call(
        kernel,
        struct((heads, rows, 2 * DH), F32),
        flops=6 * rows * rows * width,
        moved=16 * rows * width,
        grid=(heads,),
        in_specs=[column] * 4,
        out_specs=pl.BlockSpec((1, rows, 2 * DH), lambda number: (number, 0, 0)),
    )(query, key, value, grad)


def halves(state):
    high = state.astype(BF16)
    return high, (state - high.astype(F32)).astype(BF16)


def finish_keys_values(intra, key, value, suffix, number, within):
    rows = key.shape[0]

    def kernel(intra_ref, k_ref, v_ref, s_ref, out_ref):
        high, low = halves(s_ref[0])
        v, k = v_ref[...], k_ref[...]
        by_key = dot(v, high, 1, 1) + dot(v, low, 1, 1)
        by_value = dot(k, high, 1, 0) + dot(k, low, 1, 0)
        out_ref[:, :DH] = (intra_ref[0, :, :DH] + by_key).astype(BF16)
        out_ref[:, DH:] = (intra_ref[0, :, DH:] + by_value).astype(BF16)

    column = pl.BlockSpec((rows, DH), lambda step: (0, number))
    return call(
        kernel,
        struct((rows, 2 * DH), BF16),
        flops=8 * rows * DH * DH,
        moved=12 * rows * DH,
        grid=(1,),
        in_specs=[
            pl.BlockSpec((1, rows, 2 * DH), lambda step: (number, 0, 0)),
            column,
            column,
            pl.BlockSpec((1, DH, DH), lambda step: (within, 0, 0)),
        ],
        out_specs=pl.BlockSpec((rows, 2 * DH), lambda step: (0, 0)),
    )(intra, key, value, suffix)


def query_grads(key, value, grad, prefix):
    rows, width = key.shape
    heads = width // DH
    tile = rows // 2

    def kernel(k_ref, v_ref, g_ref, s_ref, out_ref):
        keep = triangle(tile, True)
        high, low = halves(s_ref[0])
        for down in range(2):
            here = pl.ds(down * tile, tile)
            upto = pl.ds(0, (down + 1) * tile)
            g = g_ref[here, :]
            scores = dot(g, v_ref[upto, :], 1, 1)
            last = jnp.where(keep, scores[:, down * tile :], 0.0).astype(BF16)
            if down:
                last = jnp.concatenate([scores[:, :tile].astype(BF16), last], axis=1)
            intra = dot(last, k_ref[upto, :], 1, 0)
            out_ref[here, :] = (intra + dot(g, high, 1, 1) + dot(g, low, 1, 1)).astype(BF16)

    column = pl.BlockSpec((rows, DH), lambda number: (0, number))
    return call(
        kernel,
        struct((rows, width), BF16),
        flops=3 * rows * rows * width,
        moved=8 * rows * width,
        grid=(heads,),
        in_specs=[column] * 3 + [pl.BlockSpec((1, DH, DH), lambda number: (number, 0, 0))],
        out_specs=column,
    )(key, value, grad, prefix)


def place_of():
    return jnp.stack([lax.axis_index("seq"), lax.axis_index("exp")]).astype(jnp.int32)


def prepare_inputs(inputs, ids, gates, place, size, experts, count):
    rows, wide = inputs.shape
    groups = count // size
    deep = wide // count

    def kernel(place_ref, x_ref, id_ref, gate_ref, *refs):
        outs, turned = refs[:size], refs[size]
        step = DH * 2
        for start in range(0, wide, step):
            turned[start : start + step, :] = x_ref[:, start : start + step].astype(F32).T.astype(BF16)
        which = lax.broadcasted_iota(jnp.int32, (experts, rows), 0)
        weight = jnp.zeros((experts, rows), F32)
        for slot in range(id_ref.shape[0]):
            weight += jnp.where(id_ref[slot : slot + 1, :] == which, gate_ref[slot : slot + 1, :], 0.0)
        parts = []
        for _ in range(3):
            part = weight.astype(BF16).astype(F32)
            parts.append(part)
            weight = weight - part
        tail = PAD - 3 * experts
        if tail:
            parts.append(jnp.zeros((tail, rows), F32))
        packed = jnp.concatenate(parts, axis=0).astype(BF16)
        me = place_ref[0]
        group, low = me // size, me % size
        for member in range(size):
            for hop in range(groups):
                block = lax.rem(group + hop, groups) * size + (low ^ member)
                source = pl.ds(pl.multiple_of(block * deep, deep), deep)
                outs[member][hop * deep : (hop + 1) * deep, :] = turned[source, :]
            outs[member][groups * deep :, :] = packed

    whole = pl.BlockSpec(memory_space=pltpu.VMEM)
    return call(
        kernel,
        [struct((groups * deep + PAD, rows), BF16)] * size,
        moved=4 * rows * wide,
        in_specs=[pl.BlockSpec(memory_space=pltpu.SMEM), whole, whole, whole],
        out_specs=[whole] * size,
        scratch_shapes=[pltpu.VMEM((wide, rows), BF16)],
    )(place, inputs, ids, gates)


def weigh_inputs(messages, place, experts):
    size = len(messages)
    deep, rows = messages[0].shape
    deep -= PAD

    def kernel(place_ref, *refs):
        out_ref = refs[size]
        expert = pl.program_id(0) ^ place_ref[1]
        for member in range(size):
            parts = refs[member][deep:, :].astype(F32)
            row = lax.broadcasted_iota(jnp.int32, parts.shape, 0)
            mine = (row < 3 * experts) & (lax.rem(row, experts) == expert)
            weight = jnp.sum(jnp.where(mine, parts, 0.0), axis=0, keepdims=True)
            out_ref[0, :, member * rows : (member + 1) * rows] = (
                refs[member][:deep, :].astype(F32) * weight
            ).astype(BF16)

    return call(
        kernel,
        struct((experts, deep, size * rows), BF16),
        flops=experts * deep * size * rows,
        moved=2 * (experts + 1) * deep * size * rows,
        grid_spec=pltpu.PrefetchScalarGridSpec(
            num_scalar_prefetch=1,
            grid=(experts,),
            in_specs=[pl.BlockSpec((deep + PAD, rows), lambda step, ref: (0, 0))] * size,
            out_specs=pl.BlockSpec((1, deep, size * rows), lambda step, ref: (step, 0, 0)),
        ),
    )(place, *messages)


def weight_product(weighted, blocks, groups):
    experts, deep, _ = weighted.shape
    rows, wide = blocks[0].shape
    size = len(blocks)
    part = deep // groups

    def kernel(w_ref, *refs):
        total = None
        for member in range(size):
            term = dot(w_ref[0, :, member * rows : (member + 1) * rows], refs[member][...], 1, 0)
            total = term if total is None else total + term
        refs[size][0] = total[:part]
        for hop in range(1, groups):
            refs[size + hop][0] = total[hop * part : (hop + 1) * part].astype(BF16)

    piece = pl.BlockSpec((1, part, wide), lambda step: (step, 0, 0))
    results = call(
        kernel,
        [struct((experts, part, wide), F32 if hop == 0 else BF16) for hop in range(groups)],
        flops=2 * experts * deep * size * rows * wide,
        moved=2 * experts * deep * size * rows + 2 * size * rows * wide + 4 * experts * deep * wide,
        grid=(experts,),
        in_specs=[pl.BlockSpec((1, deep, size * rows), lambda step: (step, 0, 0))]
        + [pl.BlockSpec((rows, wide), lambda step: (0, 0))] * size,
        out_specs=[piece] * groups,
    )(weighted, *blocks)
    return results[0], results[1:]


def add_partials(own, others):
    experts, part, wide = own.shape

    def kernel(own_ref, *refs):
        ins, outs = refs[: len(others)], refs[len(others) :]
        for expert in range(experts):
            total = own_ref[expert]
            for ref in ins:
                total = total + ref[expert].astype(F32)
            outs[expert][...] = total.astype(outs[expert].dtype)

    return call(
        kernel,
        [struct((part, wide), BF16 if expert else F32) for expert in range(experts)],
        moved=8 * experts * part * wide,
    )(own, *others)


def place_weight_grad(pieces, place, width):
    heads, experts = len(pieces), len(pieces[0])
    part = pieces[0][0].shape[0]

    def kernel(place_ref, *refs):
        out_ref = refs[heads * experts]
        for number in range(heads):
            for hop in range(experts):
                piece = refs[number * experts + hop]
                start = ((place_ref[1] ^ hop) * heads + number) * DH
                for side in range(2):
                    columns = pl.ds(pl.multiple_of(start + side * (width // 2), DH), DH)
                    out_ref[0, :, columns] = head(piece, side).astype(F32)

    whole = pl.BlockSpec(memory_space=pltpu.VMEM)
    return call(
        kernel,
        struct((1, part, width), F32),
        moved=6 * part * width,
        in_specs=[pl.BlockSpec(memory_space=pltpu.SMEM)] + [whole] * (heads * experts),
        out_specs=whole,
    )(place, *[piece for row in pieces for piece in row])


def place_keys_values(chunks):
    heads = len(chunks)
    rows = chunks[0].shape[0]

    def kernel(*refs):
        for number in range(heads):
            for side in range(2):
                refs[heads + side][:, number * DH : (number + 1) * DH] = head(refs[number], side)

    return call(kernel, [struct((rows, heads * DH), BF16)] * 2, moved=8 * rows * heads * DH)(*chunks)


def input_products(pieces, expert_weight, gate, place):
    experts, heads = len(pieces), len(pieces[0])
    rows = pieces[0][0].shape[0]
    _, wide, width = expert_weight.shape
    part = wide // experts

    def kernel(place_ref, w_ref, gate_ref, *refs):
        out_ref = refs[experts * heads]
        total = None
        for hop in range(experts):
            for number in range(heads):
                start = ((place_ref[1] ^ hop) * heads + number) * DH
                sides = [
                    w_ref[0, :, pl.ds(pl.multiple_of(start + side * (width // 2), DH), DH)]
                    for side in range(2)
                ]
                term = dot(refs[hop * heads + number][...], jnp.concatenate(sides, axis=1), 1, 1)
                total = term if total is None else total + term
        out_ref[0] = gate_ref[...] * total

    fixed = pl.BlockSpec((rows, 2 * DH), lambda step, ref: (0, 0))
    return call(
        kernel,
        struct((experts, rows, part), F32),
        flops=2 * rows * wide * width,
        moved=2 * wide * width + 2 * rows * width + 4 * rows * wide,
        limit=40,
        grid_spec=pltpu.PrefetchScalarGridSpec(
            num_scalar_prefetch=1,
            grid=(experts,),
            in_specs=[
                pl.BlockSpec((1, part, width), lambda step, ref: (0, step ^ ref[1], 0)),
                pl.BlockSpec((rows, 1), lambda step, ref: (0, 0)),
            ]
            + [fixed] * (experts * heads),
            out_specs=pl.BlockSpec((1, rows, part), lambda step, ref: (step, 0, 0)),
        ),
    )(place, expert_weight, gate, *[piece for row in pieces for piece in row])


def gather_exp(chunk, experts):
    held = [chunk]
    mask = experts // 2
    found = {0: chunk}
    while mask:
        for hop, array in list(found.items()):
            found[hop | mask] = swap(array, "exp", mask)
        mask //= 2
    return [found[hop] for hop in range(experts)]


def scatter_exp(parts):
    count = parts.shape[0]
    held = {hop: parts[hop] for hop in range(count)}
    mask = 1
    while mask < count:
        leaving = [hop for hop in sorted(held) if hop & mask]
        staying = [hop for hop in sorted(held) if not hop & mask]
        packed = jnp.stack([held[hop].astype(BF16) for hop in leaving])
        arrived = swap(packed, "exp", mask).astype(F32)
        held = {hop: held[hop] + arrived[at] for at, hop in enumerate(staying)}
        mask *= 2
    return held[0]


def per_device(query, key, value, grad, inputs, expert_ids, route_gates, expert_weight):
    rows, width = query.shape
    heads = width // DH
    experts = lax.axis_size("exp")
    count = lax.axis_size("seq")
    size = 4 if count % 4 == 0 else 1
    groups = count // size
    place = place_of()

    total, sent = own_states(query, grad)
    half = max(1, heads // 2)
    suffixes = [
        scan_states(total[at : at + half], sent[at : at + half], True) for at in range(0, heads, half)
    ]
    prefix = scan_states(*own_states(key, value), False)
    intra = intra_keys_values(query, key, value, grad)
    messages = prepare_inputs(
        inputs, expert_ids.T, route_gates.T, place, size, experts, count
    )
    messages = [messages[0]] + [swap(messages[mask], "seq", mask) for mask in range(1, size)]
    weighted = weigh_inputs(messages, place, experts)

    chunks = [
        finish_keys_values(intra, key, value, suffixes[number // half], number, number % half)
        for number in range(heads)
    ]
    pieces = []
    gathered = []
    for chunk in chunks:
        blocks = [chunk]
        if size == 4:
            across = swap(chunk, "seq", 2)
            blocks = [chunk, swap(chunk, "seq", 1), across, swap(across, "seq", 1)]
        gathered.append(gather_exp(chunk, experts))
        own, others = weight_product(weighted, blocks, groups)
        others = [shift(other, "seq", size * (hop + 1)) for hop, other in enumerate(others)]
        parts = add_partials(own, others)
        pieces.append([parts[0]] + [swap(parts[hop], "exp", hop) for hop in range(1, experts)])

    gradient_of_queries = query_grads(key, value, grad, prefix)
    gradient_of_keys, value_grad = place_keys_values(chunks)
    mine = expert_ids == lax.axis_index("exp")
    gate = jnp.sum(jnp.where(mine, route_gates, 0.0), axis=1, keepdims=True)
    returned = input_products(
        [[gathered[number][hop] for number in range(heads)] for hop in range(experts)],
        expert_weight,
        gate,
        place,
    )
    input_grad = scatter_exp(returned).astype(BF16)
    weight_grad = place_weight_grad(pieces, place, expert_weight.shape[2])
    return gradient_of_queries, gradient_of_keys, value_grad, input_grad, weight_grad


def solution(mesh):
    return jax.shard_map(
        per_device,
        mesh=mesh,
        in_specs=(
            P("seq", "exp"),
            P("seq", "exp"),
            P("seq", "exp"),
            P("seq", "exp"),
            P("seq", None),
            P("seq", None),
            P("seq", None),
            P("exp", None, None),
        ),
        out_specs=(
            P("seq", "exp"),
            P("seq", "exp"),
            P("seq", "exp"),
            P("seq", "exp"),
            P("exp", "seq", None),
        ),
        check_vma=False,
    )
```

time: 419 us -> 190 us (0.45)
  waiting for transfers between devices: 317 us -> 67.7 us
  matrix products: 48.7 us -> 0 us
  starting transfers between devices: 8.78 us -> 52.5 us
  Pallas kernels: 0 us -> 38.7 us
  between operations: 14 us -> 1.13 us
  other arithmetic: 12.3 us -> 5.54 us
  local copies, waits for them, and re-layouts: 17.1 us -> 23.3 us
    reduce_scatter x1 -> x0, waiting for transfers between devices: 245 us -> none  [per_device(): lax.psum_scatter(lax.dot_general(weighted, slot_grads, (((0,), (0,)), (()...]
    ppermute x0 -> x54, waiting for transfers between devices: none -> 67.7 us  [the longest x50 37.6 us: swap(): lax.ppermute(array, axis, [(place, place ^ mask) for place in range(count)])]
    ppermute x0 -> x54, starting transfers between devices: none -> 52.5 us  [the longest x50 48.6 us: swap(): lax.ppermute(array, axis, [(place, place ^ mask) for place in range(count)])]
    dot_general x12 -> x0, matrix products: 48.7 us -> none  [the longest x1 10.4 us: per_device(): lax.dot_general(weighted, slot_grads, (((0,), (0,)), ((), ())), preferred...]
    pallas_call x0 -> x21, Pallas kernels: none -> 38.7 us  [the longest x4 10.2 us: weight_product(): call(kernel, [struct((experts, part, wide), F32 if hop == 0 else BF16) fo...]
    all_gather x2 -> x0, waiting for transfers between devices: 35.8 us -> none  [prefix(): gathered = lax.all_gather(array.astype(jnp.bfloat16), axis)]
    all_to_all x2 -> x0, waiting for transfers between devices: 35.6 us -> none  [the longest x1 34.6 us: per_device(): lax.all_to_all(outgoing, 'exp', split_axis=0, concat_axis=3, tiled=True)]
    unnamed x16 -> x102, local copies, waits for them, and re-layouts: 5.99 us -> 22.4 us
  transfers between devices with their start and end apart: 5 -> 54, of which waited for: 4 -> 16; matrix products, arithmetic and copies ran while one was open for 13% -> 3% of each run, Pallas kernels for 0% -> 20%
where the time goes in v1:
time: 190 us; the launch traced here: 189 us
  waiting for transfers between devices  67.7 us (36%)
  starting transfers between devices  52.5 us (28%)
  Pallas kernels  38.7 us (20%)
  local copies, waits for them, and re-layouts  23.3 us (12%)
  other arithmetic  5.54 us (3%)
    ppermute x50, starting transfers between devices, swap(): lax.ppermute(array, axis, [(place, place ^ mask) for place in range(count)])  48.6 us
    ppermute x50, waiting for transfers between devices, swap(): lax.ppermute(array, axis, [(place, place ^ mask) for place in range(count)])  37.6 us
    ppermute x4, waiting for transfers between devices, shift(): lax.ppermute(array, axis, [(place, (place + step) % count) for place in r...  30.2 us
    unnamed x102, local copies, waits for them, and re-layouts  22.4 us
    pallas_call x4, Pallas kernels, weight_product(): call(kernel, [struct((experts, part, wide), F32 if hop == 0 else BF16) fo...  10.2 us
    pallas_call x1, Pallas kernels, input_products(): call(kernel, struct((experts, rows, part), F32), flops=2 * rows * wide *...  8.35 us
    ppermute x4, starting transfers between devices, shift(): lax.ppermute(array, axis, [(place, (place + step) % count) for place in r...  3.91 us
  transfers between devices with their start and end apart: 54, of which 16 were waited for; matrix products, arithmetic and copies ran while one was open for 3% of the time, Pallas kernels for 20%

profile of v1, /device:TPU:0, one launch (start us, length us, event | category | flops | bytes accessed | tf_op | source)
XLA Modules:
  0.0 188.9 jit_solution(9616294498264095534)
XLA Ops:
  0.7 1.1 copy-done.4
  1.8 1.0 copy-done.10
  3.2 3.0 %collective-permute-start.3 = (bf16[2,128,128]{2,1,0:T(8,128)(2,1)S(1)}, bf16[2,128,128]{2,1,0:T(8,128)(2,1)S(1)}, u32[]{:S(2)}, u32[]{:S(2)}) collective-permute-start(bf16[2,128,128]{2,1,0:T(8,128)(2,1)S(1)} %get-tuple-element.80), channel_id=1, source_target_pairs={{0,4},{4,0},{8,12},{12,8},{16,20},{20,16},{24,28},{28,24},{1,5},{5... | collective-permute-start | bytes 196616 | tf_op jit(solution)/shard_map/ppermute | solution.py:33
  6.3 1.0 copy-done
  7.4 1.0 copy-done.2
  8.8 2.0 %collective-permute-start = (bf16[4,128,128]{2,1,0:T(8,128)(2,1)S(1)}, bf16[4,128,128]{2,1,0:T(8,128)(2,1)S(1)}, u32[]{:S(2)}, u32[]{:S(2)}) collective-permute-start(bf16[4,128,128]{2,1,0:T(8,128)(2,1)S(1)} %get-tuple-element.39), channel_id=1, source_target_pairs={{0,4},{4,0},{8,12},{12,8},{16,20},{20,16},{24,28},{28,24},{1,5},{5... | collective-permute-start | bytes 393224 | tf_op jit(solution)/shard_map/ppermute | solution.py:33
  11.5 1.6 collective-permute-start.4
  13.6 1.2 copy-done.12
  14.8 1.8 shard_map.129
  17.3 1.6 collective-permute-start.24
  18.9 1.2 collective-permute-start.25
  20.2 2.7 %collective-permute-start.5 = (bf16[2,128,128]{2,1,0:T(8,128)(2,1)S(1)}, bf16[2,128,128]{2,1,0:T(8,128)(2,1)S(1)}, u32[]{:S(2)}, u32[]{:S(2)}) collective-permute-start(bf16[2,128,128]{2,1,0:T(8,128)(2,1)S(1)} %get-tuple-element.76), channel_id=1, source_target_pairs={{0,16},{4,20},{8,24},{12,28},{16,0},{20,4},{24,8},{28,12},{1,17},{... | collective-permute-start | bytes 196616 | tf_op jit(solution)/shard_map/ppermute | solution.py:33
  22.8 3.8 %shard_map.121.intra_ref = f32[4,512,256]{2,1,0:T(8,128)S(1)} custom-call(bf16[512,512]{1,0:T(8,128)(2,1)S(1)} %copy-done.11, bf16[512,512]{1,0:T(8,128)(2,1)S(1)} %copy-done.1, bf16[512,512]{1,0:T(8,128)(2,1)S(1)} %copy-done.3, bf16[512,512]{1,0:T(8,128)(2,1)S(1)} %copy-done.5), custom_call_target="tpu_custom_call" | custom-call | flops 805306368 | bytes 4194304 | tf_op jit(solution)/shard_map/pallas_call | solution.py:106
  26.6 4.1 %collective-permute-done.5 = bf16[2,128,128]{2,1,0:T(8,128)(2,1)S(1)} collective-permute-done((bf16[2,128,128]{2,1,0:T(8,128)(2,1)S(1)}, bf16[2,128,128]{2,1,0:T(8,128)(2,1)S(1)}, u32[]{:S(2)}, u32[]{:S(2)}) %collective-permute-start.5) | collective-permute-done | bytes 65568 | tf_op jit(solution)/shard_map/ppermute | solution.py:33
  30.6 3.4 %collective-permute-start.8 = (bf16[2,128,128]{2,1,0:T(8,128)(2,1)S(1)}, bf16[2,128,128]{2,1,0:T(8,128)(2,1)S(1)}, u32[]{:S(2)}, u32[]{:S(2)}) collective-permute-start(bf16[2,128,128]{2,1,0:T(8,128)(2,1)S(1)} %get-tuple-element.75), channel_id=1, source_target_pairs={{0,16},{4,20},{8,24},{12,28},{16,0},{20,4},{24,8},{28,12},{1,17},{... | collective-permute-start | bytes 196616 | tf_op jit(solution)/shard_map/ppermute | solution.py:33
  34.1 2.2 %collective-permute-done.8 = bf16[2,128,128]{2,1,0:T(8,128)(2,1)S(1)} collective-permute-done((bf16[2,128,128]{2,1,0:T(8,128)(2,1)S(1)}, bf16[2,128,128]{2,1,0:T(8,128)(2,1)S(1)}, u32[]{:S(2)}, u32[]{:S(2)}) %collective-permute-start.8) | collective-permute-done | bytes 65568 | tf_op jit(solution)/shard_map/ppermute | solution.py:33
  36.7 1.0 shard_map.124.refs_1_.refs_0_
  37.7 1.0 shard_map.125.refs_2_.refs_0_
  40.8 1.5 collective-permute-start.13
  44.3 1.5 collective-permute-start.15
  47.7 3.0 %collective-permute-start.27 = (bf16[512,256]{1,0:T(8,128)(2,1)S(1)}, bf16[512,256]{1,0:T(8,128)(2,1)}, u32[]{:S(2)}, u32[]{:S(2)}) collective-permute-start(bf16[512,256]{1,0:T(8,128)(2,1)S(1)} %shard_map.123.refs_0_), channel_id=1, source_target_pairs={{0,8},{4,12},{8,0},{12,4},{16,24},{20,28},{24,16},{28,20},{1,9},{5... | collective-permute-start | bytes 786440 | tf_op jit(solution)/shard_map/ppermute | solution.py:33
  50.7 4.9 %collective-permute-done.14.refs_9_ = bf16[512,256]{1,0:T(8,128)(2,1)S(1)} collective-permute-done((bf16[512,256]{1,0:T(8,128)(2,1)}, bf16[512,256]{1,0:T(8,128)(2,1)S(1)}, u32[]{:S(2)}, u32[]{:S(2)}) %collective-permute-start.14) | collective-permute-done | bytes 262176 | tf_op jit(solution)/shard_map/ppermute | solution.py:33
  55.6 5.6 %collective-permute-done.15.refs_10_ = bf16[512,256]{1,0:T(8,128)(2,1)S(1)} collective-permute-done((bf16[512,256]{1,0:T(8,128)(2,1)}, bf16[512,256]{1,0:T(8,128)(2,1)S(1)}, u32[]{:S(2)}, u32[]{:S(2)}) %collective-permute-start.15) | collective-permute-done | bytes 262176 | tf_op jit(solution)/shard_map/ppermute | solution.py:33
  61.2 4.7 %collective-permute-done.16.refs_11_ = bf16[512,256]{1,0:T(8,128)(2,1)S(1)} collective-permute-done((bf16[512,256]{1,0:T(8,128)(2,1)S(1)}, bf16[512,256]{1,0:T(8,128)(2,1)S(1)}, u32[]{:S(2)}, u32[]{:S(2)}) %collective-permute-start.16) | collective-permute-done | bytes 262176 | tf_op jit(solution)/shard_map/ppermute | solution.py:33
  67.9 2.4 %shard_map.130.w_ref = bf16[4,256,2048]{2,1,0:T(8,128)(2,1)S(1)} custom-call(s32[2]{0:T(128)S(1)} %pad_add_fusion.place_ref, bf16[272,512]{1,0:T(8,128)(2,1)S(1)} %get-tuple-element.45.refs_0_, bf16[272,512]{1,0:T(8,128)(2,1)} %collective-permute-done.23.refs_1_, bf16[272,512]{1,0:T(8,128)(2,1)} %collective-permute-done.24.refs_2_, ...), custom_call_target="tpu_custom_call" | custom-call | flops 2097152 | bytes 5242880 | tf_op jit(solution)/shard_map/pallas_call | solution.py:245
  70.4 1.4 collective-permute-start.26
  72.5 3.0 %collective-permute-start.34 = (bf16[512,256]{1,0:T(8,128)(2,1)}, bf16[512,256]{1,0:T(8,128)(2,1)S(1)}, u32[]{:S(2)}, u32[]{:S(2)}) collective-permute-start(bf16[512,256]{1,0:T(8,128)(2,1)} %shard_map.124.refs_1_.refs_0_), channel_id=1, source_target_pairs={{0,8},{4,12},{8,0},{12,4},{16,24},{20,28},{24,16},{28,20},{1,9},{5... | collective-permute-start | bytes 786440 | tf_op jit(solution)/shard_map/ppermute | solution.py:33
  75.6 1.4 collective-permute-start.28
  77.9 0.9 copy-done.41
  78.9 0.9 copy-done.43
  79.8 0.9 copy-done.45
  80.8 8.4 %shard_map.128 = f32[4,512,256]{2,1,0:T(8,128)S(1)} custom-call(s32[2]{0:T(128)S(1)} %pad_add_fusion.place_ref, bf16[1,1024,4096]{2,1,0:T(8,128)(2,1)} %w_ref.1, f32[512,1]{1,0:T(8,128)S(1)} %copy-done.29, bf16[512,256]{1,0:T(8,128)(2,1)S(1)} %shard_map.123.refs_0_, bf16[512,256]{1,0:T(8,128)(2,1)} %shard_map.124.refs_1_.refs_0_, ...), custom_call_target="tpu_custom_call" | custom-call | flops 4294967296 | bytes 14680064 | tf_op jit(solution)/shard_map/pallas_call | solution.py:363
  89.2 2.0 %collective-permute-start.48 = (bf16[512,256]{1,0:T(8,128)(2,1)S(1)}, bf16[512,256]{1,0:T(8,128)(2,1)S(1)}, u32[]{:S(2)}, u32[]{:S(2)}) collective-permute-start(bf16[512,256]{1,0:T(8,128)(2,1)S(1)} %copy-done.8), channel_id=1, source_target_pairs={{0,8},{4,12},{8,0},{12,4},{16,24},{20,28},{24,16},{28,20},{1,9},{5... | collective-permute-start | bytes 786440 | tf_op jit(solution)/shard_map/ppermute | solution.py:33
  92.0 1.4 collective-permute-start.40
  94.1 2.8 %shard_map.131 = (f32[4,128,256]{2,1,0:T(8,128)S(1)}, bf16[4,128,256]{2,1,0:T(8,128)(2,1)S(1)}) custom-call(bf16[4,256,2048]{2,1,0:T(8,128)(2,1)S(1)} %shard_map.130.w_ref, bf16[512,256]{1,0:T(8,128)(2,1)S(1)} %shard_map.123.refs_0_, bf16[512,256]{1,0:T(8,128)(2,1)S(1)} %collective-permute-done.26.refs_1_, bf16[512,256]{1,0:T(8,128)(2,1)} %collective-permute-done.27.refs_2_, ...), custom_call_target="tpu_custom_call" | custom-call | flops 1073741824 | bytes 6291456 | tf_op jit(solution)/shard_map/pallas_call | solution.py:275
  96.9 1.2 collective-permute-start.1
  98.6 2.0 %collective-permute-done.35.refs_3_ = bf16[512,256]{1,0:T(8,128)(2,1)S(1)} collective-permute-done((bf16[512,256]{1,0:T(8,128)(2,1)S(1)}, bf16[512,256]{1,0:T(8,128)(2,1)S(1)}, u32[]{:S(2)}, u32[]{:S(2)}) %collective-permute-start.35) | collective-permute-done | bytes 262176 | tf_op jit(solution)/shard_map/ppermute | solution.py:33
  101.2 2.8 %shard_map.133 = (f32[4,128,256]{2,1,0:T(8,128)S(1)}, bf16[4,128,256]{2,1,0:T(8,128)(2,1)S(1)}) custom-call(bf16[4,256,2048]{2,1,0:T(8,128)(2,1)S(1)} %shard_map.130.w_ref, bf16[512,256]{1,0:T(8,128)(2,1)} %shard_map.124.refs_1_.refs_0_, bf16[512,256]{1,0:T(8,128)(2,1)S(1)} %collective-permute-done.33.refs_1_, ...), custom_call_target="tpu_custom_call" | custom-call | flops 1073741824 | bytes 6291456 | tf_op jit(solution)/shard_map/pallas_call | solution.py:275
  106.1 5.6 %collective-permute-done.42.refs_3_ = bf16[512,256]{1,0:T(8,128)(2,1)S(1)} collective-permute-done((bf16[512,256]{1,0:T(8,128)(2,1)S(1)}, bf16[512,256]{1,0:T(8,128)(2,1)S(1)}, u32[]{:S(2)}, u32[]{:S(2)}) %collective-permute-start.42) | collective-permute-done | bytes 262176 | tf_op jit(solution)/shard_map/ppermute | solution.py:33
  111.8 2.8 %shard_map.135 = (f32[4,128,256]{2,1,0:T(8,128)S(1)}, bf16[4,128,256]{2,1,0:T(8,128)(2,1)S(1)}) custom-call(bf16[4,256,2048]{2,1,0:T(8,128)(2,1)S(1)} %shard_map.130.w_ref, bf16[512,256]{1,0:T(8,128)(2,1)} %shard_map.125.refs_2_.refs_0_, bf16[512,256]{1,0:T(8,128)(2,1)S(1)} %collective-permute-done.40.refs_1_, ...), custom_call_target="tpu_custom_call" | custom-call | flops 1073741824 | bytes 6291456 | tf_op jit(solution)/shard_map/pallas_call | solution.py:275
  115.4 2.0 %collective-permute-done.47.refs_1_ = bf16[512,256]{1,0:T(8,128)(2,1)S(1)} collective-permute-done((bf16[512,256]{1,0:T(8,128)(2,1)S(1)}, bf16[512,256]{1,0:T(8,128)(2,1)S(1)}, u32[]{:S(2)}, u32[]{:S(2)}) %collective-permute-start.47) | collective-permute-done | bytes 262176 | tf_op jit(solution)/shard_map/ppermute | solution.py:33
  118.3 2.5 %collective-permute-done.49.refs_3_ = bf16[512,256]{1,0:T(8,128)(2,1)S(1)} collective-permute-done((bf16[512,256]{1,0:T(8,128)(2,1)S(1)}, bf16[512,256]{1,0:T(8,128)(2,1)S(1)}, u32[]{:S(2)}, u32[]{:S(2)}) %collective-permute-start.49) | collective-permute-done | bytes 262176 | tf_op jit(solution)/shard_map/ppermute | solution.py:33
  121.4 1.8 shard_map.137
  123.3 2.4 %collective-permute-start.50 = (bf16[4,128,256]{2,1,0:T(8,128)(2,1)S(1)}, bf16[4,128,256]{2,1,0:T(8,128)(2,1)S(1)}, u32[]{:S(2)}, u32[]{:S(2)}) collective-permute-start(bf16[4,128,256]{2,1,0:T(8,128)(2,1)S(1)} %get-tuple-element.68), channel_id=1, source_target_pairs={{0,16},{4,20},{8,24},{12,28},{16,0},{20,4},{24,8},{28,12},{1,17},{... | collective-permute-start | bytes 786440 | tf_op jit(solution)/shard_map/ppermute | solution.py:38
  126.4 16.2 %collective-permute-done.29.refs_0_ = bf16[4,128,256]{2,1,0:T(8,128)(2,1)S(1)} collective-permute-done((bf16[4,128,256]{2,1,0:T(8,128)(2,1)S(1)}, bf16[4,128,256]{2,1,0:T(8,128)(2,1)S(1)}, u32[]{:S(2)}, u32[]{:S(2)}) %collective-permute-start.29) | collective-permute-done | bytes 262176 | tf_op jit(solution)/shard_map/ppermute | solution.py:38
  143.3 6.3 %collective-permute-done.36.refs_0_ = bf16[4,128,256]{2,1,0:T(8,128)(2,1)S(1)} collective-permute-done((bf16[4,128,256]{2,1,0:T(8,128)(2,1)S(1)}, bf16[4,128,256]{2,1,0:T(8,128)(2,1)S(1)}, u32[]{:S(2)}, u32[]{:S(2)}) %collective-permute-start.36) | collective-permute-done | bytes 262176 | tf_op jit(solution)/shard_map/ppermute | solution.py:38
  150.3 4.9 %collective-permute-done.43.refs_0_ = bf16[4,128,256]{2,1,0:T(8,128)(2,1)S(1)} collective-permute-done((bf16[4,128,256]{2,1,0:T(8,128)(2,1)S(1)}, bf16[4,128,256]{2,1,0:T(8,128)(2,1)S(1)}, u32[]{:S(2)}, u32[]{:S(2)}) %collective-permute-start.43) | collective-permute-done | bytes 262176 | tf_op jit(solution)/shard_map/ppermute | solution.py:38
  155.9 1.5 collective-permute-start.31
  157.4 2.8 %collective-permute-done.50.refs_0_ = bf16[4,128,256]{2,1,0:T(8,128)(2,1)S(1)} collective-permute-done((bf16[4,128,256]{2,1,0:T(8,128)(2,1)S(1)}, bf16[4,128,256]{2,1,0:T(8,128)(2,1)S(1)}, u32[]{:S(2)}, u32[]{:S(2)}) %collective-permute-start.50) | collective-permute-done | bytes 262176 | tf_op jit(solution)/shard_map/ppermute | solution.py:38
  160.9 0.9 copy-done.9
  161.9 2.3 %shard_map.127 = (bf16[512,512]{1,0:T(8,128)(2,1)}, bf16[512,512]{1,0:T(8,128)(2,1)}) custom-call(bf16[512,256]{1,0:T(8,128)(2,1)S(1)} %shard_map.123.refs_0_, bf16[512,256]{1,0:T(8,128)(2,1)} %shard_map.124.refs_1_.refs_0_, bf16[512,256]{1,0:T(8,128)(2,1)} %shard_map.125.refs_2_.refs_0_, bf16[512,256]{1,0:T(8,128)(2,1)S(1)} %copy-done.9), custom_call_target="tpu_custom_call" | custom-call | bytes 2097152 | tf_op jit(solution)/shard_map/pallas_call | solution.py:339
  164.1 1.0 copy-done.16
  165.2 0.9 copy-done.26
  167.2 1.0 copy-done.28
  168.3 1.7 collective-permute-start.37
  170.0 1.1 convert_element_type.80
  173.9 1.0 collective-permute-start.46
  174.9 1.2 collective-permute-done.38.refs_6_
  176.1 1.5 collective-permute-start.52
  177.6 1.4 collective-permute-start.53
  179.3 1.0 fusion.4.s_ref
  180.3 3.1 %shard_map.120 = bf16[512,512]{1,0:T(8,128)(2,1)} custom-call(bf16[512,512]{1,0:T(8,128)(2,1)S(1)} %copy-done.1, bf16[512,512]{1,0:T(8,128)(2,1)S(1)} %copy-done.3, bf16[512,512]{1,0:T(8,128)(2,1)S(1)} %copy-done.6, f32[4,128,128]{2,1,0:T(8,128)S(1)} %fusion.4.s_ref), custom_call_target="tpu_custom_call" | custom-call | flops 402653184 | bytes 2097152 | tf_op jit(solution)/shard_map/pallas_call | solution.py:170
  183.4 2.5 %shard_map.139 = f32[1,128,4096]{2,1,0:T(8,128)} custom-call(s32[2]{0:T(128)S(1)} %pad_add_fusion.place_ref, f32[128,256]{1,0:T(8,128)S(1)} %get-tuple-element.51.refs_0_, bf16[128,256]{1,0:T(8,128)(2,1)} %collective-permute-done.30.refs_1_, bf16[128,256]{1,0:T(8,128)(2,1)} %collective-permute-done.31.refs_2_, ...), custom_call_target="tpu_custom_call" | custom-call | bytes 3145728 | tf_op jit(solution)/shard_map/pallas_call | solution.py:321
  186.0 2.1 %collective-permute-done.22 = bf16[1,512,256]{2,1,0:T(8,128)(2,1)S(1)} collective-permute-done((bf16[1,512,256]{2,1,0:T(8,128)(2,1)S(1)}, bf16[1,512,256]{2,1,0:T(8,128)(2,1)S(1)}, u32[]{:S(2)}, u32[]{:S(2)}) %collective-permute-start.22) | collective-permute-done | bytes 262176 | tf_op jit(solution)/shard_map/ppermute | solution.py:33
  (184 shorter events, 28.4 us)
Async XLA Ops:
  0.6 22.2 %copy-start.1 = (bf16[512,512]{1,0:T(8,128)(2,1)S(1)}, bf16[512,512]{1,0:T(8,128)(2,1)}, u32[]{:S(2)}) copy-start(bf16[512,512]{1,0:T(8,128)(2,1)} %k_ref.11) | copy-start | bytes 1572868
  0.6 22.2 %copy-start.3 = (bf16[512,512]{1,0:T(8,128)(2,1)S(1)}, bf16[512,512]{1,0:T(8,128)(2,1)}, u32[]{:S(2)}) copy-start(bf16[512,512]{1,0:T(8,128)(2,1)} %v_ref.11) | copy-start | bytes 1572868
  3.2 7.6 %collective-permute-start.3 = (bf16[2,128,128]{2,1,0:T(8,128)(2,1)S(1)}, bf16[2,128,128]{2,1,0:T(8,128)(2,1)S(1)}, u32[]{:S(2)}, u32[]{:S(2)}) collective-permute-start(bf16[2,128,128]{2,1,0:T(8,128)(2,1)S(1)} %get-tuple-element.80), channel_id=1, source_target_pairs={{0,4},{4,0},{8,12},{12,8},{16,20},{20,16},{24,28},{28,24},{1,5},{5... | collective-permute-start | bytes 196616 | tf_op jit(solution)/shard_map/ppermute | solution.py:33
  6.2 4.5 %collective-permute-start.6 = (bf16[2,128,128]{2,1,0:T(8,128)(2,1)S(1)}, bf16[2,128,128]{2,1,0:T(8,128)(2,1)S(1)}, u32[]{:S(2)}, u32[]{:S(2)}) collective-permute-start(bf16[2,128,128]{2,1,0:T(8,128)(2,1)S(1)} %get-tuple-element.79), channel_id=1, source_target_pairs={{0,4},{4,0},{8,12},{12,8},{16,20},{20,16},{24,28},{28,24},{1,5},{5... | collective-permute-start | bytes 196616 | tf_op jit(solution)/shard_map/ppermute | solution.py:33
  8.4 14.4 %copy-start.5 = (bf16[512,512]{1,0:T(8,128)(2,1)S(1)}, bf16[512,512]{1,0:T(8,128)(2,1)}, u32[]{:S(2)}) copy-start(bf16[512,512]{1,0:T(8,128)(2,1)} %b_ref.3) | copy-start | bytes 1572868
  8.4 14.4 %copy-start.11 = (bf16[512,512]{1,0:T(8,128)(2,1)S(1)}, bf16[512,512]{1,0:T(8,128)(2,1)}, u32[]{:S(2)}) copy-start(bf16[512,512]{1,0:T(8,128)(2,1)} %a_ref.3) | copy-start | bytes 1572868
  8.8 58.1 %copy-start.13 = (f32[4,128,128]{2,1,0:T(8,128)}, f32[4,128,128]{2,1,0:T(8,128)S(1)}, u32[]{:S(2)}) copy-start(f32[4,128,128]{2,1,0:T(8,128)S(1)} %get-tuple-element.40) | copy-start | bytes 786436
  8.8 29.9 %collective-permute-start = (bf16[4,128,128]{2,1,0:T(8,128)(2,1)S(1)}, bf16[4,128,128]{2,1,0:T(8,128)(2,1)S(1)}, u32[]{:S(2)}, u32[]{:S(2)}) collective-permute-start(bf16[4,128,128]{2,1,0:T(8,128)(2,1)S(1)} %get-tuple-element.39), channel_id=1, source_target_pairs={{0,4},{4,0},{8,12},{12,8},{16,20},{20,16},{24,28},{28,24},{1,5},{5... | collective-permute-start | bytes 393224 | tf_op jit(solution)/shard_map/ppermute | solution.py:33
  11.5 7.4 %collective-permute-start.4 = (bf16[2,128,128]{2,1,0:T(8,128)(2,1)}, bf16[2,128,128]{2,1,0:T(8,128)(2,1)S(1)}, u32[]{:S(2)}, u32[]{:S(2)}) collective-permute-start(bf16[2,128,128]{2,1,0:T(8,128)(2,1)} %get-tuple-element.78), channel_id=1, source_target_pairs={{0,8},{4,12},{8,0},{12,4},{16,24},{20,28},{24,16},{28,20},{1,9},{5... | collective-permute-start | bytes 196616 | tf_op jit(solution)/shard_map/ppermute | solution.py:33
  13.0 7.1 %collective-permute-start.7 = (bf16[2,128,128]{2,1,0:T(8,128)(2,1)S(1)}, bf16[2,128,128]{2,1,0:T(8,128)(2,1)S(1)}, u32[]{:S(2)}, u32[]{:S(2)}) collective-permute-start(bf16[2,128,128]{2,1,0:T(8,128)(2,1)S(1)} %get-tuple-element.77), channel_id=1, source_target_pairs={{0,8},{4,12},{8,0},{12,4},{16,24},{20,28},{24,16},{28,20},{1,9},{5... | collective-permute-start | bytes 196616 | tf_op jit(solution)/shard_map/ppermute | solution.py:33
  16.6 22.6 %collective-permute-start.23 = (bf16[272,512]{1,0:T(8,128)(2,1)}, bf16[272,512]{1,0:T(8,128)(2,1)}, u32[]{:S(2)}, u32[]{:S(2)}) collective-permute-start(bf16[272,512]{1,0:T(8,128)(2,1)} %get-tuple-element.46), channel_id=1, source_target_pairs={{0,4},{4,0},{8,12},{12,8},{16,20},{20,16},{24,28},{28,24},{1,5},{5... | collective-permute-start | bytes 835592 | tf_op jit(solution)/shard_map/ppermute | solution.py:33
  17.3 22.3 %collective-permute-start.24 = (bf16[272,512]{1,0:T(8,128)(2,1)}, bf16[272,512]{1,0:T(8,128)(2,1)}, u32[]{:S(2)}, u32[]{:S(2)}) collective-permute-start(bf16[272,512]{1,0:T(8,128)(2,1)} %get-tuple-element.47), channel_id=1, source_target_pairs={{0,8},{4,12},{8,0},{12,4},{16,24},{20,28},{24,16},{28,20},{1,9},{5... | collective-permute-start | bytes 835592 | tf_op jit(solution)/shard_map/ppermute | solution.py:33
  18.9 21.2 %collective-permute-start.25 = (bf16[272,512]{1,0:T(8,128)(2,1)}, bf16[272,512]{1,0:T(8,128)(2,1)S(1)}, u32[]{:S(2)}, u32[]{:S(2)}) collective-permute-start(bf16[272,512]{1,0:T(8,128)(2,1)} %get-tuple-element.48), channel_id=1, source_target_pairs={{0,12},{4,8},{8,4},{12,0},{16,28},{20,24},{24,20},{28,16},{1,13},{... | collective-permute-start | bytes 835592 | tf_op jit(solution)/shard_map/ppermute | solution.py:33
  20.2 10.5 %collective-permute-start.5 = (bf16[2,128,128]{2,1,0:T(8,128)(2,1)S(1)}, bf16[2,128,128]{2,1,0:T(8,128)(2,1)S(1)}, u32[]{:S(2)}, u32[]{:S(2)}) collective-permute-start(bf16[2,128,128]{2,1,0:T(8,128)(2,1)S(1)} %get-tuple-element.76), channel_id=1, source_target_pairs={{0,16},{4,20},{8,24},{12,28},{16,0},{20,4},{24,8},{28,12},{1,17},{... | collective-permute-start | bytes 196616 | tf_op jit(solution)/shard_map/ppermute | solution.py:33
  30.6 5.7 %collective-permute-start.8 = (bf16[2,128,128]{2,1,0:T(8,128)(2,1)S(1)}, bf16[2,128,128]{2,1,0:T(8,128)(2,1)S(1)}, u32[]{:S(2)}, u32[]{:S(2)}) collective-permute-start(bf16[2,128,128]{2,1,0:T(8,128)(2,1)S(1)} %get-tuple-element.75), channel_id=1, source_target_pairs={{0,16},{4,20},{8,24},{12,28},{16,0},{20,4},{24,8},{28,12},{1,17},{... | collective-permute-start | bytes 196616 | tf_op jit(solution)/shard_map/ppermute | solution.py:33
  38.7 3.6 %collective-permute-start.9 = (bf16[512,256]{1,0:T(8,128)(2,1)S(1)}, bf16[512,256]{1,0:T(8,128)(2,1)S(1)}, u32[]{:S(2)}, u32[]{:S(2)}) collective-permute-start(bf16[512,256]{1,0:T(8,128)(2,1)S(1)} %shard_map.123.refs_0_), channel_id=1, source_target_pairs={{0,1},{1,0},{2,3},{3,2},{4,5},{5,4},{6,7},{7,6},{8,9},{9,8},{10,11... | collective-permute-start | bytes 786440 | tf_op jit(solution)/shard_map/ppermute | solution.py:33
  38.7 28.2 %copy-start.46 = (bf16[4,128,128]{2,1,0:T(8,128)(2,1)}, bf16[4,128,128]{2,1,0:T(8,128)(2,1)S(1)}, u32[]{:S(2)}) copy-start(bf16[4,128,128]{2,1,0:T(8,128)(2,1)S(1)} %collective-permute-done) | copy-start | bytes 393220
  38.7 4.9 %collective-permute-start.10 = (bf16[512,256]{1,0:T(8,128)(2,1)}, bf16[512,256]{1,0:T(8,128)(2,1)S(1)}, u32[]{:S(2)}, u32[]{:S(2)}) collective-permute-start(bf16[512,256]{1,0:T(8,128)(2,1)} %shard_map.124.refs_1_.refs_0_), channel_id=1, source_target_pairs={{0,1},{1,0},{2,3},{3,2},{4,5},{5,4},{6,7},{7,6},{8,9},{9,8},{10,11... | collective-permute-start | bytes 786440 | tf_op jit(solution)/shard_map/ppermute | solution.py:33
  39.2 6.5 %collective-permute-start.11 = (bf16[512,256]{1,0:T(8,128)(2,1)}, bf16[512,256]{1,0:T(8,128)(2,1)S(1)}, u32[]{:S(2)}, u32[]{:S(2)}) collective-permute-start(bf16[512,256]{1,0:T(8,128)(2,1)} %shard_map.125.refs_2_.refs_0_), channel_id=1, source_target_pairs={{0,1},{1,0},{2,3},{3,2},{4,5},{5,4},{6,7},{7,6},{8,9},{9,8},{10,11... | collective-permute-start | bytes 786440 | tf_op jit(solution)/shard_map/ppermute | solution.py:33
  39.6 8.1 %collective-permute-start.12 = (bf16[512,256]{1,0:T(8,128)(2,1)S(1)}, bf16[512,256]{1,0:T(8,128)(2,1)S(1)}, u32[]{:S(2)}, u32[]{:S(2)}) collective-permute-start(bf16[512,256]{1,0:T(8,128)(2,1)S(1)} %shard_map.126.refs_3_.refs_0_), channel_id=1, source_target_pairs={{0,1},{1,0},{2,3},{3,2},{4,5},{5,4},{6,7},{7,6},{8,9},{9,8},{10,11... | collective-permute-start | bytes 786440 | tf_op jit(solution)/shard_map/ppermute | solution.py:33
  40.8 9.9 %collective-permute-start.13 = (bf16[512,256]{1,0:T(8,128)(2,1)S(1)}, bf16[512,256]{1,0:T(8,128)(2,1)}, u32[]{:S(2)}, u32[]{:S(2)}) collective-permute-start(bf16[512,256]{1,0:T(8,128)(2,1)S(1)} %shard_map.123.refs_0_), channel_id=1, source_target_pairs={{0,2},{1,3},{2,0},{3,1},{4,6},{5,7},{6,4},{7,5},{8,10},{9,11},{10,... | collective-permute-start | bytes 786440 | tf_op jit(solution)/shard_map/ppermute | solution.py:33
  43.0 12.6 %collective-permute-start.14 = (bf16[512,256]{1,0:T(8,128)(2,1)}, bf16[512,256]{1,0:T(8,128)(2,1)S(1)}, u32[]{:S(2)}, u32[]{:S(2)}) collective-permute-start(bf16[512,256]{1,0:T(8,128)(2,1)} %shard_map.124.refs_1_.refs_0_), channel_id=1, source_target_pairs={{0,2},{1,3},{2,0},{3,1},{4,6},{5,7},{6,4},{7,5},{8,10},{9,11},{10,... | collective-permute-start | bytes 786440 | tf_op jit(solution)/shard_map/ppermute | solution.py:33
  44.3 17.0 %collective-permute-start.15 = (bf16[512,256]{1,0:T(8,128)(2,1)}, bf16[512,256]{1,0:T(8,128)(2,1)S(1)}, u32[]{:S(2)}, u32[]{:S(2)}) collective-permute-start(bf16[512,256]{1,0:T(8,128)(2,1)} %shard_map.125.refs_2_.refs_0_), channel_id=1, source_target_pairs={{0,2},{1,3},{2,0},{3,1},{4,6},{5,7},{6,4},{7,5},{8,10},{9,11},{10,... | collective-permute-start | bytes 786440 | tf_op jit(solution)/shard_map/ppermute | solution.py:33
  46.5 19.5 %collective-permute-start.16 = (bf16[512,256]{1,0:T(8,128)(2,1)S(1)}, bf16[512,256]{1,0:T(8,128)(2,1)S(1)}, u32[]{:S(2)}, u32[]{:S(2)}) collective-permute-start(bf16[512,256]{1,0:T(8,128)(2,1)S(1)} %shard_map.126.refs_3_.refs_0_), channel_id=1, source_target_pairs={{0,2},{1,3},{2,0},{3,1},{4,6},{5,7},{6,4},{7,5},{8,10},{9,11},{10,... | collective-permute-start | bytes 786440 | tf_op jit(solution)/shard_map/ppermute | solution.py:33
  47.7 22.6 %copy-start.38 = (bf16[512,256]{1,0:T(8,128)(2,1)}, bf16[512,256]{1,0:T(8,128)(2,1)S(1)}, u32[]{:S(2)}) copy-start(bf16[512,256]{1,0:T(8,128)(2,1)S(1)} %collective-permute-done.12.refs_7_) | copy-start | bytes 786436
  47.7 22.7 %collective-permute-start.27 = (bf16[512,256]{1,0:T(8,128)(2,1)S(1)}, bf16[512,256]{1,0:T(8,128)(2,1)}, u32[]{:S(2)}, u32[]{:S(2)}) collective-permute-start(bf16[512,256]{1,0:T(8,128)(2,1)S(1)} %shard_map.123.refs_0_), channel_id=1, source_target_pairs={{0,8},{4,12},{8,0},{12,4},{16,24},{20,28},{24,16},{28,20},{1,9},{5... | collective-permute-start | bytes 786440 | tf_op jit(solution)/shard_map/ppermute | solution.py:33
  50.7 21.1 %collective-permute-start.17 = (bf16[512,256]{1,0:T(8,128)(2,1)}, bf16[512,256]{1,0:T(8,128)(2,1)}, u32[]{:S(2)}, u32[]{:S(2)}) collective-permute-start(bf16[512,256]{1,0:T(8,128)(2,1)} %collective-permute-done.13.refs_8_), channel_id=1, source_target_pairs={{0,1},{1,0},{2,3},{3,2},{4,5},{5,4},{6,7},{7,6},{8,9},{9,8},{10,11... | collective-permute-start | bytes 786440 | tf_op jit(solution)/shard_map/ppermute | solution.py:33
  55.6 14.7 %copy-start.40 = (bf16[512,256]{1,0:T(8,128)(2,1)}, bf16[512,256]{1,0:T(8,128)(2,1)S(1)}, u32[]{:S(2)}) copy-start(bf16[512,256]{1,0:T(8,128)(2,1)S(1)} %collective-permute-done.14.refs_9_) | copy-start | bytes 786436
  55.6 16.9 %collective-permute-start.18 = (bf16[512,256]{1,0:T(8,128)(2,1)S(1)}, bf16[512,256]{1,0:T(8,128)(2,1)}, u32[]{:S(2)}, u32[]{:S(2)}) collective-permute-start(bf16[512,256]{1,0:T(8,128)(2,1)S(1)} %collective-permute-done.14.refs_9_), channel_id=1, source_target_pairs={{0,1},{1,0},{2,3},{3,2},{4,5},{5,4},{6,7},{7,6},{8,9},{9,8},{10,11... | collective-permute-start | bytes 786440 | tf_op jit(solution)/shard_map/ppermute | solution.py:33
  61.2 14.3 %collective-permute-start.19 = (bf16[512,256]{1,0:T(8,128)(2,1)S(1)}, bf16[512,256]{1,0:T(8,128)(2,1)}, u32[]{:S(2)}, u32[]{:S(2)}) collective-permute-start(bf16[512,256]{1,0:T(8,128)(2,1)S(1)} %collective-permute-done.15.refs_10_), channel_id=1, source_target_pairs={{0,1},{1,0},{2,3},{3,2},{4,5},{5,4},{6,7},{7,6},{8,9},{9,8},{10,11... | collective-permute-start | bytes 786440 | tf_op jit(solution)/shard_map/ppermute | solution.py:33
  66.0 9.6 %collective-permute-start.20 = (bf16[512,256]{1,0:T(8,128)(2,1)S(1)}, bf16[512,256]{1,0:T(8,128)(2,1)}, u32[]{:S(2)}, u32[]{:S(2)}) collective-permute-start(bf16[512,256]{1,0:T(8,128)(2,1)S(1)} %collective-permute-done.16.refs_11_), channel_id=1, source_target_pairs={{0,1},{1,0},{2,3},{3,2},{4,5},{5,4},{6,7},{7,6},{8,9},{9,8},{10,11... | collective-permute-start | bytes 786440 | tf_op jit(solution)/shard_map/ppermute | solution.py:33
  70.4 18.8 %collective-permute-start.26 = (bf16[512,256]{1,0:T(8,128)(2,1)S(1)}, bf16[512,256]{1,0:T(8,128)(2,1)S(1)}, u32[]{:S(2)}, u32[]{:S(2)}) collective-permute-start(bf16[512,256]{1,0:T(8,128)(2,1)S(1)} %shard_map.123.refs_0_), channel_id=1, source_target_pairs={{0,4},{4,0},{8,12},{12,8},{16,20},{20,16},{24,28},{28,24},{1,5},{5... | collective-permute-start | bytes 786440 | tf_op jit(solution)/shard_map/ppermute | solution.py:33
  71.8 25.1 %collective-permute-start.33 = (bf16[512,256]{1,0:T(8,128)(2,1)}, bf16[512,256]{1,0:T(8,128)(2,1)S(1)}, u32[]{:S(2)}, u32[]{:S(2)}) collective-permute-start(bf16[512,256]{1,0:T(8,128)(2,1)} %shard_map.124.refs_1_.refs_0_), channel_id=1, source_target_pairs={{0,4},{4,0},{8,12},{12,8},{16,20},{20,16},{24,28},{28,24},{1,5},{5... | collective-permute-start | bytes 786440 | tf_op jit(solution)/shard_map/ppermute | solution.py:33
  72.5 18.8 %collective-permute-start.34 = (bf16[512,256]{1,0:T(8,128)(2,1)}, bf16[512,256]{1,0:T(8,128)(2,1)S(1)}, u32[]{:S(2)}, u32[]{:S(2)}) collective-permute-start(bf16[512,256]{1,0:T(8,128)(2,1)} %shard_map.124.refs_1_.refs_0_), channel_id=1, source_target_pairs={{0,8},{4,12},{8,0},{12,4},{16,24},{20,28},{24,16},{28,20},{1,9},{5... | collective-permute-start | bytes 786440 | tf_op jit(solution)/shard_map/ppermute | solution.py:33
  75.5 16.5 %collective-permute-start.41 = (bf16[512,256]{1,0:T(8,128)(2,1)}, bf16[512,256]{1,0:T(8,128)(2,1)S(1)}, u32[]{:S(2)}, u32[]{:S(2)}) collective-permute-start(bf16[512,256]{1,0:T(8,128)(2,1)} %shard_map.125.refs_2_.refs_0_), channel_id=1, source_target_pairs={{0,8},{4,12},{8,0},{12,4},{16,24},{20,28},{24,16},{28,20},{1,9},{5... | collective-permute-start | bytes 786440 | tf_op jit(solution)/shard_map/ppermute | solution.py:33
  75.6 17.8 %collective-permute-start.28 = (bf16[512,256]{1,0:T(8,128)(2,1)}, bf16[512,256]{1,0:T(8,128)(2,1)S(1)}, u32[]{:S(2)}, u32[]{:S(2)}) collective-permute-start(bf16[512,256]{1,0:T(8,128)(2,1)} %collective-permute-done.27.refs_2_), channel_id=1, source_target_pairs={{0,4},{4,0},{8,12},{12,8},{16,20},{20,16},{24,28},{28,24},{1,5},{5... | collective-permute-start | bytes 786440 | tf_op jit(solution)/shard_map/ppermute | solution.py:33
  89.2 8.8 %collective-permute-start.48 = (bf16[512,256]{1,0:T(8,128)(2,1)S(1)}, bf16[512,256]{1,0:T(8,128)(2,1)S(1)}, u32[]{:S(2)}, u32[]{:S(2)}) collective-permute-start(bf16[512,256]{1,0:T(8,128)(2,1)S(1)} %copy-done.8), channel_id=1, source_target_pairs={{0,8},{4,12},{8,0},{12,4},{16,24},{20,28},{24,16},{28,20},{1,9},{5... | collective-permute-start | bytes 786440 | tf_op jit(solution)/shard_map/ppermute | solution.py:33
  91.3 9.2 %collective-permute-start.35 = (bf16[512,256]{1,0:T(8,128)(2,1)S(1)}, bf16[512,256]{1,0:T(8,128)(2,1)S(1)}, u32[]{:S(2)}, u32[]{:S(2)}) collective-permute-start(bf16[512,256]{1,0:T(8,128)(2,1)S(1)} %collective-permute-done.34.refs_2_), channel_id=1, source_target_pairs={{0,4},{4,0},{8,12},{12,8},{16,20},{20,16},{24,28},{28,24},{1,5},{5... | collective-permute-start | bytes 786440 | tf_op jit(solution)/shard_map/ppermute | solution.py:33
  92.0 14.2 %collective-permute-start.40 = (bf16[512,256]{1,0:T(8,128)(2,1)}, bf16[512,256]{1,0:T(8,128)(2,1)S(1)}, u32[]{:S(2)}, u32[]{:S(2)}) collective-permute-start(bf16[512,256]{1,0:T(8,128)(2,1)} %shard_map.125.refs_2_.refs_0_), channel_id=1, source_target_pairs={{0,4},{4,0},{8,12},{12,8},{16,20},{20,16},{24,28},{28,24},{1,5},{5... | collective-permute-start | bytes 786440 | tf_op jit(solution)/shard_map/ppermute | solution.py:33
  93.4 18.3 %collective-permute-start.42 = (bf16[512,256]{1,0:T(8,128)(2,1)S(1)}, bf16[512,256]{1,0:T(8,128)(2,1)S(1)}, u32[]{:S(2)}, u32[]{:S(2)}) collective-permute-start(bf16[512,256]{1,0:T(8,128)(2,1)S(1)} %collective-permute-done.41.refs_2_), channel_id=1, source_target_pairs={{0,4},{4,0},{8,12},{12,8},{16,20},{20,16},{24,28},{28,24},{1,5},{5... | collective-permute-start | bytes 786440 | tf_op jit(solution)/shard_map/ppermute | solution.py:33
  96.9 26.4 %collective-permute-start.1 = (bf16[4,128,128]{2,1,0:T(8,128)(2,1)S(1)}, bf16[4,128,128]{2,1,0:T(8,128)(2,1)S(1)}, u32[]{:S(2)}, u32[]{:S(2)}) collective-permute-start(bf16[4,128,128]{2,1,0:T(8,128)(2,1)S(1)} %fusion.7), channel_id=1, source_target_pairs={{0,8},{4,12},{8,0},{12,4},{16,24},{20,28},{24,16},{28,20},{1,9},{5... | collective-permute-start | bytes 393224 | tf_op jit(solution)/shard_map/ppermute | solution.py:33
  98.0 19.3 %collective-permute-start.47 = (bf16[512,256]{1,0:T(8,128)(2,1)S(1)}, bf16[512,256]{1,0:T(8,128)(2,1)S(1)}, u32[]{:S(2)}, u32[]{:S(2)}) collective-permute-start(bf16[512,256]{1,0:T(8,128)(2,1)S(1)} %copy-done.8), channel_id=1, source_target_pairs={{0,4},{4,0},{8,12},{12,8},{16,20},{20,16},{24,28},{28,24},{1,5},{5... | collective-permute-start | bytes 786440 | tf_op jit(solution)/shard_map/ppermute | solution.py:33
  100.5 20.3 %collective-permute-start.49 = (bf16[512,256]{1,0:T(8,128)(2,1)S(1)}, bf16[512,256]{1,0:T(8,128)(2,1)S(1)}, u32[]{:S(2)}, u32[]{:S(2)}) collective-permute-start(bf16[512,256]{1,0:T(8,128)(2,1)S(1)} %collective-permute-done.48.refs_2_), channel_id=1, source_target_pairs={{0,4},{4,0},{8,12},{12,8},{16,20},{20,16},{24,28},{28,24},{1,5},{5... | collective-permute-start | bytes 786440 | tf_op jit(solution)/shard_map/ppermute | solution.py:33
  106.1 62.1 %collective-permute-start.21 = (bf16[2,512,256]{2,1,0:T(8,128)(2,1)}, bf16[2,512,256]{2,1,0:T(8,128)(2,1)}, u32[]{:S(2)}, u32[]{:S(2)}) collective-permute-start(bf16[2,512,256]{2,1,0:T(8,128)(2,1)} %pad_maximum_fusion), channel_id=1, source_target_pairs={{0,1},{1,0},{2,3},{3,2},{4,5},{5,4},{6,7},{7,6},{8,9},{9,8},{10,11... | collective-permute-start | bytes 1572872 | tf_op jit(solution)/shard_map/ppermute | solution.py:33
  111.7 30.8 %collective-permute-start.29 = (bf16[4,128,256]{2,1,0:T(8,128)(2,1)S(1)}, bf16[4,128,256]{2,1,0:T(8,128)(2,1)S(1)}, u32[]{:S(2)}, u32[]{:S(2)}) collective-permute-start(bf16[4,128,256]{2,1,0:T(8,128)(2,1)S(1)} %get-tuple-element.50), channel_id=1, source_target_pairs={{0,16},{4,20},{8,24},{12,28},{16,0},{20,4},{24,8},{28,12},{1,17},{... | collective-permute-start | bytes 786440 | tf_op jit(solution)/shard_map/ppermute | solution.py:38
  117.4 32.2 %collective-permute-start.36 = (bf16[4,128,256]{2,1,0:T(8,128)(2,1)S(1)}, bf16[4,128,256]{2,1,0:T(8,128)(2,1)S(1)}, u32[]{:S(2)}, u32[]{:S(2)}) collective-permute-start(bf16[4,128,256]{2,1,0:T(8,128)(2,1)S(1)} %get-tuple-element.56), channel_id=1, source_target_pairs={{0,16},{4,20},{8,24},{12,28},{16,0},{20,4},{24,8},{28,12},{1,17},{... | collective-permute-start | bytes 786440 | tf_op jit(solution)/shard_map/ppermute | solution.py:38
  120.8 34.4 %collective-permute-start.43 = (bf16[4,128,256]{2,1,0:T(8,128)(2,1)S(1)}, bf16[4,128,256]{2,1,0:T(8,128)(2,1)S(1)}, u32[]{:S(2)}, u32[]{:S(2)}) collective-permute-start(bf16[4,128,256]{2,1,0:T(8,128)(2,1)S(1)} %get-tuple-element.62), channel_id=1, source_target_pairs={{0,16},{4,20},{8,24},{12,28},{16,0},{20,4},{24,8},{28,12},{1,17},{... | collective-permute-start | bytes 786440 | tf_op jit(solution)/shard_map/ppermute | solution.py:38
  123.2 20.0 %copy-start.19 = (f32[4,128,256]{2,1,0:T(8,128)}, f32[4,128,256]{2,1,0:T(8,128)S(1)}, u32[]{:S(2)}) copy-start(f32[4,128,256]{2,1,0:T(8,128)S(1)} %get-tuple-element.67.own_ref) | copy-start | bytes 1572868
  123.3 36.9 %copy-start.49 = (bf16[4,128,128]{2,1,0:T(8,128)(2,1)}, bf16[4,128,128]{2,1,0:T(8,128)(2,1)S(1)}, u32[]{:S(2)}) copy-start(bf16[4,128,128]{2,1,0:T(8,128)(2,1)S(1)} %collective-permute-done.1) | copy-start | bytes 393220
  123.3 36.9 %collective-permute-start.50 = (bf16[4,128,256]{2,1,0:T(8,128)(2,1)S(1)}, bf16[4,128,256]{2,1,0:T(8,128)(2,1)S(1)}, u32[]{:S(2)}, u32[]{:S(2)}) collective-permute-start(bf16[4,128,256]{2,1,0:T(8,128)(2,1)S(1)} %get-tuple-element.68), channel_id=1, source_target_pairs={{0,16},{4,20},{8,24},{12,28},{16,0},{20,4},{24,8},{28,12},{1,17},{... | collective-permute-start | bytes 786440 | tf_op jit(solution)/shard_map/ppermute | solution.py:38
  142.6 28.5 %collective-permute-start.2 = (bf16[4,128,128]{2,1,0:T(8,128)(2,1)}, bf16[4,128,128]{2,1,0:T(8,128)(2,1)}, u32[]{:S(2)}, u32[]{:S(2)}) collective-permute-start(bf16[4,128,128]{2,1,0:T(8,128)(2,1)} %fusion.5), channel_id=1, source_target_pairs={{0,16},{4,20},{8,24},{12,28},{16,0},{20,4},{24,8},{28,12},{1,17},{... | collective-permute-start | bytes 393224 | tf_op jit(solution)/shard_map/ppermute | solution.py:33
  150.3 21.4 %collective-permute-start.30 = (bf16[128,256]{1,0:T(8,128)(2,1)}, bf16[128,256]{1,0:T(8,128)(2,1)}, u32[]{:S(2)}, u32[]{:S(2)}) collective-permute-start(bf16[128,256]{1,0:T(8,128)(2,1)} %get-tuple-element.52), channel_id=1, source_target_pairs={{0,1},{1,0},{2,3},{3,2},{4,5},{5,4},{6,7},{7,6},{8,9},{9,8},{10,11... | collective-permute-start | bytes 196616 | tf_op jit(solution)/shard_map/ppermute | solution.py:33
  155.9 16.6 %collective-permute-start.31 = (bf16[128,256]{1,0:T(8,128)(2,1)}, bf16[128,256]{1,0:T(8,128)(2,1)}, u32[]{:S(2)}, u32[]{:S(2)}) collective-permute-start(bf16[128,256]{1,0:T(8,128)(2,1)} %get-tuple-element.53), channel_id=1, source_target_pairs={{0,2},{1,3},{2,0},{3,1},{4,6},{5,7},{6,4},{7,5},{8,10},{9,11},{10,... | collective-permute-start | bytes 196616 | tf_op jit(solution)/shard_map/ppermute | solution.py:33
  160.9 12.4 %collective-permute-start.32 = (bf16[128,256]{1,0:T(8,128)(2,1)}, bf16[128,256]{1,0:T(8,128)(2,1)}, u32[]{:S(2)}, u32[]{:S(2)}) collective-permute-start(bf16[128,256]{1,0:T(8,128)(2,1)} %get-tuple-element.54), channel_id=1, source_target_pairs={{0,3},{1,2},{2,1},{3,0},{4,7},{5,6},{6,5},{7,4},{8,11},{9,10},{10,... | collective-permute-start | bytes 196616 | tf_op jit(solution)/shard_map/ppermute | solution.py:33
  168.3 5.6 %collective-permute-start.37 = (bf16[128,256]{1,0:T(8,128)(2,1)S(1)}, bf16[128,256]{1,0:T(8,128)(2,1)S(1)}, u32[]{:S(2)}, u32[]{:S(2)}) collective-permute-start(bf16[128,256]{1,0:T(8,128)(2,1)S(1)} %get-tuple-element.58), channel_id=1, source_target_pairs={{0,1},{1,0},{2,3},{3,2},{4,5},{5,4},{6,7},{7,6},{8,9},{9,8},{10,11... | collective-permute-start | bytes 196616 | tf_op jit(solution)/shard_map/ppermute | solution.py:33
  171.1 5.0 %collective-permute-start.38 = (bf16[128,256]{1,0:T(8,128)(2,1)S(1)}, bf16[128,256]{1,0:T(8,128)(2,1)S(1)}, u32[]{:S(2)}, u32[]{:S(2)}) collective-permute-start(bf16[128,256]{1,0:T(8,128)(2,1)S(1)} %get-tuple-element.59), channel_id=1, source_target_pairs={{0,2},{1,3},{2,0},{3,1},{4,6},{5,7},{6,4},{7,5},{8,10},{9,11},{10,... | collective-permute-start | bytes 196616 | tf_op jit(solution)/shard_map/ppermute | solution.py:33
  171.7 4.4 %collective-permute-start.39 = (bf16[128,256]{1,0:T(8,128)(2,1)S(1)}, bf16[128,256]{1,0:T(8,128)(2,1)S(1)}, u32[]{:S(2)}, u32[]{:S(2)}) collective-permute-start(bf16[128,256]{1,0:T(8,128)(2,1)S(1)} %get-tuple-element.60), channel_id=1, source_target_pairs={{0,3},{1,2},{2,1},{3,0},{4,7},{5,6},{6,5},{7,4},{8,11},{9,10},{10,... | collective-permute-start | bytes 196616 | tf_op jit(solution)/shard_map/ppermute | solution.py:33
  172.6 5.0 %collective-permute-start.44 = (bf16[128,256]{1,0:T(8,128)(2,1)S(1)}, bf16[128,256]{1,0:T(8,128)(2,1)S(1)}, u32[]{:S(2)}, u32[]{:S(2)}) collective-permute-start(bf16[128,256]{1,0:T(8,128)(2,1)S(1)} %get-tuple-element.64), channel_id=1, source_target_pairs={{0,1},{1,0},{2,3},{3,2},{4,5},{5,4},{6,7},{7,6},{8,9},{9,8},{10,11... | collective-permute-start | bytes 196616 | tf_op jit(solution)/shard_map/ppermute | solution.py:33
  173.3 5.7 %collective-permute-start.45 = (bf16[128,256]{1,0:T(8,128)(2,1)S(1)}, bf16[128,256]{1,0:T(8,128)(2,1)S(1)}, u32[]{:S(2)}, u32[]{:S(2)}) collective-permute-start(bf16[128,256]{1,0:T(8,128)(2,1)S(1)} %get-tuple-element.65), channel_id=1, source_target_pairs={{0,2},{1,3},{2,0},{3,1},{4,6},{5,7},{6,4},{7,5},{8,10},{9,11},{10,... | collective-permute-start | bytes 196616 | tf_op jit(solution)/shard_map/ppermute | solution.py:33
  173.9 9.5 %collective-permute-start.46 = (bf16[128,256]{1,0:T(8,128)(2,1)S(1)}, bf16[128,256]{1,0:T(8,128)(2,1)S(1)}, u32[]{:S(2)}, u32[]{:S(2)}) collective-permute-start(bf16[128,256]{1,0:T(8,128)(2,1)S(1)} %get-tuple-element.66), channel_id=1, source_target_pairs={{0,3},{1,2},{2,1},{3,0},{4,7},{5,6},{6,5},{7,4},{8,11},{9,10},{10,... | collective-permute-start | bytes 196616 | tf_op jit(solution)/shard_map/ppermute | solution.py:33
  176.1 7.3 %collective-permute-start.51 = (bf16[128,256]{1,0:T(8,128)(2,1)S(1)}, bf16[128,256]{1,0:T(8,128)(2,1)S(1)}, u32[]{:S(2)}, u32[]{:S(2)}) collective-permute-start(bf16[128,256]{1,0:T(8,128)(2,1)S(1)} %get-tuple-element.70), channel_id=1, source_target_pairs={{0,1},{1,0},{2,3},{3,2},{4,5},{5,4},{6,7},{7,6},{8,9},{9,8},{10,11... | collective-permute-start | bytes 196616 | tf_op jit(solution)/shard_map/ppermute | solution.py:33
  176.1 7.3 %collective-permute-start.52 = (bf16[128,256]{1,0:T(8,128)(2,1)S(1)}, bf16[128,256]{1,0:T(8,128)(2,1)S(1)}, u32[]{:S(2)}, u32[]{:S(2)}) collective-permute-start(bf16[128,256]{1,0:T(8,128)(2,1)S(1)} %get-tuple-element.71), channel_id=1, source_target_pairs={{0,2},{1,3},{2,0},{3,1},{4,6},{5,7},{6,4},{7,5},{8,10},{9,11},{10,... | collective-permute-start | bytes 196616 | tf_op jit(solution)/shard_map/ppermute | solution.py:33
  177.6 5.9 %collective-permute-start.53 = (bf16[128,256]{1,0:T(8,128)(2,1)S(1)}, bf16[128,256]{1,0:T(8,128)(2,1)S(1)}, u32[]{:S(2)}, u32[]{:S(2)}) collective-permute-start(bf16[128,256]{1,0:T(8,128)(2,1)S(1)} %get-tuple-element.72), channel_id=1, source_target_pairs={{0,3},{1,2},{2,1},{3,0},{4,7},{5,6},{6,5},{7,4},{8,11},{9,10},{10,... | collective-permute-start | bytes 196616 | tf_op jit(solution)/shard_map/ppermute | solution.py:33
  179.0 9.1 %collective-permute-start.22 = (bf16[1,512,256]{2,1,0:T(8,128)(2,1)S(1)}, bf16[1,512,256]{2,1,0:T(8,128)(2,1)S(1)}, u32[]{:S(2)}, u32[]{:S(2)}) collective-permute-start(bf16[1,512,256]{2,1,0:T(8,128)(2,1)S(1)} %fusion), channel_id=1, source_target_pairs={{0,2},{1,3},{2,0},{3,1},{4,6},{5,7},{6,4},{7,5},{8,10},{9,11},{10,... | collective-permute-start | bytes 786440 | tf_op jit(solution)/shard_map/ppermute | solution.py:33
  (41 other events, 158.5 us)

commit v2 on v0

v2 whole, which is shorter than its diff:
```python
import functools

import jax
import jax.numpy as jnp
from jax import lax
from jax.experimental import pallas as pl
from jax.experimental.pallas import tpu as pltpu
from jax.sharding import PartitionSpec as P

DH = 128
PAD = 16
MIB = 1 << 20
BF16 = jnp.bfloat16
F32 = jnp.float32
VMEM = pl.BlockSpec(memory_space=pltpu.VMEM)
SMEM = pl.BlockSpec(memory_space=pltpu.SMEM)
HBM = pl.BlockSpec(memory_space=pltpu.HBM)


def struct(shape, dtype):
    return jax.ShapeDtypeStruct(shape, dtype)


TOKEN = struct((8, 128), F32)


def call(kernel, out_shape, operands, specs, wait=(), limit=16, cost=0, **options):
    known = len(operands)

    def body(*refs):
        kernel(*refs[:known], *refs[known + len(wait) :])

    grid = options.pop("grid", ())
    out_specs = options.pop("out_specs", VMEM)
    scratch = options.pop("scratch_shapes", ())
    prefetch = options.pop("prefetch", 0)
    if out_specs is VMEM and isinstance(out_shape, (list, tuple)):
        out_specs = [VMEM] * len(out_shape)
    return pl.pallas_call(
        body,
        out_shape=out_shape,
        grid_spec=pltpu.PrefetchScalarGridSpec(
            num_scalar_prefetch=prefetch,
            grid=grid,
            in_specs=list(specs) + [pl.BlockSpec(memory_space=pl.ANY)] * len(wait),
            out_specs=out_specs,
            scratch_shapes=scratch,
        ),
        cost_estimate=pl.CostEstimate(flops=cost, bytes_accessed=0, transcendentals=0),
        compiler_params=pltpu.CompilerParams(vmem_limit_bytes=limit * MIB),
        **options,
    )(*operands, *wait)


def swap(array, axis, mask):
    count = lax.axis_size(axis)
    return lax.ppermute(array, axis, [(place, place ^ mask) for place in range(count)])


def shift(array, axis, step):
    count = lax.axis_size(axis)
    return lax.ppermute(array, axis, [(place, (place + step) % count) for place in range(count)])


def dot(a, b, left, right):
    return lax.dot_general(a, b, (((left,), (right,)), ((), ())), preferred_element_type=F32)


def head(ref, number):
    return ref[:, number * DH : (number + 1) * DH]


def own_states(first, second, wait=()):
    rows, width = first.shape
    heads = width // DH

    def kernel(a_ref, b_ref, wide_ref, narrow_ref, a_kept, b_kept):
        for number in range(heads):
            state = dot(head(a_ref, number), head(b_ref, number), 0, 0)
            wide_ref[number] = state
            narrow_ref[number] = state.astype(BF16)
        a_kept[...] = a_ref[...]
        b_kept[...] = b_ref[...]

    shapes = [struct((heads, DH, DH), F32), struct((heads, DH, DH), BF16)] + [struct((rows, width), BF16)] * 2
    return call(kernel, shapes, (first, second), [VMEM] * 2, wait, cost=6 * rows * width * DH)


def after(array, *earlier):
    return lax.optimization_barrier((array, *earlier))[0]


def add_arrived(total, arrived, last, wait=()):
    def kernel(total_ref, arrived_ref, narrow_ref, *wide):
        added = total_ref[...] + arrived_ref[...].astype(F32)
        narrow_ref[...] = added.astype(BF16)
        for ref in wide:
            ref[...] = added

    shapes = [struct(total.shape, BF16)] + ([] if last else [struct(total.shape, F32)])
    sent, *total = call(kernel, shapes, (total, arrived), [VMEM] * 2, wait)
    return (total[0] if total else None), sent


def touch(wait):
    def kernel(out_ref):
        out_ref[...] = jnp.zeros_like(out_ref)

    return call(kernel, TOKEN, (), (), wait)


def stack(first, second, at, wait=()):
    def kernel(a_ref, b_ref, out_ref):
        for place, ref in enumerate((a_ref, b_ref)):
            out_ref[place] = ref[...] if at[place] is None else ref[at[place]]

    return call(kernel, struct((2, *first.shape[-2:]), first.dtype), (first, second), [VMEM] * 2, wait)


def gathered_state(place, refs, number, backward):
    state = None
    for step, ref in enumerate(refs):
        lower = ((place >> step) & 1) == 0
        term = jnp.where(lower == backward, ref[number].astype(F32), 0.0)
        state = term if state is None else state + term
    return state


def triangle(size, lower):
    down = lax.broadcasted_iota(jnp.int32, (size, size), 0)
    across = lax.broadcasted_iota(jnp.int32, (size, size), 1)
    return down >= across if lower else down <= across


def intra_keys_values(query, key, value, grad, first, many, wait=()):
    rows = query.shape[0]
    tile = rows // 2

    def kernel(q_ref, k_ref, v_ref, g_ref, out_ref):
        keep = triangle(tile, False)
        for number in range(many):
            q, k, v, g = (head(ref, first + number) for ref in (q_ref, k_ref, v_ref, g_ref))
            for down in range(2):
                here = slice(down * tile, (down + 1) * tile)
                rest = slice(down * tile, rows)
                for left, right, other, place in ((v, g, q, 0), (k, q, g, DH)):
                    scores = dot(left[here], right[rest], 1, 1)
                    kept = jnp.where(keep, scores[:, :tile], 0.0).astype(BF16)
                    if down == 0:
                        kept = jnp.concatenate([kept, scores[:, tile:].astype(BF16)], axis=1)
                    out_ref[number, here, place : place + DH] = dot(kept, other[rest], 1, 0)

    return call(
        kernel,
        struct((many, rows, 2 * DH), F32),
        (query, key, value, grad),
        [VMEM] * 4,
        wait,
        cost=24 * rows * rows * many * DH,
    )


def halves(state):
    high = state.astype(BF16)
    return high, (state - high.astype(F32)).astype(BF16)


def finish_keys_values(intra, key, value, arrived, place, sets, known=(), wait=()):
    where = [(array, at) for array in range(len(intra)) for at in range(intra[array].shape[0])]
    rows, wide = intra[0].shape[1:]
    needed = sorted({start + at for start, many in sets for at in range(many or 1)})

    def kernel(place_ref, k_ref, v_ref, *refs):
        states, refs = refs[: len(arrived)], refs[len(arrived) :]
        intra_refs, refs = refs[: len(intra)], refs[len(intra) :]
        known_refs, outs = refs[: len(known)], refs[len(known) :]
        for number in needed:
            if number < len(known):
                both = known_refs[number][...]
            else:
                high, low = halves(gathered_state(place_ref[0], states, number, True))
                v, k = head(v_ref, number), head(k_ref, number)
                by_key = dot(v, high, 1, 1) + dot(v, low, 1, 1)
                by_value = dot(k, high, 1, 0) + dot(k, low, 1, 0)
                array, at = where[number]
                both = intra_refs[array][at] + jnp.concatenate([by_key, by_value], axis=1)
                both = both.astype(BF16)
            for out, (start, many) in zip(outs, sets):
                if many is None and number == start:
                    out[...] = both
                elif many is not None and start <= number < start + many:
                    out[number - start] = both

    shapes = [struct((rows, wide) if many is None else (many, rows, wide), BF16) for _, many in sets]
    operands = (place, key, value, *arrived, *intra, *known)
    return call(kernel, shapes, operands, [SMEM] + [VMEM] * (len(operands) - 1), wait)


def query_grads(key, value, grad, arrived, place, wait=()):
    rows, width = key.shape
    heads = width // DH
    tile = rows // 2

    def kernel(place_ref, k_ref, v_ref, g_ref, *refs):
        out_ref, token_ref, done, sems = refs[len(arrived) :]
        token_ref[...] = jnp.zeros_like(token_ref)
        copies = []
        keep = triangle(tile, True)
        for number in range(heads):
            high, low = halves(gathered_state(place_ref[0], refs[: len(arrived)], number, False))
            k, v, grad_of = head(k_ref, number), head(v_ref, number), head(g_ref, number)
            for down in range(2):
                upto = (down + 1) * tile
                g = grad_of[down * tile : upto]
                scores = dot(g, v[:upto], 1, 1)
                last = jnp.where(keep, scores[:, down * tile :], 0.0).astype(BF16)
                if down:
                    last = jnp.concatenate([scores[:, :tile].astype(BF16), last], axis=1)
                intra = dot(last, k[:upto], 1, 0)
                whole_grad = intra + dot(g, high, 1, 1) + dot(g, low, 1, 1)
                done[number, down * tile : upto, :] = whole_grad.astype(BF16)
            columns = slice(number * DH, (number + 1) * DH)
            copies.append(pltpu.make_async_copy(done.at[number], out_ref.at[:, columns], sems.at[number]))
            copies[-1].start()
        for copy in copies:
            copy.wait()

    return call(
        kernel,
        [struct((rows, width), BF16), TOKEN],
        (place, key, value, grad, *arrived),
        [SMEM] + [VMEM] * (3 + len(arrived)),
        wait,
        cost=24 * rows * rows * width,
        out_specs=[HBM, VMEM],
        scratch_shapes=[pltpu.VMEM((heads, rows, DH), BF16), pltpu.SemaphoreType.DMA((heads,))],
    )


def place_of():
    return jnp.stack([lax.axis_index("seq"), lax.axis_index("exp")]).astype(jnp.int32)


def prepare_inputs(inputs, ids, gates, place, size, experts, count, wait=()):
    rows, wide = inputs.shape
    groups = count // size
    deep = wide // count
    half = rows // 2

    def kernel(place_ref, x_ref, id_ref, gate_ref, *refs):
        own_ref, one_ref, two_ref, column_ref, turned = refs
        outs = [own_ref, one_ref, two_ref.at[0], two_ref.at[1]]
        step = DH * 2
        for start in range(0, wide, step):
            turned[start : start + step, :] = x_ref[:, start : start + step].astype(F32).T.astype(BF16)
        which = lax.broadcasted_iota(jnp.int32, (experts, rows), 0)
        weight = jnp.zeros((experts, rows), F32)
        for slot in range(id_ref.shape[0]):
            weight += jnp.where(id_ref[slot : slot + 1, :] == which, gate_ref[slot : slot + 1, :], 0.0)
        mine = jnp.sum(jnp.where(which == place_ref[1], weight, 0.0), axis=0, keepdims=True)
        column_ref[...] = jnp.broadcast_to(mine, (8, rows)).T[:, :1]
        parts = []
        for _ in range(3):
            part = weight.astype(BF16).astype(F32)
            parts.append(part)
            weight = weight - part
        tail = PAD - 3 * experts
        if tail:
            parts.append(jnp.zeros((tail, rows), F32))
        packed = jnp.concatenate(parts, axis=0)
        me = place_ref[0]
        odd = place_ref[1] & 1
        group, low = me // size, me % size
        columns = pl.ds(pl.multiple_of(odd * half, half), half)
        side = jnp.where(odd == 1, packed[:, half:], packed[:, :half]).astype(BF16)
        for member in range(size):
            for hop in range(groups):
                block = lax.rem(group + hop, groups) * size + (low ^ member)
                source = pl.ds(pl.multiple_of(block * deep, deep), deep)
                part = turned[source, columns] if member else turned[source, :]
                outs[member][hop * deep : (hop + 1) * deep, :] = part
            outs[member][groups * deep :, :] = side if member else packed.astype(BF16)

    tall = groups * deep + PAD
    shapes = [struct((tall, rows), BF16), struct((tall, half), BF16), struct((2, tall, half), BF16)]
    return call(
        kernel,
        shapes + [struct((rows, 1), F32)],
        (place, inputs, ids, gates),
        [SMEM] + [VMEM] * 3,
        wait,
        scratch_shapes=[pltpu.VMEM((wide, rows), BF16)],
    )


def weigh_inputs(own, halves_of, place, experts, wait=()):
    deep, rows = own.shape
    deep -= PAD
    half = rows // 2
    size = 1 + len(halves_of)
    flat = [entry for pair in halves_of for entry in pair]

    def kernel(place_ref, own_ref, *refs):
        out_ref = refs[len(flat)]
        odd = place_ref[1] & 1
        for at in range(1 + len(flat)):
            ref = own_ref if at == 0 else refs[at - 1].at[flat[at - 1][1]]
            columns = ref[:deep, :].astype(F32)
            parts = ref[deep:, :].astype(F32)
            row = lax.broadcasted_iota(jnp.int32, parts.shape, 0)
            for step in range(experts):
                mine = (row < 3 * experts) & (lax.rem(row, experts) == (step ^ place_ref[1]))
                weight = jnp.sum(jnp.where(mine, parts, 0.0), axis=0, keepdims=True)
                scaled = (columns * weight).astype(BF16)
                if at == 0:
                    out_ref[step, :, :rows] = scaled
                else:
                    side = odd if at % 2 else 1 - odd
                    start = pl.multiple_of((at + 1) // 2 * rows + side * half, half)
                    out_ref[step, :, pl.ds(start, half)] = scaled

    return call(
        kernel,
        struct((experts, deep, size * rows), BF16),
        (place, own, *[array for array, _ in flat]),
        [SMEM] + [VMEM] * (1 + len(flat)),
        wait,
    )


def weight_product(weighted, blocks, groups, wait=()):
    experts, deep, _ = weighted.shape
    rows, wide = blocks[0][0].shape[-2:]
    size = len(blocks)
    part = deep // groups

    def kernel(w_ref, *refs):
        outs = refs[size:]
        for expert in range(experts):
            total = None
            for member in range(size):
                left = w_ref[expert, :, member * rows : (member + 1) * rows]
                at = blocks[member][1]
                right = refs[member][...] if at is None else refs[member][at]
                term = dot(left, right, 1, 0)
                total = term if total is None else total + term
            for hop in range(groups):
                piece = total[hop * part : (hop + 1) * part]
                outs[hop][expert] = piece.astype(outs[hop].dtype)

    results = call(
        kernel,
        [struct((experts, part, wide), BF16 if hop else F32) for hop in range(groups)],
        (weighted, *[array for array, _ in blocks]),
        [VMEM] * (1 + size),
        wait,
        cost=2 * experts * deep * size * rows * wide,
    )
    return results[0], results[1:]


def add_partials(owns, others, sets, wait=()):
    experts, part, wide = owns[0].shape
    chunks = len(owns)
    flat = [ref for chunk in range(chunks) for ref in (owns[chunk], *others[chunk])]
    each = len(flat) // chunks

    def kernel(*refs):
        outs = refs[len(flat) :]
        for chunk in range(chunks):
            for out, hops in zip(outs, sets):
                for at, hop in enumerate(hops):
                    total = refs[chunk * each][hop]
                    for ref in refs[chunk * each + 1 : (chunk + 1) * each]:
                        total = total + ref[hop].astype(F32)
                    out[at, chunk] = total.astype(out.dtype)

    return call(
        kernel,
        [struct((len(hops), chunks, part, wide), BF16 if hops[0] else F32) for hops in sets],
        flat,
        [VMEM] * len(flat),
        wait,
    )


def place_weight_grad(pieces, place, width):
    experts = len(pieces[0])
    counts = [row[0].shape[1] for row in pieces]
    heads = sum(counts)
    part = pieces[0][0].shape[2]
    flat = [piece for row in pieces for piece in row]
    slots = heads * experts * 2

    def kernel(place_ref, *refs):
        out_ref, ready, sems = refs[len(flat) :]
        copies = []
        number = 0
        for at, many in enumerate(counts):
            for within in range(many):
                for hop in range(experts):
                    start = ((place_ref[1] ^ hop) * heads + number) * DH
                    for side in range(2):
                        slot = (number * experts + hop) * 2 + side
                        piece = refs[at * experts + hop][0, within, :, side * DH : (side + 1) * DH]
                        ready[slot] = piece.astype(F32)
                        columns = pl.ds(pl.multiple_of(start + side * (width // 2), DH), DH)
                        copy = pltpu.make_async_copy(
                            ready.at[slot], out_ref.at[0, :, columns], sems.at[slot]
                        )
                        copy.start()
                        copies.append(copy)
                number += 1
        for copy in copies:
            copy.wait()

    return call(
        kernel,
        struct((1, part, width), F32),
        (place, *flat),
        [SMEM] + [VMEM] * len(flat),
        out_specs=HBM,
        scratch_shapes=[pltpu.VMEM((slots, part, DH), F32), pltpu.SemaphoreType.DMA((slots,))],
    )


def place_keys_values(chunks, wait=()):
    heads, rows, _ = chunks.shape

    def kernel(chunks_ref, *refs):
        token_ref, sems = refs[2:]
        token_ref[...] = jnp.zeros_like(token_ref)
        copies = []
        for number in range(heads):
            for side in range(2):
                source = chunks_ref.at[number, :, side * DH : (side + 1) * DH]
                target = refs[side].at[:, number * DH : (number + 1) * DH]
                copies.append(pltpu.make_async_copy(source, target, sems.at[number * 2 + side]))
        for copy in copies:
            copy.start()
        for copy in copies:
            copy.wait()

    return call(
        kernel,
        [struct((rows, heads * DH), BF16)] * 2 + [TOKEN],
        (chunks,),
        [VMEM],
        wait,
        out_specs=[HBM] * 2 + [VMEM],
        scratch_shapes=[pltpu.SemaphoreType.DMA((2 * heads,))],
    )


def input_products(pieces, expert_weight, gate, place, wait=()):
    experts = len(pieces)
    heads, rows, _ = pieces[0].shape
    _, wide, width = expert_weight.shape
    part = wide // experts
    even = experts // 2

    def kernel(place_ref, w_ref, gate_ref, *refs):
        keep_ref, send_ref = refs[experts:]
        for out in range(experts):
            taken = pl.ds(pl.multiple_of((place_ref[1] ^ out) * part, part), part)
            total = None
            for hop in range(experts):
                for number in range(heads):
                    start = ((place_ref[1] ^ hop) * heads + number) * DH
                    sides = [
                        w_ref[0, taken, pl.ds(pl.multiple_of(start + side * (width // 2), DH), DH)]
                        for side in range(2)
                    ]
                    term = dot(refs[hop][number], jnp.concatenate(sides, axis=1), 1, 1)
                    total = term if total is None else total + term
            total = gate_ref[...] * total
            if out % 2:
                send_ref[out // 2] = total.astype(BF16)
            else:
                keep_ref[out // 2] = total

    return call(
        kernel,
        [struct((even, rows, part), F32), struct((even, rows, part), BF16)],
        (place, expert_weight, gate, *pieces),
        [SMEM] + [VMEM] * (2 + experts),
        wait,
        cost=2 * rows * wide * width,
    )


def add_parts(keep, arrived, wait=()):
    count, rows, wide = keep.shape
    half = count // 2

    def kernel(keep_ref, arrived_ref, *outs):
        for at in range(count):
            total = keep_ref[at] + arrived_ref[at].astype(F32)
            if count == 1:
                outs[0][...] = total.astype(BF16)
            else:
                outs[at // half][at % half] = total.astype(outs[at // half].dtype)

    if count == 1:
        shapes = struct((rows, wide), BF16)
    else:
        shapes = [struct((half, rows, wide), F32), struct((half, rows, wide), BF16)]
    return call(kernel, shapes, (keep, arrived), [VMEM] * 2, wait)


def per_device(query, key, value, grad, inputs, expert_ids, route_gates, expert_weight):
    width = query.shape[1]
    heads = width // DH
    experts = lax.axis_size("exp")
    count = lax.axis_size("seq")
    size = 4
    groups = count // size
    many = heads // 2
    place = place_of()

    own_columns, one, two, gate = prepare_inputs(
        inputs, expert_ids.T, route_gates.T, place, size, experts, count
    )
    by_two = swap(two, "seq", 2)

    total, sent, query, grad = own_states(query, grad, [two])
    later = [swap(sent, "seq", 1)]
    other_total, other_sent, key, value = own_states(key, value, [sent])
    total, sent = add_arrived(total, later[0], False, [other_sent])
    later.append(swap(sent, "seq", 2))
    earlier = [swap(after(other_sent, sent), "seq", 1)]
    by_one = swap(stack(one, by_two, (None, 1), [sent]), "seq", 1)
    first_half = intra_keys_values(query, key, value, grad, 0, many, [sent])
    waits = [first_half]
    mask = 4
    while mask < count:
        total, sent = add_arrived(total, later[-1], 2 * mask >= count, waits)
        later.append(swap(sent, "seq", mask))
        other_total, other_sent = add_arrived(other_total, earlier[-1], False, [sent])
        earlier.append(swap(other_sent, "seq", mask // 2))
        waits = [other_sent]
        mask *= 2
    second_half = intra_keys_values(query, key, value, grad, many, heads - many, [sent])
    by_two_other, by_one_other = swap(by_two, "exp", 1), swap(by_one, "exp", 1)
    weighted = weigh_inputs(
        own_columns,
        [
            [(by_one, 0), (by_one_other, 0)],
            [(by_two, 0), (by_two_other, 0)],
            [(by_one, 1), (by_one_other, 1)],
        ],
        place,
        experts,
        [second_half],
    )
    other_total, other_sent = add_arrived(other_total, earlier[-1], True, [weighted])

    intra = [first_half, second_half]
    (lead,) = finish_keys_values(intra, key, value, later, place, [(0, None)], (), [other_sent])
    near = [(swap(lead, "seq", 1), None)]
    across = [(swap(lead, "seq", 2), None)]
    every, second, rest = finish_keys_values(
        intra, key, value, later, place, [(0, heads), (1, None), (2, heads - 2)], (lead,)
    )
    earlier.append(swap(after(other_sent, every), "seq", count // 2))
    across.append((swap(second, "seq", 2), None))
    rest = swap(rest, "seq", 2)
    across += [(rest, at) for at in range(heads - 2)]
    far = swap(every, "exp", 2)
    pieces = [every, swap(every, "exp", 1), far, swap(far, "exp", 1)]
    relayed = [(swap(after(across[0][0], near[0][0]), "seq", 1), None)]
    owns, others = [], []
    waits = []
    for number in range(heads):
        if number:
            stacked = stack(
                every, across[number][0], (number, across[number][1]), [relayed[number - 1][0]]
            )
            pair = swap(stacked, "seq", 1)
            near.append((pair, 0))
            relayed.append((pair, 1))
        if number == 1:
            gradient_of_keys, value_grad, token = place_keys_values(every, [stacked])
            waits = [token]
        elif number == 2:
            gradient_of_queries, token = query_grads(key, value, grad, earlier, place, [stacked])
            waits = [token]
        elif number == 3:
            keep, send = input_products(pieces, expert_weight, gate, place, [stacked])
            waits = [send]
        if number >= 2:
            waits.append(touch([*others[number - 2], owns[number - 1]]))
        own, other = weight_product(
            weighted, [(every, number), near[number], across[number], relayed[number]], groups, waits
        )
        owns.append(own)
        others.append([shift(array, "seq", size * (hop + 1)) for hop, array in enumerate(other)])
    keep, send = add_parts(keep, swap(send, "exp", 1), [owns[-1]])
    input_grad = add_parts(keep, swap(send, "exp", 2))

    hops = [[hop] for hop in range(experts)]
    placed = []
    for members in (slice(0, heads - 1), slice(heads - 1, heads)):
        own, *parts = add_partials(owns[members], others[members], hops)
        placed.append([own] + [swap(part, "exp", hop + 1) for hop, part in enumerate(parts)])
    weight_grad = place_weight_grad(placed, place, expert_weight.shape[2])
    return gradient_of_queries, gradient_of_keys, value_grad, input_grad, weight_grad


def solution(mesh):
    return jax.shard_map(
        per_device,
        mesh=mesh,
        in_specs=(
            P("seq", "exp"),
            P("seq", "exp"),
            P("seq", "exp"),
            P("seq", "exp"),
            P("seq", None),
            P("seq", None),
            P("seq", None),
            P("exp", None, None),
        ),
        out_specs=(
            P("seq", "exp"),
            P("seq", "exp"),
            P("seq", "exp"),
            P("seq", "exp"),
            P("exp", "seq", None),
        ),
        check_vma=False,
    )
```

time: 419 us -> 136 us (0.32)
  waiting for transfers between devices: 317 us -> 71.3 us
  matrix products: 48.7 us -> 0 us
  Pallas kernels: 0 us -> 25.1 us
  starting transfers between devices: 8.78 us -> 29.5 us
  between operations: 14 us -> 0.99 us
  other arithmetic: 12.3 us -> 0.08 us
  local copies, waits for them, and re-layouts: 17.1 us -> 6.77 us
    reduce_scatter x1 -> x0, waiting for transfers between devices: 245 us -> none  [per_device(): lax.psum_scatter(lax.dot_general(weighted, slot_grads, (((0,), (0,)), (()...]
    ppermute x0 -> x33, waiting for transfers between devices: none -> 71.3 us  [the longest x29 51.8 us: swap(): lax.ppermute(array, axis, [(place, place ^ mask) for place in range(count)])]
    dot_general x12 -> x0, matrix products: 48.7 us -> none  [the longest x1 10.4 us: per_device(): lax.dot_general(weighted, slot_grads, (((0,), (0,)), ((), ())), preferred...]
    all_gather x2 -> x0, waiting for transfers between devices: 35.8 us -> none  [prefix(): gathered = lax.all_gather(array.astype(jnp.bfloat16), axis)]
    all_to_all x2 -> x0, waiting for transfers between devices: 35.6 us -> none  [the longest x1 34.6 us: per_device(): lax.all_to_all(outgoing, 'exp', split_axis=0, concat_axis=3, tiled=True)]
    ppermute x0 -> x33, starting transfers between devices: none -> 29.5 us  [the longest x29 24.4 us: swap(): lax.ppermute(array, axis, [(place, place ^ mask) for place in range(count)])]
    pallas_call x0 -> x30, Pallas kernels: none -> 25.1 us  [call(): pl.pallas_call(body, out_shape=out_shape, grid_spec=pltpu.PrefetchScalarG...]
    all_to_all x2 -> x0, starting transfers between devices: 8.48 us -> none  [the longest x1 4.77 us: per_device(): lax.all_to_all(outgoing, 'exp', split_axis=0, concat_axis=3, tiled=True)]
  transfers between devices with their start and end apart: 5 -> 33, of which waited for: 4 -> 18; matrix products, arithmetic and copies ran while one was open for 13% -> 0% of each run, Pallas kernels for 0% -> 16%
where the time goes in v2:
time: 136 us; the launch traced here: 134 us
  waiting for transfers between devices  71.3 us (52%)
  starting transfers between devices  29.5 us (22%)
  Pallas kernels  25.1 us (18%)
  local copies, waits for them, and re-layouts  6.77 us (5%)
    ppermute x29, waiting for transfers between devices, swap(): lax.ppermute(array, axis, [(place, place ^ mask) for place in range(count)])  51.8 us
    pallas_call x30, Pallas kernels, call(): pl.pallas_call(body, out_shape=out_shape, grid_spec=pltpu.PrefetchScalarG...  25.1 us
    ppermute x29, starting transfers between devices, swap(): lax.ppermute(array, axis, [(place, place ^ mask) for place in range(count)])  24.4 us
    ppermute x4, waiting for transfers between devices, shift(): lax.ppermute(array, axis, [(place, (place + step) % count) for place in r...  19.5 us
    unnamed x18, local copies, waits for them, and re-layouts  6.77 us
    ppermute x4, starting transfers between devices, shift(): lax.ppermute(array, axis, [(place, (place + step) % count) for place in r...  5.02 us
  transfers between devices with their start and end apart: 33, of which 18 were waited for; matrix products, arithmetic and copies ran while one was open for 0% of the time, Pallas kernels for 16%

profile of v2, /device:TPU:0, one launch (start us, length us, event | category | flops | bytes accessed | tf_op | source)
XLA Modules:
  0.0 133.7 jit_solution(7630974879819799761)
XLA Ops:
  0.7 1.2 copy-done
  1.9 0.7 copy-done.5
  2.6 0.7 copy-done.6
  3.3 1.0 shard_map.119
  4.3 3.1 %collective-permute-start.4 = (bf16[2,272,256]{2,1,0:T(8,128)(2,1)S(1)}, bf16[2,272,256]{2,1,0:T(8,128)(2,1)S(1)}, u32[]{:S(2)}, u32[]{:S(2)}) collective-permute-start(bf16[2,272,256]{2,1,0:T(8,128)(2,1)S(1)} %get-tuple-element.52.refs_2_), channel_id=1, source_target_pairs={{0,8},{4,12},{8,0},{12,4},{16,24},{20,28},{24,16},{28,20},{1,9},{5... | collective-permute-start | bytes 835592 | tf_op jit(solution)/shard_map/ppermute | solution.py:57
  7.4 1.0 copy-done.3
  8.4 1.0 copy-done.4
  9.4 0.3 shard_map.120
  9.8 1.6 %collective-permute-start = (bf16[4,128,128]{2,1,0:T(8,128)(2,1)S(1)}, bf16[4,128,128]{2,1,0:T(8,128)(2,1)S(1)}, u32[]{:S(2)}, u32[]{:S(2)}) collective-permute-start(bf16[4,128,128]{2,1,0:T(8,128)(2,1)S(1)} %get-tuple-element.53.refs_2_), channel_id=1, source_target_pairs={{0,4},{4,0},{8,12},{12,8},{16,20},{20,16},{24,28},{28,24},{1,5},{5... | collective-permute-start | bytes 393224 | tf_op jit(solution)/shard_map/ppermute | solution.py:57
  11.4 1.0 copy-done.1
  12.4 1.0 copy-done.2
  13.5 0.3 shard_map.121
  13.8 1.0 collective-permute-done.refs_1_.refs_3_
  14.9 1.6 %collective-permute-start.5 = (bf16[2,272,256]{2,1,0:T(8,128)(2,1)S(1)}, bf16[2,272,256]{2,1,0:T(8,128)(2,1)S(1)}, u32[]{:S(2)}, u32[]{:S(2)}) collective-permute-start(bf16[2,272,256]{2,1,0:T(8,128)(2,1)S(1)} %shard_map.126), channel_id=1, source_target_pairs={{0,4},{4,0},{8,12},{12,8},{16,20},{20,16},{24,28},{28,24},{1,5},{5... | collective-permute-start | bytes 835592 | tf_op jit(solution)/shard_map/ppermute | solution.py:57
  16.5 0.9 collective-permute-start.2
  17.4 0.5 collective-permute-start.1
  17.9 5.8 %collective-permute-done.5.refs_2_.refs_6_ = bf16[2,272,256]{2,1,0:T(8,128)(2,1)S(1)} collective-permute-done((bf16[2,272,256]{2,1,0:T(8,128)(2,1)S(1)}, bf16[2,272,256]{2,1,0:T(8,128)(2,1)S(1)}, u32[]{:S(2)}, u32[]{:S(2)}) %collective-permute-start.5) | collective-permute-done | bytes 278560 | tf_op jit(solution)/shard_map/ppermute | solution.py:57
  23.6 1.3 %shard_map.123.refs_2_.refs_6_ = f32[2,512,256]{2,1,0:T(8,128)S(1)} custom-call(bf16[512,512]{1,0:T(8,128)(2,1)S(1)} %get-tuple-element.63.refs_0_, bf16[512,512]{1,0:T(8,128)(2,1)S(1)} %get-tuple-element.54.refs_1_, bf16[512,512]{1,0:T(8,128)(2,1)S(1)} %get-tuple-element.55.refs_2_, bf16[512,512]{1,0:T(8,128)(2,1)S(1)} %get-tuple-element.56.refs_3_, ...), custom_call_target="tpu_custom_call" | custom-call | flops 1610612736 | tf_op jit(solution)/shard_map/pallas_call | solution.py:39
  25.0 2.7 %collective-permute-start.8 = (bf16[4,128,128]{2,1,0:T(8,128)(2,1)S(1)}, bf16[4,128,128]{2,1,0:T(8,128)(2,1)S(1)}, u32[]{:S(2)}, u32[]{:S(2)}) collective-permute-start(bf16[4,128,128]{2,1,0:T(8,128)(2,1)S(1)} %shard_map.124.refs_2_.refs_4_), channel_id=1, source_target_pairs={{0,16},{4,20},{8,24},{12,28},{16,0},{20,4},{24,8},{28,12},{1,17},{... | collective-permute-start | bytes 393224 | tf_op jit(solution)/shard_map/ppermute | solution.py:57
  27.7 1.2 collective-permute-start.3
  28.9 1.3 %shard_map.127.refs_8_.refs_7_ = f32[2,512,256]{2,1,0:T(8,128)S(1)} custom-call(bf16[512,512]{1,0:T(8,128)(2,1)S(1)} %get-tuple-element.63.refs_0_, bf16[512,512]{1,0:T(8,128)(2,1)S(1)} %get-tuple-element.54.refs_1_, bf16[512,512]{1,0:T(8,128)(2,1)S(1)} %get-tuple-element.55.refs_2_, bf16[512,512]{1,0:T(8,128)(2,1)S(1)} %get-tuple-element.56.refs_3_, ...), custom_call_target="tpu_custom_call" | custom-call | flops 1610612736 | tf_op jit(solution)/shard_map/pallas_call | solution.py:39
  30.3 1.3 shard_map.128.refs_2_.refs_0_
  31.6 4.0 %collective-permute-done.3.refs_1_.refs_5_ = bf16[4,128,128]{2,1,0:T(8,128)(2,1)S(1)} collective-permute-done((bf16[4,128,128]{2,1,0:T(8,128)(2,1)S(1)}, bf16[4,128,128]{2,1,0:T(8,128)(2,1)S(1)}, u32[]{:S(2)}, u32[]{:S(2)}) %collective-permute-start.3) | collective-permute-done | bytes 131104 | tf_op jit(solution)/shard_map/ppermute | solution.py:57
  35.6 0.8 shard_map.130.refs_8_
  36.5 1.1 shard_map.131
  37.6 1.6 %collective-permute-start.17 = (bf16[4,512,256]{2,1,0:T(8,128)(2,1)S(1)}, bf16[4,512,256]{2,1,0:T(8,128)(2,1)S(1)}, u32[]{:S(2)}, u32[]{:S(2)}) collective-permute-start(bf16[4,512,256]{2,1,0:T(8,128)(2,1)S(1)} %get-tuple-element.68.refs_0_.refs_3_.refs_1_), channel_id=1, source_target_pairs={{0,2},{1,3},{2,0},{3,1},{4,6},{5,7},{6,4},{7,5},{8,10},{9,11},{10,... | collective-permute-start | bytes 3145736 | tf_op jit(solution)/shard_map/ppermute | solution.py:57
  39.2 1.5 %collective-permute-start.13 = (bf16[512,256]{1,0:T(8,128)(2,1)S(1)}, bf16[512,256]{1,0:T(8,128)(2,1)S(1)}, u32[]{:S(2)}, u32[]{:S(2)}) collective-permute-start(bf16[512,256]{1,0:T(8,128)(2,1)S(1)} %shard_map.130.refs_8_), channel_id=1, source_target_pairs={{0,4},{4,0},{8,12},{12,8},{16,20},{20,16},{24,28},{28,24},{1,5},{5... | collective-permute-start | bytes 786440 | tf_op jit(solution)/shard_map/ppermute | solution.py:57
  40.7 0.9 collective-permute-start.12
  41.6 1.1 collective-permute-start.11
  42.7 3.8 %collective-permute-done.13.refs_2_ = bf16[512,256]{1,0:T(8,128)(2,1)S(1)} collective-permute-done((bf16[512,256]{1,0:T(8,128)(2,1)S(1)}, bf16[512,256]{1,0:T(8,128)(2,1)S(1)}, u32[]{:S(2)}, u32[]{:S(2)}) %collective-permute-start.13) | collective-permute-done | bytes 262176 | tf_op jit(solution)/shard_map/ppermute | solution.py:57
  46.5 3.4 %collective-permute-done.12.refs_3_ = bf16[512,256]{1,0:T(8,128)(2,1)S(1)} collective-permute-done((bf16[512,256]{1,0:T(8,128)(2,1)S(1)}, bf16[512,256]{1,0:T(8,128)(2,1)S(1)}, u32[]{:S(2)}, u32[]{:S(2)}) %collective-permute-start.12) | collective-permute-done | bytes 262176 | tf_op jit(solution)/shard_map/ppermute | solution.py:57
  49.9 0.5 collective-permute-start.14
  50.4 0.9 collective-permute-start.10
  51.3 4.2 %collective-permute-done.11.refs_1_.refs_3_ = bf16[512,256]{1,0:T(8,128)(2,1)S(1)} collective-permute-done((bf16[512,256]{1,0:T(8,128)(2,1)S(1)}, bf16[512,256]{1,0:T(8,128)(2,1)S(1)}, u32[]{:S(2)}, u32[]{:S(2)}) %collective-permute-start.11) | collective-permute-done | bytes 262176 | tf_op jit(solution)/shard_map/ppermute | solution.py:57
  55.5 3.2 %collective-permute-done.14.refs_2_.refs_4_ = bf16[512,256]{1,0:T(8,128)(2,1)S(1)} collective-permute-done((bf16[512,256]{1,0:T(8,128)(2,1)S(1)}, bf16[512,256]{1,0:T(8,128)(2,1)S(1)}, u32[]{:S(2)}, u32[]{:S(2)}) %collective-permute-start.14) | collective-permute-done | bytes 262176 | tf_op jit(solution)/shard_map/ppermute | solution.py:57
  58.7 0.5 collective-permute-start.15
  59.3 2.9 %collective-permute-done.17.refs_5_ = bf16[4,512,256]{2,1,0:T(8,128)(2,1)S(1)} collective-permute-done((bf16[4,512,256]{2,1,0:T(8,128)(2,1)S(1)}, bf16[4,512,256]{2,1,0:T(8,128)(2,1)S(1)}, u32[]{:S(2)}, u32[]{:S(2)}) %collective-permute-start.17) | collective-permute-done | bytes 1048608 | tf_op jit(solution)/shard_map/ppermute | solution.py:57
  62.1 2.5 %collective-permute-done.10.refs_1_.refs_3_ = bf16[2,512,256]{2,1,0:T(8,128)(2,1)S(1)} collective-permute-done((bf16[2,512,256]{2,1,0:T(8,128)(2,1)S(1)}, bf16[2,512,256]{2,1,0:T(8,128)(2,1)S(1)}, u32[]{:S(2)}, u32[]{:S(2)}) %collective-permute-start.10) | collective-permute-done | bytes 524320 | tf_op jit(solution)/shard_map/ppermute | solution.py:57
  64.6 6.0 %collective-permute-done.15.refs_2_.refs_4_ = bf16[2,512,256]{2,1,0:T(8,128)(2,1)S(1)} collective-permute-done((bf16[2,512,256]{2,1,0:T(8,128)(2,1)S(1)}, bf16[2,512,256]{2,1,0:T(8,128)(2,1)S(1)}, u32[]{:S(2)}, u32[]{:S(2)}) %collective-permute-start.15) | collective-permute-done | bytes 524320 | tf_op jit(solution)/shard_map/ppermute | solution.py:57
  70.7 1.0 shard_map.135
  71.8 1.3 shard_map.139
  73.1 3.0 %collective-permute-start.23 = (bf16[4,128,256]{2,1,0:T(8,128)(2,1)S(1)}, bf16[4,128,256]{2,1,0:T(8,128)(2,1)S(1)}, u32[]{:S(2)}, u32[]{:S(2)}) collective-permute-start(bf16[4,128,256]{2,1,0:T(8,128)(2,1)S(1)} %get-tuple-element.82), channel_id=1, source_target_pairs={{0,16},{4,20},{8,24},{12,28},{16,0},{20,4},{24,8},{28,12},{1,17},{... | collective-permute-start | bytes 786440 | tf_op jit(solution)/shard_map/ppermute | solution.py:62
  76.0 1.2 shard_map.138
  77.3 4.9 %collective-permute-done.19.refs_2_.refs_4_ = bf16[2,512,256]{2,1,0:T(8,128)(2,1)S(1)} collective-permute-done((bf16[2,512,256]{2,1,0:T(8,128)(2,1)S(1)}, bf16[2,512,256]{2,1,0:T(8,128)(2,1)S(1)}, u32[]{:S(2)}, u32[]{:S(2)}) %collective-permute-start.19) | collective-permute-done | bytes 524320 | tf_op jit(solution)/shard_map/ppermute | solution.py:57
  82.3 5.3 %shard_map.137 = (f32[2,512,256]{2,1,0:T(8,128)S(1)}, bf16[2,512,256]{2,1,0:T(8,128)(2,1)S(1)}) custom-call(s32[2]{0:T(128)S(1)} %pad_add_fusion.refs_0_, bf16[1,1024,4096]{2,1,0:T(8,128)(2,1)S(1)} %bitcast.7, f32[512,1]{1,0:T(8,128)S(1)} %get-tuple-element.76.refs_2_, bf16[4,512,256]{2,1,0:T(8,128)(2,1)S(1)} %get-tuple-element.68.refs_0_.refs_3_.refs_1_, ...), custom_call_target="tpu_custom_call" | custom-call | flops 4294967296 | tf_op jit(solution)/shard_map/pallas_call | solution.py:39
  87.8 2.7 %shard_map.134 = (bf16[512,512]{1,0:T(8,128)(2,1)}, f32[8,128]{1,0:T(8,128)S(1)}) custom-call(s32[2]{0:T(128)S(1)} %pad_add_fusion.refs_0_, bf16[512,512]{1,0:T(8,128)(2,1)S(1)} %get-tuple-element.54.refs_1_, bf16[512,512]{1,0:T(8,128)(2,1)S(1)} %get-tuple-element.55.refs_2_, bf16[512,512]{1,0:T(8,128)(2,1)S(1)} %get-tuple-element.56.refs_3_, ...), custom_call_target="tpu_custom_call" | custom-call | flops 3221225472 | tf_op jit(solution)/shard_map/pallas_call | solution.py:39
  90.6 2.4 %collective-permute-done.23.refs_0_.refs_1_ = bf16[4,128,256]{2,1,0:T(8,128)(2,1)S(1)} collective-permute-done((bf16[4,128,256]{2,1,0:T(8,128)(2,1)S(1)}, bf16[4,128,256]{2,1,0:T(8,128)(2,1)S(1)}, u32[]{:S(2)}, u32[]{:S(2)}) %collective-permute-start.23) | collective-permute-done | bytes 262176 | tf_op jit(solution)/shard_map/ppermute | solution.py:62
  93.0 1.2 shard_map.141
  94.3 0.5 collective-permute-start.25
  94.8 1.0 collective-permute-done.22.refs_0_.refs_3_
  95.8 1.2 shard_map.143
  97.1 1.5 %collective-permute-start.29 = (bf16[4,128,256]{2,1,0:T(8,128)(2,1)S(1)}, bf16[4,128,256]{2,1,0:T(8,128)(2,1)S(1)}, u32[]{:S(2)}, u32[]{:S(2)}) collective-permute-start(bf16[4,128,256]{2,1,0:T(8,128)(2,1)S(1)} %get-tuple-element.94), channel_id=1, source_target_pairs={{0,16},{4,20},{8,24},{12,28},{16,0},{20,4},{24,8},{28,12},{1,17},{... | collective-permute-start | bytes 786440 | tf_op jit(solution)/shard_map/ppermute | solution.py:62
  98.6 12.1 %collective-permute-done.25.refs_5_ = bf16[4,128,256]{2,1,0:T(8,128)(2,1)S(1)} collective-permute-done((bf16[4,128,256]{2,1,0:T(8,128)(2,1)S(1)}, bf16[4,128,256]{2,1,0:T(8,128)(2,1)S(1)}, u32[]{:S(2)}, u32[]{:S(2)}) %collective-permute-start.25) | collective-permute-done | bytes 262176 | tf_op jit(solution)/shard_map/ppermute | solution.py:62
  110.7 0.1 shard_map.146
  110.9 2.0 %collective-permute-start.27 = (bf16[1,3,128,256]{3,2,1,0:T(8,128)(2,1)S(1)}, bf16[1,3,128,256]{3,2,1,0:T(8,128)(2,1)S(1)}, u32[]{:S(2)}, u32[]{:S(2)}) collective-permute-start(bf16[1,3,128,256]{3,2,1,0:T(8,128)(2,1)S(1)} %get-tuple-element.92), channel_id=1, source_target_pairs={{0,2},{1,3},{2,0},{3,1},{4,6},{5,7},{6,4},{7,5},{8,10},{9,11},{10,... | collective-permute-start | bytes 589832 | tf_op jit(solution)/shard_map/ppermute | solution.py:57
  113.2 1.4 %collective-permute-start.28 = (bf16[1,3,128,256]{3,2,1,0:T(8,128)(2,1)S(1)}, bf16[1,3,128,256]{3,2,1,0:T(8,128)(2,1)S(1)}, u32[]{:S(2)}, u32[]{:S(2)}) collective-permute-start(bf16[1,3,128,256]{3,2,1,0:T(8,128)(2,1)S(1)} %get-tuple-element.93), channel_id=1, source_target_pairs={{0,3},{1,2},{2,1},{3,0},{4,7},{5,6},{6,5},{7,4},{8,11},{9,10},{10,... | collective-permute-start | bytes 589832 | tf_op jit(solution)/shard_map/ppermute | solution.py:57
  114.7 3.9 %collective-permute-done.29.refs_1_ = bf16[4,128,256]{2,1,0:T(8,128)(2,1)S(1)} collective-permute-done((bf16[4,128,256]{2,1,0:T(8,128)(2,1)S(1)}, bf16[4,128,256]{2,1,0:T(8,128)(2,1)S(1)}, u32[]{:S(2)}, u32[]{:S(2)}) %collective-permute-start.29) | collective-permute-done | bytes 262176 | tf_op jit(solution)/shard_map/ppermute | solution.py:62
  118.7 1.0 collective-permute-start.31
  119.8 0.9 collective-permute-start.32
  120.6 7.4 %collective-permute-done.28.refs_4_ = bf16[1,3,128,256]{3,2,1,0:T(8,128)(2,1)S(1)} collective-permute-done((bf16[1,3,128,256]{3,2,1,0:T(8,128)(2,1)S(1)}, bf16[1,3,128,256]{3,2,1,0:T(8,128)(2,1)S(1)}, u32[]{:S(2)}, u32[]{:S(2)}) %collective-permute-start.28) | collective-permute-done | bytes 196640 | tf_op jit(solution)/shard_map/ppermute | solution.py:57
  128.0 2.0 %collective-permute-done.31.refs_7_ = bf16[1,1,128,256]{3,2,1,0:T(8,128)(2,1)S(1)} collective-permute-done((bf16[1,1,128,256]{3,2,1,0:T(8,128)(2,1)S(1)}, bf16[1,1,128,256]{3,2,1,0:T(8,128)(2,1)S(1)}, u32[]{:S(2)}, u32[]{:S(2)}) %collective-permute-start.31) | collective-permute-done | bytes 65568 | tf_op jit(solution)/shard_map/ppermute | solution.py:57
  130.0 0.8 collective-permute-done.32.refs_8_
  130.8 2.1 %shard_map.148 = f32[1,128,4096]{2,1,0:T(8,128)} custom-call(s32[2]{0:T(128)S(1)} %pad_add_fusion.refs_0_, f32[1,3,128,256]{3,2,1,0:T(8,128)S(1)} %get-tuple-element.90.refs_1_, bf16[1,3,128,256]{3,2,1,0:T(8,128)(2,1)S(1)} %collective-permute-done.26.refs_2_, bf16[1,3,128,256]{3,2,1,0:T(8,128)(2,1)S(1)} %collective-permute-done.27.refs_3_, ...), custom_call_target="tpu_custom_call" | custom-call | tf_op jit(solution)/shard_map/pallas_call | solution.py:39
  132.9 0.8 shard_map.145
  (52 shorter events, 1.2 us)
Async XLA Ops:
  0.7 1.2 copy-start
  1.9 0.7 copy-start.5
  2.6 0.7 copy-start.6
  4.3 10.6 %collective-permute-start.4 = (bf16[2,272,256]{2,1,0:T(8,128)(2,1)S(1)}, bf16[2,272,256]{2,1,0:T(8,128)(2,1)S(1)}, u32[]{:S(2)}, u32[]{:S(2)}) collective-permute-start(bf16[2,272,256]{2,1,0:T(8,128)(2,1)S(1)} %get-tuple-element.52.refs_2_), channel_id=1, source_target_pairs={{0,8},{4,12},{8,0},{12,4},{16,24},{20,28},{24,16},{28,20},{1,9},{5... | collective-permute-start | bytes 835592 | tf_op jit(solution)/shard_map/ppermute | solution.py:57
  7.4 1.0 copy-start.3
  8.4 1.0 copy-start.4
  9.8 5.0 %collective-permute-start = (bf16[4,128,128]{2,1,0:T(8,128)(2,1)S(1)}, bf16[4,128,128]{2,1,0:T(8,128)(2,1)S(1)}, u32[]{:S(2)}, u32[]{:S(2)}) collective-permute-start(bf16[4,128,128]{2,1,0:T(8,128)(2,1)S(1)} %get-tuple-element.53.refs_2_), channel_id=1, source_target_pairs={{0,4},{4,0},{8,12},{12,8},{16,20},{20,16},{24,28},{28,24},{1,5},{5... | collective-permute-start | bytes 393224 | tf_op jit(solution)/shard_map/ppermute | solution.py:57
  11.4 1.0 copy-start.1
  12.4 1.0 copy-start.2
  14.9 8.7 %collective-permute-start.5 = (bf16[2,272,256]{2,1,0:T(8,128)(2,1)S(1)}, bf16[2,272,256]{2,1,0:T(8,128)(2,1)S(1)}, u32[]{:S(2)}, u32[]{:S(2)}) collective-permute-start(bf16[2,272,256]{2,1,0:T(8,128)(2,1)S(1)} %shard_map.126), channel_id=1, source_target_pairs={{0,4},{4,0},{8,12},{12,8},{16,20},{20,16},{24,28},{28,24},{1,5},{5... | collective-permute-start | bytes 835592 | tf_op jit(solution)/shard_map/ppermute | solution.py:57
  16.5 8.5 %collective-permute-start.2 = (bf16[4,128,128]{2,1,0:T(8,128)(2,1)S(1)}, bf16[4,128,128]{2,1,0:T(8,128)(2,1)S(1)}, u32[]{:S(2)}, u32[]{:S(2)}) collective-permute-start(bf16[4,128,128]{2,1,0:T(8,128)(2,1)S(1)} %get-tuple-element.59.refs_4_.refs_2_), channel_id=1, source_target_pairs={{0,8},{4,12},{8,0},{12,4},{16,24},{20,28},{24,16},{28,20},{1,9},{5... | collective-permute-start | bytes 393224 | tf_op jit(solution)/shard_map/ppermute | solution.py:57
  17.4 10.3 %collective-permute-start.1 = (bf16[4,128,128]{2,1,0:T(8,128)(2,1)S(1)}, bf16[4,128,128]{2,1,0:T(8,128)(2,1)S(1)}, u32[]{:S(2)}, u32[]{:S(2)}) collective-permute-start(bf16[4,128,128]{2,1,0:T(8,128)(2,1)S(1)} %get-tuple-element.60.refs_2_), channel_id=1, source_target_pairs={{0,4},{4,0},{8,12},{12,8},{16,20},{20,16},{24,28},{28,24},{1,5},{5... | collective-permute-start | bytes 393224 | tf_op jit(solution)/shard_map/ppermute | solution.py:57
  17.9 12.4 %collective-permute-start.7 = (bf16[2,272,256]{2,1,0:T(8,128)(2,1)S(1)}, bf16[2,272,256]{2,1,0:T(8,128)(2,1)S(1)}, u32[]{:S(2)}, u32[]{:S(2)}) collective-permute-start(bf16[2,272,256]{2,1,0:T(8,128)(2,1)S(1)} %collective-permute-done.4.refs_1_.refs_4_), channel_id=1, source_target_pairs={{0,1},{1,0},{2,3},{3,2},{4,5},{5,4},{6,7},{7,6},{8,9},{9,8},{10,11... | collective-permute-start | bytes 835592 | tf_op jit(solution)/shard_map/ppermute | solution.py:57
  23.6 6.7 %collective-permute-start.6 = (bf16[2,272,256]{2,1,0:T(8,128)(2,1)S(1)}, bf16[2,272,256]{2,1,0:T(8,128)(2,1)S(1)}, u32[]{:S(2)}, u32[]{:S(2)}) collective-permute-start(bf16[2,272,256]{2,1,0:T(8,128)(2,1)S(1)} %collective-permute-done.5.refs_2_.refs_6_), channel_id=1, source_target_pairs={{0,1},{1,0},{2,3},{3,2},{4,5},{5,4},{6,7},{7,6},{8,9},{9,8},{10,11... | collective-permute-start | bytes 835592 | tf_op jit(solution)/shard_map/ppermute | solution.py:57
  25.0 10.6 %collective-permute-start.8 = (bf16[4,128,128]{2,1,0:T(8,128)(2,1)S(1)}, bf16[4,128,128]{2,1,0:T(8,128)(2,1)S(1)}, u32[]{:S(2)}, u32[]{:S(2)}) collective-permute-start(bf16[4,128,128]{2,1,0:T(8,128)(2,1)S(1)} %shard_map.124.refs_2_.refs_4_), channel_id=1, source_target_pairs={{0,16},{4,20},{8,24},{12,28},{16,0},{20,4},{24,8},{28,12},{1,17},{... | collective-permute-start | bytes 393224 | tf_op jit(solution)/shard_map/ppermute | solution.py:57
  27.7 7.8 %collective-permute-start.3 = (bf16[4,128,128]{2,1,0:T(8,128)(2,1)S(1)}, bf16[4,128,128]{2,1,0:T(8,128)(2,1)S(1)}, u32[]{:S(2)}, u32[]{:S(2)}) collective-permute-start(bf16[4,128,128]{2,1,0:T(8,128)(2,1)S(1)} %get-tuple-element.64), channel_id=1, source_target_pairs={{0,8},{4,12},{8,0},{12,4},{16,24},{20,28},{24,16},{28,20},{1,9},{5... | collective-permute-start | bytes 393224 | tf_op jit(solution)/shard_map/ppermute | solution.py:57
  37.6 24.5 %collective-permute-start.17 = (bf16[4,512,256]{2,1,0:T(8,128)(2,1)S(1)}, bf16[4,512,256]{2,1,0:T(8,128)(2,1)S(1)}, u32[]{:S(2)}, u32[]{:S(2)}) collective-permute-start(bf16[4,512,256]{2,1,0:T(8,128)(2,1)S(1)} %get-tuple-element.68.refs_0_.refs_3_.refs_1_), channel_id=1, source_target_pairs={{0,2},{1,3},{2,0},{3,1},{4,6},{5,7},{6,4},{7,5},{8,10},{9,11},{10,... | collective-permute-start | bytes 3145736 | tf_op jit(solution)/shard_map/ppermute | solution.py:57
  39.2 7.3 %collective-permute-start.13 = (bf16[512,256]{1,0:T(8,128)(2,1)S(1)}, bf16[512,256]{1,0:T(8,128)(2,1)S(1)}, u32[]{:S(2)}, u32[]{:S(2)}) collective-permute-start(bf16[512,256]{1,0:T(8,128)(2,1)S(1)} %shard_map.130.refs_8_), channel_id=1, source_target_pairs={{0,4},{4,0},{8,12},{12,8},{16,20},{20,16},{24,28},{28,24},{1,5},{5... | collective-permute-start | bytes 786440 | tf_op jit(solution)/shard_map/ppermute | solution.py:57
  40.7 9.2 %collective-permute-start.12 = (bf16[512,256]{1,0:T(8,128)(2,1)S(1)}, bf16[512,256]{1,0:T(8,128)(2,1)S(1)}, u32[]{:S(2)}, u32[]{:S(2)}) collective-permute-start(bf16[512,256]{1,0:T(8,128)(2,1)S(1)} %shard_map.130.refs_8_), channel_id=1, source_target_pairs={{0,8},{4,12},{8,0},{12,4},{16,24},{20,28},{24,16},{28,20},{1,9},{5... | collective-permute-start | bytes 786440 | tf_op jit(solution)/shard_map/ppermute | solution.py:57
  41.6 14.0 %collective-permute-start.11 = (bf16[512,256]{1,0:T(8,128)(2,1)S(1)}, bf16[512,256]{1,0:T(8,128)(2,1)S(1)}, u32[]{:S(2)}, u32[]{:S(2)}) collective-permute-start(bf16[512,256]{1,0:T(8,128)(2,1)S(1)} %get-tuple-element.71), channel_id=1, source_target_pairs={{0,8},{4,12},{8,0},{12,4},{16,24},{20,28},{24,16},{28,20},{1,9},{5... | collective-permute-start | bytes 786440 | tf_op jit(solution)/shard_map/ppermute | solution.py:57
  49.9 8.8 %collective-permute-start.14 = (bf16[512,256]{1,0:T(8,128)(2,1)S(1)}, bf16[512,256]{1,0:T(8,128)(2,1)S(1)}, u32[]{:S(2)}, u32[]{:S(2)}) collective-permute-start(bf16[512,256]{1,0:T(8,128)(2,1)S(1)} %collective-permute-done.12.refs_3_), channel_id=1, source_target_pairs={{0,4},{4,0},{8,12},{12,8},{16,20},{20,16},{24,28},{28,24},{1,5},{5... | collective-permute-start | bytes 786440 | tf_op jit(solution)/shard_map/ppermute | solution.py:57
  50.4 14.2 %collective-permute-start.10 = (bf16[2,512,256]{2,1,0:T(8,128)(2,1)S(1)}, bf16[2,512,256]{2,1,0:T(8,128)(2,1)S(1)}, u32[]{:S(2)}, u32[]{:S(2)}) collective-permute-start(bf16[2,512,256]{2,1,0:T(8,128)(2,1)S(1)} %get-tuple-element.70), channel_id=1, source_target_pairs={{0,8},{4,12},{8,0},{12,4},{16,24},{20,28},{24,16},{28,20},{1,9},{5... | collective-permute-start | bytes 1572872 | tf_op jit(solution)/shard_map/ppermute | solution.py:57
  58.7 11.8 %collective-permute-start.15 = (bf16[2,512,256]{2,1,0:T(8,128)(2,1)S(1)}, bf16[2,512,256]{2,1,0:T(8,128)(2,1)S(1)}, u32[]{:S(2)}, u32[]{:S(2)}) collective-permute-start(bf16[2,512,256]{2,1,0:T(8,128)(2,1)S(1)} %shard_map.132.refs_1_), channel_id=1, source_target_pairs={{0,4},{4,0},{8,12},{12,8},{16,20},{20,16},{24,28},{28,24},{1,5},{5... | collective-permute-start | bytes 1572872 | tf_op jit(solution)/shard_map/ppermute | solution.py:57
  59.3 22.9 %collective-permute-start.16 = (bf16[4,512,256]{2,1,0:T(8,128)(2,1)S(1)}, bf16[4,512,256]{2,1,0:T(8,128)(2,1)S(1)}, u32[]{:S(2)}, u32[]{:S(2)}) collective-permute-start(bf16[4,512,256]{2,1,0:T(8,128)(2,1)S(1)} %get-tuple-element.68.refs_0_.refs_3_.refs_1_), channel_id=1, source_target_pairs={{0,1},{1,0},{2,3},{3,2},{4,5},{5,4},{6,7},{7,6},{8,9},{9,8},{10,11... | collective-permute-start | bytes 3145736 | tf_op jit(solution)/shard_map/ppermute | solution.py:57
  62.1 20.2 %collective-permute-start.18 = (bf16[4,512,256]{2,1,0:T(8,128)(2,1)S(1)}, bf16[4,512,256]{2,1,0:T(8,128)(2,1)S(1)}, u32[]{:S(2)}, u32[]{:S(2)}) collective-permute-start(bf16[4,512,256]{2,1,0:T(8,128)(2,1)S(1)} %collective-permute-done.17.refs_5_), channel_id=1, source_target_pairs={{0,1},{1,0},{2,3},{3,2},{4,5},{5,4},{6,7},{7,6},{8,9},{9,8},{10,11... | collective-permute-start | bytes 3145736 | tf_op jit(solution)/shard_map/ppermute | solution.py:57
  70.6 11.6 %collective-permute-start.19 = (bf16[2,512,256]{2,1,0:T(8,128)(2,1)S(1)}, bf16[2,512,256]{2,1,0:T(8,128)(2,1)S(1)}, u32[]{:S(2)}, u32[]{:S(2)}) collective-permute-start(bf16[2,512,256]{2,1,0:T(8,128)(2,1)S(1)} %shard_map.133.refs_7_), channel_id=1, source_target_pairs={{0,4},{4,0},{8,12},{12,8},{16,20},{20,16},{24,28},{28,24},{1,5},{5... | collective-permute-start | bytes 1572872 | tf_op jit(solution)/shard_map/ppermute | solution.py:57
  70.7 17.2 %collective-permute-start.9 = (bf16[4,128,128]{2,1,0:T(8,128)(2,1)S(1)}, bf16[4,128,128]{2,1,0:T(8,128)(2,1)S(1)}, u32[]{:S(2)}, u32[]{:S(2)}) collective-permute-start(bf16[4,128,128]{2,1,0:T(8,128)(2,1)S(1)} %shard_map.129.refs_8_), channel_id=1, source_target_pairs={{0,16},{4,20},{8,24},{12,28},{16,0},{20,4},{24,8},{28,12},{1,17},{... | collective-permute-start | bytes 393224 | tf_op jit(solution)/shard_map/ppermute | solution.py:57
  71.8 10.5 %slice-start = ((s8[8388608]{0:T(1024)(128)(4,1)}), s8[4194304]{0:T(1024)(128)(4,1)S(1)}, s32[]{:S(2)}) async-start(s8[8388608]{0:T(1024)(128)(4,1)} %bitcast.6), calls=%async_computation | async-start | bytes 8388608
  73.1 20.0 %collective-permute-start.23 = (bf16[4,128,256]{2,1,0:T(8,128)(2,1)S(1)}, bf16[4,128,256]{2,1,0:T(8,128)(2,1)S(1)}, u32[]{:S(2)}, u32[]{:S(2)}) collective-permute-start(bf16[4,128,256]{2,1,0:T(8,128)(2,1)S(1)} %get-tuple-element.82), channel_id=1, source_target_pairs={{0,16},{4,20},{8,24},{12,28},{16,0},{20,4},{24,8},{28,12},{1,17},{... | collective-permute-start | bytes 786440 | tf_op jit(solution)/shard_map/ppermute | solution.py:62
  76.0 6.3 %slice-start.1 = ((s8[8388608]{0:T(1024)(128)(4,1)}), s8[4194304]{0:T(1024)(128)(4,1)S(1)}, s32[]{:S(2)}) async-start(s8[8388608]{0:T(1024)(128)(4,1)} %bitcast.6), calls=%async_computation.1 | async-start | bytes 8388608
  82.2 13.7 %collective-permute-start.22 = (bf16[4,128,256]{2,1,0:T(8,128)(2,1)S(1)}, bf16[4,128,256]{2,1,0:T(8,128)(2,1)S(1)}, u32[]{:S(2)}, u32[]{:S(2)}) collective-permute-start(bf16[4,128,256]{2,1,0:T(8,128)(2,1)S(1)} %get-tuple-element.80), channel_id=1, source_target_pairs={{0,16},{4,20},{8,24},{12,28},{16,0},{20,4},{24,8},{28,12},{1,17},{... | collective-permute-start | bytes 786440 | tf_op jit(solution)/shard_map/ppermute | solution.py:62
  82.2 13.6 %collective-permute-start.21 = (bf16[2,512,256]{2,1,0:T(8,128)(2,1)S(1)}, bf16[2,512,256]{2,1,0:T(8,128)(2,1)S(1)}, u32[]{:S(2)}, u32[]{:S(2)}) collective-permute-start(bf16[2,512,256]{2,1,0:T(8,128)(2,1)S(1)} %shard_map.136.refs_7_), channel_id=1, source_target_pairs={{0,4},{4,0},{8,12},{12,8},{16,20},{20,16},{24,28},{28,24},{1,5},{5... | collective-permute-start | bytes 1572872 | tf_op jit(solution)/shard_map/ppermute | solution.py:57
  87.7 25.3 %collective-permute-start.20 = (bf16[2,512,256]{2,1,0:T(8,128)(2,1)S(1)}, bf16[2,512,256]{2,1,0:T(8,128)(2,1)S(1)}, u32[]{:S(2)}, u32[]{:S(2)}) collective-permute-start(bf16[2,512,256]{2,1,0:T(8,128)(2,1)S(1)} %get-tuple-element.78.refs_5_), channel_id=1, source_target_pairs={{0,1},{1,0},{2,3},{3,2},{4,5},{5,4},{6,7},{7,6},{8,9},{9,8},{10,11... | collective-permute-start | bytes 1572872 | tf_op jit(solution)/shard_map/ppermute | solution.py:57
  94.3 16.4 %collective-permute-start.25 = (bf16[4,128,256]{2,1,0:T(8,128)(2,1)S(1)}, bf16[4,128,256]{2,1,0:T(8,128)(2,1)S(1)}, u32[]{:S(2)}, u32[]{:S(2)}) collective-permute-start(bf16[4,128,256]{2,1,0:T(8,128)(2,1)S(1)} %get-tuple-element.89), channel_id=1, source_target_pairs={{0,16},{4,20},{8,24},{12,28},{16,0},{20,4},{24,8},{28,12},{1,17},{... | collective-permute-start | bytes 786440 | tf_op jit(solution)/shard_map/ppermute | solution.py:62
  97.1 21.5 %collective-permute-start.29 = (bf16[4,128,256]{2,1,0:T(8,128)(2,1)S(1)}, bf16[4,128,256]{2,1,0:T(8,128)(2,1)S(1)}, u32[]{:S(2)}, u32[]{:S(2)}) collective-permute-start(bf16[4,128,256]{2,1,0:T(8,128)(2,1)S(1)} %get-tuple-element.94), channel_id=1, source_target_pairs={{0,16},{4,20},{8,24},{12,28},{16,0},{20,4},{24,8},{28,12},{1,17},{... | collective-permute-start | bytes 786440 | tf_op jit(solution)/shard_map/ppermute | solution.py:62
  110.8 7.9 %collective-permute-start.26 = (bf16[1,3,128,256]{3,2,1,0:T(8,128)(2,1)S(1)}, bf16[1,3,128,256]{3,2,1,0:T(8,128)(2,1)S(1)}, u32[]{:S(2)}, u32[]{:S(2)}) collective-permute-start(bf16[1,3,128,256]{3,2,1,0:T(8,128)(2,1)S(1)} %get-tuple-element.91), channel_id=1, source_target_pairs={{0,1},{1,0},{2,3},{3,2},{4,5},{5,4},{6,7},{7,6},{8,9},{9,8},{10,11... | collective-permute-start | bytes 589832 | tf_op jit(solution)/shard_map/ppermute | solution.py:57
  110.9 8.8 %collective-permute-start.27 = (bf16[1,3,128,256]{3,2,1,0:T(8,128)(2,1)S(1)}, bf16[1,3,128,256]{3,2,1,0:T(8,128)(2,1)S(1)}, u32[]{:S(2)}, u32[]{:S(2)}) collective-permute-start(bf16[1,3,128,256]{3,2,1,0:T(8,128)(2,1)S(1)} %get-tuple-element.92), channel_id=1, source_target_pairs={{0,2},{1,3},{2,0},{3,1},{4,6},{5,7},{6,4},{7,5},{8,10},{9,11},{10,... | collective-permute-start | bytes 589832 | tf_op jit(solution)/shard_map/ppermute | solution.py:57
  113.1 19.8 %collective-permute-start.24 = (bf16[1,512,256]{2,1,0:T(8,128)(2,1)S(1)}, bf16[1,512,256]{2,1,0:T(8,128)(2,1)S(1)}, u32[]{:S(2)}, u32[]{:S(2)}) collective-permute-start(bf16[1,512,256]{2,1,0:T(8,128)(2,1)S(1)} %get-tuple-element.87), channel_id=1, source_target_pairs={{0,2},{1,3},{2,0},{3,1},{4,6},{5,7},{6,4},{7,5},{8,10},{9,11},{10,... | collective-permute-start | bytes 786440 | tf_op jit(solution)/shard_map/ppermute | solution.py:57
  113.2 14.8 %collective-permute-start.28 = (bf16[1,3,128,256]{3,2,1,0:T(8,128)(2,1)S(1)}, bf16[1,3,128,256]{3,2,1,0:T(8,128)(2,1)S(1)}, u32[]{:S(2)}, u32[]{:S(2)}) collective-permute-start(bf16[1,3,128,256]{3,2,1,0:T(8,128)(2,1)S(1)} %get-tuple-element.93), channel_id=1, source_target_pairs={{0,3},{1,2},{2,1},{3,0},{4,7},{5,6},{6,5},{7,4},{8,11},{9,10},{10,... | collective-permute-start | bytes 589832 | tf_op jit(solution)/shard_map/ppermute | solution.py:57
  118.7 9.4 %collective-permute-start.30 = (bf16[1,1,128,256]{3,2,1,0:T(8,128)(2,1)S(1)}, bf16[1,1,128,256]{3,2,1,0:T(8,128)(2,1)S(1)}, u32[]{:S(2)}, u32[]{:S(2)}) collective-permute-start(bf16[1,1,128,256]{3,2,1,0:T(8,128)(2,1)S(1)} %get-tuple-element.96), channel_id=1, source_target_pairs={{0,1},{1,0},{2,3},{3,2},{4,5},{5,4},{6,7},{7,6},{8,9},{9,8},{10,11... | collective-permute-start | bytes 196616 | tf_op jit(solution)/shard_map/ppermute | solution.py:57
  118.7 11.2 %collective-permute-start.31 = (bf16[1,1,128,256]{3,2,1,0:T(8,128)(2,1)S(1)}, bf16[1,1,128,256]{3,2,1,0:T(8,128)(2,1)S(1)}, u32[]{:S(2)}, u32[]{:S(2)}) collective-permute-start(bf16[1,1,128,256]{3,2,1,0:T(8,128)(2,1)S(1)} %get-tuple-element.97), channel_id=1, source_target_pairs={{0,2},{1,3},{2,0},{3,1},{4,6},{5,7},{6,4},{7,5},{8,10},{9,11},{10,... | collective-permute-start | bytes 196616 | tf_op jit(solution)/shard_map/ppermute | solution.py:57
  119.8 11.0 %collective-permute-start.32 = (bf16[1,1,128,256]{3,2,1,0:T(8,128)(2,1)S(1)}, bf16[1,1,128,256]{3,2,1,0:T(8,128)(2,1)S(1)}, u32[]{:S(2)}, u32[]{:S(2)}) collective-permute-start(bf16[1,1,128,256]{3,2,1,0:T(8,128)(2,1)S(1)} %get-tuple-element.98), channel_id=1, source_target_pairs={{0,3},{1,2},{2,1},{3,0},{4,7},{5,6},{6,5},{7,4},{8,11},{9,10},{10,... | collective-permute-start | bytes 196616 | tf_op jit(solution)/shard_map/ppermute | solution.py:57

commit v3 on v2

--- a/solution.py
+++ b/solution.py
@@ -9,6 +9,7 @@
 
 DH = 128
 PAD = 16
+FIRST = 59
 MIB = 1 << 20
 BF16 = jnp.bfloat16
 F32 = jnp.float32
@@ -70,22 +71,6 @@
     return ref[:, number * DH : (number + 1) * DH]
 
 
-def own_states(first, second, wait=()):
-    rows, width = first.shape
-    heads = width // DH
-
-    def kernel(a_ref, b_ref, wide_ref, narrow_ref, a_kept, b_kept):
-        for number in range(heads):
-            state = dot(head(a_ref, number), head(b_ref, number), 0, 0)
-            wide_ref[number] = state
-            narrow_ref[number] = state.astype(BF16)
-        a_kept[...] = a_ref[...]
-        b_kept[...] = b_ref[...]
-
-    shapes = [struct((heads, DH, DH), F32), struct((heads, DH, DH), BF16)] + [struct((rows, width), BF16)] * 2
-    return call(kernel, shapes, (first, second), [VMEM] * 2, wait, cost=6 * rows * width * DH)
-
-
 def after(array, *earlier):
     return lax.optimization_barrier((array, *earlier))[0]
 
@@ -196,18 +181,14 @@
     return call(kernel, shapes, operands, [SMEM] + [VMEM] * (len(operands) - 1), wait)
 
 
-def query_grads(key, value, grad, arrived, place, wait=()):
+def intra_queries(key, value, grad, wait=()):
     rows, width = key.shape
     heads = width // DH
     tile = rows // 2
 
-    def kernel(place_ref, k_ref, v_ref, g_ref, *refs):
-        out_ref, token_ref, done, sems = refs[len(arrived) :]
-        token_ref[...] = jnp.zeros_like(token_ref)
-        copies = []
+    def kernel(k_ref, v_ref, g_ref, out_ref):
         keep = triangle(tile, True)
         for number in range(heads):
-            high, low = halves(gathered_state(place_ref[0], refs[: len(arrived)], number, False))
             k, v, grad_of = head(k_ref, number), head(v_ref, number), head(g_ref, number)
             for down in range(2):
                 upto = (down + 1) * tile
@@ -216,10 +197,30 @@
                 last = jnp.where(keep, scores[:, down * tile :], 0.0).astype(BF16)
                 if down:
                     last = jnp.concatenate([scores[:, :tile].astype(BF16), last], axis=1)
-                intra = dot(last, k[:upto], 1, 0)
-                whole_grad = intra + dot(g, high, 1, 1) + dot(g, low, 1, 1)
-                done[number, down * tile : upto, :] = whole_grad.astype(BF16)
+                out_ref[down * tile : upto, number * DH : (number + 1) * DH] = dot(last, k[:upto], 1, 0)
+
+    return call(
+        kernel,
+        struct((rows, width), F32),
+        (key, value, grad),
+        [VMEM] * 3,
+        wait,
+        cost=24 * rows * rows * width,
+    )
+
+
+def finish_queries(intra, grad, arrived, place, wait=()):
+    rows, width = grad.shape
+    heads = width // DH
+
+    def kernel(place_ref, intra_ref, g_ref, *refs):
+        out_ref, done, sems = refs[len(arrived) :]
+        copies = []
+        for number in range(heads):
+            high, low = halves(gathered_state(place_ref[0], refs[: len(arrived)], number, False))
             columns = slice(number * DH, (number + 1) * DH)
+            g = g_ref[:, columns]
+            done[number] = (intra_ref[:, columns] + dot(g, high, 1, 1) + dot(g, low, 1, 1)).astype(BF16)
             copies.append(pltpu.make_async_copy(done.at[number], out_ref.at[:, columns], sems.at[number]))
             copies[-1].start()
         for copy in copies:
@@ -227,12 +228,11 @@
 
     return call(
         kernel,
-        [struct((rows, width), BF16), TOKEN],
-        (place, key, value, grad, *arrived),
-        [SMEM] + [VMEM] * (3 + len(arrived)),
-        wait,
-        cost=24 * rows * rows * width,
-        out_specs=[HBM, VMEM],
+        struct((rows, width), BF16),
+        (place, intra, grad, *arrived),
+        [SMEM] + [VMEM] * (2 + len(arrived)),
+        wait,
+        out_specs=HBM,
         scratch_shapes=[pltpu.VMEM((heads, rows, DH), BF16), pltpu.SemaphoreType.DMA((heads,))],
     )
 
@@ -241,21 +241,39 @@
     return jnp.stack([lax.axis_index("seq"), lax.axis_index("exp")]).astype(jnp.int32)
 
 
-def prepare_inputs(inputs, ids, gates, place, size, experts, count, wait=()):
-    rows, wide = inputs.shape
+def begin(query, grad, inputs, ids, gates, place, size, experts, count):
+    rows, width = query.shape
+    wide = inputs.shape[1]
+    heads = width // DH
     groups = count // size
     deep = wide // count
     half = rows // 2
-
-    def kernel(place_ref, x_ref, id_ref, gate_ref, *refs):
-        own_ref, one_ref, two_ref, column_ref, turned = refs
-        outs = [own_ref, one_ref, two_ref.at[0], two_ref.at[1]]
+    tall = groups * deep + PAD
+
+    def kernel(place_ref, *refs):
+        sources, refs = refs[:5], refs[5:]
+        sent_ref, refs = refs[0], refs[1:]
+        outs, column_ref, refs = refs[:size], refs[size], refs[size + 1 :]
+        held, sems, turned = refs[:5], refs[5], refs[6]
+        copies = [
+            pltpu.make_async_copy(source, target, sems.at[at])
+            for at, (source, target) in enumerate(zip(sources, held))
+        ]
+        for copy in copies:
+            copy.start()
+        q_ref, g_ref, x_ref, id_ref, gate_ref = held
+        copies[0].wait()
+        copies[1].wait()
+        for number in range(heads):
+            sent_ref[number] = dot(head(q_ref, number), head(g_ref, number), 0, 0).astype(BF16)
+        for copy in copies[2:]:
+            copy.wait()
         step = DH * 2
         for start in range(0, wide, step):
             turned[start : start + step, :] = x_ref[:, start : start + step].astype(F32).T.astype(BF16)
         which = lax.broadcasted_iota(jnp.int32, (experts, rows), 0)
         weight = jnp.zeros((experts, rows), F32)
-        for slot in range(id_ref.shape[0]):
+        for slot in range(ids.shape[0]):
             weight += jnp.where(id_ref[slot : slot + 1, :] == which, gate_ref[slot : slot + 1, :], 0.0)
         mine = jnp.sum(jnp.where(which == place_ref[1], weight, 0.0), axis=0, keepdims=True)
         column_ref[...] = jnp.broadcast_to(mine, (8, rows)).T[:, :1]
@@ -281,16 +299,49 @@
                 outs[member][hop * deep : (hop + 1) * deep, :] = part
             outs[member][groups * deep :, :] = side if member else packed.astype(BF16)
 
-    tall = groups * deep + PAD
-    shapes = [struct((tall, rows), BF16), struct((tall, half), BF16), struct((2, tall, half), BF16)]
-    return call(
-        kernel,
-        shapes + [struct((rows, 1), F32)],
-        (place, inputs, ids, gates),
-        [SMEM] + [VMEM] * 3,
-        wait,
-        scratch_shapes=[pltpu.VMEM((wide, rows), BF16)],
-    )
+    messages = [struct((tall, half if member else rows), BF16) for member in range(size)]
+    return call(
+        kernel,
+        [struct((heads, DH, DH), BF16)] + messages + [struct((rows, 1), F32)],
+        (place, query, grad, inputs, ids, gates),
+        [SMEM] + [HBM] * 5,
+        limit=FIRST,
+        cost=12 * rows * width * DH,
+        scratch_shapes=[pltpu.VMEM((rows, width), BF16)] * 2
+        + [
+            pltpu.VMEM((rows, wide), BF16),
+            pltpu.VMEM(ids.shape, jnp.int32),
+            pltpu.VMEM(gates.shape, F32),
+            pltpu.SemaphoreType.DMA((5,)),
+            pltpu.VMEM((wide, rows), BF16),
+        ],
+    )
+
+
+def own_states(first, second, arrived=None, last=False, wait=()):
+    rows, width = first.shape
+    heads = width // DH
+    extra = [] if arrived is None else [arrived]
+
+    def kernel(a_ref, b_ref, *refs):
+        outs = refs[len(extra) :]
+        for number in range(heads):
+            state = dot(head(a_ref, number), head(b_ref, number), 0, 0)
+            for ref in refs[: len(extra)]:
+                state = state + ref[number].astype(F32)
+            for out in outs:
+                out[number] = state.astype(out.dtype)
+
+    shapes = [struct((heads, DH, DH), BF16)] + ([] if last else [struct((heads, DH, DH), F32)])
+    sent, *total = call(
+        kernel,
+        shapes,
+        (first, second, *extra),
+        [VMEM] * (2 + len(extra)),
+        wait,
+        cost=6 * rows * width * DH,
+    )
+    return (total[0] if total else None), sent
 
 
 def weigh_inputs(own, halves_of, place, experts, wait=()):
@@ -304,7 +355,7 @@
         out_ref = refs[len(flat)]
         odd = place_ref[1] & 1
         for at in range(1 + len(flat)):
-            ref = own_ref if at == 0 else refs[at - 1].at[flat[at - 1][1]]
+            ref = own_ref if at == 0 else refs[at - 1]
             columns = ref[:deep, :].astype(F32)
             parts = ref[deep:, :].astype(F32)
             row = lax.broadcasted_iota(jnp.int32, parts.shape, 0)
@@ -322,7 +373,7 @@
     return call(
         kernel,
         struct((experts, deep, size * rows), BF16),
-        (place, own, *[array for array, _ in flat]),
+        (place, own, *flat),
         [SMEM] + [VMEM] * (1 + len(flat)),
         wait,
     )
@@ -424,17 +475,19 @@
     )
 
 
-def place_keys_values(chunks, wait=()):
-    heads, rows, _ = chunks.shape
-
-    def kernel(chunks_ref, *refs):
-        token_ref, sems = refs[2:]
+def place_keys_values(packs, wait=()):
+    where = [(pack, at) for pack in range(len(packs)) for at in range(packs[pack].shape[0])]
+    heads = len(where)
+    rows = packs[0].shape[1]
+
+    def kernel(*refs):
+        outs, token_ref, sems = refs[len(packs) : len(packs) + 2], refs[len(packs) + 2], refs[len(packs) + 3]
         token_ref[...] = jnp.zeros_like(token_ref)
         copies = []
-        for number in range(heads):
+        for number, (pack, at) in enumerate(where):
             for side in range(2):
-                source = chunks_ref.at[number, :, side * DH : (side + 1) * DH]
-                target = refs[side].at[:, number * DH : (number + 1) * DH]
+                source = refs[pack].at[at, :, side * DH : (side + 1) * DH]
+                target = outs[side].at[:, number * DH : (number + 1) * DH]
                 copies.append(pltpu.make_async_copy(source, target, sems.at[number * 2 + side]))
         for copy in copies:
             copy.start()
@@ -444,8 +497,8 @@
     return call(
         kernel,
         [struct((rows, heads * DH), BF16)] * 2 + [TOKEN],
-        (chunks,),
-        [VMEM],
+        packs,
+        [VMEM] * len(packs),
         wait,
         out_specs=[HBM] * 2 + [VMEM],
         scratch_shapes=[pltpu.SemaphoreType.DMA((2 * heads,))],
@@ -454,24 +507,27 @@
 
 def input_products(pieces, expert_weight, gate, place, wait=()):
     experts = len(pieces)
-    heads, rows, _ = pieces[0].shape
+    packs = len(pieces[0])
+    where = [(pack, at) for pack in range(packs) for at in range(pieces[0][pack].shape[0])]
+    heads = len(where)
+    rows = pieces[0][0].shape[1]
     _, wide, width = expert_weight.shape
     part = wide // experts
     even = experts // 2
 
     def kernel(place_ref, w_ref, gate_ref, *refs):
-        keep_ref, send_ref = refs[experts:]
+        keep_ref, send_ref = refs[experts * packs :]
         for out in range(experts):
             taken = pl.ds(pl.multiple_of((place_ref[1] ^ out) * part, part), part)
             total = None
             for hop in range(experts):
-                for number in range(heads):
+                for number, (pack, at) in enumerate(where):
                     start = ((place_ref[1] ^ hop) * heads + number) * DH
                     sides = [
                         w_ref[0, taken, pl.ds(pl.multiple_of(start + side * (width // 2), DH), DH)]
                         for side in range(2)
                     ]
-                    term = dot(refs[hop][number], jnp.concatenate(sides, axis=1), 1, 1)
+                    term = dot(refs[hop * packs + pack][at], jnp.concatenate(sides, axis=1), 1, 1)
                     total = term if total is None else total + term
             total = gate_ref[...] * total
             if out % 2:
@@ -479,11 +535,12 @@
             else:
                 keep_ref[out // 2] = total
 
+    flat = [piece for row in pieces for piece in row]
     return call(
         kernel,
         [struct((even, rows, part), F32), struct((even, rows, part), BF16)],
-        (place, expert_weight, gate, *pieces),
-        [SMEM] + [VMEM] * (2 + experts),
+        (place, expert_weight, gate, *flat),
+        [SMEM] + [VMEM] * (2 + len(flat)),
         wait,
         cost=2 * rows * wide * width,
     )
@@ -518,91 +575,92 @@
     many = heads // 2
     place = place_of()
 
-    own_columns, one, two, gate = prepare_inputs(
-        inputs, expert_ids.T, route_gates.T, place, size, experts, count
-    )
-    by_two = swap(two, "seq", 2)
-
-    total, sent, query, grad = own_states(query, grad, [two])
+    sent, own_columns, one, two, three, gate = begin(
+        query, grad, inputs, expert_ids.T, route_gates.T, place, size, experts, count
+    )
+    by_two, relay = swap(two, "seq", 2), swap(three, "seq", 2)
     later = [swap(sent, "seq", 1)]
-    other_total, other_sent, key, value = own_states(key, value, [sent])
-    total, sent = add_arrived(total, later[0], False, [other_sent])
+    intra = [intra_keys_values(query, key, value, grad, 0, many)]
+    total, sent = own_states(query, grad, later[0], count == 4, [relay, intra[0]])
     later.append(swap(sent, "seq", 2))
-    earlier = [swap(after(other_sent, sent), "seq", 1)]
-    by_one = swap(stack(one, by_two, (None, 1), [sent]), "seq", 1)
-    first_half = intra_keys_values(query, key, value, grad, 0, many, [sent])
-    waits = [first_half]
+    other_total, other_sent = own_states(key, value, None, False, [sent])
+    earlier = [swap(other_sent, "seq", 1)]
+    intra.append(intra_keys_values(query, key, value, grad, many, heads - many, [other_sent]))
     mask = 4
+    waits = [intra[-1]]
     while mask < count:
         total, sent = add_arrived(total, later[-1], 2 * mask >= count, waits)
         later.append(swap(sent, "seq", mask))
-        other_total, other_sent = add_arrived(other_total, earlier[-1], False, [sent])
-        earlier.append(swap(other_sent, "seq", mask // 2))
-        waits = [other_sent]
+        waits = []
         mask *= 2
-    second_half = intra_keys_values(query, key, value, grad, many, heads - many, [sent])
-    by_two_other, by_one_other = swap(by_two, "exp", 1), swap(by_one, "exp", 1)
-    weighted = weigh_inputs(
-        own_columns,
-        [
-            [(by_one, 0), (by_one_other, 0)],
-            [(by_two, 0), (by_two_other, 0)],
-            [(by_one, 1), (by_one_other, 1)],
-        ],
-        place,
-        experts,
-        [second_half],
-    )
-    other_total, other_sent = add_arrived(other_total, earlier[-1], True, [weighted])
-
-    intra = [first_half, second_half]
-    (lead,) = finish_keys_values(intra, key, value, later, place, [(0, None)], (), [other_sent])
+    other_total, other_sent = add_arrived(other_total, earlier[0], False, [sent])
+    halves_of = [swap(one, "seq", 1), by_two, swap(relay, "seq", 1)]
+    arrived = touch(halves_of)
+    halves_of = [[half, swap(half, "exp", 1)] for half in halves_of]
+
+    (lead,) = finish_keys_values(intra, key, value, later, place, [(0, None)], (), [other_sent, arrived])
     near = [(swap(lead, "seq", 1), None)]
     across = [(swap(lead, "seq", 2), None)]
-    every, second, rest = finish_keys_values(
-        intra, key, value, later, place, [(0, heads), (1, None), (2, heads - 2)], (lead,)
-    )
-    earlier.append(swap(after(other_sent, every), "seq", count // 2))
+    front, second, rest = finish_keys_values(
+        intra, key, value, later, place, [(0, 2), (1, None), (2, heads - 2)], (lead,)
+    )
+    packs = [front, rest]
+    weighted = weigh_inputs(own_columns, halves_of, place, experts, [front])
+    own_heads = [(front, 0), (front, 1)] + [(rest, at) for at in range(heads - 2)]
     across.append((swap(second, "seq", 2), None))
-    rest = swap(rest, "seq", 2)
-    across += [(rest, at) for at in range(heads - 2)]
-    far = swap(every, "exp", 2)
-    pieces = [every, swap(every, "exp", 1), far, swap(far, "exp", 1)]
-    relayed = [(swap(after(across[0][0], near[0][0]), "seq", 1), None)]
+    rest_across = swap(rest, "seq", 2)
+    across += [(rest_across, at) for at in range(heads - 2)]
+    far = [swap(pack, "exp", 2) for pack in packs]
+    close = [swap(pack, "exp", 1) for pack in packs]
+    pieces = [packs, close, far, [swap(pack, "exp", 1) for pack in far]]
+    relayed = [(swap(after(across[0][0], near[0][0], weighted), "seq", 1), None)]
     owns, others = [], []
-    waits = []
+    fillers = []
     for number in range(heads):
         if number:
-            stacked = stack(
-                every, across[number][0], (number, across[number][1]), [relayed[number - 1][0]]
-            )
+            waits = [owns[number - 1]]
+            if number >= 2:
+                waits.append(touch(others[number - 2] + [owns[number - 1]]))
+            (mine, at), (came, came_at) = own_heads[number], across[number]
+            stacked = stack(mine, came, (at, came_at), waits)
             pair = swap(stacked, "seq", 1)
             near.append((pair, 0))
             relayed.append((pair, 1))
-        if number == 1:
-            gradient_of_keys, value_grad, token = place_keys_values(every, [stacked])
-            waits = [token]
+        if number == 0:
+            gradient_of_keys, value_grad, token = place_keys_values(packs, [weighted])
+            fillers = [token]
+        elif number == 1:
+            intra_query = intra_queries(key, value, grad, [owns[0]])
+            fillers = [intra_query]
         elif number == 2:
-            gradient_of_queries, token = query_grads(key, value, grad, earlier, place, [stacked])
-            waits = [token]
+            keep, send = input_products(pieces, expert_weight, gate, place, [owns[1]])
+            fillers = [send]
         elif number == 3:
-            keep, send = input_products(pieces, expert_weight, gate, place, [stacked])
-            waits = [send]
-        if number >= 2:
-            waits.append(touch([*others[number - 2], owns[number - 1]]))
+            mask = 2
+            while 2 * mask < count:
+                earlier.append(swap(other_sent, "seq", mask))
+                if 4 * mask < count:
+                    other_total, other_sent = add_arrived(other_total, earlier[-1], False)
+                mask *= 2
+            keep, send = add_parts(keep, swap(send, "exp", 1))
+            fillers = [touch(others[2]), touch([earlier[-1]]), send]
         own, other = weight_product(
-            weighted, [(every, number), near[number], across[number], relayed[number]], groups, waits
+            weighted, [own_heads[number], near[number], across[number], relayed[number]], groups, fillers
         )
         owns.append(own)
         others.append([shift(array, "seq", size * (hop + 1)) for hop, array in enumerate(other)])
-    keep, send = add_parts(keep, swap(send, "exp", 1), [owns[-1]])
     input_grad = add_parts(keep, swap(send, "exp", 2))
+    _, other_sent = add_arrived(other_total, earlier[-1], True, [owns[3]])
+    earlier.append(swap(other_sent, "seq", count // 2))
+    gradient_of_queries = finish_queries(intra_query, grad, earlier, place)
 
     hops = [[hop] for hop in range(experts)]
     placed = []
+    waits = []
     for members in (slice(0, heads - 1), slice(heads - 1, heads)):
-        own, *parts = add_partials(owns[members], others[members], hops)
+        own, *parts = add_partials(owns[members], others[members], hops, waits)
         placed.append([own] + [swap(part, "exp", hop + 1) for hop, part in enumerate(parts)])
+        waits = [touch(placed[0])]
     weight_grad = place_weight_grad(placed, place, expert_weight.shape[2])
     return gradient_of_queries, gradient_of_keys, value_grad, input_grad, weight_grad
 

time: 136 us -> 124 us (0.912); the launches traced: 134 us -> 124 us
  waiting for transfers between devices: 71.3 us -> 50.1 us
  starting transfers between devices: 29.5 us -> 39.5 us
  Pallas kernels: 25.1 us -> 28.2 us
  local copies, waits for them, and re-layouts: 6.77 us -> 4.21 us
    ppermute x29 -> x35, waiting for transfers between devices: 51.8 us -> 39.6 us  [swap(): lax.ppermute(array, axis, [(place, place ^ mask) for place in range(count)])]
    ppermute x4, waiting for transfers between devices: 19.5 us -> 10.5 us  [shift(): lax.ppermute(array, axis, [(place, (place + step) % count) for place in r...]
    ppermute x29 -> x35, starting transfers between devices: 24.4 us -> 32.5 us  [swap(): lax.ppermute(array, axis, [(place, place ^ mask) for place in range(count)])]
    pallas_call x30 -> x33, Pallas kernels: 25.1 us -> 28.2 us  [call(): pl.pallas_call(body, out_shape=out_shape, grid_spec=pltpu.PrefetchScalarG...]
    unnamed x18 -> x24, local copies, waits for them, and re-layouts: 6.77 us -> 4.21 us
    ppermute x4, starting transfers between devices: 5.02 us -> 6.99 us  [shift(): lax.ppermute(array, axis, [(place, (place + step) % count) for place in r...]
  transfers between devices with their start and end apart: 33 -> 39, of which waited for: 18 -> 18; matrix products, arithmetic and copies ran while one was open for 0% -> 0% of each run, Pallas kernels for 16% -> 16%
where the time goes in v3:
time: 124 us
  waiting for transfers between devices  50.1 us (40%)
  starting transfers between devices  39.5 us (32%)
  Pallas kernels  28.2 us (23%)
  local copies, waits for them, and re-layouts  4.21 us (3%)
    ppermute x35, waiting for transfers between devices, swap(): lax.ppermute(array, axis, [(place, place ^ mask) for place in range(count)])  39.6 us
    ppermute x35, starting transfers between devices, swap(): lax.ppermute(array, axis, [(place, place ^ mask) for place in range(count)])  32.5 us
    pallas_call x33, Pallas kernels, call(): pl.pallas_call(body, out_shape=out_shape, grid_spec=pltpu.PrefetchScalarG...  28.2 us
    ppermute x4, waiting for transfers between devices, shift(): lax.ppermute(array, axis, [(place, (place + step) % count) for place in r...  10.5 us
    ppermute x4, starting transfers between devices, shift(): lax.ppermute(array, axis, [(place, (place + step) % count) for place in r...  6.99 us
    unnamed x24, local copies, waits for them, and re-layouts  4.21 us
  transfers between devices with their start and end apart: 39, of which 18 were waited for; matrix products, arithmetic and copies ran while one was open for 0% of the time, Pallas kernels for 16%

profile of v3, /device:TPU:0, one launch (start us, length us, event | category | flops | bytes accessed | tf_op | source)
XLA Modules:
  0.0 123.8 jit_solution(11401574995611096788)
XLA Ops:
  0.6 0.6 pad_add_fusion.refs_0_
  1.2 3.7 %shard_map.119 = (bf16[4,128,128]{2,1,0:T(8,128)(2,1)}, bf16[272,512]{1,0:T(8,128)(2,1)}, bf16[272,256]{1,0:T(8,128)(2,1)}, bf16[272,256]{1,0:T(8,128)(2,1)}, bf...) custom-call(s32[2]{0:T(128)} %pad_add_fusion.refs_0_, bf16[512,512]{1,0:T(8,128)(2,1)} %refs_0_.8, bf16[512,512]{1,0:T(8,128)(2,1)} %refs_2_.13, ...), custom_call_target="tpu_custom_call" | custom-call | flops 402653184 | tf_op jit(solution)/shard_map/pallas_call | solution.py:40
  4.9 3.0 %collective-permute-start.7 = (bf16[4,128,128]{2,1,0:T(8,128)(2,1)}, bf16[4,128,128]{2,1,0:T(8,128)(2,1)S(1)}, u32[]{:S(2)}, u32[]{:S(2)}) collective-permute-start(bf16[4,128,128]{2,1,0:T(8,128)(2,1)} %get-tuple-element.48), channel_id=1, source_target_pairs={{0,4},{4,0},{8,12},{12,8},{16,20},{20,16},{24,28},{28,24},{1,5},{5... | collective-permute-start | bytes 393224 | tf_op jit(solution)/shard_map/ppermute | solution.py:58
  8.0 1.6 %collective-permute-start.4 = (bf16[272,256]{1,0:T(8,128)(2,1)}, bf16[272,256]{1,0:T(8,128)(2,1)S(1)}, u32[]{:S(2)}, u32[]{:S(2)}) collective-permute-start(bf16[272,256]{1,0:T(8,128)(2,1)} %get-tuple-element.47), channel_id=1, source_target_pairs={{0,8},{4,12},{8,0},{12,4},{16,24},{20,28},{24,16},{28,20},{1,9},{5... | collective-permute-start | bytes 417800 | tf_op jit(solution)/shard_map/ppermute | solution.py:58
  9.6 0.5 collective-permute-start
  10.1 1.0 copy-done
  11.1 1.0 copy-done.2
  12.2 1.0 copy-done.4
  13.2 1.0 copy-done.6
  14.3 1.4 %shard_map.120.refs_4_.refs_6_ = f32[2,512,256]{2,1,0:T(8,128)S(1)} custom-call(bf16[512,512]{1,0:T(8,128)(2,1)S(1)} %copy-done.6, bf16[512,512]{1,0:T(8,128)(2,1)S(1)} %copy-done, bf16[512,512]{1,0:T(8,128)(2,1)S(1)} %copy-done.2, bf16[512,512]{1,0:T(8,128)(2,1)S(1)} %copy-done.4), custom_call_target="tpu_custom_call" | custom-call | flops 1610612736 | tf_op jit(solution)/shard_map/pallas_call | solution.py:40
  16.3 2.1 %collective-permute-start.8 = (bf16[4,128,128]{2,1,0:T(8,128)(2,1)S(1)}, bf16[4,128,128]{2,1,0:T(8,128)(2,1)S(1)}, u32[]{:S(2)}, u32[]{:S(2)}) collective-permute-start(bf16[4,128,128]{2,1,0:T(8,128)(2,1)S(1)} %get-tuple-element.49.refs_2_), channel_id=1, source_target_pairs={{0,8},{4,12},{8,0},{12,4},{16,24},{20,28},{24,16},{28,20},{1,9},{5... | collective-permute-start | bytes 393224 | tf_op jit(solution)/shard_map/ppermute | solution.py:58
  18.4 1.5 %collective-permute-start.10 = (bf16[4,128,128]{2,1,0:T(8,128)(2,1)S(1)}, bf16[4,128,128]{2,1,0:T(8,128)(2,1)S(1)}, u32[]{:S(2)}, u32[]{:S(2)}) collective-permute-start(bf16[4,128,128]{2,1,0:T(8,128)(2,1)S(1)} %get-tuple-element.51.refs_4_), channel_id=1, source_target_pairs={{0,4},{4,0},{8,12},{12,8},{16,20},{20,16},{24,28},{28,24},{1,5},{5... | collective-permute-start | bytes 393224 | tf_op jit(solution)/shard_map/ppermute | solution.py:58
  19.9 0.5 collective-permute-start.5
  20.4 1.4 %shard_map.123.refs_2_.refs_7_ = f32[2,512,256]{2,1,0:T(8,128)S(1)} custom-call(bf16[512,512]{1,0:T(8,128)(2,1)S(1)} %copy-done.6, bf16[512,512]{1,0:T(8,128)(2,1)S(1)} %copy-done.1, bf16[512,512]{1,0:T(8,128)(2,1)S(1)} %copy-done.2, bf16[512,512]{1,0:T(8,128)(2,1)S(1)} %copy-done.4, bf16[4,128,128]{2,1,0:T(8,128)(2,1)S(1)} %get-tuple-element.51.refs_4_), custom_call_target="tpu_custom_call" | custom-call | flops 1610612736 | tf_op jit(solution)/shard_map/pallas_call | solution.py:40
  21.8 2.6 %collective-permute-start.9 = (bf16[4,128,128]{2,1,0:T(8,128)(2,1)S(1)}, bf16[4,128,128]{2,1,0:T(8,128)(2,1)S(1)}, u32[]{:S(2)}, u32[]{:S(2)}) collective-permute-start(bf16[4,128,128]{2,1,0:T(8,128)(2,1)S(1)} %shard_map.124.refs_2_), channel_id=1, source_target_pairs={{0,16},{4,20},{8,24},{12,28},{16,0},{20,4},{24,8},{28,12},{1,17},{... | collective-permute-start | bytes 393224 | tf_op jit(solution)/shard_map/ppermute | solution.py:58
  24.6 0.7 collective-permute-done.5.refs_2_.refs_6_
  25.2 3.9 %collective-permute-done.9.refs_5_ = bf16[4,128,128]{2,1,0:T(8,128)(2,1)S(1)} collective-permute-done((bf16[4,128,128]{2,1,0:T(8,128)(2,1)S(1)}, bf16[4,128,128]{2,1,0:T(8,128)(2,1)S(1)}, u32[]{:S(2)}, u32[]{:S(2)}) %collective-permute-start.9) | collective-permute-done | bytes 131104 | tf_op jit(solution)/shard_map/ppermute | solution.py:58
  29.2 0.8 shard_map.127.refs_8_
  30.0 1.6 %collective-permute-start.11 = (bf16[512,256]{1,0:T(8,128)(2,1)S(1)}, bf16[512,256]{1,0:T(8,128)(2,1)S(1)}, u32[]{:S(2)}, u32[]{:S(2)}) collective-permute-start(bf16[512,256]{1,0:T(8,128)(2,1)S(1)} %shard_map.127.refs_8_), channel_id=1, source_target_pairs={{0,4},{4,0},{8,12},{12,8},{16,20},{20,16},{24,28},{28,24},{1,5},{5... | collective-permute-start | bytes 786440 | tf_op jit(solution)/shard_map/ppermute | solution.py:58
  31.6 0.7 collective-permute-start.12
  32.3 0.5 collective-permute-start.3
  32.8 1.1 shard_map.128
  34.2 1.3 %shard_map.129.refs_2_.refs_0_ = bf16[4,256,2048]{2,1,0:T(8,128)(2,1)S(1)} custom-call(s32[2]{0:T(128)S(1)} %copy-done.8, bf16[272,512]{1,0:T(8,128)(2,1)S(1)} %copy-done.7, bf16[272,256]{1,0:T(8,128)(2,1)S(1)} %collective-permute-done.refs_0_.refs_2_, bf16[272,256]{1,0:T(8,128)(2,1)S(1)} %collective-permute-done.1.refs_3_, ...), custom_call_target="tpu_custom_call" | custom-call | tf_op jit(solution)/shard_map/pallas_call | solution.py:40
  35.4 1.0 collective-permute-done.11.refs_2_
  36.5 1.5 %collective-permute-done.12.refs_3_ = bf16[512,256]{1,0:T(8,128)(2,1)S(1)} collective-permute-done((bf16[512,256]{1,0:T(8,128)(2,1)S(1)}, bf16[512,256]{1,0:T(8,128)(2,1)S(1)}, u32[]{:S(2)}, u32[]{:S(2)}) %collective-permute-start.12) | collective-permute-done | bytes 262176 | tf_op jit(solution)/shard_map/ppermute | solution.py:58
  38.0 0.5 collective-permute-start.13
  38.5 0.7 collective-permute-start.16
  39.2 1.5 %collective-permute-start.22 = (bf16[2,512,256]{2,1,0:T(8,128)(2,1)S(1)}, bf16[2,512,256]{2,1,0:T(8,128)(2,1)S(1)}, u32[]{:S(2)}, u32[]{:S(2)}) collective-permute-start(bf16[2,512,256]{2,1,0:T(8,128)(2,1)S(1)} %get-tuple-element.54.refs_8_.refs_0_.refs_1_.refs_3_), channel_id=1, source_target_pairs={{0,2},{1,3},{2,0},{3,1},{4,6},{5,7},{6,4},{7,5},{8,10},{9,11},{10,... | collective-permute-start | bytes 1572872 | tf_op jit(solution)/shard_map/ppermute | solution.py:58
  40.7 0.5 collective-permute-start.23
  41.2 1.0 shard_map.130
  42.2 2.1 %collective-permute-done.13.refs_4_ = bf16[512,256]{1,0:T(8,128)(2,1)S(1)} collective-permute-done((bf16[512,256]{1,0:T(8,128)(2,1)S(1)}, bf16[512,256]{1,0:T(8,128)(2,1)S(1)}, u32[]{:S(2)}, u32[]{:S(2)}) %collective-permute-start.13) | collective-permute-done | bytes 262176 | tf_op jit(solution)/shard_map/ppermute | solution.py:58
  44.4 1.2 %shard_map.131 = (f32[4,128,256]{2,1,0:T(8,128)S(1)}, bf16[4,128,256]{2,1,0:T(8,128)(2,1)S(1)}) custom-call(bf16[4,256,2048]{2,1,0:T(8,128)(2,1)S(1)} %shard_map.129.refs_2_.refs_0_, bf16[2,512,256]{2,1,0:T(8,128)(2,1)S(1)} %get-tuple-element.54.refs_8_.refs_0_.refs_1_.refs_3_, bf16[512,256]{1,0:T(8,128)(2,1)S(1)} %collective-permute-done.11.refs_2_, ...), custom_call_target="tpu_custom_call" | custom-call | flops 1073741824 | tf_op jit(solution)/shard_map/pallas_call | solution.py:40
  45.7 0.8 collective-permute-start.17
  46.5 2.9 %collective-permute-start.18 = (bf16[4,128,256]{2,1,0:T(8,128)(2,1)S(1)}, bf16[4,128,256]{2,1,0:T(8,128)(2,1)S(1)}, u32[]{:S(2)}, u32[]{:S(2)}) collective-permute-start(bf16[4,128,256]{2,1,0:T(8,128)(2,1)S(1)} %get-tuple-element.62), channel_id=1, source_target_pairs={{0,16},{4,20},{8,24},{12,28},{16,0},{20,4},{24,8},{28,12},{1,17},{... | collective-permute-start | bytes 786440 | tf_op jit(solution)/shard_map/ppermute | solution.py:63
  49.4 1.2 collective-permute-start.15
  50.6 3.5 %collective-permute-done.22.refs_7_ = bf16[2,512,256]{2,1,0:T(8,128)(2,1)S(1)} collective-permute-done((bf16[2,512,256]{2,1,0:T(8,128)(2,1)S(1)}, bf16[2,512,256]{2,1,0:T(8,128)(2,1)S(1)}, u32[]{:S(2)}, u32[]{:S(2)}) %collective-permute-start.22) | collective-permute-done | bytes 524320 | tf_op jit(solution)/shard_map/ppermute | solution.py:58
  54.0 8.2 %collective-permute-done.23.refs_8_ = bf16[2,512,256]{2,1,0:T(8,128)(2,1)S(1)} collective-permute-done((bf16[2,512,256]{2,1,0:T(8,128)(2,1)S(1)}, bf16[2,512,256]{2,1,0:T(8,128)(2,1)S(1)}, u32[]{:S(2)}, u32[]{:S(2)}) %collective-permute-start.23) | collective-permute-done | bytes 524320 | tf_op jit(solution)/shard_map/ppermute | solution.py:58
  62.2 0.5 collective-permute-start.24
  62.8 1.4 %shard_map.132.refs_5_.refs_1_ = f32[512,512]{1,0:T(8,128)S(1)} custom-call(bf16[512,512]{1,0:T(8,128)(2,1)S(1)} %copy-done.1, bf16[512,512]{1,0:T(8,128)(2,1)S(1)} %copy-done.3, bf16[512,512]{1,0:T(8,128)(2,1)S(1)} %copy-done.5, f32[4,128,256]{2,1,0:T(8,128)S(1)} %get-tuple-element.58.refs_3_.refs_2_.refs_0_), custom_call_target="tpu_custom_call" | custom-call | flops 3221225472 | tf_op jit(solution)/shard_map/pallas_call | solution.py:40
  64.3 1.3 %shard_map.134 = (f32[4,128,256]{2,1,0:T(8,128)S(1)}, bf16[4,128,256]{2,1,0:T(8,128)(2,1)S(1)}) custom-call(bf16[4,256,2048]{2,1,0:T(8,128)(2,1)S(1)} %shard_map.129.refs_2_.refs_0_, bf16[2,512,256]{2,1,0:T(8,128)(2,1)S(1)} %get-tuple-element.54.refs_8_.refs_0_.refs_1_.refs_3_, bf16[2,512,256]{2,1,0:T(8,128)(2,1)S(1)} %collective-permute-done.17.refs_2_.refs_4_, ...), custom_call_target="tpu_custom_call" | custom-call | flops 1073741824 | tf_op jit(solution)/shard_map/pallas_call | solution.py:40
  65.6 0.9 collective-permute-done.15.refs_1_.refs_3_
  66.5 1.6 %collective-permute-start.19 = (bf16[2,512,256]{2,1,0:T(8,128)(2,1)S(1)}, bf16[2,512,256]{2,1,0:T(8,128)(2,1)S(1)}, u32[]{:S(2)}, u32[]{:S(2)}) collective-permute-start(bf16[2,512,256]{2,1,0:T(8,128)(2,1)S(1)} %shard_map.136), channel_id=1, source_target_pairs={{0,4},{4,0},{8,12},{12,8},{16,20},{20,16},{24,28},{28,24},{1,5},{5... | collective-permute-start | bytes 1572872 | tf_op jit(solution)/shard_map/ppermute | solution.py:58
  68.1 1.4 %collective-permute-start.26 = (bf16[4,128,256]{2,1,0:T(8,128)(2,1)S(1)}, bf16[4,128,256]{2,1,0:T(8,128)(2,1)S(1)}, u32[]{:S(2)}, u32[]{:S(2)}) collective-permute-start(bf16[4,128,256]{2,1,0:T(8,128)(2,1)S(1)} %get-tuple-element.66), channel_id=1, source_target_pairs={{0,16},{4,20},{8,24},{12,28},{16,0},{20,4},{24,8},{28,12},{1,17},{... | collective-permute-start | bytes 786440 | tf_op jit(solution)/shard_map/ppermute | solution.py:63
  69.6 5.3 %shard_map.137 = (f32[2,512,256]{2,1,0:T(8,128)S(1)}, bf16[2,512,256]{2,1,0:T(8,128)(2,1)S(1)}) custom-call(s32[2]{0:T(128)S(1)} %copy-done.8, bf16[1,1024,4096]{2,1,0:T(8,128)(2,1)S(1)} %bitcast.5, f32[512,1]{1,0:T(8,128)S(1)} %copy-done.9, bf16[2,512,256]{2,1,0:T(8,128)(2,1)S(1)} %get-tuple-element.54.refs_8_.refs_0_.refs_1_.refs_3_, ...), custom_call_target="tpu_custom_call" | custom-call | flops 4294967296 | tf_op jit(solution)/shard_map/pallas_call | solution.py:40
  75.0 5.0 %collective-permute-done.19.refs_2_.refs_4_ = bf16[2,512,256]{2,1,0:T(8,128)(2,1)S(1)} collective-permute-done((bf16[2,512,256]{2,1,0:T(8,128)(2,1)S(1)}, bf16[2,512,256]{2,1,0:T(8,128)(2,1)S(1)}, u32[]{:S(2)}, u32[]{:S(2)}) %collective-permute-start.19) | collective-permute-done | bytes 524320 | tf_op jit(solution)/shard_map/ppermute | solution.py:58
  79.9 1.2 %shard_map.138 = (f32[4,128,256]{2,1,0:T(8,128)S(1)}, bf16[4,128,256]{2,1,0:T(8,128)(2,1)S(1)}) custom-call(bf16[4,256,2048]{2,1,0:T(8,128)(2,1)S(1)} %shard_map.129.refs_2_.refs_0_, bf16[2,512,256]{2,1,0:T(8,128)(2,1)S(1)} %get-tuple-element.56.refs_1_.refs_0_.refs_4_, bf16[2,512,256]{2,1,0:T(8,128)(2,1)S(1)} %collective-permute-done.19.refs_2_.refs_4_, ...), custom_call_target="tpu_custom_call" | custom-call | flops 1073741824 | tf_op jit(solution)/shard_map/pallas_call | solution.py:40
  81.2 0.9 collective-permute-done.26.refs_0_.refs_3_
  82.1 0.7 collective-permute-start.27
  82.8 2.3 %collective-permute-start.28 = (bf16[4,128,256]{2,1,0:T(8,128)(2,1)S(1)}, bf16[4,128,256]{2,1,0:T(8,128)(2,1)S(1)}, u32[]{:S(2)}, u32[]{:S(2)}) collective-permute-start(bf16[4,128,256]{2,1,0:T(8,128)(2,1)S(1)} %get-tuple-element.67), channel_id=1, source_target_pairs={{0,16},{4,20},{8,24},{12,28},{16,0},{20,4},{24,8},{28,12},{1,17},{... | collective-permute-start | bytes 786440 | tf_op jit(solution)/shard_map/ppermute | solution.py:63
  85.2 1.7 %collective-permute-start.14 = (bf16[4,128,128]{2,1,0:T(8,128)(2,1)S(1)}, bf16[4,128,128]{2,1,0:T(8,128)(2,1)S(1)}, u32[]{:S(2)}, u32[]{:S(2)}) collective-permute-start(bf16[4,128,128]{2,1,0:T(8,128)(2,1)S(1)} %get-tuple-element.53.refs_8_), channel_id=1, source_target_pairs={{0,8},{4,12},{8,0},{12,4},{16,24},{20,28},{24,16},{28,20},{1,9},{5... | collective-permute-start | bytes 393224 | tf_op jit(solution)/shard_map/ppermute | solution.py:58
  86.9 6.2 %collective-permute-done.14.refs_0_.refs_1_.refs_4_ = bf16[4,128,128]{2,1,0:T(8,128)(2,1)S(1)} collective-permute-done((bf16[4,128,128]{2,1,0:T(8,128)(2,1)S(1)}, bf16[4,128,128]{2,1,0:T(8,128)(2,1)S(1)}, u32[]{:S(2)}, u32[]{:S(2)}) %collective-permute-start.14) | collective-permute-done | bytes 131104 | tf_op jit(solution)/shard_map/ppermute | solution.py:58
  93.2 3.4 %collective-permute-done.28.refs_0_.refs_5_ = bf16[4,128,256]{2,1,0:T(8,128)(2,1)S(1)} collective-permute-done((bf16[4,128,256]{2,1,0:T(8,128)(2,1)S(1)}, bf16[4,128,256]{2,1,0:T(8,128)(2,1)S(1)}, u32[]{:S(2)}, u32[]{:S(2)}) %collective-permute-start.28) | collective-permute-done | bytes 262176 | tf_op jit(solution)/shard_map/ppermute | solution.py:63
  96.8 1.2 %shard_map.144 = (f32[4,128,256]{2,1,0:T(8,128)S(1)}, bf16[4,128,256]{2,1,0:T(8,128)(2,1)S(1)}) custom-call(bf16[4,256,2048]{2,1,0:T(8,128)(2,1)S(1)} %shard_map.129.refs_2_.refs_0_, bf16[2,512,256]{2,1,0:T(8,128)(2,1)S(1)} %get-tuple-element.56.refs_1_.refs_0_.refs_4_, bf16[2,512,256]{2,1,0:T(8,128)(2,1)S(1)} %collective-permute-done.27.refs_2_.refs_4_, ...), custom_call_target="tpu_custom_call" | custom-call | flops 1073741824 | tf_op jit(solution)/shard_map/pallas_call | solution.py:40
  98.4 1.5 %collective-permute-start.33 = (bf16[1,3,128,256]{3,2,1,0:T(8,128)(2,1)S(1)}, bf16[1,3,128,256]{3,2,1,0:T(8,128)(2,1)S(1)}, u32[]{:S(2)}, u32[]{:S(2)}) collective-permute-start(bf16[1,3,128,256]{3,2,1,0:T(8,128)(2,1)S(1)} %get-tuple-element.76), channel_id=1, source_target_pairs={{0,2},{1,3},{2,0},{3,1},{4,6},{5,7},{6,4},{7,5},{8,10},{9,11},{10,... | collective-permute-start | bytes 589832 | tf_op jit(solution)/shard_map/ppermute | solution.py:58
  100.3 1.5 %collective-permute-start.31 = (bf16[1,512,256]{2,1,0:T(8,128)(2,1)S(1)}, bf16[1,512,256]{2,1,0:T(8,128)(2,1)S(1)}, u32[]{:S(2)}, u32[]{:S(2)}) collective-permute-start(bf16[1,512,256]{2,1,0:T(8,128)(2,1)S(1)} %get-tuple-element.69.refs_7_), channel_id=1, source_target_pairs={{0,2},{1,3},{2,0},{3,1},{4,6},{5,7},{6,4},{7,5},{8,10},{9,11},{10,... | collective-permute-start | bytes 786440 | tf_op jit(solution)/shard_map/ppermute | solution.py:58
  101.8 2.6 %collective-permute-start.30 = (bf16[4,128,128]{2,1,0:T(8,128)(2,1)S(1)}, bf16[4,128,128]{2,1,0:T(8,128)(2,1)S(1)}, u32[]{:S(2)}, u32[]{:S(2)}) collective-permute-start(bf16[4,128,128]{2,1,0:T(8,128)(2,1)S(1)} %shard_map.145), channel_id=1, source_target_pairs={{0,16},{4,20},{8,24},{12,28},{16,0},{20,4},{24,8},{28,12},{1,17},{... | collective-permute-start | bytes 393224 | tf_op jit(solution)/shard_map/ppermute | solution.py:58
  104.5 1.7 %collective-permute-done.33.refs_2_.refs_3_ = bf16[1,3,128,256]{3,2,1,0:T(8,128)(2,1)S(1)} collective-permute-done((bf16[1,3,128,256]{3,2,1,0:T(8,128)(2,1)S(1)}, bf16[1,3,128,256]{3,2,1,0:T(8,128)(2,1)S(1)}, u32[]{:S(2)}, u32[]{:S(2)}) %collective-permute-start.33) | collective-permute-done | bytes 196640 | tf_op jit(solution)/shard_map/ppermute | solution.py:58
  106.1 3.4 %collective-permute-done.34.refs_3_.refs_4_ = bf16[1,3,128,256]{3,2,1,0:T(8,128)(2,1)S(1)} collective-permute-done((bf16[1,3,128,256]{3,2,1,0:T(8,128)(2,1)S(1)}, bf16[1,3,128,256]{3,2,1,0:T(8,128)(2,1)S(1)}, u32[]{:S(2)}, u32[]{:S(2)}) %collective-permute-start.34) | collective-permute-done | bytes 196640 | tf_op jit(solution)/shard_map/ppermute | solution.py:58
  109.6 6.2 %collective-permute-done.35.refs_1_ = bf16[4,128,256]{2,1,0:T(8,128)(2,1)S(1)} collective-permute-done((bf16[4,128,256]{2,1,0:T(8,128)(2,1)S(1)}, bf16[4,128,256]{2,1,0:T(8,128)(2,1)S(1)}, u32[]{:S(2)}, u32[]{:S(2)}) %collective-permute-start.35) | collective-permute-done | bytes 262176 | tf_op jit(solution)/shard_map/ppermute | solution.py:63
  115.9 1.6 %collective-permute-start.37 = (bf16[1,1,128,256]{3,2,1,0:T(8,128)(2,1)S(1)}, bf16[1,1,128,256]{3,2,1,0:T(8,128)(2,1)S(1)}, u32[]{:S(2)}, u32[]{:S(2)}) collective-permute-start(bf16[1,1,128,256]{3,2,1,0:T(8,128)(2,1)S(1)} %get-tuple-element.81), channel_id=1, source_target_pairs={{0,2},{1,3},{2,0},{3,1},{4,6},{5,7},{6,4},{7,5},{8,10},{9,11},{10,... | collective-permute-start | bytes 196616 | tf_op jit(solution)/shard_map/ppermute | solution.py:58
  117.8 0.8 shard_map.147
  118.6 1.7 %shard_map.146 = bf16[512,512]{1,0:T(8,128)(2,1)} custom-call(s32[2]{0:T(128)S(1)} %copy-done.8, f32[512,512]{1,0:T(8,128)S(1)} %shard_map.132.refs_5_.refs_1_, bf16[512,512]{1,0:T(8,128)(2,1)S(1)} %copy-done.5, bf16[4,128,128]{2,1,0:T(8,128)(2,1)S(1)} %collective-permute-done.10.refs_1_.refs_3_, ...), custom_call_target="tpu_custom_call" | custom-call | tf_op jit(solution)/shard_map/pallas_call | solution.py:40
  120.4 1.1 collective-permute-done.38.refs_8_
  121.5 2.1 %shard_map.151 = f32[1,128,4096]{2,1,0:T(8,128)} custom-call(s32[2]{0:T(128)S(1)} %copy-done.8, f32[1,3,128,256]{3,2,1,0:T(8,128)S(1)} %get-tuple-element.74.refs_0_.refs_1_, bf16[1,3,128,256]{3,2,1,0:T(8,128)(2,1)S(1)} %collective-permute-done.32.refs_1_.refs_2_, bf16[1,3,128,256]{3,2,1,0:T(8,128)(2,1)S(1)} %collective-permute-done.33.refs_2_.refs_3_, ...), custom_call_target="tpu_custom_call" | custom-call | tf_op jit(solution)/shard_map/pallas_call | solution.py:40
  (73 shorter events, 2.9 us)
Async XLA Ops:
  1.2 14.7 %copy-start.1 = (bf16[512,512]{1,0:T(8,128)(2,1)S(1)}, bf16[512,512]{1,0:T(8,128)(2,1)}, u32[]{:S(2)}) copy-start(bf16[512,512]{1,0:T(8,128)(2,1)} %refs_0_.9) | copy-start | bytes 1572868
  4.9 10.7 %collective-permute-start.7 = (bf16[4,128,128]{2,1,0:T(8,128)(2,1)}, bf16[4,128,128]{2,1,0:T(8,128)(2,1)S(1)}, u32[]{:S(2)}, u32[]{:S(2)}) collective-permute-start(bf16[4,128,128]{2,1,0:T(8,128)(2,1)} %get-tuple-element.48), channel_id=1, source_target_pairs={{0,4},{4,0},{8,12},{12,8},{16,20},{20,16},{24,28},{28,24},{1,5},{5... | collective-permute-start | bytes 393224 | tf_op jit(solution)/shard_map/ppermute | solution.py:58
  8.0 7.6 %collective-permute-start.4 = (bf16[272,256]{1,0:T(8,128)(2,1)}, bf16[272,256]{1,0:T(8,128)(2,1)S(1)}, u32[]{:S(2)}, u32[]{:S(2)}) collective-permute-start(bf16[272,256]{1,0:T(8,128)(2,1)} %get-tuple-element.47), channel_id=1, source_target_pairs={{0,8},{4,12},{8,0},{12,4},{16,24},{20,28},{24,16},{28,20},{1,9},{5... | collective-permute-start | bytes 417800 | tf_op jit(solution)/shard_map/ppermute | solution.py:58
  9.6 15.0 %collective-permute-start = (bf16[272,256]{1,0:T(8,128)(2,1)}, bf16[272,256]{1,0:T(8,128)(2,1)S(1)}, u32[]{:S(2)}, u32[]{:S(2)}) collective-permute-start(bf16[272,256]{1,0:T(8,128)(2,1)} %get-tuple-element.45), channel_id=1, source_target_pairs={{0,4},{4,0},{8,12},{12,8},{16,20},{20,16},{24,28},{28,24},{1,5},{5... | collective-permute-start | bytes 417800 | tf_op jit(solution)/shard_map/ppermute | solution.py:58
  10.1 14.5 %collective-permute-start.2 = (bf16[272,256]{1,0:T(8,128)(2,1)}, bf16[272,256]{1,0:T(8,128)(2,1)S(1)}, u32[]{:S(2)}, u32[]{:S(2)}) collective-permute-start(bf16[272,256]{1,0:T(8,128)(2,1)} %get-tuple-element.46), channel_id=1, source_target_pairs={{0,8},{4,12},{8,0},{12,4},{16,24},{20,28},{24,16},{28,20},{1,9},{5... | collective-permute-start | bytes 417800 | tf_op jit(solution)/shard_map/ppermute | solution.py:58
  10.1 1.0 copy-start
  11.1 1.0 copy-start.2
  12.2 1.0 copy-start.4
  13.2 1.0 copy-start.6
  16.3 5.5 %collective-permute-start.8 = (bf16[4,128,128]{2,1,0:T(8,128)(2,1)S(1)}, bf16[4,128,128]{2,1,0:T(8,128)(2,1)S(1)}, u32[]{:S(2)}, u32[]{:S(2)}) collective-permute-start(bf16[4,128,128]{2,1,0:T(8,128)(2,1)S(1)} %get-tuple-element.49.refs_2_), channel_id=1, source_target_pairs={{0,8},{4,12},{8,0},{12,4},{16,24},{20,28},{24,16},{28,20},{1,9},{5... | collective-permute-start | bytes 393224 | tf_op jit(solution)/shard_map/ppermute | solution.py:58
  18.4 10.8 %copy-start.8 = (s32[2]{0:T(128)S(1)}, s32[2]{0:T(128)}, u32[]{:S(2)}) copy-start(s32[2]{0:T(128)} %pad_add_fusion.refs_0_) | copy-start | bytes 28
  18.4 6.1 %collective-permute-start.10 = (bf16[4,128,128]{2,1,0:T(8,128)(2,1)S(1)}, bf16[4,128,128]{2,1,0:T(8,128)(2,1)S(1)}, u32[]{:S(2)}, u32[]{:S(2)}) collective-permute-start(bf16[4,128,128]{2,1,0:T(8,128)(2,1)S(1)} %get-tuple-element.51.refs_4_), channel_id=1, source_target_pairs={{0,4},{4,0},{8,12},{12,8},{16,20},{20,16},{24,28},{28,24},{1,5},{5... | collective-permute-start | bytes 393224 | tf_op jit(solution)/shard_map/ppermute | solution.py:58
  19.9 5.3 %collective-permute-start.5 = (bf16[272,256]{1,0:T(8,128)(2,1)S(1)}, bf16[272,256]{1,0:T(8,128)(2,1)S(1)}, u32[]{:S(2)}, u32[]{:S(2)}) collective-permute-start(bf16[272,256]{1,0:T(8,128)(2,1)S(1)} %collective-permute-done.4.refs_3_), channel_id=1, source_target_pairs={{0,4},{4,0},{8,12},{12,8},{16,20},{20,16},{24,28},{28,24},{1,5},{5... | collective-permute-start | bytes 417800 | tf_op jit(solution)/shard_map/ppermute | solution.py:58
  21.8 7.3 %collective-permute-start.9 = (bf16[4,128,128]{2,1,0:T(8,128)(2,1)S(1)}, bf16[4,128,128]{2,1,0:T(8,128)(2,1)S(1)}, u32[]{:S(2)}, u32[]{:S(2)}) collective-permute-start(bf16[4,128,128]{2,1,0:T(8,128)(2,1)S(1)} %shard_map.124.refs_2_), channel_id=1, source_target_pairs={{0,16},{4,20},{8,24},{12,28},{16,0},{20,4},{24,8},{28,12},{1,17},{... | collective-permute-start | bytes 393224 | tf_op jit(solution)/shard_map/ppermute | solution.py:58
  24.5 9.6 %copy-start.7 = (bf16[272,512]{1,0:T(8,128)(2,1)S(1)}, bf16[272,512]{1,0:T(8,128)(2,1)}, u32[]{:S(2)}) copy-start(bf16[272,512]{1,0:T(8,128)(2,1)} %get-tuple-element.44.refs_1_) | copy-start | bytes 835588
  30.0 6.4 %collective-permute-start.11 = (bf16[512,256]{1,0:T(8,128)(2,1)S(1)}, bf16[512,256]{1,0:T(8,128)(2,1)S(1)}, u32[]{:S(2)}, u32[]{:S(2)}) collective-permute-start(bf16[512,256]{1,0:T(8,128)(2,1)S(1)} %shard_map.127.refs_8_), channel_id=1, source_target_pairs={{0,4},{4,0},{8,12},{12,8},{16,20},{20,16},{24,28},{28,24},{1,5},{5... | collective-permute-start | bytes 786440 | tf_op jit(solution)/shard_map/ppermute | solution.py:58
  31.6 6.4 %collective-permute-start.12 = (bf16[512,256]{1,0:T(8,128)(2,1)S(1)}, bf16[512,256]{1,0:T(8,128)(2,1)S(1)}, u32[]{:S(2)}, u32[]{:S(2)}) collective-permute-start(bf16[512,256]{1,0:T(8,128)(2,1)S(1)} %shard_map.127.refs_8_), channel_id=1, source_target_pairs={{0,8},{4,12},{8,0},{12,4},{16,24},{20,28},{24,16},{28,20},{1,9},{5... | collective-permute-start | bytes 786440 | tf_op jit(solution)/shard_map/ppermute | solution.py:58
  32.3 1.7 %collective-permute-start.1 = (bf16[272,256]{1,0:T(8,128)(2,1)S(1)}, bf16[272,256]{1,0:T(8,128)(2,1)S(1)}, u32[]{:S(2)}, u32[]{:S(2)}) collective-permute-start(bf16[272,256]{1,0:T(8,128)(2,1)S(1)} %collective-permute-done.refs_0_.refs_2_), channel_id=1, source_target_pairs={{0,1},{1,0},{2,3},{3,2},{4,5},{5,4},{6,7},{7,6},{8,9},{9,8},{10,11... | collective-permute-start | bytes 417800 | tf_op jit(solution)/shard_map/ppermute | solution.py:58
  32.3 1.7 %collective-permute-start.3 = (bf16[272,256]{1,0:T(8,128)(2,1)S(1)}, bf16[272,256]{1,0:T(8,128)(2,1)S(1)}, u32[]{:S(2)}, u32[]{:S(2)}) collective-permute-start(bf16[272,256]{1,0:T(8,128)(2,1)S(1)} %collective-permute-done.2.refs_1_.refs_4_), channel_id=1, source_target_pairs={{0,1},{1,0},{2,3},{3,2},{4,5},{5,4},{6,7},{7,6},{8,9},{9,8},{10,11... | collective-permute-start | bytes 417800 | tf_op jit(solution)/shard_map/ppermute | solution.py:58
  32.8 1.4 %collective-permute-start.6 = (bf16[272,256]{1,0:T(8,128)(2,1)S(1)}, bf16[272,256]{1,0:T(8,128)(2,1)S(1)}, u32[]{:S(2)}, u32[]{:S(2)}) collective-permute-start(bf16[272,256]{1,0:T(8,128)(2,1)S(1)} %collective-permute-done.5.refs_2_.refs_6_), channel_id=1, source_target_pairs={{0,1},{1,0},{2,3},{3,2},{4,5},{5,4},{6,7},{7,6},{8,9},{9,8},{10,11... | collective-permute-start | bytes 417800 | tf_op jit(solution)/shard_map/ppermute | solution.py:58
  38.0 6.4 %collective-permute-start.13 = (bf16[512,256]{1,0:T(8,128)(2,1)S(1)}, bf16[512,256]{1,0:T(8,128)(2,1)S(1)}, u32[]{:S(2)}, u32[]{:S(2)}) collective-permute-start(bf16[512,256]{1,0:T(8,128)(2,1)S(1)} %collective-permute-done.12.refs_3_), channel_id=1, source_target_pairs={{0,4},{4,0},{8,12},{12,8},{16,20},{20,16},{24,28},{28,24},{1,5},{5... | collective-permute-start | bytes 786440 | tf_op jit(solution)/shard_map/ppermute | solution.py:58
  38.5 7.1 %collective-permute-start.16 = (bf16[512,256]{1,0:T(8,128)(2,1)S(1)}, bf16[512,256]{1,0:T(8,128)(2,1)S(1)}, u32[]{:S(2)}, u32[]{:S(2)}) collective-permute-start(bf16[512,256]{1,0:T(8,128)(2,1)S(1)} %get-tuple-element.60), channel_id=1, source_target_pairs={{0,8},{4,12},{8,0},{12,4},{16,24},{20,28},{24,16},{28,20},{1,9},{5... | collective-permute-start | bytes 786440 | tf_op jit(solution)/shard_map/ppermute | solution.py:58
  39.2 14.9 %collective-permute-start.22 = (bf16[2,512,256]{2,1,0:T(8,128)(2,1)S(1)}, bf16[2,512,256]{2,1,0:T(8,128)(2,1)S(1)}, u32[]{:S(2)}, u32[]{:S(2)}) collective-permute-start(bf16[2,512,256]{2,1,0:T(8,128)(2,1)S(1)} %get-tuple-element.54.refs_8_.refs_0_.refs_1_.refs_3_), channel_id=1, source_target_pairs={{0,2},{1,3},{2,0},{3,1},{4,6},{5,7},{6,4},{7,5},{8,10},{9,11},{10,... | collective-permute-start | bytes 1572872 | tf_op jit(solution)/shard_map/ppermute | solution.py:58
  40.7 21.6 %collective-permute-start.23 = (bf16[2,512,256]{2,1,0:T(8,128)(2,1)S(1)}, bf16[2,512,256]{2,1,0:T(8,128)(2,1)S(1)}, u32[]{:S(2)}, u32[]{:S(2)}) collective-permute-start(bf16[2,512,256]{2,1,0:T(8,128)(2,1)S(1)} %get-tuple-element.56.refs_1_.refs_0_.refs_4_), channel_id=1, source_target_pairs={{0,2},{1,3},{2,0},{3,1},{4,6},{5,7},{6,4},{7,5},{8,10},{9,11},{10,... | collective-permute-start | bytes 1572872 | tf_op jit(solution)/shard_map/ppermute | solution.py:58
  42.2 20.6 %copy-start.3 = (bf16[512,512]{1,0:T(8,128)(2,1)S(1)}, bf16[512,512]{1,0:T(8,128)(2,1)}, u32[]{:S(2)}) copy-start(bf16[512,512]{1,0:T(8,128)(2,1)} %refs_1_.16) | copy-start | bytes 1572868
  42.2 20.6 %copy-start.5 = (bf16[512,512]{1,0:T(8,128)(2,1)S(1)}, bf16[512,512]{1,0:T(8,128)(2,1)}, u32[]{:S(2)}) copy-start(bf16[512,512]{1,0:T(8,128)(2,1)} %refs_2_.13) | copy-start | bytes 1572868
  45.6 23.9 %slice-start = ((s8[8388608]{0:T(1024)(128)(4,1)}), s8[4194304]{0:T(1024)(128)(4,1)S(1)}, s32[]{:S(2)}) async-start(s8[8388608]{0:T(1024)(128)(4,1)} %bitcast.4), calls=%async_computation | async-start | bytes 8388608
  45.7 17.1 %collective-permute-start.17 = (bf16[2,512,256]{2,1,0:T(8,128)(2,1)S(1)}, bf16[2,512,256]{2,1,0:T(8,128)(2,1)S(1)}, u32[]{:S(2)}, u32[]{:S(2)}) collective-permute-start(bf16[2,512,256]{2,1,0:T(8,128)(2,1)S(1)} %shard_map.133), channel_id=1, source_target_pairs={{0,4},{4,0},{8,12},{12,8},{16,20},{20,16},{24,28},{28,24},{1,5},{5... | collective-permute-start | bytes 1572872 | tf_op jit(solution)/shard_map/ppermute | solution.py:58
  46.5 23.0 %slice-start.1 = ((s8[8388608]{0:T(1024)(128)(4,1)}), s8[4194304]{0:T(1024)(128)(4,1)S(1)}, s32[]{:S(2)}) async-start(s8[8388608]{0:T(1024)(128)(4,1)} %bitcast.4), calls=%async_computation.1 | async-start | bytes 8388608
  46.5 15.8 %collective-permute-start.18 = (bf16[4,128,256]{2,1,0:T(8,128)(2,1)S(1)}, bf16[4,128,256]{2,1,0:T(8,128)(2,1)S(1)}, u32[]{:S(2)}, u32[]{:S(2)}) collective-permute-start(bf16[4,128,256]{2,1,0:T(8,128)(2,1)S(1)} %get-tuple-element.62), channel_id=1, source_target_pairs={{0,16},{4,20},{8,24},{12,28},{16,0},{20,4},{24,8},{28,12},{1,17},{... | collective-permute-start | bytes 786440 | tf_op jit(solution)/shard_map/ppermute | solution.py:63
  49.4 17.1 %collective-permute-start.15 = (bf16[2,512,256]{2,1,0:T(8,128)(2,1)S(1)}, bf16[2,512,256]{2,1,0:T(8,128)(2,1)S(1)}, u32[]{:S(2)}, u32[]{:S(2)}) collective-permute-start(bf16[2,512,256]{2,1,0:T(8,128)(2,1)S(1)} %get-tuple-element.56.refs_1_.refs_0_.refs_4_), channel_id=1, source_target_pairs={{0,8},{4,12},{8,0},{12,4},{16,24},{20,28},{24,16},{28,20},{1,9},{5... | collective-permute-start | bytes 1572872 | tf_op jit(solution)/shard_map/ppermute | solution.py:58
  54.0 14.1 %collective-permute-start.20 = (bf16[2,512,256]{2,1,0:T(8,128)(2,1)S(1)}, bf16[2,512,256]{2,1,0:T(8,128)(2,1)S(1)}, u32[]{:S(2)}, u32[]{:S(2)}) collective-permute-start(bf16[2,512,256]{2,1,0:T(8,128)(2,1)S(1)} %get-tuple-element.54.refs_8_.refs_0_.refs_1_.refs_3_), channel_id=1, source_target_pairs={{0,1},{1,0},{2,3},{3,2},{4,5},{5,4},{6,7},{7,6},{8,9},{9,8},{10,11... | collective-permute-start | bytes 1572872 | tf_op jit(solution)/shard_map/ppermute | solution.py:58
  62.2 7.3 %collective-permute-start.21 = (bf16[2,512,256]{2,1,0:T(8,128)(2,1)S(1)}, bf16[2,512,256]{2,1,0:T(8,128)(2,1)S(1)}, u32[]{:S(2)}, u32[]{:S(2)}) collective-permute-start(bf16[2,512,256]{2,1,0:T(8,128)(2,1)S(1)} %get-tuple-element.56.refs_1_.refs_0_.refs_4_), channel_id=1, source_target_pairs={{0,1},{1,0},{2,3},{3,2},{4,5},{5,4},{6,7},{7,6},{8,9},{9,8},{10,11... | collective-permute-start | bytes 1572872 | tf_op jit(solution)/shard_map/ppermute | solution.py:58
  62.2 7.3 %collective-permute-start.24 = (bf16[2,512,256]{2,1,0:T(8,128)(2,1)S(1)}, bf16[2,512,256]{2,1,0:T(8,128)(2,1)S(1)}, u32[]{:S(2)}, u32[]{:S(2)}) collective-permute-start(bf16[2,512,256]{2,1,0:T(8,128)(2,1)S(1)} %collective-permute-done.22.refs_7_), channel_id=1, source_target_pairs={{0,1},{1,0},{2,3},{3,2},{4,5},{5,4},{6,7},{7,6},{8,9},{9,8},{10,11... | collective-permute-start | bytes 1572872 | tf_op jit(solution)/shard_map/ppermute | solution.py:58
  62.8 6.8 %collective-permute-start.25 = (bf16[2,512,256]{2,1,0:T(8,128)(2,1)S(1)}, bf16[2,512,256]{2,1,0:T(8,128)(2,1)S(1)}, u32[]{:S(2)}, u32[]{:S(2)}) collective-permute-start(bf16[2,512,256]{2,1,0:T(8,128)(2,1)S(1)} %collective-permute-done.23.refs_8_), channel_id=1, source_target_pairs={{0,1},{1,0},{2,3},{3,2},{4,5},{5,4},{6,7},{7,6},{8,9},{9,8},{10,11... | collective-permute-start | bytes 1572872 | tf_op jit(solution)/shard_map/ppermute | solution.py:58
  64.3 5.3 %copy-start.9 = (f32[512,1]{1,0:T(8,128)S(1)}, f32[512,1]{1,0:T(8,128)}, u32[]{:S(2)}) copy-start(f32[512,1]{1,0:T(8,128)} %get-tuple-element.63.refs_2_) | copy-start | bytes 6148
  66.5 13.4 %collective-permute-start.19 = (bf16[2,512,256]{2,1,0:T(8,128)(2,1)S(1)}, bf16[2,512,256]{2,1,0:T(8,128)(2,1)S(1)}, u32[]{:S(2)}, u32[]{:S(2)}) collective-permute-start(bf16[2,512,256]{2,1,0:T(8,128)(2,1)S(1)} %shard_map.136), channel_id=1, source_target_pairs={{0,4},{4,0},{8,12},{12,8},{16,20},{20,16},{24,28},{28,24},{1,5},{5... | collective-permute-start | bytes 1572872 | tf_op jit(solution)/shard_map/ppermute | solution.py:58
  68.1 14.0 %collective-permute-start.26 = (bf16[4,128,256]{2,1,0:T(8,128)(2,1)S(1)}, bf16[4,128,256]{2,1,0:T(8,128)(2,1)S(1)}, u32[]{:S(2)}, u32[]{:S(2)}) collective-permute-start(bf16[4,128,256]{2,1,0:T(8,128)(2,1)S(1)} %get-tuple-element.66), channel_id=1, source_target_pairs={{0,16},{4,20},{8,24},{12,28},{16,0},{20,4},{24,8},{28,12},{1,17},{... | collective-permute-start | bytes 786440 | tf_op jit(solution)/shard_map/ppermute | solution.py:63
  74.9 18.2 %collective-permute-start.29 = (bf16[2,512,256]{2,1,0:T(8,128)(2,1)S(1)}, bf16[2,512,256]{2,1,0:T(8,128)(2,1)S(1)}, u32[]{:S(2)}, u32[]{:S(2)}) collective-permute-start(bf16[2,512,256]{2,1,0:T(8,128)(2,1)S(1)} %get-tuple-element.64.refs_5_), channel_id=1, source_target_pairs={{0,1},{1,0},{2,3},{3,2},{4,5},{5,4},{6,7},{7,6},{8,9},{9,8},{10,11... | collective-permute-start | bytes 1572872 | tf_op jit(solution)/shard_map/ppermute | solution.py:58
  82.1 14.6 %collective-permute-start.27 = (bf16[2,512,256]{2,1,0:T(8,128)(2,1)S(1)}, bf16[2,512,256]{2,1,0:T(8,128)(2,1)S(1)}, u32[]{:S(2)}, u32[]{:S(2)}) collective-permute-start(bf16[2,512,256]{2,1,0:T(8,128)(2,1)S(1)} %shard_map.140), channel_id=1, source_target_pairs={{0,4},{4,0},{8,12},{12,8},{16,20},{20,16},{24,28},{28,24},{1,5},{5... | collective-permute-start | bytes 1572872 | tf_op jit(solution)/shard_map/ppermute | solution.py:58
  82.8 13.8 %collective-permute-start.28 = (bf16[4,128,256]{2,1,0:T(8,128)(2,1)S(1)}, bf16[4,128,256]{2,1,0:T(8,128)(2,1)S(1)}, u32[]{:S(2)}, u32[]{:S(2)}) collective-permute-start(bf16[4,128,256]{2,1,0:T(8,128)(2,1)S(1)} %get-tuple-element.67), channel_id=1, source_target_pairs={{0,16},{4,20},{8,24},{12,28},{16,0},{20,4},{24,8},{28,12},{1,17},{... | collective-permute-start | bytes 786440 | tf_op jit(solution)/shard_map/ppermute | solution.py:63
  85.2 8.0 %collective-permute-start.14 = (bf16[4,128,128]{2,1,0:T(8,128)(2,1)S(1)}, bf16[4,128,128]{2,1,0:T(8,128)(2,1)S(1)}, u32[]{:S(2)}, u32[]{:S(2)}) collective-permute-start(bf16[4,128,128]{2,1,0:T(8,128)(2,1)S(1)} %get-tuple-element.53.refs_8_), channel_id=1, source_target_pairs={{0,8},{4,12},{8,0},{12,4},{16,24},{20,28},{24,16},{28,20},{1,9},{5... | collective-permute-start | bytes 393224 | tf_op jit(solution)/shard_map/ppermute | solution.py:58
  98.0 17.8 %collective-permute-start.35 = (bf16[4,128,256]{2,1,0:T(8,128)(2,1)S(1)}, bf16[4,128,256]{2,1,0:T(8,128)(2,1)S(1)}, u32[]{:S(2)}, u32[]{:S(2)}) collective-permute-start(bf16[4,128,256]{2,1,0:T(8,128)(2,1)S(1)} %get-tuple-element.78), channel_id=1, source_target_pairs={{0,16},{4,20},{8,24},{12,28},{16,0},{20,4},{24,8},{28,12},{1,17},{... | collective-permute-start | bytes 786440 | tf_op jit(solution)/shard_map/ppermute | solution.py:63
  98.4 3.4 %collective-permute-start.32 = (bf16[1,3,128,256]{3,2,1,0:T(8,128)(2,1)S(1)}, bf16[1,3,128,256]{3,2,1,0:T(8,128)(2,1)S(1)}, u32[]{:S(2)}, u32[]{:S(2)}) collective-permute-start(bf16[1,3,128,256]{3,2,1,0:T(8,128)(2,1)S(1)} %get-tuple-element.75), channel_id=1, source_target_pairs={{0,1},{1,0},{2,3},{3,2},{4,5},{5,4},{6,7},{7,6},{8,9},{9,8},{10,11... | collective-permute-start | bytes 589832 | tf_op jit(solution)/shard_map/ppermute | solution.py:58
  98.4 7.7 %collective-permute-start.33 = (bf16[1,3,128,256]{3,2,1,0:T(8,128)(2,1)S(1)}, bf16[1,3,128,256]{3,2,1,0:T(8,128)(2,1)S(1)}, u32[]{:S(2)}, u32[]{:S(2)}) collective-permute-start(bf16[1,3,128,256]{3,2,1,0:T(8,128)(2,1)S(1)} %get-tuple-element.76), channel_id=1, source_target_pairs={{0,2},{1,3},{2,0},{3,1},{4,6},{5,7},{6,4},{7,5},{8,10},{9,11},{10,... | collective-permute-start | bytes 589832 | tf_op jit(solution)/shard_map/ppermute | solution.py:58
  99.9 9.6 %collective-permute-start.34 = (bf16[1,3,128,256]{3,2,1,0:T(8,128)(2,1)S(1)}, bf16[1,3,128,256]{3,2,1,0:T(8,128)(2,1)S(1)}, u32[]{:S(2)}, u32[]{:S(2)}) collective-permute-start(bf16[1,3,128,256]{3,2,1,0:T(8,128)(2,1)S(1)} %get-tuple-element.77), channel_id=1, source_target_pairs={{0,3},{1,2},{2,1},{3,0},{4,7},{5,6},{6,5},{7,4},{8,11},{9,10},{10,... | collective-permute-start | bytes 589832 | tf_op jit(solution)/shard_map/ppermute | solution.py:58
  100.3 17.5 %collective-permute-start.31 = (bf16[1,512,256]{2,1,0:T(8,128)(2,1)S(1)}, bf16[1,512,256]{2,1,0:T(8,128)(2,1)S(1)}, u32[]{:S(2)}, u32[]{:S(2)}) collective-permute-start(bf16[1,512,256]{2,1,0:T(8,128)(2,1)S(1)} %get-tuple-element.69.refs_7_), channel_id=1, source_target_pairs={{0,2},{1,3},{2,0},{3,1},{4,6},{5,7},{6,4},{7,5},{8,10},{9,11},{10,... | collective-permute-start | bytes 786440 | tf_op jit(solution)/shard_map/ppermute | solution.py:58
  101.8 16.7 %collective-permute-start.30 = (bf16[4,128,128]{2,1,0:T(8,128)(2,1)S(1)}, bf16[4,128,128]{2,1,0:T(8,128)(2,1)S(1)}, u32[]{:S(2)}, u32[]{:S(2)}) collective-permute-start(bf16[4,128,128]{2,1,0:T(8,128)(2,1)S(1)} %shard_map.145), channel_id=1, source_target_pairs={{0,16},{4,20},{8,24},{12,28},{16,0},{20,4},{24,8},{28,12},{1,17},{... | collective-permute-start | bytes 393224 | tf_op jit(solution)/shard_map/ppermute | solution.py:58
  115.9 4.5 %collective-permute-start.36 = (bf16[1,1,128,256]{3,2,1,0:T(8,128)(2,1)S(1)}, bf16[1,1,128,256]{3,2,1,0:T(8,128)(2,1)S(1)}, u32[]{:S(2)}, u32[]{:S(2)}) collective-permute-start(bf16[1,1,128,256]{3,2,1,0:T(8,128)(2,1)S(1)} %get-tuple-element.80), channel_id=1, source_target_pairs={{0,1},{1,0},{2,3},{3,2},{4,5},{5,4},{6,7},{7,6},{8,9},{9,8},{10,11... | collective-permute-start | bytes 196616 | tf_op jit(solution)/shard_map/ppermute | solution.py:58
  115.9 4.5 %collective-permute-start.37 = (bf16[1,1,128,256]{3,2,1,0:T(8,128)(2,1)S(1)}, bf16[1,1,128,256]{3,2,1,0:T(8,128)(2,1)S(1)}, u32[]{:S(2)}, u32[]{:S(2)}) collective-permute-start(bf16[1,1,128,256]{3,2,1,0:T(8,128)(2,1)S(1)} %get-tuple-element.81), channel_id=1, source_target_pairs={{0,2},{1,3},{2,0},{3,1},{4,6},{5,7},{6,4},{7,5},{8,10},{9,11},{10,... | collective-permute-start | bytes 196616 | tf_op jit(solution)/shard_map/ppermute | solution.py:58
  117.5 4.0 %collective-permute-start.38 = (bf16[1,1,128,256]{3,2,1,0:T(8,128)(2,1)S(1)}, bf16[1,1,128,256]{3,2,1,0:T(8,128)(2,1)S(1)}, u32[]{:S(2)}, u32[]{:S(2)}) collective-permute-start(bf16[1,1,128,256]{3,2,1,0:T(8,128)(2,1)S(1)} %get-tuple-element.82), channel_id=1, source_target_pairs={{0,3},{1,2},{2,1},{3,0},{4,7},{5,6},{6,5},{7,4},{8,11},{9,10},{10,... | collective-permute-start | bytes 196616 | tf_op jit(solution)/shard_map/ppermute | solution.py:58

commit v4 on v3

--- a/solution.py
+++ b/solution.py
@@ -9,7 +9,7 @@
 
 DH = 128
 PAD = 16
-FIRST = 59
+FIRST = 60.25
 MIB = 1 << 20
 BF16 = jnp.bfloat16
 F32 = jnp.float32
@@ -48,7 +48,7 @@
             scratch_shapes=scratch,
         ),
         cost_estimate=pl.CostEstimate(flops=cost, bytes_accessed=0, transcendentals=0),
-        compiler_params=pltpu.CompilerParams(vmem_limit_bytes=limit * MIB),
+        compiler_params=pltpu.CompilerParams(vmem_limit_bytes=int(limit * MIB)),
         **options,
     )(*operands, *wait)
 
@@ -75,16 +75,14 @@
     return lax.optimization_barrier((array, *earlier))[0]
 
 
-def add_arrived(total, arrived, last, wait=()):
-    def kernel(total_ref, arrived_ref, narrow_ref, *wide):
-        added = total_ref[...] + arrived_ref[...].astype(F32)
+def add_arrived(total, arrived, wait=()):
+    def kernel(total_ref, arrived_ref, wide_ref, narrow_ref):
+        added = total_ref[...].astype(F32) + arrived_ref[...].astype(F32)
+        wide_ref[...] = added
         narrow_ref[...] = added.astype(BF16)
-        for ref in wide:
-            ref[...] = added
-
-    shapes = [struct(total.shape, BF16)] + ([] if last else [struct(total.shape, F32)])
-    sent, *total = call(kernel, shapes, (total, arrived), [VMEM] * 2, wait)
-    return (total[0] if total else None), sent
+
+    shapes = [struct(total.shape, F32), struct(total.shape, BF16)]
+    return call(kernel, shapes, (total, arrived), [VMEM] * 2, wait)
 
 
 def touch(wait):
@@ -102,13 +100,43 @@
     return call(kernel, struct((2, *first.shape[-2:]), first.dtype), (first, second), [VMEM] * 2, wait)
 
 
-def gathered_state(place, refs, number, backward):
+def last_states(total, arrived, own, wait=()):
+    def kernel(total_ref, arrived_ref, own_ref, out_ref):
+        half = lax.axis_size("seq") // 2
+        added = total_ref[...].astype(F32) + arrived_ref[...].astype(F32)
+        out_ref[...] = jnp.where(lax.axis_index("seq") >= half, added.astype(BF16), own_ref[...])
+
+    return call(kernel, struct(own.shape, BF16), (total, arrived, own), [VMEM] * 3, wait)
+
+
+def later_state(refs, number):
     state = None
     for step, ref in enumerate(refs):
-        lower = ((place >> step) & 1) == 0
-        term = jnp.where(lower == backward, ref[number].astype(F32), 0.0)
+        lower = ((lax.axis_index("seq") >> step) & 1) == 0
+        term = jnp.where(lower, ref[number].astype(F32), 0.0)
         state = term if state is None else state + term
     return state
+
+
+def earlier_state(came_ref, refs, number):
+    state = None
+    half = came_ref[number].astype(F32)
+    for step, ref in enumerate(refs):
+        upper = ((lax.axis_index("seq") >> step) & 1) == 1
+        term = jnp.where(upper, ref[0, number].astype(F32), 0.0)
+        state = term if state is None else state + term
+        half = half + ref[1, number].astype(F32)
+    return state + jnp.where(lax.axis_index("seq") >= lax.axis_size("seq") // 2, half, 0.0)
+
+
+def add_both(first, second, wait=()):
+    def kernel(*refs):
+        for at in range(2):
+            for out in refs[2:]:
+                out[at] = refs[at][...].astype(out.dtype)
+
+    shape = (2, *first.shape)
+    return call(kernel, [struct(shape, F32), struct(shape, BF16)], (first, second), [VMEM] * 2, wait)
 
 
 def triangle(size, lower):
@@ -150,12 +178,12 @@
     return high, (state - high.astype(F32)).astype(BF16)
 
 
-def finish_keys_values(intra, key, value, arrived, place, sets, known=(), wait=()):
+def finish_keys_values(intra, key, value, arrived, sets, known=(), wait=()):
     where = [(array, at) for array in range(len(intra)) for at in range(intra[array].shape[0])]
     rows, wide = intra[0].shape[1:]
     needed = sorted({start + at for start, many in sets for at in range(many or 1)})
 
-    def kernel(place_ref, k_ref, v_ref, *refs):
+    def kernel(k_ref, v_ref, *refs):
         states, refs = refs[: len(arrived)], refs[len(arrived) :]
         intra_refs, refs = refs[: len(intra)], refs[len(intra) :]
         known_refs, outs = refs[: len(known)], refs[len(known) :]
@@ -163,7 +191,7 @@
             if number < len(known):
                 both = known_refs[number][...]
             else:
-                high, low = halves(gathered_state(place_ref[0], states, number, True))
+                high, low = halves(later_state(states, number))
                 v, k = head(v_ref, number), head(k_ref, number)
                 by_key = dot(v, high, 1, 1) + dot(v, low, 1, 1)
                 by_value = dot(k, high, 1, 0) + dot(k, low, 1, 0)
@@ -177,8 +205,8 @@
                     out[number - start] = both
 
     shapes = [struct((rows, wide) if many is None else (many, rows, wide), BF16) for _, many in sets]
-    operands = (place, key, value, *arrived, *intra, *known)
-    return call(kernel, shapes, operands, [SMEM] + [VMEM] * (len(operands) - 1), wait)
+    operands = (key, value, *arrived, *intra, *known)
+    return call(kernel, shapes, operands, [VMEM] * len(operands), wait)
 
 
 def intra_queries(key, value, grad, wait=()):
@@ -209,15 +237,15 @@
     )
 
 
-def finish_queries(intra, grad, arrived, place, wait=()):
+def finish_queries(intra, grad, came, arrived, wait=()):
     rows, width = grad.shape
     heads = width // DH
 
-    def kernel(place_ref, intra_ref, g_ref, *refs):
+    def kernel(intra_ref, g_ref, came_ref, *refs):
         out_ref, done, sems = refs[len(arrived) :]
         copies = []
         for number in range(heads):
-            high, low = halves(gathered_state(place_ref[0], refs[: len(arrived)], number, False))
+            high, low = halves(earlier_state(came_ref, refs[: len(arrived)], number))
             columns = slice(number * DH, (number + 1) * DH)
             g = g_ref[:, columns]
             done[number] = (intra_ref[:, columns] + dot(g, high, 1, 1) + dot(g, low, 1, 1)).astype(BF16)
@@ -229,19 +257,15 @@
     return call(
         kernel,
         struct((rows, width), BF16),
-        (place, intra, grad, *arrived),
-        [SMEM] + [VMEM] * (2 + len(arrived)),
+        (intra, grad, came, *arrived),
+        [VMEM] * (3 + len(arrived)),
         wait,
         out_specs=HBM,
         scratch_shapes=[pltpu.VMEM((heads, rows, DH), BF16), pltpu.SemaphoreType.DMA((heads,))],
     )
 
 
-def place_of():
-    return jnp.stack([lax.axis_index("seq"), lax.axis_index("exp")]).astype(jnp.int32)
-
-
-def begin(query, grad, inputs, ids, gates, place, size, experts, count):
+def begin(query, grad, inputs, ids, gates, size, experts, count):
     rows, width = query.shape
     wide = inputs.shape[1]
     heads = width // DH
@@ -250,7 +274,8 @@
     half = rows // 2
     tall = groups * deep + PAD
 
-    def kernel(place_ref, *refs):
+    def kernel(*refs):
+        me, mine_at = lax.axis_index("seq"), lax.axis_index("exp")
         sources, refs = refs[:5], refs[5:]
         sent_ref, refs = refs[0], refs[1:]
         outs, column_ref, refs = refs[:size], refs[size], refs[size + 1 :]
@@ -275,7 +300,7 @@
         weight = jnp.zeros((experts, rows), F32)
         for slot in range(ids.shape[0]):
             weight += jnp.where(id_ref[slot : slot + 1, :] == which, gate_ref[slot : slot + 1, :], 0.0)
-        mine = jnp.sum(jnp.where(which == place_ref[1], weight, 0.0), axis=0, keepdims=True)
+        mine = jnp.sum(jnp.where(which == mine_at, weight, 0.0), axis=0, keepdims=True)
         column_ref[...] = jnp.broadcast_to(mine, (8, rows)).T[:, :1]
         parts = []
         for _ in range(3):
@@ -286,8 +311,7 @@
         if tail:
             parts.append(jnp.zeros((tail, rows), F32))
         packed = jnp.concatenate(parts, axis=0)
-        me = place_ref[0]
-        odd = place_ref[1] & 1
+        odd = mine_at & 1
         group, low = me // size, me % size
         columns = pl.ds(pl.multiple_of(odd * half, half), half)
         side = jnp.where(odd == 1, packed[:, half:], packed[:, :half]).astype(BF16)
@@ -303,8 +327,8 @@
     return call(
         kernel,
         [struct((heads, DH, DH), BF16)] + messages + [struct((rows, 1), F32)],
-        (place, query, grad, inputs, ids, gates),
-        [SMEM] + [HBM] * 5,
+        (query, grad, inputs, ids, gates),
+        [HBM] * 5,
         limit=FIRST,
         cost=12 * rows * width * DH,
         scratch_shapes=[pltpu.VMEM((rows, width), BF16)] * 2
@@ -318,49 +342,35 @@
     )
 
 
-def own_states(first, second, arrived=None, last=False, wait=()):
+def own_states(first, second):
     rows, width = first.shape
     heads = width // DH
-    extra = [] if arrived is None else [arrived]
-
-    def kernel(a_ref, b_ref, *refs):
-        outs = refs[len(extra) :]
+
+    def kernel(a_ref, b_ref, out_ref):
         for number in range(heads):
-            state = dot(head(a_ref, number), head(b_ref, number), 0, 0)
-            for ref in refs[: len(extra)]:
-                state = state + ref[number].astype(F32)
-            for out in outs:
-                out[number] = state.astype(out.dtype)
-
-    shapes = [struct((heads, DH, DH), BF16)] + ([] if last else [struct((heads, DH, DH), F32)])
-    sent, *total = call(
-        kernel,
-        shapes,
-        (first, second, *extra),
-        [VMEM] * (2 + len(extra)),
-        wait,
-        cost=6 * rows * width * DH,
-    )
-    return (total[0] if total else None), sent
-
-
-def weigh_inputs(own, halves_of, place, experts, wait=()):
+            out_ref[number] = dot(head(a_ref, number), head(b_ref, number), 0, 0).astype(BF16)
+
+    shape = struct((heads, DH, DH), BF16)
+    return call(kernel, shape, (first, second), [VMEM] * 2, cost=6 * rows * width * DH)
+
+
+def weigh_inputs(own, halves_of, experts, wait=()):
     deep, rows = own.shape
     deep -= PAD
     half = rows // 2
     size = 1 + len(halves_of)
     flat = [entry for pair in halves_of for entry in pair]
 
-    def kernel(place_ref, own_ref, *refs):
+    def kernel(own_ref, *refs):
         out_ref = refs[len(flat)]
-        odd = place_ref[1] & 1
+        odd = lax.axis_index("exp") & 1
         for at in range(1 + len(flat)):
             ref = own_ref if at == 0 else refs[at - 1]
             columns = ref[:deep, :].astype(F32)
             parts = ref[deep:, :].astype(F32)
             row = lax.broadcasted_iota(jnp.int32, parts.shape, 0)
             for step in range(experts):
-                mine = (row < 3 * experts) & (lax.rem(row, experts) == (step ^ place_ref[1]))
+                mine = (row < 3 * experts) & (lax.rem(row, experts) == (step ^ lax.axis_index("exp")))
                 weight = jnp.sum(jnp.where(mine, parts, 0.0), axis=0, keepdims=True)
                 scaled = (columns * weight).astype(BF16)
                 if at == 0:
@@ -373,8 +383,8 @@
     return call(
         kernel,
         struct((experts, deep, size * rows), BF16),
-        (place, own, *flat),
-        [SMEM] + [VMEM] * (1 + len(flat)),
+        (own, *flat),
+        [VMEM] * (1 + len(flat)),
         wait,
     )
 
@@ -435,43 +445,38 @@
     )
 
 
-def place_weight_grad(pieces, place, width):
-    experts = len(pieces[0])
-    counts = [row[0].shape[1] for row in pieces]
-    heads = sum(counts)
-    part = pieces[0][0].shape[2]
-    flat = [piece for row in pieces for piece in row]
-    slots = heads * experts * 2
-
-    def kernel(place_ref, *refs):
-        out_ref, ready, sems = refs[len(flat) :]
+def place_weight_grad(pieces, width, first, heads, before=None, wait=()):
+    experts = len(pieces)
+    _, many, part, _ = pieces[0].shape
+    extra = [] if before is None else [before]
+    slots = many * experts * 2
+
+    def kernel(*refs):
+        out_ref, token_ref, ready, sems = refs[experts + len(extra) :]
+        token_ref[...] = jnp.zeros_like(token_ref)
         copies = []
-        number = 0
-        for at, many in enumerate(counts):
-            for within in range(many):
-                for hop in range(experts):
-                    start = ((place_ref[1] ^ hop) * heads + number) * DH
-                    for side in range(2):
-                        slot = (number * experts + hop) * 2 + side
-                        piece = refs[at * experts + hop][0, within, :, side * DH : (side + 1) * DH]
-                        ready[slot] = piece.astype(F32)
-                        columns = pl.ds(pl.multiple_of(start + side * (width // 2), DH), DH)
-                        copy = pltpu.make_async_copy(
-                            ready.at[slot], out_ref.at[0, :, columns], sems.at[slot]
-                        )
-                        copy.start()
-                        copies.append(copy)
-                number += 1
+        for number in range(many):
+            for hop in range(experts):
+                start = ((lax.axis_index("exp") ^ hop) * heads + first + number) * DH
+                for side in range(2):
+                    slot = (number * experts + hop) * 2 + side
+                    ready[slot] = refs[hop][0, number, :, side * DH : (side + 1) * DH].astype(F32)
+                    columns = pl.ds(pl.multiple_of(start + side * (width // 2), DH), DH)
+                    copy = pltpu.make_async_copy(ready.at[slot], out_ref.at[0, :, columns], sems.at[slot])
+                    copy.start()
+                    copies.append(copy)
         for copy in copies:
             copy.wait()
 
     return call(
         kernel,
-        struct((1, part, width), F32),
-        (place, *flat),
-        [SMEM] + [VMEM] * len(flat),
-        out_specs=HBM,
+        [struct((1, part, width), F32), TOKEN],
+        (*pieces, *extra),
+        [VMEM] * experts + [HBM] * len(extra),
+        wait,
+        out_specs=[HBM, VMEM],
         scratch_shapes=[pltpu.VMEM((slots, part, DH), F32), pltpu.SemaphoreType.DMA((slots,))],
+        input_output_aliases={experts: 0} if extra else {},
     )
 
 
@@ -505,7 +510,7 @@
     )
 
 
-def input_products(pieces, expert_weight, gate, place, wait=()):
+def input_products(pieces, expert_weight, gate, wait=()):
     experts = len(pieces)
     packs = len(pieces[0])
     where = [(pack, at) for pack in range(packs) for at in range(pieces[0][pack].shape[0])]
@@ -515,14 +520,14 @@
     part = wide // experts
     even = experts // 2
 
-    def kernel(place_ref, w_ref, gate_ref, *refs):
-        keep_ref, send_ref = refs[experts * packs :]
+    def kernel(w_ref, gate_ref, *refs):
+        keep_ref, *send_refs = refs[experts * packs :]
         for out in range(experts):
-            taken = pl.ds(pl.multiple_of((place_ref[1] ^ out) * part, part), part)
+            taken = pl.ds(pl.multiple_of((lax.axis_index("exp") ^ out) * part, part), part)
             total = None
             for hop in range(experts):
                 for number, (pack, at) in enumerate(where):
-                    start = ((place_ref[1] ^ hop) * heads + number) * DH
+                    start = ((lax.axis_index("exp") ^ hop) * heads + number) * DH
                     sides = [
                         w_ref[0, taken, pl.ds(pl.multiple_of(start + side * (width // 2), DH), DH)]
                         for side in range(2)
@@ -531,16 +536,16 @@
                     total = term if total is None else total + term
             total = gate_ref[...] * total
             if out % 2:
-                send_ref[out // 2] = total.astype(BF16)
+                send_refs[out // 2][...] = total.astype(BF16)
             else:
                 keep_ref[out // 2] = total
 
     flat = [piece for row in pieces for piece in row]
     return call(
         kernel,
-        [struct((even, rows, part), F32), struct((even, rows, part), BF16)],
-        (place, expert_weight, gate, *flat),
-        [SMEM] + [VMEM] * (2 + len(flat)),
+        [struct((even, rows, part), F32)] + [struct((rows, part), BF16)] * even,
+        (expert_weight, gate, *flat),
+        [VMEM] * (2 + len(flat)),
         wait,
         cost=2 * rows * wide * width,
     )
@@ -550,19 +555,22 @@
     count, rows, wide = keep.shape
     half = count // 2
 
-    def kernel(keep_ref, arrived_ref, *outs):
+    def kernel(keep_ref, *refs):
+        arrived_refs, outs = refs[:count], refs[count:]
+        if not half:
+            outs[1][...] = jnp.zeros_like(outs[1])
         for at in range(count):
-            total = keep_ref[at] + arrived_ref[at].astype(F32)
-            if count == 1:
-                outs[0][...] = total.astype(BF16)
+            total = keep_ref[at] + arrived_refs[at][...].astype(F32)
+            if at < half:
+                outs[0][at] = total
             else:
-                outs[at // half][at % half] = total.astype(outs[at // half].dtype)
-
-    if count == 1:
-        shapes = struct((rows, wide), BF16)
+                outs[at - half + min(half, 1)][...] = total.astype(BF16)
+
+    if half:
+        shapes = [struct((half, rows, wide), F32)] + [struct((rows, wide), BF16)] * (count - half)
     else:
-        shapes = [struct((half, rows, wide), F32), struct((half, rows, wide), BF16)]
-    return call(kernel, shapes, (keep, arrived), [VMEM] * 2, wait)
+        shapes = [struct((rows, wide), BF16), TOKEN]
+    return call(kernel, shapes, (keep, *arrived), [VMEM] * (1 + count), wait)
 
 
 def per_device(query, key, value, grad, inputs, expert_ids, route_gates, expert_weight):
@@ -573,40 +581,38 @@
     size = 4
     groups = count // size
     many = heads // 2
-    place = place_of()
 
     sent, own_columns, one, two, three, gate = begin(
-        query, grad, inputs, expert_ids.T, route_gates.T, place, size, experts, count
+        query, grad, inputs, expert_ids.T, route_gates.T, size, experts, count
     )
     by_two, relay = swap(two, "seq", 2), swap(three, "seq", 2)
     later = [swap(sent, "seq", 1)]
-    intra = [intra_keys_values(query, key, value, grad, 0, many)]
-    total, sent = own_states(query, grad, later[0], count == 4, [relay, intra[0]])
+    other_state = own_states(key, value)
+    total, sent = add_arrived(sent, later[0], [other_state])
     later.append(swap(sent, "seq", 2))
-    other_total, other_sent = own_states(key, value, None, False, [sent])
-    earlier = [swap(other_sent, "seq", 1)]
-    intra.append(intra_keys_values(query, key, value, grad, many, heads - many, [other_sent]))
     mask = 4
-    waits = [intra[-1]]
-    while mask < count:
-        total, sent = add_arrived(total, later[-1], 2 * mask >= count, waits)
+    while 2 * mask < count:
+        total, sent = add_arrived(total, later[-1])
         later.append(swap(sent, "seq", mask))
-        waits = []
         mask *= 2
-    other_total, other_sent = add_arrived(other_total, earlier[0], False, [sent])
+    sent = last_states(total, later[-1], other_state, [relay])
+    came = swap(sent, "seq", mask)
+    later.append(came)
+    intra = [intra_keys_values(query, key, value, grad, 0, many, [sent])]
+    intra.append(intra_keys_values(query, key, value, grad, many, heads - many, [intra[0]]))
     halves_of = [swap(one, "seq", 1), by_two, swap(relay, "seq", 1)]
     arrived = touch(halves_of)
     halves_of = [[half, swap(half, "exp", 1)] for half in halves_of]
 
-    (lead,) = finish_keys_values(intra, key, value, later, place, [(0, None)], (), [other_sent, arrived])
+    (lead,) = finish_keys_values(intra, key, value, later, [(0, None)], (), [intra[1], arrived])
     near = [(swap(lead, "seq", 1), None)]
     across = [(swap(lead, "seq", 2), None)]
-    front, second, rest = finish_keys_values(
-        intra, key, value, later, place, [(0, 2), (1, None), (2, heads - 2)], (lead,)
-    )
-    packs = [front, rest]
-    weighted = weigh_inputs(own_columns, halves_of, place, experts, [front])
-    own_heads = [(front, 0), (front, 1)] + [(rest, at) for at in range(heads - 2)]
+    every, second, rest = finish_keys_values(
+        intra, key, value, later, [(0, heads), (1, None), (2, heads - 2)], (lead,), [pair[1] for pair in halves_of]
+    )
+    packs = [every]
+    weighted = weigh_inputs(own_columns, halves_of, experts)
+    own_heads = [(every, at) for at in range(heads)]
     across.append((swap(second, "seq", 2), None))
     rest_across = swap(rest, "seq", 2)
     across += [(rest_across, at) for at in range(heads - 2)]
@@ -621,8 +627,8 @@
             waits = [owns[number - 1]]
             if number >= 2:
                 waits.append(touch(others[number - 2] + [owns[number - 1]]))
-            (mine, at), (came, came_at) = own_heads[number], across[number]
-            stacked = stack(mine, came, (at, came_at), waits)
+            (mine, at), (passed, passed_at) = own_heads[number], across[number]
+            stacked = stack(mine, passed, (at, passed_at), waits)
             pair = swap(stacked, "seq", 1)
             near.append((pair, 0))
             relayed.append((pair, 1))
@@ -633,35 +639,39 @@
             intra_query = intra_queries(key, value, grad, [owns[0]])
             fillers = [intra_query]
         elif number == 2:
-            keep, send = input_products(pieces, expert_weight, gate, place, [owns[1]])
-            fillers = [send]
+            fillers = []
         elif number == 3:
-            mask = 2
-            while 2 * mask < count:
-                earlier.append(swap(other_sent, "seq", mask))
-                if 4 * mask < count:
-                    other_total, other_sent = add_arrived(other_total, earlier[-1], False)
-                mask *= 2
-            keep, send = add_parts(keep, swap(send, "exp", 1))
-            fillers = [touch(others[2]), touch([earlier[-1]]), send]
+            total, sent = add_both(other_state, came, [owns[2]])
+            earlier = [swap(sent, "seq", 1)]
+            keep, *send = input_products(pieces, expert_weight, gate, [owns[2]])
+            fillers = [touch(others[2]), send[0]]
         own, other = weight_product(
             weighted, [own_heads[number], near[number], across[number], relayed[number]], groups, fillers
         )
         owns.append(own)
         others.append([shift(array, "seq", size * (hop + 1)) for hop, array in enumerate(other)])
-    input_grad = add_parts(keep, swap(send, "exp", 2))
-    _, other_sent = add_arrived(other_total, earlier[-1], True, [owns[3]])
-    earlier.append(swap(other_sent, "seq", count // 2))
-    gradient_of_queries = finish_queries(intra_query, grad, earlier, place)
+    mask = 1
+    while keep.ndim == 3:
+        keep, *send = add_parts(keep, [swap(part, "exp", mask) for part in send])
+        mask *= 2
+    input_grad, input_token = keep, send[0]
+    mask = 2
+    while 2 * mask < count:
+        total, sent = add_arrived(total, earlier[-1])
+        earlier.append(swap(sent, "seq", mask))
+        mask *= 2
+    gradient_of_queries = finish_queries(intra_query, grad, came, earlier)
 
     hops = [[hop] for hop in range(experts)]
-    placed = []
-    waits = []
-    for members in (slice(0, heads - 1), slice(heads - 1, heads)):
-        own, *parts = add_partials(owns[members], others[members], hops, waits)
-        placed.append([own] + [swap(part, "exp", hop + 1) for hop, part in enumerate(parts)])
-        waits = [touch(placed[0])]
-    weight_grad = place_weight_grad(placed, place, expert_weight.shape[2])
+    weight_grad = None
+    waits, placing = [], []
+    for first, last in ((0, heads - 1), (heads - 1, heads)):
+        own, *parts = add_partials(owns[first:last], others[first:last], hops, waits)
+        parts = [own] + [swap(part, "exp", hop + 1) for hop, part in enumerate(parts)]
+        weight_grad, token = place_weight_grad(
+            parts, expert_weight.shape[2], first, heads, weight_grad, placing
+        )
+        waits, placing = [token], [input_token]
     return gradient_of_queries, gradient_of_keys, value_grad, input_grad, weight_grad
 
 

time: 124 us -> 114 us (0.919)
  waiting for transfers between devices: 50.1 us -> 43.9 us
  Pallas kernels: 28.2 us -> 26.1 us
    ppermute x35 -> x32, waiting for transfers between devices: 39.6 us -> 29.7 us  [swap(): lax.ppermute(array, axis, [(place, place ^ mask) for place in range(count)])]
    ppermute x4, waiting for transfers between devices: 10.5 us -> 14.2 us  [shift(): lax.ppermute(array, axis, [(place, (place + step) % count) for place in r...]
    pallas_call x33 -> x32, Pallas kernels: 28.2 us -> 26.1 us  [call(): pl.pallas_call(body, out_shape=out_shape, grid_spec=pltpu.PrefetchScalarG...]
    unnamed x24 -> x22, local copies, waits for them, and re-layouts: 4.21 us -> 3.02 us
    ppermute x35 -> x32, starting transfers between devices: 32.5 us -> 32.3 us  [swap(): lax.ppermute(array, axis, [(place, place ^ mask) for place in range(count)])]
  transfers between devices with their start and end apart: 39 -> 36, of which waited for: 18 -> 18; matrix products, arithmetic and copies ran while one was open for 0% -> 0% of each run, Pallas kernels for 16% -> 19%
where the time goes in v4:
time: 114 us; the launch traced here: 113 us
  waiting for transfers between devices  43.9 us (39%)
  starting transfers between devices  38.5 us (34%)
  Pallas kernels  26.1 us (23%)
  local copies, waits for them, and re-layouts  3.02 us (3%)
  between operations  1.2 us (1%)
    ppermute x32, starting transfers between devices, swap(): lax.ppermute(array, axis, [(place, place ^ mask) for place in range(count)])  32.3 us
    ppermute x32, waiting for transfers between devices, swap(): lax.ppermute(array, axis, [(place, place ^ mask) for place in range(count)])  29.7 us
    pallas_call x32, Pallas kernels, call(): pl.pallas_call(body, out_shape=out_shape, grid_spec=pltpu.PrefetchScalarG...  26.1 us
    ppermute x4, waiting for transfers between devices, shift(): lax.ppermute(array, axis, [(place, (place + step) % count) for place in r...  14.2 us
    ppermute x4, starting transfers between devices, shift(): lax.ppermute(array, axis, [(place, (place + step) % count) for place in r...  6.2 us
    unnamed x22, local copies, waits for them, and re-layouts  3.02 us
  transfers between devices with their start and end apart: 36, of which 18 were waited for; matrix products, arithmetic and copies ran while one was open for 0% of the time, Pallas kernels for 19%

profile of v4, /device:TPU:0, one launch (start us, length us, event | category | flops | bytes accessed | tf_op | source)
XLA Modules:
  0.0 112.7 jit_solution(6716223565300537405)
XLA Ops:
  0.7 3.0 %shard_map.119 = (bf16[4,128,128]{2,1,0:T(8,128)(2,1)}, bf16[272,512]{1,0:T(8,128)(2,1)}, bf16[272,256]{1,0:T(8,128)(2,1)}, bf16[272,256]{1,0:T(8,128)(2,1)}, bf...) custom-call(bf16[512,512]{1,0:T(8,128)(2,1)} %refs_0_.11, bf16[512,512]{1,0:T(8,128)(2,1)} %refs_1_.15, ...), custom_call_target="tpu_custom_call" | custom-call | flops 402653184 | tf_op jit(solution)/shard_map/pallas_call | solution.py:40
  3.7 3.0 %collective-permute-start.7 = (bf16[4,128,128]{2,1,0:T(8,128)(2,1)}, bf16[4,128,128]{2,1,0:T(8,128)(2,1)S(1)}, u32[]{:S(2)}, u32[]{:S(2)}) collective-permute-start(bf16[4,128,128]{2,1,0:T(8,128)(2,1)} %get-tuple-element.53.refs_0_), channel_id=1, source_target_pairs={{0,4},{4,0},{8,12},{12,8},{16,20},{20,16},{24,28},{28,24},{1,5},{5... | collective-permute-start | bytes 393224 | tf_op jit(solution)/shard_map/ppermute | solution.py:58
  6.8 2.0 %collective-permute-start.2 = (bf16[272,256]{1,0:T(8,128)(2,1)}, bf16[272,256]{1,0:T(8,128)(2,1)S(1)}, u32[]{:S(2)}, u32[]{:S(2)}) collective-permute-start(bf16[272,256]{1,0:T(8,128)(2,1)} %get-tuple-element.51), channel_id=1, source_target_pairs={{0,8},{4,12},{8,0},{12,4},{16,24},{20,28},{24,16},{28,20},{1,9},{5... | collective-permute-start | bytes 417800 | tf_op jit(solution)/shard_map/ppermute | solution.py:58
  8.9 1.0 copy-done
  9.9 1.0 copy-done.2
  11.0 0.3 shard_map.121.refs_2_.refs_0_
  11.3 0.9 copy-done.7
  12.3 2.2 %collective-permute-start.8 = (bf16[4,128,128]{2,1,0:T(8,128)(2,1)S(1)}, bf16[4,128,128]{2,1,0:T(8,128)(2,1)S(1)}, u32[]{:S(2)}, u32[]{:S(2)}) collective-permute-start(bf16[4,128,128]{2,1,0:T(8,128)(2,1)S(1)} %get-tuple-element.54), channel_id=1, source_target_pairs={{0,8},{4,12},{8,0},{12,4},{16,24},{20,28},{24,16},{28,20},{1,9},{5... | collective-permute-start | bytes 393224 | tf_op jit(solution)/shard_map/ppermute | solution.py:58
  14.4 0.5 collective-permute-start.3
  14.9 1.4 %collective-permute-done.4.refs_3_ = bf16[272,256]{1,0:T(8,128)(2,1)S(1)} collective-permute-done((bf16[272,256]{1,0:T(8,128)(2,1)}, bf16[272,256]{1,0:T(8,128)(2,1)S(1)}, u32[]{:S(2)}, u32[]{:S(2)}) %collective-permute-start.4) | collective-permute-done | bytes 139296 | tf_op jit(solution)/shard_map/ppermute | solution.py:58
  16.3 1.7 %collective-permute-start.5 = (bf16[272,256]{1,0:T(8,128)(2,1)S(1)}, bf16[272,256]{1,0:T(8,128)(2,1)S(1)}, u32[]{:S(2)}, u32[]{:S(2)}) collective-permute-start(bf16[272,256]{1,0:T(8,128)(2,1)S(1)} %collective-permute-done.4.refs_3_), channel_id=1, source_target_pairs={{0,4},{4,0},{8,12},{12,8},{16,20},{20,16},{24,28},{28,24},{1,5},{5... | collective-permute-start | bytes 417800 | tf_op jit(solution)/shard_map/ppermute | solution.py:58
  18.1 2.8 %collective-permute-start.9 = (bf16[4,128,128]{2,1,0:T(8,128)(2,1)S(1)}, bf16[4,128,128]{2,1,0:T(8,128)(2,1)S(1)}, u32[]{:S(2)}, u32[]{:S(2)}) collective-permute-start(bf16[4,128,128]{2,1,0:T(8,128)(2,1)S(1)} %shard_map.123.refs_4_), channel_id=1, source_target_pairs={{0,16},{4,20},{8,24},{12,28},{16,0},{20,4},{24,8},{28,12},{1,17},{... | collective-permute-start | bytes 393224 | tf_op jit(solution)/shard_map/ppermute | solution.py:58
  20.8 1.4 %shard_map.124.refs_4_.refs_5_ = f32[2,512,256]{2,1,0:T(8,128)S(1)} custom-call(bf16[512,512]{1,0:T(8,128)(2,1)S(1)} %copy-done.5, bf16[512,512]{1,0:T(8,128)(2,1)S(1)} %copy-done.1, bf16[512,512]{1,0:T(8,128)(2,1)S(1)} %copy-done.3, bf16[512,512]{1,0:T(8,128)(2,1)S(1)} %copy-done.4, bf16[4,128,128]{2,1,0:T(8,128)(2,1)S(1)} %shard_map.123.refs_4_), custom_call_target="tpu_custom_call" | custom-call | flops 1610612736 | tf_op jit(solution)/shard_map/pallas_call | solution.py:40
  22.3 1.3 %shard_map.125.refs_6_.refs_7_ = f32[2,512,256]{2,1,0:T(8,128)S(1)} custom-call(bf16[512,512]{1,0:T(8,128)(2,1)S(1)} %copy-done.5, bf16[512,512]{1,0:T(8,128)(2,1)S(1)} %copy-done.1, bf16[512,512]{1,0:T(8,128)(2,1)S(1)} %copy-done.3, bf16[512,512]{1,0:T(8,128)(2,1)S(1)} %copy-done.4, f32[2,512,256]{2,1,0:T(8,128)S(1)} %shard_map.124.refs_4_.refs_5_), custom_call_target="tpu_custom_call" | custom-call | flops 1610612736 | tf_op jit(solution)/shard_map/pallas_call | solution.py:40
  23.7 2.6 %collective-permute-done.9.refs_4_.refs_1_.refs_2_ = bf16[4,128,128]{2,1,0:T(8,128)(2,1)S(1)} collective-permute-done((bf16[4,128,128]{2,1,0:T(8,128)(2,1)S(1)}, bf16[4,128,128]{2,1,0:T(8,128)(2,1)S(1)}, u32[]{:S(2)}, u32[]{:S(2)}) %collective-permute-start.9) | collective-permute-done | bytes 131104 | tf_op jit(solution)/shard_map/ppermute | solution.py:58
  26.2 0.3 shard_map.127.refs_7_
  26.6 0.6 shard_map.128
  27.2 1.6 %collective-permute-start.21 = (bf16[4,512,256]{2,1,0:T(8,128)(2,1)S(1)}, bf16[4,512,256]{2,1,0:T(8,128)(2,1)S(1)}, u32[]{:S(2)}, u32[]{:S(2)}) collective-permute-start(bf16[4,512,256]{2,1,0:T(8,128)(2,1)S(1)} %get-tuple-element.56.refs_0_.refs_1_.refs_2_), channel_id=1, source_target_pairs={{0,2},{1,3},{2,0},{3,1},{4,6},{5,7},{6,4},{7,5},{8,10},{9,11},{10,... | collective-permute-start | bytes 3145736 | tf_op jit(solution)/shard_map/ppermute | solution.py:58
  28.8 1.5 %collective-permute-start.10 = (bf16[512,256]{1,0:T(8,128)(2,1)S(1)}, bf16[512,256]{1,0:T(8,128)(2,1)S(1)}, u32[]{:S(2)}, u32[]{:S(2)}) collective-permute-start(bf16[512,256]{1,0:T(8,128)(2,1)S(1)} %shard_map.127.refs_7_), channel_id=1, source_target_pairs={{0,4},{4,0},{8,12},{12,8},{16,20},{20,16},{24,28},{28,24},{1,5},{5... | collective-permute-start | bytes 786440 | tf_op jit(solution)/shard_map/ppermute | solution.py:58
  30.3 0.7 collective-permute-start.11
  31.0 0.7 shard_map.120.refs_1_.refs_0_
  31.7 3.5 %collective-permute-done.10.refs_2_ = bf16[512,256]{1,0:T(8,128)(2,1)S(1)} collective-permute-done((bf16[512,256]{1,0:T(8,128)(2,1)S(1)}, bf16[512,256]{1,0:T(8,128)(2,1)S(1)}, u32[]{:S(2)}, u32[]{:S(2)}) %collective-permute-start.10) | collective-permute-done | bytes 262176 | tf_op jit(solution)/shard_map/ppermute | solution.py:58
  35.1 1.5 %collective-permute-done.11.refs_3_ = bf16[512,256]{1,0:T(8,128)(2,1)S(1)} collective-permute-done((bf16[512,256]{1,0:T(8,128)(2,1)S(1)}, bf16[512,256]{1,0:T(8,128)(2,1)S(1)}, u32[]{:S(2)}, u32[]{:S(2)}) %collective-permute-start.11) | collective-permute-done | bytes 262176 | tf_op jit(solution)/shard_map/ppermute | solution.py:58
  36.7 0.5 collective-permute-start.12
  37.2 1.3 %collective-permute-start.14 = (bf16[512,256]{1,0:T(8,128)(2,1)S(1)}, bf16[512,256]{1,0:T(8,128)(2,1)S(1)}, u32[]{:S(2)}, u32[]{:S(2)}) collective-permute-start(bf16[512,256]{1,0:T(8,128)(2,1)S(1)} %get-tuple-element.61), channel_id=1, source_target_pairs={{0,8},{4,12},{8,0},{12,4},{16,24},{20,28},{24,16},{28,20},{1,9},{5... | collective-permute-start | bytes 786440 | tf_op jit(solution)/shard_map/ppermute | solution.py:58
  38.4 1.0 shard_map.129
  39.5 3.6 %collective-permute-done.12.refs_4_ = bf16[512,256]{1,0:T(8,128)(2,1)S(1)} collective-permute-done((bf16[512,256]{1,0:T(8,128)(2,1)S(1)}, bf16[512,256]{1,0:T(8,128)(2,1)S(1)}, u32[]{:S(2)}, u32[]{:S(2)}) %collective-permute-start.12) | collective-permute-done | bytes 262176 | tf_op jit(solution)/shard_map/ppermute | solution.py:58
  43.0 1.3 %shard_map.130 = (f32[4,128,256]{2,1,0:T(8,128)S(1)}, bf16[4,128,256]{2,1,0:T(8,128)(2,1)S(1)}) custom-call(bf16[4,256,2048]{2,1,0:T(8,128)(2,1)S(1)} %shard_map.120.refs_1_.refs_0_, bf16[4,512,256]{2,1,0:T(8,128)(2,1)S(1)} %get-tuple-element.56.refs_0_.refs_1_.refs_2_, bf16[512,256]{1,0:T(8,128)(2,1)S(1)} %collective-permute-done.10.refs_2_, ...), custom_call_target="tpu_custom_call" | custom-call | flops 1073741824 | tf_op jit(solution)/shard_map/pallas_call | solution.py:40
  44.4 0.8 collective-permute-start.15
  45.2 1.3 %collective-permute-start.13 = (bf16[2,512,256]{2,1,0:T(8,128)(2,1)S(1)}, bf16[2,512,256]{2,1,0:T(8,128)(2,1)S(1)}, u32[]{:S(2)}, u32[]{:S(2)}) collective-permute-start(bf16[2,512,256]{2,1,0:T(8,128)(2,1)S(1)} %get-tuple-element.60), channel_id=1, source_target_pairs={{0,8},{4,12},{8,0},{12,4},{16,24},{20,28},{24,16},{28,20},{1,9},{5... | collective-permute-start | bytes 1572872 | tf_op jit(solution)/shard_map/ppermute | solution.py:58
  46.4 3.4 %collective-permute-start.16 = (bf16[4,128,256]{2,1,0:T(8,128)(2,1)S(1)}, bf16[4,128,256]{2,1,0:T(8,128)(2,1)S(1)}, u32[]{:S(2)}, u32[]{:S(2)}) collective-permute-start(bf16[4,128,256]{2,1,0:T(8,128)(2,1)S(1)} %get-tuple-element.63), channel_id=1, source_target_pairs={{0,16},{4,20},{8,24},{12,28},{16,0},{20,4},{24,8},{28,12},{1,17},{... | collective-permute-start | bytes 786440 | tf_op jit(solution)/shard_map/ppermute | solution.py:63
  49.8 0.4 collective-permute-done.21.refs_4_
  50.2 1.4 %shard_map.131.refs_5_.refs_0_ = f32[512,512]{1,0:T(8,128)S(1)} custom-call(bf16[512,512]{1,0:T(8,128)(2,1)S(1)} %copy-done.1, bf16[512,512]{1,0:T(8,128)(2,1)S(1)} %copy-done.3, bf16[512,512]{1,0:T(8,128)(2,1)S(1)} %copy-done.4, f32[4,128,256]{2,1,0:T(8,128)S(1)} %get-tuple-element.59.refs_3_.refs_2_.refs_0_), custom_call_target="tpu_custom_call" | custom-call | flops 3221225472 | tf_op jit(solution)/shard_map/pallas_call | solution.py:40
  51.7 2.6 %collective-permute-done.15.refs_2_.refs_4_ = bf16[2,512,256]{2,1,0:T(8,128)(2,1)S(1)} collective-permute-done((bf16[2,512,256]{2,1,0:T(8,128)(2,1)S(1)}, bf16[2,512,256]{2,1,0:T(8,128)(2,1)S(1)}, u32[]{:S(2)}, u32[]{:S(2)}) %collective-permute-start.15) | collective-permute-done | bytes 524320 | tf_op jit(solution)/shard_map/ppermute | solution.py:58
  54.3 1.2 %shard_map.133 = (f32[4,128,256]{2,1,0:T(8,128)S(1)}, bf16[4,128,256]{2,1,0:T(8,128)(2,1)S(1)}) custom-call(bf16[4,256,2048]{2,1,0:T(8,128)(2,1)S(1)} %shard_map.120.refs_1_.refs_0_, bf16[4,512,256]{2,1,0:T(8,128)(2,1)S(1)} %get-tuple-element.56.refs_0_.refs_1_.refs_2_, bf16[2,512,256]{2,1,0:T(8,128)(2,1)S(1)} %collective-permute-done.15.refs_2_.refs_4_, ...), custom_call_target="tpu_custom_call" | custom-call | flops 1073741824 | tf_op jit(solution)/shard_map/pallas_call | solution.py:40
  55.5 4.4 %collective-permute-done.16.refs_0_.refs_1_ = bf16[4,128,256]{2,1,0:T(8,128)(2,1)S(1)} collective-permute-done((bf16[4,128,256]{2,1,0:T(8,128)(2,1)S(1)}, bf16[4,128,256]{2,1,0:T(8,128)(2,1)S(1)}, u32[]{:S(2)}, u32[]{:S(2)}) %collective-permute-start.16) | collective-permute-done | bytes 262176 | tf_op jit(solution)/shard_map/ppermute | solution.py:63
  59.9 0.7 collective-permute-done.13.refs_1_.refs_3_
  60.7 1.5 %collective-permute-start.17 = (bf16[2,512,256]{2,1,0:T(8,128)(2,1)S(1)}, bf16[2,512,256]{2,1,0:T(8,128)(2,1)S(1)}, u32[]{:S(2)}, u32[]{:S(2)}) collective-permute-start(bf16[2,512,256]{2,1,0:T(8,128)(2,1)S(1)} %shard_map.135), channel_id=1, source_target_pairs={{0,4},{4,0},{8,12},{12,8},{16,20},{20,16},{24,28},{28,24},{1,5},{5... | collective-permute-start | bytes 1572872 | tf_op jit(solution)/shard_map/ppermute | solution.py:58
  62.2 2.7 %collective-permute-start.26 = (bf16[4,128,256]{2,1,0:T(8,128)(2,1)S(1)}, bf16[4,128,256]{2,1,0:T(8,128)(2,1)S(1)}, u32[]{:S(2)}, u32[]{:S(2)}) collective-permute-start(bf16[4,128,256]{2,1,0:T(8,128)(2,1)S(1)} %get-tuple-element.77), channel_id=1, source_target_pairs={{0,16},{4,20},{8,24},{12,28},{16,0},{20,4},{24,8},{28,12},{1,17},{... | collective-permute-start | bytes 786440 | tf_op jit(solution)/shard_map/ppermute | solution.py:63
  65.0 8.6 %collective-permute-done.17.refs_2_.refs_4_ = bf16[2,512,256]{2,1,0:T(8,128)(2,1)S(1)} collective-permute-done((bf16[2,512,256]{2,1,0:T(8,128)(2,1)S(1)}, bf16[2,512,256]{2,1,0:T(8,128)(2,1)S(1)}, u32[]{:S(2)}, u32[]{:S(2)}) %collective-permute-start.17) | collective-permute-done | bytes 524320 | tf_op jit(solution)/shard_map/ppermute | solution.py:58
  73.5 1.2 %shard_map.136 = (f32[4,128,256]{2,1,0:T(8,128)S(1)}, bf16[4,128,256]{2,1,0:T(8,128)(2,1)S(1)}) custom-call(bf16[4,256,2048]{2,1,0:T(8,128)(2,1)S(1)} %shard_map.120.refs_1_.refs_0_, bf16[4,512,256]{2,1,0:T(8,128)(2,1)S(1)} %get-tuple-element.56.refs_0_.refs_1_.refs_2_, bf16[2,512,256]{2,1,0:T(8,128)(2,1)S(1)} %collective-permute-done.17.refs_2_.refs_4_, ...), custom_call_target="tpu_custom_call" | custom-call | flops 1073741824 | tf_op jit(solution)/shard_map/pallas_call | solution.py:40
  74.8 0.2 collective-permute-done.26.refs_0_.refs_3_
  75.0 1.5 %collective-permute-start.27 = (bf16[2,512,256]{2,1,0:T(8,128)(2,1)S(1)}, bf16[2,512,256]{2,1,0:T(8,128)(2,1)S(1)}, u32[]{:S(2)}, u32[]{:S(2)}) collective-permute-start(bf16[2,512,256]{2,1,0:T(8,128)(2,1)S(1)} %shard_map.144), channel_id=1, source_target_pairs={{0,4},{4,0},{8,12},{12,8},{16,20},{20,16},{24,28},{28,24},{1,5},{5... | collective-permute-start | bytes 1572872 | tf_op jit(solution)/shard_map/ppermute | solution.py:58
  76.6 0.7 collective-permute-start.18
  77.3 4.8 %shard_map.140 = (f32[2,512,256]{2,1,0:T(8,128)S(1)}, bf16[512,256]{1,0:T(8,128)(2,1)S(1)}, bf16[512,256]{1,0:T(8,128)(2,1)S(1)}) custom-call(bf16[1,1024,4096]{2,1,0:T(8,128)(2,1)S(1)} %bitcast.3, f32[512,1]{1,0:T(8,128)S(1)} %copy-done.8, bf16[4,512,256]{2,1,0:T(8,128)(2,1)S(1)} %get-tuple-element.56.refs_0_.refs_1_.refs_2_, ...), custom_call_target="tpu_custom_call" | custom-call | flops 4294967296 | tf_op jit(solution)/shard_map/pallas_call | solution.py:40
  82.2 0.5 collective-permute-start.24
  82.7 6.8 %collective-permute-done.28.refs_0_.refs_5_ = bf16[4,128,256]{2,1,0:T(8,128)(2,1)S(1)} collective-permute-done((bf16[4,128,256]{2,1,0:T(8,128)(2,1)S(1)}, bf16[4,128,256]{2,1,0:T(8,128)(2,1)S(1)}, u32[]{:S(2)}, u32[]{:S(2)}) %collective-permute-start.28) | collective-permute-done | bytes 262176 | tf_op jit(solution)/shard_map/ppermute | solution.py:63
  89.5 0.1 shard_map.147
  89.9 1.2 %shard_map.146 = (f32[4,128,256]{2,1,0:T(8,128)S(1)}, bf16[4,128,256]{2,1,0:T(8,128)(2,1)S(1)}) custom-call(bf16[4,256,2048]{2,1,0:T(8,128)(2,1)S(1)} %shard_map.120.refs_1_.refs_0_, bf16[4,512,256]{2,1,0:T(8,128)(2,1)S(1)} %get-tuple-element.56.refs_0_.refs_1_.refs_2_, bf16[2,512,256]{2,1,0:T(8,128)(2,1)S(1)} %collective-permute-done.27.refs_2_.refs_4_, ...), custom_call_target="tpu_custom_call" | custom-call | flops 1073741824 | tf_op jit(solution)/shard_map/pallas_call | solution.py:40
  91.2 1.5 %collective-permute-done.18.refs_1_.refs_3_ = bf16[2,4,128,128]{3,2,1,0:T(8,128)(2,1)S(1)} collective-permute-done((bf16[2,4,128,128]{3,2,1,0:T(8,128)(2,1)S(1)}, bf16[2,4,128,128]{3,2,1,0:T(8,128)(2,1)S(1)}, u32[]{:S(2)}, u32[]{:S(2)}) %collective-permute-start.18) | collective-permute-done | bytes 262176 | tf_op jit(solution)/shard_map/ppermute | solution.py:58
  92.7 0.5 collective-permute-start.31
  93.2 0.9 shard_map.138
  94.1 4.0 %collective-permute-start.19 = (bf16[2,4,128,128]{3,2,1,0:T(8,128)(2,1)S(1)}, bf16[2,4,128,128]{3,2,1,0:T(8,128)(2,1)S(1)}, u32[]{:S(2)}, u32[]{:S(2)}) collective-permute-start(bf16[2,4,128,128]{3,2,1,0:T(8,128)(2,1)S(1)} %get-tuple-element.67), channel_id=1, source_target_pairs={{0,8},{4,12},{8,0},{12,4},{16,24},{20,28},{24,16},{28,20},{1,9},{5... | collective-permute-start | bytes 786440 | tf_op jit(solution)/shard_map/ppermute | solution.py:58
  98.2 1.6 %collective-permute-start.25 = (bf16[512,256]{1,0:T(8,128)(2,1)S(1)}, bf16[512,256]{1,0:T(8,128)(2,1)S(1)}, u32[]{:S(2)}, u32[]{:S(2)}) collective-permute-start(bf16[512,256]{1,0:T(8,128)(2,1)S(1)} %get-tuple-element.75), channel_id=1, source_target_pairs={{0,2},{1,3},{2,0},{3,1},{4,6},{5,7},{6,4},{7,5},{8,10},{9,11},{10,... | collective-permute-start | bytes 786440 | tf_op jit(solution)/shard_map/ppermute | solution.py:58
  99.8 0.2 collective-permute-done.31.refs_2_
  99.9 1.3 %collective-permute-done.32.refs_3_ = bf16[1,3,128,256]{3,2,1,0:T(8,128)(2,1)S(1)} collective-permute-done((bf16[1,3,128,256]{3,2,1,0:T(8,128)(2,1)S(1)}, bf16[1,3,128,256]{3,2,1,0:T(8,128)(2,1)S(1)}, u32[]{:S(2)}, u32[]{:S(2)}) %collective-permute-start.32) | collective-permute-done | bytes 196640 | tf_op jit(solution)/shard_map/ppermute | solution.py:58
  101.2 1.3 %shard_map.148 = (f32[1,128,4096]{2,1,0:T(8,128)}, f32[8,128]{1,0:T(8,128)S(1)}) custom-call(f32[1,3,128,256]{3,2,1,0:T(8,128)S(1)} %get-tuple-element.81.refs_0_, bf16[1,3,128,256]{3,2,1,0:T(8,128)(2,1)S(1)} %collective-permute-done.30.refs_1_, bf16[1,3,128,256]{3,2,1,0:T(8,128)(2,1)S(1)} %collective-permute-done.31.refs_2_, ...), custom_call_target="tpu_custom_call" | custom-call | tf_op jit(solution)/shard_map/pallas_call | solution.py:40
  102.6 2.7 %collective-permute-done.29.refs_1_ = bf16[4,128,256]{2,1,0:T(8,128)(2,1)S(1)} collective-permute-done((bf16[4,128,256]{2,1,0:T(8,128)(2,1)S(1)}, bf16[4,128,256]{2,1,0:T(8,128)(2,1)S(1)}, u32[]{:S(2)}, u32[]{:S(2)}) %collective-permute-start.29) | collective-permute-done | bytes 262176 | tf_op jit(solution)/shard_map/ppermute | solution.py:63
  105.4 0.6 collective-permute-start.34
  106.0 1.3 %collective-permute-start.35 = (bf16[1,1,128,256]{3,2,1,0:T(8,128)(2,1)S(1)}, bf16[1,1,128,256]{3,2,1,0:T(8,128)(2,1)S(1)}, u32[]{:S(2)}, u32[]{:S(2)}) collective-permute-start(bf16[1,1,128,256]{3,2,1,0:T(8,128)(2,1)S(1)} %get-tuple-element.89), channel_id=1, source_target_pairs={{0,3},{1,2},{2,1},{3,0},{4,7},{5,6},{6,5},{7,4},{8,11},{9,10},{10,... | collective-permute-start | bytes 196616 | tf_op jit(solution)/shard_map/ppermute | solution.py:58
  107.3 1.8 %collective-permute-done.19.refs_4_ = bf16[2,4,128,128]{3,2,1,0:T(8,128)(2,1)S(1)} collective-permute-done((bf16[2,4,128,128]{3,2,1,0:T(8,128)(2,1)S(1)}, bf16[2,4,128,128]{3,2,1,0:T(8,128)(2,1)S(1)}, u32[]{:S(2)}, u32[]{:S(2)}) %collective-permute-start.19) | collective-permute-done | bytes 262176 | tf_op jit(solution)/shard_map/ppermute | solution.py:58
  109.1 1.2 %shard_map.139 = bf16[512,512]{1,0:T(8,128)(2,1)} custom-call(f32[512,512]{1,0:T(8,128)S(1)} %shard_map.131.refs_5_.refs_0_, bf16[512,512]{1,0:T(8,128)(2,1)S(1)} %copy-done.4, bf16[4,128,128]{2,1,0:T(8,128)(2,1)S(1)} %collective-permute-done.9.refs_4_.refs_1_.refs_2_, bf16[2,4,128,128]{3,2,1,0:T(8,128)(2,1)S(1)} %collective-permute-done.18.refs_1_.refs_3_, ...), custom_call_target="tpu_custom_call" | custom-call | tf_op jit(solution)/shard_map/pallas_call | solution.py:40
  110.3 0.7 shard_map.142
  111.1 1.4 %shard_map.150 = (f32[1,128,4096]{2,1,0:T(8,128)}, f32[8,128]{1,0:T(8,128)}) custom-call(f32[1,1,128,256]{3,2,1,0:T(8,128)S(1)} %get-tuple-element.86.refs_0_, bf16[1,1,128,256]{3,2,1,0:T(8,128)(2,1)S(1)} %collective-permute-done.33.refs_1_, bf16[1,1,128,256]{3,2,1,0:T(8,128)(2,1)S(1)} %collective-permute-done.34.refs_2_, ...), custom_call_target="tpu_custom_call", output_to_operand_aliasing={{0}: (4, {})} | custom-call | tf_op jit(solution)/shard_map/pallas_call | solution.py:40
  (63 shorter events, 1.1 us)
Async XLA Ops:
  0.6 20.2 %copy-start.4 = (bf16[512,512]{1,0:T(8,128)(2,1)S(1)}, bf16[512,512]{1,0:T(8,128)(2,1)}, u32[]{:S(2)}) copy-start(bf16[512,512]{1,0:T(8,128)(2,1)} %refs_1_.15) | copy-start | bytes 1572868
  0.6 20.2 %copy-start.5 = (bf16[512,512]{1,0:T(8,128)(2,1)S(1)}, bf16[512,512]{1,0:T(8,128)(2,1)}, u32[]{:S(2)}) copy-start(bf16[512,512]{1,0:T(8,128)(2,1)} %refs_0_.11) | copy-start | bytes 1572868
  0.7 20.2 %copy-start.1 = (bf16[512,512]{1,0:T(8,128)(2,1)S(1)}, bf16[512,512]{1,0:T(8,128)(2,1)}, u32[]{:S(2)}) copy-start(bf16[512,512]{1,0:T(8,128)(2,1)} %refs_0_.14) | copy-start | bytes 1572868
  0.7 20.2 %copy-start.3 = (bf16[512,512]{1,0:T(8,128)(2,1)S(1)}, bf16[512,512]{1,0:T(8,128)(2,1)}, u32[]{:S(2)}) copy-start(bf16[512,512]{1,0:T(8,128)(2,1)} %refs_1_.14) | copy-start | bytes 1572868
  3.7 7.6 %collective-permute-start.7 = (bf16[4,128,128]{2,1,0:T(8,128)(2,1)}, bf16[4,128,128]{2,1,0:T(8,128)(2,1)S(1)}, u32[]{:S(2)}, u32[]{:S(2)}) collective-permute-start(bf16[4,128,128]{2,1,0:T(8,128)(2,1)} %get-tuple-element.53.refs_0_), channel_id=1, source_target_pairs={{0,4},{4,0},{8,12},{12,8},{16,20},{20,16},{24,28},{28,24},{1,5},{5... | collective-permute-start | bytes 393224 | tf_op jit(solution)/shard_map/ppermute | solution.py:58
  6.8 7.7 %collective-permute-start = (bf16[272,256]{1,0:T(8,128)(2,1)}, bf16[272,256]{1,0:T(8,128)(2,1)S(1)}, u32[]{:S(2)}, u32[]{:S(2)}) collective-permute-start(bf16[272,256]{1,0:T(8,128)(2,1)} %get-tuple-element.50), channel_id=1, source_target_pairs={{0,4},{4,0},{8,12},{12,8},{16,20},{20,16},{24,28},{28,24},{1,5},{5... | collective-permute-start | bytes 417800 | tf_op jit(solution)/shard_map/ppermute | solution.py:58
  6.8 7.6 %collective-permute-start.2 = (bf16[272,256]{1,0:T(8,128)(2,1)}, bf16[272,256]{1,0:T(8,128)(2,1)S(1)}, u32[]{:S(2)}, u32[]{:S(2)}) collective-permute-start(bf16[272,256]{1,0:T(8,128)(2,1)} %get-tuple-element.51), channel_id=1, source_target_pairs={{0,8},{4,12},{8,0},{12,4},{16,24},{20,28},{24,16},{28,20},{1,9},{5... | collective-permute-start | bytes 417800 | tf_op jit(solution)/shard_map/ppermute | solution.py:58
  8.8 7.5 %collective-permute-start.4 = (bf16[272,256]{1,0:T(8,128)(2,1)}, bf16[272,256]{1,0:T(8,128)(2,1)S(1)}, u32[]{:S(2)}, u32[]{:S(2)}) collective-permute-start(bf16[272,256]{1,0:T(8,128)(2,1)} %get-tuple-element.52), channel_id=1, source_target_pairs={{0,8},{4,12},{8,0},{12,4},{16,24},{20,28},{24,16},{28,20},{1,9},{5... | collective-permute-start | bytes 417800 | tf_op jit(solution)/shard_map/ppermute | solution.py:58
  8.9 1.0 copy-start
  9.9 1.0 copy-start.2
  11.3 0.9 copy-start.7
  12.3 5.7 %collective-permute-start.8 = (bf16[4,128,128]{2,1,0:T(8,128)(2,1)S(1)}, bf16[4,128,128]{2,1,0:T(8,128)(2,1)S(1)}, u32[]{:S(2)}, u32[]{:S(2)}) collective-permute-start(bf16[4,128,128]{2,1,0:T(8,128)(2,1)S(1)} %get-tuple-element.54), channel_id=1, source_target_pairs={{0,8},{4,12},{8,0},{12,4},{16,24},{20,28},{24,16},{28,20},{1,9},{5... | collective-permute-start | bytes 393224 | tf_op jit(solution)/shard_map/ppermute | solution.py:58
  14.4 12.1 %collective-permute-start.1 = (bf16[272,256]{1,0:T(8,128)(2,1)S(1)}, bf16[272,256]{1,0:T(8,128)(2,1)S(1)}, u32[]{:S(2)}, u32[]{:S(2)}) collective-permute-start(bf16[272,256]{1,0:T(8,128)(2,1)S(1)} %collective-permute-done.refs_1_.refs_0_), channel_id=1, source_target_pairs={{0,1},{1,0},{2,3},{3,2},{4,5},{5,4},{6,7},{7,6},{8,9},{9,8},{10,11... | collective-permute-start | bytes 417800 | tf_op jit(solution)/shard_map/ppermute | solution.py:58
  14.4 12.1 %collective-permute-start.3 = (bf16[272,256]{1,0:T(8,128)(2,1)S(1)}, bf16[272,256]{1,0:T(8,128)(2,1)S(1)}, u32[]{:S(2)}, u32[]{:S(2)}) collective-permute-start(bf16[272,256]{1,0:T(8,128)(2,1)S(1)} %collective-permute-done.2.refs_3_.refs_1_), channel_id=1, source_target_pairs={{0,1},{1,0},{2,3},{3,2},{4,5},{5,4},{6,7},{7,6},{8,9},{9,8},{10,11... | collective-permute-start | bytes 417800 | tf_op jit(solution)/shard_map/ppermute | solution.py:58
  16.3 5.9 %collective-permute-start.5 = (bf16[272,256]{1,0:T(8,128)(2,1)S(1)}, bf16[272,256]{1,0:T(8,128)(2,1)S(1)}, u32[]{:S(2)}, u32[]{:S(2)}) collective-permute-start(bf16[272,256]{1,0:T(8,128)(2,1)S(1)} %collective-permute-done.4.refs_3_), channel_id=1, source_target_pairs={{0,4},{4,0},{8,12},{12,8},{16,20},{20,16},{24,28},{28,24},{1,5},{5... | collective-permute-start | bytes 417800 | tf_op jit(solution)/shard_map/ppermute | solution.py:58
  18.1 8.2 %collective-permute-start.9 = (bf16[4,128,128]{2,1,0:T(8,128)(2,1)S(1)}, bf16[4,128,128]{2,1,0:T(8,128)(2,1)S(1)}, u32[]{:S(2)}, u32[]{:S(2)}) collective-permute-start(bf16[4,128,128]{2,1,0:T(8,128)(2,1)S(1)} %shard_map.123.refs_4_), channel_id=1, source_target_pairs={{0,16},{4,20},{8,24},{12,28},{16,0},{20,4},{24,8},{28,12},{1,17},{... | collective-permute-start | bytes 393224 | tf_op jit(solution)/shard_map/ppermute | solution.py:58
  22.2 4.4 %collective-permute-start.6 = (bf16[272,256]{1,0:T(8,128)(2,1)S(1)}, bf16[272,256]{1,0:T(8,128)(2,1)S(1)}, u32[]{:S(2)}, u32[]{:S(2)}) collective-permute-start(bf16[272,256]{1,0:T(8,128)(2,1)S(1)} %collective-permute-done.5.refs_5_.refs_2_), channel_id=1, source_target_pairs={{0,1},{1,0},{2,3},{3,2},{4,5},{5,4},{6,7},{7,6},{8,9},{9,8},{10,11... | collective-permute-start | bytes 417800 | tf_op jit(solution)/shard_map/ppermute | solution.py:58
  23.6 7.3 %copy-start.6 = (bf16[272,512]{1,0:T(8,128)(2,1)S(1)}, bf16[272,512]{1,0:T(8,128)(2,1)}, u32[]{:S(2)}) copy-start(bf16[272,512]{1,0:T(8,128)(2,1)} %get-tuple-element.49.refs_0_) | copy-start | bytes 835588
  27.2 23.1 %collective-permute-start.21 = (bf16[4,512,256]{2,1,0:T(8,128)(2,1)S(1)}, bf16[4,512,256]{2,1,0:T(8,128)(2,1)S(1)}, u32[]{:S(2)}, u32[]{:S(2)}) collective-permute-start(bf16[4,512,256]{2,1,0:T(8,128)(2,1)S(1)} %get-tuple-element.56.refs_0_.refs_1_.refs_2_), channel_id=1, source_target_pairs={{0,2},{1,3},{2,0},{3,1},{4,6},{5,7},{6,4},{7,5},{8,10},{9,11},{10,... | collective-permute-start | bytes 3145736 | tf_op jit(solution)/shard_map/ppermute | solution.py:58
  28.8 6.4 %collective-permute-start.10 = (bf16[512,256]{1,0:T(8,128)(2,1)S(1)}, bf16[512,256]{1,0:T(8,128)(2,1)S(1)}, u32[]{:S(2)}, u32[]{:S(2)}) collective-permute-start(bf16[512,256]{1,0:T(8,128)(2,1)S(1)} %shard_map.127.refs_7_), channel_id=1, source_target_pairs={{0,4},{4,0},{8,12},{12,8},{16,20},{20,16},{24,28},{28,24},{1,5},{5... | collective-permute-start | bytes 786440 | tf_op jit(solution)/shard_map/ppermute | solution.py:58
  30.3 6.4 %collective-permute-start.11 = (bf16[512,256]{1,0:T(8,128)(2,1)S(1)}, bf16[512,256]{1,0:T(8,128)(2,1)S(1)}, u32[]{:S(2)}, u32[]{:S(2)}) collective-permute-start(bf16[512,256]{1,0:T(8,128)(2,1)S(1)} %shard_map.127.refs_7_), channel_id=1, source_target_pairs={{0,8},{4,12},{8,0},{12,4},{16,24},{20,28},{24,16},{28,20},{1,9},{5... | collective-permute-start | bytes 786440 | tf_op jit(solution)/shard_map/ppermute | solution.py:58
  36.7 6.4 %collective-permute-start.12 = (bf16[512,256]{1,0:T(8,128)(2,1)S(1)}, bf16[512,256]{1,0:T(8,128)(2,1)S(1)}, u32[]{:S(2)}, u32[]{:S(2)}) collective-permute-start(bf16[512,256]{1,0:T(8,128)(2,1)S(1)} %collective-permute-done.11.refs_3_), channel_id=1, source_target_pairs={{0,4},{4,0},{8,12},{12,8},{16,20},{20,16},{24,28},{28,24},{1,5},{5... | collective-permute-start | bytes 786440 | tf_op jit(solution)/shard_map/ppermute | solution.py:58
  37.2 7.1 %collective-permute-start.14 = (bf16[512,256]{1,0:T(8,128)(2,1)S(1)}, bf16[512,256]{1,0:T(8,128)(2,1)S(1)}, u32[]{:S(2)}, u32[]{:S(2)}) collective-permute-start(bf16[512,256]{1,0:T(8,128)(2,1)S(1)} %get-tuple-element.61), channel_id=1, source_target_pairs={{0,8},{4,12},{8,0},{12,4},{16,24},{20,28},{24,16},{28,20},{1,9},{5... | collective-permute-start | bytes 786440 | tf_op jit(solution)/shard_map/ppermute | solution.py:58
  44.4 9.9 %collective-permute-start.15 = (bf16[2,512,256]{2,1,0:T(8,128)(2,1)S(1)}, bf16[2,512,256]{2,1,0:T(8,128)(2,1)S(1)}, u32[]{:S(2)}, u32[]{:S(2)}) collective-permute-start(bf16[2,512,256]{2,1,0:T(8,128)(2,1)S(1)} %shard_map.132), channel_id=1, source_target_pairs={{0,4},{4,0},{8,12},{12,8},{16,20},{20,16},{24,28},{28,24},{1,5},{5... | collective-permute-start | bytes 1572872 | tf_op jit(solution)/shard_map/ppermute | solution.py:58
  45.2 15.5 %collective-permute-start.13 = (bf16[2,512,256]{2,1,0:T(8,128)(2,1)S(1)}, bf16[2,512,256]{2,1,0:T(8,128)(2,1)S(1)}, u32[]{:S(2)}, u32[]{:S(2)}) collective-permute-start(bf16[2,512,256]{2,1,0:T(8,128)(2,1)S(1)} %get-tuple-element.60), channel_id=1, source_target_pairs={{0,8},{4,12},{8,0},{12,4},{16,24},{20,28},{24,16},{28,20},{1,9},{5... | collective-permute-start | bytes 1572872 | tf_op jit(solution)/shard_map/ppermute | solution.py:58
  46.4 30.8 %collective-permute-start.20 = (bf16[4,512,256]{2,1,0:T(8,128)(2,1)S(1)}, bf16[4,512,256]{2,1,0:T(8,128)(2,1)S(1)}, u32[]{:S(2)}, u32[]{:S(2)}) collective-permute-start(bf16[4,512,256]{2,1,0:T(8,128)(2,1)S(1)} %get-tuple-element.56.refs_0_.refs_1_.refs_2_), channel_id=1, source_target_pairs={{0,1},{1,0},{2,3},{3,2},{4,5},{5,4},{6,7},{7,6},{8,9},{9,8},{10,11... | collective-permute-start | bytes 3145736 | tf_op jit(solution)/shard_map/ppermute | solution.py:58
  46.4 13.5 %collective-permute-start.16 = (bf16[4,128,256]{2,1,0:T(8,128)(2,1)S(1)}, bf16[4,128,256]{2,1,0:T(8,128)(2,1)S(1)}, u32[]{:S(2)}, u32[]{:S(2)}) collective-permute-start(bf16[4,128,256]{2,1,0:T(8,128)(2,1)S(1)} %get-tuple-element.63), channel_id=1, source_target_pairs={{0,16},{4,20},{8,24},{12,28},{16,0},{20,4},{24,8},{28,12},{1,17},{... | collective-permute-start | bytes 786440 | tf_op jit(solution)/shard_map/ppermute | solution.py:63
  50.2 27.0 %collective-permute-start.22 = (bf16[4,512,256]{2,1,0:T(8,128)(2,1)S(1)}, bf16[4,512,256]{2,1,0:T(8,128)(2,1)S(1)}, u32[]{:S(2)}, u32[]{:S(2)}) collective-permute-start(bf16[4,512,256]{2,1,0:T(8,128)(2,1)S(1)} %collective-permute-done.21.refs_4_), channel_id=1, source_target_pairs={{0,1},{1,0},{2,3},{3,2},{4,5},{5,4},{6,7},{7,6},{8,9},{9,8},{10,11... | collective-permute-start | bytes 3145736 | tf_op jit(solution)/shard_map/ppermute | solution.py:58
  54.3 23.0 %slice-start = ((s8[8388608]{0:T(1024)(128)(4,1)}), s8[4194304]{0:T(1024)(128)(4,1)S(1)}, s32[]{:S(2)}) async-start(s8[8388608]{0:T(1024)(128)(4,1)} %bitcast.2), calls=%async_computation | async-start | bytes 8388608
  60.7 12.8 %collective-permute-start.17 = (bf16[2,512,256]{2,1,0:T(8,128)(2,1)S(1)}, bf16[2,512,256]{2,1,0:T(8,128)(2,1)S(1)}, u32[]{:S(2)}, u32[]{:S(2)}) collective-permute-start(bf16[2,512,256]{2,1,0:T(8,128)(2,1)S(1)} %shard_map.135), channel_id=1, source_target_pairs={{0,4},{4,0},{8,12},{12,8},{16,20},{20,16},{24,28},{28,24},{1,5},{5... | collective-permute-start | bytes 1572872 | tf_op jit(solution)/shard_map/ppermute | solution.py:58
  62.2 15.1 %slice-start.1 = ((s8[8388608]{0:T(1024)(128)(4,1)}), s8[4194304]{0:T(1024)(128)(4,1)S(1)}, s32[]{:S(2)}) async-start(s8[8388608]{0:T(1024)(128)(4,1)} %bitcast.2), calls=%async_computation.1 | async-start | bytes 8388608
  62.2 15.1 %copy-start.8 = (f32[512,1]{1,0:T(8,128)S(1)}, f32[512,1]{1,0:T(8,128)}, u32[]{:S(2)}) copy-start(f32[512,1]{1,0:T(8,128)} %get-tuple-element.70.refs_1_) | copy-start | bytes 6148
  62.2 12.8 %collective-permute-start.26 = (bf16[4,128,256]{2,1,0:T(8,128)(2,1)S(1)}, bf16[4,128,256]{2,1,0:T(8,128)(2,1)S(1)}, u32[]{:S(2)}, u32[]{:S(2)}) collective-permute-start(bf16[4,128,256]{2,1,0:T(8,128)(2,1)S(1)} %get-tuple-element.77), channel_id=1, source_target_pairs={{0,16},{4,20},{8,24},{12,28},{16,0},{20,4},{24,8},{28,12},{1,17},{... | collective-permute-start | bytes 786440 | tf_op jit(solution)/shard_map/ppermute | solution.py:63
  75.0 14.8 %collective-permute-start.27 = (bf16[2,512,256]{2,1,0:T(8,128)(2,1)S(1)}, bf16[2,512,256]{2,1,0:T(8,128)(2,1)S(1)}, u32[]{:S(2)}, u32[]{:S(2)}) collective-permute-start(bf16[2,512,256]{2,1,0:T(8,128)(2,1)S(1)} %shard_map.144), channel_id=1, source_target_pairs={{0,4},{4,0},{8,12},{12,8},{16,20},{20,16},{24,28},{28,24},{1,5},{5... | collective-permute-start | bytes 1572872 | tf_op jit(solution)/shard_map/ppermute | solution.py:58
  76.6 16.1 %collective-permute-start.18 = (bf16[2,4,128,128]{3,2,1,0:T(8,128)(2,1)S(1)}, bf16[2,4,128,128]{3,2,1,0:T(8,128)(2,1)S(1)}, u32[]{:S(2)}, u32[]{:S(2)}) collective-permute-start(bf16[2,4,128,128]{3,2,1,0:T(8,128)(2,1)S(1)} %get-tuple-element.65), channel_id=1, source_target_pairs={{0,4},{4,0},{8,12},{12,8},{16,20},{20,16},{24,28},{28,24},{1,5},{5... | collective-permute-start | bytes 786440 | tf_op jit(solution)/shard_map/ppermute | solution.py:58
  77.3 12.3 %collective-permute-start.28 = (bf16[4,128,256]{2,1,0:T(8,128)(2,1)S(1)}, bf16[4,128,256]{2,1,0:T(8,128)(2,1)S(1)}, u32[]{:S(2)}, u32[]{:S(2)}) collective-permute-start(bf16[4,128,256]{2,1,0:T(8,128)(2,1)S(1)} %get-tuple-element.78), channel_id=1, source_target_pairs={{0,16},{4,20},{8,24},{12,28},{16,0},{20,4},{24,8},{28,12},{1,17},{... | collective-permute-start | bytes 786440 | tf_op jit(solution)/shard_map/ppermute | solution.py:63
  82.1 11.9 %collective-permute-start.23 = (bf16[512,256]{1,0:T(8,128)(2,1)S(1)}, bf16[512,256]{1,0:T(8,128)(2,1)S(1)}, u32[]{:S(2)}, u32[]{:S(2)}) collective-permute-start(bf16[512,256]{1,0:T(8,128)(2,1)S(1)} %get-tuple-element.72.refs_6_), channel_id=1, source_target_pairs={{0,1},{1,0},{2,3},{3,2},{4,5},{5,4},{6,7},{7,6},{8,9},{9,8},{10,11... | collective-permute-start | bytes 786440 | tf_op jit(solution)/shard_map/ppermute | solution.py:58
  82.2 11.9 %collective-permute-start.24 = (bf16[512,256]{1,0:T(8,128)(2,1)S(1)}, bf16[512,256]{1,0:T(8,128)(2,1)S(1)}, u32[]{:S(2)}, u32[]{:S(2)}) collective-permute-start(bf16[512,256]{1,0:T(8,128)(2,1)S(1)} %get-tuple-element.73), channel_id=1, source_target_pairs={{0,1},{1,0},{2,3},{3,2},{4,5},{5,4},{6,7},{7,6},{8,9},{9,8},{10,11... | collective-permute-start | bytes 786440 | tf_op jit(solution)/shard_map/ppermute | solution.py:58
  89.7 8.5 %collective-permute-start.30 = (bf16[1,3,128,256]{3,2,1,0:T(8,128)(2,1)S(1)}, bf16[1,3,128,256]{3,2,1,0:T(8,128)(2,1)S(1)}, u32[]{:S(2)}, u32[]{:S(2)}) collective-permute-start(bf16[1,3,128,256]{3,2,1,0:T(8,128)(2,1)S(1)} %get-tuple-element.82), channel_id=1, source_target_pairs={{0,1},{1,0},{2,3},{3,2},{4,5},{5,4},{6,7},{7,6},{8,9},{9,8},{10,11... | collective-permute-start | bytes 589832 | tf_op jit(solution)/shard_map/ppermute | solution.py:58
  91.1 14.2 %collective-permute-start.29 = (bf16[4,128,256]{2,1,0:T(8,128)(2,1)S(1)}, bf16[4,128,256]{2,1,0:T(8,128)(2,1)S(1)}, u32[]{:S(2)}, u32[]{:S(2)}) collective-permute-start(bf16[4,128,256]{2,1,0:T(8,128)(2,1)S(1)} %get-tuple-element.80), channel_id=1, source_target_pairs={{0,16},{4,20},{8,24},{12,28},{16,0},{20,4},{24,8},{28,12},{1,17},{... | collective-permute-start | bytes 786440 | tf_op jit(solution)/shard_map/ppermute | solution.py:63
  92.7 7.2 %collective-permute-start.31 = (bf16[1,3,128,256]{3,2,1,0:T(8,128)(2,1)S(1)}, bf16[1,3,128,256]{3,2,1,0:T(8,128)(2,1)S(1)}, u32[]{:S(2)}, u32[]{:S(2)}) collective-permute-start(bf16[1,3,128,256]{3,2,1,0:T(8,128)(2,1)S(1)} %get-tuple-element.83), channel_id=1, source_target_pairs={{0,2},{1,3},{2,0},{3,1},{4,6},{5,7},{6,4},{7,5},{8,10},{9,11},{10,... | collective-permute-start | bytes 589832 | tf_op jit(solution)/shard_map/ppermute | solution.py:58
  94.1 7.2 %collective-permute-start.32 = (bf16[1,3,128,256]{3,2,1,0:T(8,128)(2,1)S(1)}, bf16[1,3,128,256]{3,2,1,0:T(8,128)(2,1)S(1)}, u32[]{:S(2)}, u32[]{:S(2)}) collective-permute-start(bf16[1,3,128,256]{3,2,1,0:T(8,128)(2,1)S(1)} %get-tuple-element.84), channel_id=1, source_target_pairs={{0,3},{1,2},{2,1},{3,0},{4,7},{5,6},{6,5},{7,4},{8,11},{9,10},{10,... | collective-permute-start | bytes 589832 | tf_op jit(solution)/shard_map/ppermute | solution.py:58
  94.1 15.0 %collective-permute-start.19 = (bf16[2,4,128,128]{3,2,1,0:T(8,128)(2,1)S(1)}, bf16[2,4,128,128]{3,2,1,0:T(8,128)(2,1)S(1)}, u32[]{:S(2)}, u32[]{:S(2)}) collective-permute-start(bf16[2,4,128,128]{3,2,1,0:T(8,128)(2,1)S(1)} %get-tuple-element.67), channel_id=1, source_target_pairs={{0,8},{4,12},{8,0},{12,4},{16,24},{20,28},{24,16},{28,20},{1,9},{5... | collective-permute-start | bytes 786440 | tf_op jit(solution)/shard_map/ppermute | solution.py:58
  98.2 12.1 %collective-permute-start.25 = (bf16[512,256]{1,0:T(8,128)(2,1)S(1)}, bf16[512,256]{1,0:T(8,128)(2,1)S(1)}, u32[]{:S(2)}, u32[]{:S(2)}) collective-permute-start(bf16[512,256]{1,0:T(8,128)(2,1)S(1)} %get-tuple-element.75), channel_id=1, source_target_pairs={{0,2},{1,3},{2,0},{3,1},{4,6},{5,7},{6,4},{7,5},{8,10},{9,11},{10,... | collective-permute-start | bytes 786440 | tf_op jit(solution)/shard_map/ppermute | solution.py:58
  105.3 5.7 %collective-permute-start.33 = (bf16[1,1,128,256]{3,2,1,0:T(8,128)(2,1)S(1)}, bf16[1,1,128,256]{3,2,1,0:T(8,128)(2,1)S(1)}, u32[]{:S(2)}, u32[]{:S(2)}) collective-permute-start(bf16[1,1,128,256]{3,2,1,0:T(8,128)(2,1)S(1)} %get-tuple-element.87), channel_id=1, source_target_pairs={{0,1},{1,0},{2,3},{3,2},{4,5},{5,4},{6,7},{7,6},{8,9},{9,8},{10,11... | collective-permute-start | bytes 196616 | tf_op jit(solution)/shard_map/ppermute | solution.py:58
  105.4 5.7 %collective-permute-start.34 = (bf16[1,1,128,256]{3,2,1,0:T(8,128)(2,1)S(1)}, bf16[1,1,128,256]{3,2,1,0:T(8,128)(2,1)S(1)}, u32[]{:S(2)}, u32[]{:S(2)}) collective-permute-start(bf16[1,1,128,256]{3,2,1,0:T(8,128)(2,1)S(1)} %get-tuple-element.88), channel_id=1, source_target_pairs={{0,2},{1,3},{2,0},{3,1},{4,6},{5,7},{6,4},{7,5},{8,10},{9,11},{10,... | collective-permute-start | bytes 196616 | tf_op jit(solution)/shard_map/ppermute | solution.py:58
  106.0 5.1 %collective-permute-start.35 = (bf16[1,1,128,256]{3,2,1,0:T(8,128)(2,1)S(1)}, bf16[1,1,128,256]{3,2,1,0:T(8,128)(2,1)S(1)}, u32[]{:S(2)}, u32[]{:S(2)}) collective-permute-start(bf16[1,1,128,256]{3,2,1,0:T(8,128)(2,1)S(1)} %get-tuple-element.89), channel_id=1, source_target_pairs={{0,3},{1,2},{2,1},{3,0},{4,7},{5,6},{6,5},{7,4},{8,11},{9,10},{10,... | collective-permute-start | bytes 196616 | tf_op jit(solution)/shard_map/ppermute | solution.py:58

commit v5 on v4

--- a/solution.py
+++ b/solution.py
@@ -621,12 +621,13 @@
     pieces = [packs, close, far, [swap(pack, "exp", 1) for pack in far]]
     relayed = [(swap(after(across[0][0], near[0][0], weighted), "seq", 1), None)]
     owns, others = [], []
+    close_token = touch(close)
     fillers = []
     for number in range(heads):
         if number:
             waits = [owns[number - 1]]
             if number >= 2:
-                waits.append(touch(others[number - 2] + [owns[number - 1]]))
+                waits.append(touch(others[number - 2] + [owns[number - 1], close_token]))
             (mine, at), (passed, passed_at) = own_heads[number], across[number]
             stacked = stack(mine, passed, (at, passed_at), waits)
             pair = swap(stacked, "seq", 1)
@@ -641,10 +642,10 @@
         elif number == 2:
             fillers = []
         elif number == 3:
-            total, sent = add_both(other_state, came, [owns[2]])
+            total, sent = add_both(other_state, came, [owns[2], others[1][0]])
             earlier = [swap(sent, "seq", 1)]
             keep, *send = input_products(pieces, expert_weight, gate, [owns[2]])
-            fillers = [touch(others[2]), send[0]]
+            fillers = [touch(others[2])]
         own, other = weight_product(
             weighted, [own_heads[number], near[number], across[number], relayed[number]], groups, fillers
         )

time: 114 us -> 113 us (level)
  waiting for transfers between devices: 43.9 us -> 42.1 us
  starting transfers between devices: 38.5 us -> 39.8 us
    ppermute x4, starting transfers between devices: 6.2 us -> 8.99 us  [shift(): lax.ppermute(array, axis, [(place, (place + step) % count) for place in r...]
    ppermute x4, waiting for transfers between devices: 14.2 us -> 12.1 us  [shift(): lax.ppermute(array, axis, [(place, (place + step) % count) for place in r...]
    ppermute x32, starting transfers between devices: 32.3 us -> 30.8 us  [swap(): lax.ppermute(array, axis, [(place, place ^ mask) for place in range(count)])]
    pallas_call x32 -> x33, Pallas kernels: 26.1 us -> 26.1 us  [call(): pl.pallas_call(body, out_shape=out_shape, grid_spec=pltpu.PrefetchScalarG...]
  transfers between devices with their start and end apart: 36 -> 36, of which waited for: 18 -> 20; matrix products, arithmetic and copies ran while one was open for 0% -> 0% of each run, Pallas kernels for 19% -> 19%
where the time goes in v5:
time: 113 us; the launch traced here: 112 us
  waiting for transfers between devices  42.1 us (37%)
  starting transfers between devices  39.8 us (35%)
  Pallas kernels  26.1 us (23%)
  local copies, waits for them, and re-layouts  3.02 us (3%)
  between operations  1.18 us (1%)
    ppermute x32, starting transfers between devices, swap(): lax.ppermute(array, axis, [(place, place ^ mask) for place in range(count)])  30.8 us
    ppermute x32, waiting for transfers between devices, swap(): lax.ppermute(array, axis, [(place, place ^ mask) for place in range(count)])  30 us
    pallas_call x33, Pallas kernels, call(): pl.pallas_call(body, out_shape=out_shape, grid_spec=pltpu.PrefetchScalarG...  26.1 us
    ppermute x4, waiting for transfers between devices, shift(): lax.ppermute(array, axis, [(place, (place + step) % count) for place in r...  12.1 us
    ppermute x4, starting transfers between devices, shift(): lax.ppermute(array, axis, [(place, (place + step) % count) for place in r...  8.99 us
    unnamed x22, local copies, waits for them, and re-layouts  3.02 us
  transfers between devices with their start and end apart: 36, of which 20 were waited for; matrix products, arithmetic and copies ran while one was open for 0% of the time, Pallas kernels for 19%

profile of v5, /device:TPU:0, one launch (start us, length us, event | category | flops | bytes accessed | tf_op | source)
XLA Modules:
  0.0 112.2 jit_solution(9452511489675405584)
XLA Ops:
  0.7 3.0 %shard_map.119 = (bf16[4,128,128]{2,1,0:T(8,128)(2,1)}, bf16[272,512]{1,0:T(8,128)(2,1)}, bf16[272,256]{1,0:T(8,128)(2,1)}, bf16[272,256]{1,0:T(8,128)(2,1)}, bf...) custom-call(bf16[512,512]{1,0:T(8,128)(2,1)} %refs_0_.11, bf16[512,512]{1,0:T(8,128)(2,1)} %refs_1_.15, ...), custom_call_target="tpu_custom_call" | custom-call | flops 402653184 | tf_op jit(solution)/shard_map/pallas_call | solution.py:40
  3.7 3.0 %collective-permute-start.7 = (bf16[4,128,128]{2,1,0:T(8,128)(2,1)}, bf16[4,128,128]{2,1,0:T(8,128)(2,1)S(1)}, u32[]{:S(2)}, u32[]{:S(2)}) collective-permute-start(bf16[4,128,128]{2,1,0:T(8,128)(2,1)} %get-tuple-element.53.refs_0_), channel_id=1, source_target_pairs={{0,4},{4,0},{8,12},{12,8},{16,20},{20,16},{24,28},{28,24},{1,5},{5... | collective-permute-start | bytes 393224 | tf_op jit(solution)/shard_map/ppermute | solution.py:58
  6.8 1.6 %collective-permute-start.4 = (bf16[272,256]{1,0:T(8,128)(2,1)}, bf16[272,256]{1,0:T(8,128)(2,1)S(1)}, u32[]{:S(2)}, u32[]{:S(2)}) collective-permute-start(bf16[272,256]{1,0:T(8,128)(2,1)} %get-tuple-element.52), channel_id=1, source_target_pairs={{0,8},{4,12},{8,0},{12,4},{16,24},{20,28},{24,16},{28,20},{1,9},{5... | collective-permute-start | bytes 417800 | tf_op jit(solution)/shard_map/ppermute | solution.py:58
  8.3 0.5 collective-permute-start
  8.9 1.0 copy-done
  9.9 1.0 copy-done.2
  11.3 0.9 copy-done.7
  12.3 2.2 %collective-permute-start.8 = (bf16[4,128,128]{2,1,0:T(8,128)(2,1)S(1)}, bf16[4,128,128]{2,1,0:T(8,128)(2,1)S(1)}, u32[]{:S(2)}, u32[]{:S(2)}) collective-permute-start(bf16[4,128,128]{2,1,0:T(8,128)(2,1)S(1)} %get-tuple-element.54), channel_id=1, source_target_pairs={{0,8},{4,12},{8,0},{12,4},{16,24},{20,28},{24,16},{28,20},{1,9},{5... | collective-permute-start | bytes 393224 | tf_op jit(solution)/shard_map/ppermute | solution.py:58
  14.4 1.5 %collective-permute-start.5 = (bf16[272,256]{1,0:T(8,128)(2,1)S(1)}, bf16[272,256]{1,0:T(8,128)(2,1)S(1)}, u32[]{:S(2)}, u32[]{:S(2)}) collective-permute-start(bf16[272,256]{1,0:T(8,128)(2,1)S(1)} %collective-permute-done.4.refs_3_), channel_id=1, source_target_pairs={{0,4},{4,0},{8,12},{12,8},{16,20},{20,16},{24,28},{28,24},{1,5},{5... | collective-permute-start | bytes 417800 | tf_op jit(solution)/shard_map/ppermute | solution.py:58
  16.5 1.4 %collective-permute-done.8.refs_1_.refs_3_ = bf16[4,128,128]{2,1,0:T(8,128)(2,1)S(1)} collective-permute-done((bf16[4,128,128]{2,1,0:T(8,128)(2,1)S(1)}, bf16[4,128,128]{2,1,0:T(8,128)(2,1)S(1)}, u32[]{:S(2)}, u32[]{:S(2)}) %collective-permute-start.8) | collective-permute-done | bytes 131104 | tf_op jit(solution)/shard_map/ppermute | solution.py:58
  17.9 2.7 %collective-permute-start.9 = (bf16[4,128,128]{2,1,0:T(8,128)(2,1)S(1)}, bf16[4,128,128]{2,1,0:T(8,128)(2,1)S(1)}, u32[]{:S(2)}, u32[]{:S(2)}) collective-permute-start(bf16[4,128,128]{2,1,0:T(8,128)(2,1)S(1)} %shard_map.123.refs_4_), channel_id=1, source_target_pairs={{0,16},{4,20},{8,24},{12,28},{16,0},{20,4},{24,8},{28,12},{1,17},{... | collective-permute-start | bytes 393224 | tf_op jit(solution)/shard_map/ppermute | solution.py:58
  20.6 1.3 %shard_map.124.refs_4_.refs_5_ = f32[2,512,256]{2,1,0:T(8,128)S(1)} custom-call(bf16[512,512]{1,0:T(8,128)(2,1)S(1)} %copy-done.5, bf16[512,512]{1,0:T(8,128)(2,1)S(1)} %copy-done.1, bf16[512,512]{1,0:T(8,128)(2,1)S(1)} %copy-done.3, bf16[512,512]{1,0:T(8,128)(2,1)S(1)} %copy-done.4, bf16[4,128,128]{2,1,0:T(8,128)(2,1)S(1)} %shard_map.123.refs_4_), custom_call_target="tpu_custom_call" | custom-call | flops 1610612736 | tf_op jit(solution)/shard_map/pallas_call | solution.py:40
  22.1 1.3 %shard_map.125.refs_6_.refs_7_ = f32[2,512,256]{2,1,0:T(8,128)S(1)} custom-call(bf16[512,512]{1,0:T(8,128)(2,1)S(1)} %copy-done.5, bf16[512,512]{1,0:T(8,128)(2,1)S(1)} %copy-done.1, bf16[512,512]{1,0:T(8,128)(2,1)S(1)} %copy-done.3, bf16[512,512]{1,0:T(8,128)(2,1)S(1)} %copy-done.4, f32[2,512,256]{2,1,0:T(8,128)S(1)} %shard_map.124.refs_4_.refs_5_), custom_call_target="tpu_custom_call" | custom-call | flops 1610612736 | tf_op jit(solution)/shard_map/pallas_call | solution.py:40
  23.4 2.7 %collective-permute-done.9.refs_4_.refs_1_.refs_2_ = bf16[4,128,128]{2,1,0:T(8,128)(2,1)S(1)} collective-permute-done((bf16[4,128,128]{2,1,0:T(8,128)(2,1)S(1)}, bf16[4,128,128]{2,1,0:T(8,128)(2,1)S(1)}, u32[]{:S(2)}, u32[]{:S(2)}) %collective-permute-start.9) | collective-permute-done | bytes 131104 | tf_op jit(solution)/shard_map/ppermute | solution.py:58
  26.5 0.6 shard_map.128
  27.1 1.4 %collective-permute-start.22 = (bf16[4,512,256]{2,1,0:T(8,128)(2,1)S(1)}, bf16[4,512,256]{2,1,0:T(8,128)(2,1)S(1)}, u32[]{:S(2)}, u32[]{:S(2)}) collective-permute-start(bf16[4,512,256]{2,1,0:T(8,128)(2,1)S(1)} %get-tuple-element.56.refs_0_.refs_1_.refs_2_), channel_id=1, source_target_pairs={{0,2},{1,3},{2,0},{3,1},{4,6},{5,7},{6,4},{7,5},{8,10},{9,11},{10,... | collective-permute-start | bytes 3145736 | tf_op jit(solution)/shard_map/ppermute | solution.py:58
  28.4 0.8 collective-permute-start.10
  29.2 0.7 collective-permute-start.11
  29.9 0.7 shard_map.120.refs_1_.refs_0_
  30.6 4.2 %collective-permute-done.10.refs_2_ = bf16[512,256]{1,0:T(8,128)(2,1)S(1)} collective-permute-done((bf16[512,256]{1,0:T(8,128)(2,1)S(1)}, bf16[512,256]{1,0:T(8,128)(2,1)S(1)}, u32[]{:S(2)}, u32[]{:S(2)}) %collective-permute-start.10) | collective-permute-done | bytes 262176 | tf_op jit(solution)/shard_map/ppermute | solution.py:58
  34.8 0.8 collective-permute-done.11.refs_3_
  35.6 1.2 %collective-permute-start.12 = (bf16[512,256]{1,0:T(8,128)(2,1)S(1)}, bf16[512,256]{1,0:T(8,128)(2,1)S(1)}, u32[]{:S(2)}, u32[]{:S(2)}) collective-permute-start(bf16[512,256]{1,0:T(8,128)(2,1)S(1)} %collective-permute-done.11.refs_3_), channel_id=1, source_target_pairs={{0,4},{4,0},{8,12},{12,8},{16,20},{20,16},{24,28},{28,24},{1,5},{5... | collective-permute-start | bytes 786440 | tf_op jit(solution)/shard_map/ppermute | solution.py:58
  36.8 1.1 %collective-permute-start.14 = (bf16[512,256]{1,0:T(8,128)(2,1)S(1)}, bf16[512,256]{1,0:T(8,128)(2,1)S(1)}, u32[]{:S(2)}, u32[]{:S(2)}) collective-permute-start(bf16[512,256]{1,0:T(8,128)(2,1)S(1)} %get-tuple-element.61), channel_id=1, source_target_pairs={{0,8},{4,12},{8,0},{12,4},{16,24},{20,28},{24,16},{28,20},{1,9},{5... | collective-permute-start | bytes 786440 | tf_op jit(solution)/shard_map/ppermute | solution.py:58
  38.0 1.0 shard_map.129
  39.0 2.9 %collective-permute-done.12.refs_4_ = bf16[512,256]{1,0:T(8,128)(2,1)S(1)} collective-permute-done((bf16[512,256]{1,0:T(8,128)(2,1)S(1)}, bf16[512,256]{1,0:T(8,128)(2,1)S(1)}, u32[]{:S(2)}, u32[]{:S(2)}) %collective-permute-start.12) | collective-permute-done | bytes 262176 | tf_op jit(solution)/shard_map/ppermute | solution.py:58
  42.0 1.3 %shard_map.130 = (f32[4,128,256]{2,1,0:T(8,128)S(1)}, bf16[4,128,256]{2,1,0:T(8,128)(2,1)S(1)}) custom-call(bf16[4,256,2048]{2,1,0:T(8,128)(2,1)S(1)} %shard_map.120.refs_1_.refs_0_, bf16[4,512,256]{2,1,0:T(8,128)(2,1)S(1)} %get-tuple-element.56.refs_0_.refs_1_.refs_2_, bf16[512,256]{1,0:T(8,128)(2,1)S(1)} %collective-permute-done.10.refs_2_, ...), custom_call_target="tpu_custom_call" | custom-call | flops 1073741824 | tf_op jit(solution)/shard_map/pallas_call | solution.py:40
  43.3 1.3 %collective-permute-start.15 = (bf16[2,512,256]{2,1,0:T(8,128)(2,1)S(1)}, bf16[2,512,256]{2,1,0:T(8,128)(2,1)S(1)}, u32[]{:S(2)}, u32[]{:S(2)}) collective-permute-start(bf16[2,512,256]{2,1,0:T(8,128)(2,1)S(1)} %shard_map.132), channel_id=1, source_target_pairs={{0,4},{4,0},{8,12},{12,8},{16,20},{20,16},{24,28},{28,24},{1,5},{5... | collective-permute-start | bytes 1572872 | tf_op jit(solution)/shard_map/ppermute | solution.py:58
  44.6 1.1 %collective-permute-start.13 = (bf16[2,512,256]{2,1,0:T(8,128)(2,1)S(1)}, bf16[2,512,256]{2,1,0:T(8,128)(2,1)S(1)}, u32[]{:S(2)}, u32[]{:S(2)}) collective-permute-start(bf16[2,512,256]{2,1,0:T(8,128)(2,1)S(1)} %get-tuple-element.60), channel_id=1, source_target_pairs={{0,8},{4,12},{8,0},{12,4},{16,24},{20,28},{24,16},{28,20},{1,9},{5... | collective-permute-start | bytes 1572872 | tf_op jit(solution)/shard_map/ppermute | solution.py:58
  45.7 3.4 %collective-permute-start.16 = (bf16[4,128,256]{2,1,0:T(8,128)(2,1)S(1)}, bf16[4,128,256]{2,1,0:T(8,128)(2,1)S(1)}, u32[]{:S(2)}, u32[]{:S(2)}) collective-permute-start(bf16[4,128,256]{2,1,0:T(8,128)(2,1)S(1)} %get-tuple-element.63), channel_id=1, source_target_pairs={{0,16},{4,20},{8,24},{12,28},{16,0},{20,4},{24,8},{28,12},{1,17},{... | collective-permute-start | bytes 786440 | tf_op jit(solution)/shard_map/ppermute | solution.py:63
  49.1 2.3 %collective-permute-done.22.refs_4_ = bf16[4,512,256]{2,1,0:T(8,128)(2,1)S(1)} collective-permute-done((bf16[4,512,256]{2,1,0:T(8,128)(2,1)S(1)}, bf16[4,512,256]{2,1,0:T(8,128)(2,1)S(1)}, u32[]{:S(2)}, u32[]{:S(2)}) %collective-permute-start.22) | collective-permute-done | bytes 1048608 | tf_op jit(solution)/shard_map/ppermute | solution.py:58
  51.4 1.4 %shard_map.131.refs_5_.refs_0_ = f32[512,512]{1,0:T(8,128)S(1)} custom-call(bf16[512,512]{1,0:T(8,128)(2,1)S(1)} %copy-done.1, bf16[512,512]{1,0:T(8,128)(2,1)S(1)} %copy-done.3, bf16[512,512]{1,0:T(8,128)(2,1)S(1)} %copy-done.4, f32[4,128,256]{2,1,0:T(8,128)S(1)} %get-tuple-element.59.refs_3_.refs_2_.refs_0_), custom_call_target="tpu_custom_call" | custom-call | flops 3221225472 | tf_op jit(solution)/shard_map/pallas_call | solution.py:40
  52.9 0.7 collective-permute-done.15.refs_2_.refs_4_
  53.6 1.2 %shard_map.133 = (f32[4,128,256]{2,1,0:T(8,128)S(1)}, bf16[4,128,256]{2,1,0:T(8,128)(2,1)S(1)}) custom-call(bf16[4,256,2048]{2,1,0:T(8,128)(2,1)S(1)} %shard_map.120.refs_1_.refs_0_, bf16[4,512,256]{2,1,0:T(8,128)(2,1)S(1)} %get-tuple-element.56.refs_0_.refs_1_.refs_2_, bf16[2,512,256]{2,1,0:T(8,128)(2,1)S(1)} %collective-permute-done.15.refs_2_.refs_4_, ...), custom_call_target="tpu_custom_call" | custom-call | flops 1073741824 | tf_op jit(solution)/shard_map/pallas_call | solution.py:40
  54.9 4.5 %collective-permute-done.16.refs_0_.refs_1_ = bf16[4,128,256]{2,1,0:T(8,128)(2,1)S(1)} collective-permute-done((bf16[4,128,256]{2,1,0:T(8,128)(2,1)S(1)}, bf16[4,128,256]{2,1,0:T(8,128)(2,1)S(1)}, u32[]{:S(2)}, u32[]{:S(2)}) %collective-permute-start.16) | collective-permute-done | bytes 262176 | tf_op jit(solution)/shard_map/ppermute | solution.py:63
  59.4 0.7 collective-permute-done.13.refs_1_.refs_3_
  60.1 1.5 %collective-permute-start.18 = (bf16[2,512,256]{2,1,0:T(8,128)(2,1)S(1)}, bf16[2,512,256]{2,1,0:T(8,128)(2,1)S(1)}, u32[]{:S(2)}, u32[]{:S(2)}) collective-permute-start(bf16[2,512,256]{2,1,0:T(8,128)(2,1)S(1)} %shard_map.136), channel_id=1, source_target_pairs={{0,4},{4,0},{8,12},{12,8},{16,20},{20,16},{24,28},{28,24},{1,5},{5... | collective-permute-start | bytes 1572872 | tf_op jit(solution)/shard_map/ppermute | solution.py:58
  61.7 2.6 %collective-permute-start.19 = (bf16[4,128,256]{2,1,0:T(8,128)(2,1)S(1)}, bf16[4,128,256]{2,1,0:T(8,128)(2,1)S(1)}, u32[]{:S(2)}, u32[]{:S(2)}) collective-permute-start(bf16[4,128,256]{2,1,0:T(8,128)(2,1)S(1)} %get-tuple-element.65), channel_id=1, source_target_pairs={{0,16},{4,20},{8,24},{12,28},{16,0},{20,4},{24,8},{28,12},{1,17},{... | collective-permute-start | bytes 786440 | tf_op jit(solution)/shard_map/ppermute | solution.py:63
  64.3 7.0 %collective-permute-done.18.refs_2_.refs_4_ = bf16[2,512,256]{2,1,0:T(8,128)(2,1)S(1)} collective-permute-done((bf16[2,512,256]{2,1,0:T(8,128)(2,1)S(1)}, bf16[2,512,256]{2,1,0:T(8,128)(2,1)S(1)}, u32[]{:S(2)}, u32[]{:S(2)}) %collective-permute-start.18) | collective-permute-done | bytes 524320 | tf_op jit(solution)/shard_map/ppermute | solution.py:58
  71.3 1.2 %shard_map.137 = (f32[4,128,256]{2,1,0:T(8,128)S(1)}, bf16[4,128,256]{2,1,0:T(8,128)(2,1)S(1)}) custom-call(bf16[4,256,2048]{2,1,0:T(8,128)(2,1)S(1)} %shard_map.120.refs_1_.refs_0_, bf16[4,512,256]{2,1,0:T(8,128)(2,1)S(1)} %get-tuple-element.56.refs_0_.refs_1_.refs_2_, bf16[2,512,256]{2,1,0:T(8,128)(2,1)S(1)} %collective-permute-done.18.refs_2_.refs_4_, ...), custom_call_target="tpu_custom_call" | custom-call | flops 1073741824 | tf_op jit(solution)/shard_map/pallas_call | solution.py:40
  72.6 1.8 %collective-permute-done.19.refs_3_.refs_0_ = bf16[4,128,256]{2,1,0:T(8,128)(2,1)S(1)} collective-permute-done((bf16[4,128,256]{2,1,0:T(8,128)(2,1)S(1)}, bf16[4,128,256]{2,1,0:T(8,128)(2,1)S(1)}, u32[]{:S(2)}, u32[]{:S(2)}) %collective-permute-start.19) | collective-permute-done | bytes 262176 | tf_op jit(solution)/shard_map/ppermute | solution.py:63
  74.4 0.8 collective-permute-start.27
  75.2 1.6 %collective-permute-start.28 = (bf16[4,128,256]{2,1,0:T(8,128)(2,1)S(1)}, bf16[4,128,256]{2,1,0:T(8,128)(2,1)S(1)}, u32[]{:S(2)}, u32[]{:S(2)}) collective-permute-start(bf16[4,128,256]{2,1,0:T(8,128)(2,1)S(1)} %get-tuple-element.78), channel_id=1, source_target_pairs={{0,16},{4,20},{8,24},{12,28},{16,0},{20,4},{24,8},{28,12},{1,17},{... | collective-permute-start | bytes 786440 | tf_op jit(solution)/shard_map/ppermute | solution.py:63
  76.9 1.7 %collective-permute-start.20 = (bf16[2,4,128,128]{3,2,1,0:T(8,128)(2,1)S(1)}, bf16[2,4,128,128]{3,2,1,0:T(8,128)(2,1)S(1)}, u32[]{:S(2)}, u32[]{:S(2)}) collective-permute-start(bf16[2,4,128,128]{3,2,1,0:T(8,128)(2,1)S(1)} %get-tuple-element.66), channel_id=1, source_target_pairs={{0,4},{4,0},{8,12},{12,8},{16,20},{20,16},{24,28},{28,24},{1,5},{5... | collective-permute-start | bytes 786440 | tf_op jit(solution)/shard_map/ppermute | solution.py:58
  78.6 4.8 %shard_map.141 = (f32[2,512,256]{2,1,0:T(8,128)S(1)}, bf16[512,256]{1,0:T(8,128)(2,1)S(1)}, bf16[512,256]{1,0:T(8,128)(2,1)S(1)}) custom-call(bf16[1,1024,4096]{2,1,0:T(8,128)(2,1)S(1)} %bitcast.3, f32[512,1]{1,0:T(8,128)S(1)} %copy-done.8, bf16[4,512,256]{2,1,0:T(8,128)(2,1)S(1)} %get-tuple-element.56.refs_0_.refs_1_.refs_2_, ...), custom_call_target="tpu_custom_call" | custom-call | flops 4294967296 | tf_op jit(solution)/shard_map/pallas_call | solution.py:40
  83.5 0.5 collective-permute-start.25
  84.0 4.2 %collective-permute-done.28.refs_0_.refs_5_ = bf16[4,128,256]{2,1,0:T(8,128)(2,1)S(1)} collective-permute-done((bf16[4,128,256]{2,1,0:T(8,128)(2,1)S(1)}, bf16[4,128,256]{2,1,0:T(8,128)(2,1)S(1)}, u32[]{:S(2)}, u32[]{:S(2)}) %collective-permute-start.28) | collective-permute-done | bytes 262176 | tf_op jit(solution)/shard_map/ppermute | solution.py:63
  88.4 0.9 collective-permute-done.27.refs_2_.refs_4_
  89.3 1.2 %shard_map.147 = (f32[4,128,256]{2,1,0:T(8,128)S(1)}, bf16[4,128,256]{2,1,0:T(8,128)(2,1)S(1)}) custom-call(bf16[4,256,2048]{2,1,0:T(8,128)(2,1)S(1)} %shard_map.120.refs_1_.refs_0_, bf16[4,512,256]{2,1,0:T(8,128)(2,1)S(1)} %get-tuple-element.56.refs_0_.refs_1_.refs_2_, bf16[2,512,256]{2,1,0:T(8,128)(2,1)S(1)} %collective-permute-done.27.refs_2_.refs_4_, ...), custom_call_target="tpu_custom_call" | custom-call | flops 1073741824 | tf_op jit(solution)/shard_map/pallas_call | solution.py:40
  90.6 1.3 %collective-permute-start.29 = (bf16[4,128,256]{2,1,0:T(8,128)(2,1)S(1)}, bf16[4,128,256]{2,1,0:T(8,128)(2,1)S(1)}, u32[]{:S(2)}, u32[]{:S(2)}) collective-permute-start(bf16[4,128,256]{2,1,0:T(8,128)(2,1)S(1)} %get-tuple-element.80), channel_id=1, source_target_pairs={{0,16},{4,20},{8,24},{12,28},{16,0},{20,4},{24,8},{28,12},{1,17},{... | collective-permute-start | bytes 786440 | tf_op jit(solution)/shard_map/ppermute | solution.py:63
  91.9 1.0 collective-permute-done.20.refs_1_.refs_3_
  92.9 0.7 collective-permute-start.31
  93.6 0.9 shard_map.139
  94.4 2.1 %collective-permute-start.21 = (bf16[2,4,128,128]{3,2,1,0:T(8,128)(2,1)S(1)}, bf16[2,4,128,128]{3,2,1,0:T(8,128)(2,1)S(1)}, u32[]{:S(2)}, u32[]{:S(2)}) collective-permute-start(bf16[2,4,128,128]{3,2,1,0:T(8,128)(2,1)S(1)} %get-tuple-element.68), channel_id=1, source_target_pairs={{0,8},{4,12},{8,0},{12,4},{16,24},{20,28},{24,16},{28,20},{1,9},{5... | collective-permute-start | bytes 786440 | tf_op jit(solution)/shard_map/ppermute | solution.py:58
  96.7 1.6 %collective-permute-start.26 = (bf16[512,256]{1,0:T(8,128)(2,1)S(1)}, bf16[512,256]{1,0:T(8,128)(2,1)S(1)}, u32[]{:S(2)}, u32[]{:S(2)}) collective-permute-start(bf16[512,256]{1,0:T(8,128)(2,1)S(1)} %get-tuple-element.76), channel_id=1, source_target_pairs={{0,2},{1,3},{2,0},{3,1},{4,6},{5,7},{6,4},{7,5},{8,10},{9,11},{10,... | collective-permute-start | bytes 786440 | tf_op jit(solution)/shard_map/ppermute | solution.py:58
  98.3 1.4 %collective-permute-done.31.refs_2_ = bf16[1,3,128,256]{3,2,1,0:T(8,128)(2,1)S(1)} collective-permute-done((bf16[1,3,128,256]{3,2,1,0:T(8,128)(2,1)S(1)}, bf16[1,3,128,256]{3,2,1,0:T(8,128)(2,1)S(1)}, u32[]{:S(2)}, u32[]{:S(2)}) %collective-permute-start.31) | collective-permute-done | bytes 196640 | tf_op jit(solution)/shard_map/ppermute | solution.py:58
  99.6 2.0 %collective-permute-done.32.refs_3_ = bf16[1,3,128,256]{3,2,1,0:T(8,128)(2,1)S(1)} collective-permute-done((bf16[1,3,128,256]{3,2,1,0:T(8,128)(2,1)S(1)}, bf16[1,3,128,256]{3,2,1,0:T(8,128)(2,1)S(1)}, u32[]{:S(2)}, u32[]{:S(2)}) %collective-permute-start.32) | collective-permute-done | bytes 196640 | tf_op jit(solution)/shard_map/ppermute | solution.py:58
  101.6 1.3 %shard_map.149 = (f32[1,128,4096]{2,1,0:T(8,128)}, f32[8,128]{1,0:T(8,128)S(1)}) custom-call(f32[1,3,128,256]{3,2,1,0:T(8,128)S(1)} %get-tuple-element.81.refs_0_, bf16[1,3,128,256]{3,2,1,0:T(8,128)(2,1)S(1)} %collective-permute-done.30.refs_1_, bf16[1,3,128,256]{3,2,1,0:T(8,128)(2,1)S(1)} %collective-permute-done.31.refs_2_, ...), custom_call_target="tpu_custom_call" | custom-call | tf_op jit(solution)/shard_map/pallas_call | solution.py:40
  103.0 1.6 %collective-permute-done.29.refs_1_ = bf16[4,128,256]{2,1,0:T(8,128)(2,1)S(1)} collective-permute-done((bf16[4,128,256]{2,1,0:T(8,128)(2,1)S(1)}, bf16[4,128,256]{2,1,0:T(8,128)(2,1)S(1)}, u32[]{:S(2)}, u32[]{:S(2)}) %collective-permute-start.29) | collective-permute-done | bytes 262176 | tf_op jit(solution)/shard_map/ppermute | solution.py:63
  104.7 0.8 collective-permute-start.33
  105.8 1.0 collective-permute-start.35
  106.9 1.5 %collective-permute-done.21.refs_4_ = bf16[2,4,128,128]{3,2,1,0:T(8,128)(2,1)S(1)} collective-permute-done((bf16[2,4,128,128]{3,2,1,0:T(8,128)(2,1)S(1)}, bf16[2,4,128,128]{3,2,1,0:T(8,128)(2,1)S(1)}, u32[]{:S(2)}, u32[]{:S(2)}) %collective-permute-start.21) | collective-permute-done | bytes 262176 | tf_op jit(solution)/shard_map/ppermute | solution.py:58
  108.4 1.2 %shard_map.140 = bf16[512,512]{1,0:T(8,128)(2,1)} custom-call(f32[512,512]{1,0:T(8,128)S(1)} %shard_map.131.refs_5_.refs_0_, bf16[512,512]{1,0:T(8,128)(2,1)S(1)} %copy-done.4, bf16[4,128,128]{2,1,0:T(8,128)(2,1)S(1)} %collective-permute-done.9.refs_4_.refs_1_.refs_2_, bf16[2,4,128,128]{3,2,1,0:T(8,128)(2,1)S(1)} %collective-permute-done.20.refs_1_.refs_3_, ...), custom_call_target="tpu_custom_call" | custom-call | tf_op jit(solution)/shard_map/pallas_call | solution.py:40
  109.6 0.7 shard_map.143
  110.5 1.4 %shard_map.151 = (f32[1,128,4096]{2,1,0:T(8,128)}, f32[8,128]{1,0:T(8,128)}) custom-call(f32[1,1,128,256]{3,2,1,0:T(8,128)S(1)} %get-tuple-element.86.refs_0_, bf16[1,1,128,256]{3,2,1,0:T(8,128)(2,1)S(1)} %collective-permute-done.33.refs_1_, bf16[1,1,128,256]{3,2,1,0:T(8,128)(2,1)S(1)} %collective-permute-done.34.refs_2_, ...), custom_call_target="tpu_custom_call", output_to_operand_aliasing={{0}: (4, {})} | custom-call | tf_op jit(solution)/shard_map/pallas_call | solution.py:40
  (64 shorter events, 2.6 us)
Async XLA Ops:
  0.6 20.0 %copy-start.4 = (bf16[512,512]{1,0:T(8,128)(2,1)S(1)}, bf16[512,512]{1,0:T(8,128)(2,1)}, u32[]{:S(2)}) copy-start(bf16[512,512]{1,0:T(8,128)(2,1)} %refs_1_.15) | copy-start | bytes 1572868
  0.6 20.0 %copy-start.5 = (bf16[512,512]{1,0:T(8,128)(2,1)S(1)}, bf16[512,512]{1,0:T(8,128)(2,1)}, u32[]{:S(2)}) copy-start(bf16[512,512]{1,0:T(8,128)(2,1)} %refs_0_.11) | copy-start | bytes 1572868
  0.7 20.0 %copy-start.3 = (bf16[512,512]{1,0:T(8,128)(2,1)S(1)}, bf16[512,512]{1,0:T(8,128)(2,1)}, u32[]{:S(2)}) copy-start(bf16[512,512]{1,0:T(8,128)(2,1)} %refs_1_.14) | copy-start | bytes 1572868
  0.7 19.9 %copy-start.1 = (bf16[512,512]{1,0:T(8,128)(2,1)S(1)}, bf16[512,512]{1,0:T(8,128)(2,1)}, u32[]{:S(2)}) copy-start(bf16[512,512]{1,0:T(8,128)(2,1)} %refs_0_.14) | copy-start | bytes 1572868
  3.7 7.6 %collective-permute-start.7 = (bf16[4,128,128]{2,1,0:T(8,128)(2,1)}, bf16[4,128,128]{2,1,0:T(8,128)(2,1)S(1)}, u32[]{:S(2)}, u32[]{:S(2)}) collective-permute-start(bf16[4,128,128]{2,1,0:T(8,128)(2,1)} %get-tuple-element.53.refs_0_), channel_id=1, source_target_pairs={{0,4},{4,0},{8,12},{12,8},{16,20},{20,16},{24,28},{28,24},{1,5},{5... | collective-permute-start | bytes 393224 | tf_op jit(solution)/shard_map/ppermute | solution.py:58
  6.8 7.7 %collective-permute-start.4 = (bf16[272,256]{1,0:T(8,128)(2,1)}, bf16[272,256]{1,0:T(8,128)(2,1)S(1)}, u32[]{:S(2)}, u32[]{:S(2)}) collective-permute-start(bf16[272,256]{1,0:T(8,128)(2,1)} %get-tuple-element.52), channel_id=1, source_target_pairs={{0,8},{4,12},{8,0},{12,4},{16,24},{20,28},{24,16},{28,20},{1,9},{5... | collective-permute-start | bytes 417800 | tf_op jit(solution)/shard_map/ppermute | solution.py:58
  8.3 7.6 %collective-permute-start = (bf16[272,256]{1,0:T(8,128)(2,1)}, bf16[272,256]{1,0:T(8,128)(2,1)S(1)}, u32[]{:S(2)}, u32[]{:S(2)}) collective-permute-start(bf16[272,256]{1,0:T(8,128)(2,1)} %get-tuple-element.50), channel_id=1, source_target_pairs={{0,4},{4,0},{8,12},{12,8},{16,20},{20,16},{24,28},{28,24},{1,5},{5... | collective-permute-start | bytes 417800 | tf_op jit(solution)/shard_map/ppermute | solution.py:58
  8.8 7.3 %collective-permute-start.2 = (bf16[272,256]{1,0:T(8,128)(2,1)}, bf16[272,256]{1,0:T(8,128)(2,1)S(1)}, u32[]{:S(2)}, u32[]{:S(2)}) collective-permute-start(bf16[272,256]{1,0:T(8,128)(2,1)} %get-tuple-element.51), channel_id=1, source_target_pairs={{0,8},{4,12},{8,0},{12,4},{16,24},{20,28},{24,16},{28,20},{1,9},{5... | collective-permute-start | bytes 417800 | tf_op jit(solution)/shard_map/ppermute | solution.py:58
  8.9 1.0 copy-start
  9.9 1.0 copy-start.2
  11.3 0.9 copy-start.7
  12.3 5.6 %collective-permute-start.8 = (bf16[4,128,128]{2,1,0:T(8,128)(2,1)S(1)}, bf16[4,128,128]{2,1,0:T(8,128)(2,1)S(1)}, u32[]{:S(2)}, u32[]{:S(2)}) collective-permute-start(bf16[4,128,128]{2,1,0:T(8,128)(2,1)S(1)} %get-tuple-element.54), channel_id=1, source_target_pairs={{0,8},{4,12},{8,0},{12,4},{16,24},{20,28},{24,16},{28,20},{1,9},{5... | collective-permute-start | bytes 393224 | tf_op jit(solution)/shard_map/ppermute | solution.py:58
  14.4 7.5 %collective-permute-start.5 = (bf16[272,256]{1,0:T(8,128)(2,1)S(1)}, bf16[272,256]{1,0:T(8,128)(2,1)S(1)}, u32[]{:S(2)}, u32[]{:S(2)}) collective-permute-start(bf16[272,256]{1,0:T(8,128)(2,1)S(1)} %collective-permute-done.4.refs_3_), channel_id=1, source_target_pairs={{0,4},{4,0},{8,12},{12,8},{16,20},{20,16},{24,28},{28,24},{1,5},{5... | collective-permute-start | bytes 417800 | tf_op jit(solution)/shard_map/ppermute | solution.py:58
  16.0 10.5 %collective-permute-start.1 = (bf16[272,256]{1,0:T(8,128)(2,1)S(1)}, bf16[272,256]{1,0:T(8,128)(2,1)S(1)}, u32[]{:S(2)}, u32[]{:S(2)}) collective-permute-start(bf16[272,256]{1,0:T(8,128)(2,1)S(1)} %collective-permute-done.refs_1_.refs_0_), channel_id=1, source_target_pairs={{0,1},{1,0},{2,3},{3,2},{4,5},{5,4},{6,7},{7,6},{8,9},{9,8},{10,11... | collective-permute-start | bytes 417800 | tf_op jit(solution)/shard_map/ppermute | solution.py:58
  16.2 10.3 %collective-permute-start.3 = (bf16[272,256]{1,0:T(8,128)(2,1)S(1)}, bf16[272,256]{1,0:T(8,128)(2,1)S(1)}, u32[]{:S(2)}, u32[]{:S(2)}) collective-permute-start(bf16[272,256]{1,0:T(8,128)(2,1)S(1)} %collective-permute-done.2.refs_3_.refs_1_), channel_id=1, source_target_pairs={{0,1},{1,0},{2,3},{3,2},{4,5},{5,4},{6,7},{7,6},{8,9},{9,8},{10,11... | collective-permute-start | bytes 417800 | tf_op jit(solution)/shard_map/ppermute | solution.py:58
  17.9 8.2 %collective-permute-start.9 = (bf16[4,128,128]{2,1,0:T(8,128)(2,1)S(1)}, bf16[4,128,128]{2,1,0:T(8,128)(2,1)S(1)}, u32[]{:S(2)}, u32[]{:S(2)}) collective-permute-start(bf16[4,128,128]{2,1,0:T(8,128)(2,1)S(1)} %shard_map.123.refs_4_), channel_id=1, source_target_pairs={{0,16},{4,20},{8,24},{12,28},{16,0},{20,4},{24,8},{28,12},{1,17},{... | collective-permute-start | bytes 393224 | tf_op jit(solution)/shard_map/ppermute | solution.py:58
  22.0 4.5 %collective-permute-start.6 = (bf16[272,256]{1,0:T(8,128)(2,1)S(1)}, bf16[272,256]{1,0:T(8,128)(2,1)S(1)}, u32[]{:S(2)}, u32[]{:S(2)}) collective-permute-start(bf16[272,256]{1,0:T(8,128)(2,1)S(1)} %collective-permute-done.5.refs_5_.refs_2_), channel_id=1, source_target_pairs={{0,1},{1,0},{2,3},{3,2},{4,5},{5,4},{6,7},{7,6},{8,9},{9,8},{10,11... | collective-permute-start | bytes 417800 | tf_op jit(solution)/shard_map/ppermute | solution.py:58
  23.4 6.5 %copy-start.6 = (bf16[272,512]{1,0:T(8,128)(2,1)S(1)}, bf16[272,512]{1,0:T(8,128)(2,1)}, u32[]{:S(2)}) copy-start(bf16[272,512]{1,0:T(8,128)(2,1)} %get-tuple-element.49.refs_0_) | copy-start | bytes 835588
  27.1 24.4 %collective-permute-start.22 = (bf16[4,512,256]{2,1,0:T(8,128)(2,1)S(1)}, bf16[4,512,256]{2,1,0:T(8,128)(2,1)S(1)}, u32[]{:S(2)}, u32[]{:S(2)}) collective-permute-start(bf16[4,512,256]{2,1,0:T(8,128)(2,1)S(1)} %get-tuple-element.56.refs_0_.refs_1_.refs_2_), channel_id=1, source_target_pairs={{0,2},{1,3},{2,0},{3,1},{4,6},{5,7},{6,4},{7,5},{8,10},{9,11},{10,... | collective-permute-start | bytes 3145736 | tf_op jit(solution)/shard_map/ppermute | solution.py:58
  28.4 6.4 %collective-permute-start.10 = (bf16[512,256]{1,0:T(8,128)(2,1)S(1)}, bf16[512,256]{1,0:T(8,128)(2,1)S(1)}, u32[]{:S(2)}, u32[]{:S(2)}) collective-permute-start(bf16[512,256]{1,0:T(8,128)(2,1)S(1)} %shard_map.127.refs_7_), channel_id=1, source_target_pairs={{0,4},{4,0},{8,12},{12,8},{16,20},{20,16},{24,28},{28,24},{1,5},{5... | collective-permute-start | bytes 786440 | tf_op jit(solution)/shard_map/ppermute | solution.py:58
  29.2 6.4 %collective-permute-start.11 = (bf16[512,256]{1,0:T(8,128)(2,1)S(1)}, bf16[512,256]{1,0:T(8,128)(2,1)S(1)}, u32[]{:S(2)}, u32[]{:S(2)}) collective-permute-start(bf16[512,256]{1,0:T(8,128)(2,1)S(1)} %shard_map.127.refs_7_), channel_id=1, source_target_pairs={{0,8},{4,12},{8,0},{12,4},{16,24},{20,28},{24,16},{28,20},{1,9},{5... | collective-permute-start | bytes 786440 | tf_op jit(solution)/shard_map/ppermute | solution.py:58
  29.9 24.9 %collective-permute-start.17 = (bf16[4,512,256]{2,1,0:T(8,128)(2,1)S(1)}, bf16[4,512,256]{2,1,0:T(8,128)(2,1)S(1)}, u32[]{:S(2)}, u32[]{:S(2)}) collective-permute-start(bf16[4,512,256]{2,1,0:T(8,128)(2,1)S(1)} %get-tuple-element.56.refs_0_.refs_1_.refs_2_), channel_id=1, source_target_pairs={{0,1},{1,0},{2,3},{3,2},{4,5},{5,4},{6,7},{7,6},{8,9},{9,8},{10,11... | collective-permute-start | bytes 3145736 | tf_op jit(solution)/shard_map/ppermute | solution.py:58
  35.6 6.4 %collective-permute-start.12 = (bf16[512,256]{1,0:T(8,128)(2,1)S(1)}, bf16[512,256]{1,0:T(8,128)(2,1)S(1)}, u32[]{:S(2)}, u32[]{:S(2)}) collective-permute-start(bf16[512,256]{1,0:T(8,128)(2,1)S(1)} %collective-permute-done.11.refs_3_), channel_id=1, source_target_pairs={{0,4},{4,0},{8,12},{12,8},{16,20},{20,16},{24,28},{28,24},{1,5},{5... | collective-permute-start | bytes 786440 | tf_op jit(solution)/shard_map/ppermute | solution.py:58
  36.8 6.4 %collective-permute-start.14 = (bf16[512,256]{1,0:T(8,128)(2,1)S(1)}, bf16[512,256]{1,0:T(8,128)(2,1)S(1)}, u32[]{:S(2)}, u32[]{:S(2)}) collective-permute-start(bf16[512,256]{1,0:T(8,128)(2,1)S(1)} %get-tuple-element.61), channel_id=1, source_target_pairs={{0,8},{4,12},{8,0},{12,4},{16,24},{20,28},{24,16},{28,20},{1,9},{5... | collective-permute-start | bytes 786440 | tf_op jit(solution)/shard_map/ppermute | solution.py:58
  43.3 10.3 %collective-permute-start.15 = (bf16[2,512,256]{2,1,0:T(8,128)(2,1)S(1)}, bf16[2,512,256]{2,1,0:T(8,128)(2,1)S(1)}, u32[]{:S(2)}, u32[]{:S(2)}) collective-permute-start(bf16[2,512,256]{2,1,0:T(8,128)(2,1)S(1)} %shard_map.132), channel_id=1, source_target_pairs={{0,4},{4,0},{8,12},{12,8},{16,20},{20,16},{24,28},{28,24},{1,5},{5... | collective-permute-start | bytes 1572872 | tf_op jit(solution)/shard_map/ppermute | solution.py:58
  44.6 15.5 %collective-permute-start.13 = (bf16[2,512,256]{2,1,0:T(8,128)(2,1)S(1)}, bf16[2,512,256]{2,1,0:T(8,128)(2,1)S(1)}, u32[]{:S(2)}, u32[]{:S(2)}) collective-permute-start(bf16[2,512,256]{2,1,0:T(8,128)(2,1)S(1)} %get-tuple-element.60), channel_id=1, source_target_pairs={{0,8},{4,12},{8,0},{12,4},{16,24},{20,28},{24,16},{28,20},{1,9},{5... | collective-permute-start | bytes 1572872 | tf_op jit(solution)/shard_map/ppermute | solution.py:58
  45.7 13.6 %collective-permute-start.16 = (bf16[4,128,256]{2,1,0:T(8,128)(2,1)S(1)}, bf16[4,128,256]{2,1,0:T(8,128)(2,1)S(1)}, u32[]{:S(2)}, u32[]{:S(2)}) collective-permute-start(bf16[4,128,256]{2,1,0:T(8,128)(2,1)S(1)} %get-tuple-element.63), channel_id=1, source_target_pairs={{0,16},{4,20},{8,24},{12,28},{16,0},{20,4},{24,8},{28,12},{1,17},{... | collective-permute-start | bytes 786440 | tf_op jit(solution)/shard_map/ppermute | solution.py:63
  51.4 27.2 %collective-permute-start.23 = (bf16[4,512,256]{2,1,0:T(8,128)(2,1)S(1)}, bf16[4,512,256]{2,1,0:T(8,128)(2,1)S(1)}, u32[]{:S(2)}, u32[]{:S(2)}) collective-permute-start(bf16[4,512,256]{2,1,0:T(8,128)(2,1)S(1)} %collective-permute-done.22.refs_4_), channel_id=1, source_target_pairs={{0,1},{1,0},{2,3},{3,2},{4,5},{5,4},{6,7},{7,6},{8,9},{9,8},{10,11... | collective-permute-start | bytes 3145736 | tf_op jit(solution)/shard_map/ppermute | solution.py:58
  54.8 23.8 %slice-start = ((s8[8388608]{0:T(1024)(128)(4,1)}), s8[4194304]{0:T(1024)(128)(4,1)S(1)}, s32[]{:S(2)}) async-start(s8[8388608]{0:T(1024)(128)(4,1)} %bitcast.2), calls=%async_computation | async-start | bytes 8388608
  60.1 11.2 %collective-permute-start.18 = (bf16[2,512,256]{2,1,0:T(8,128)(2,1)S(1)}, bf16[2,512,256]{2,1,0:T(8,128)(2,1)S(1)}, u32[]{:S(2)}, u32[]{:S(2)}) collective-permute-start(bf16[2,512,256]{2,1,0:T(8,128)(2,1)S(1)} %shard_map.136), channel_id=1, source_target_pairs={{0,4},{4,0},{8,12},{12,8},{16,20},{20,16},{24,28},{28,24},{1,5},{5... | collective-permute-start | bytes 1572872 | tf_op jit(solution)/shard_map/ppermute | solution.py:58
  61.7 17.0 %slice-start.1 = ((s8[8388608]{0:T(1024)(128)(4,1)}), s8[4194304]{0:T(1024)(128)(4,1)S(1)}, s32[]{:S(2)}) async-start(s8[8388608]{0:T(1024)(128)(4,1)} %bitcast.2), calls=%async_computation.1 | async-start | bytes 8388608
  61.7 17.0 %copy-start.8 = (f32[512,1]{1,0:T(8,128)S(1)}, f32[512,1]{1,0:T(8,128)}, u32[]{:S(2)}) copy-start(f32[512,1]{1,0:T(8,128)} %get-tuple-element.71.refs_1_) | copy-start | bytes 6148
  61.7 12.7 %collective-permute-start.19 = (bf16[4,128,256]{2,1,0:T(8,128)(2,1)S(1)}, bf16[4,128,256]{2,1,0:T(8,128)(2,1)S(1)}, u32[]{:S(2)}, u32[]{:S(2)}) collective-permute-start(bf16[4,128,256]{2,1,0:T(8,128)(2,1)S(1)} %get-tuple-element.65), channel_id=1, source_target_pairs={{0,16},{4,20},{8,24},{12,28},{16,0},{20,4},{24,8},{28,12},{1,17},{... | collective-permute-start | bytes 786440 | tf_op jit(solution)/shard_map/ppermute | solution.py:63
  74.4 14.9 %collective-permute-start.27 = (bf16[2,512,256]{2,1,0:T(8,128)(2,1)S(1)}, bf16[2,512,256]{2,1,0:T(8,128)(2,1)S(1)}, u32[]{:S(2)}, u32[]{:S(2)}) collective-permute-start(bf16[2,512,256]{2,1,0:T(8,128)(2,1)S(1)} %shard_map.145), channel_id=1, source_target_pairs={{0,4},{4,0},{8,12},{12,8},{16,20},{20,16},{24,28},{28,24},{1,5},{5... | collective-permute-start | bytes 1572872 | tf_op jit(solution)/shard_map/ppermute | solution.py:58
  75.2 13.0 %collective-permute-start.28 = (bf16[4,128,256]{2,1,0:T(8,128)(2,1)S(1)}, bf16[4,128,256]{2,1,0:T(8,128)(2,1)S(1)}, u32[]{:S(2)}, u32[]{:S(2)}) collective-permute-start(bf16[4,128,256]{2,1,0:T(8,128)(2,1)S(1)} %get-tuple-element.78), channel_id=1, source_target_pairs={{0,16},{4,20},{8,24},{12,28},{16,0},{20,4},{24,8},{28,12},{1,17},{... | collective-permute-start | bytes 786440 | tf_op jit(solution)/shard_map/ppermute | solution.py:63
  76.9 16.0 %collective-permute-start.20 = (bf16[2,4,128,128]{3,2,1,0:T(8,128)(2,1)S(1)}, bf16[2,4,128,128]{3,2,1,0:T(8,128)(2,1)S(1)}, u32[]{:S(2)}, u32[]{:S(2)}) collective-permute-start(bf16[2,4,128,128]{3,2,1,0:T(8,128)(2,1)S(1)} %get-tuple-element.66), channel_id=1, source_target_pairs={{0,4},{4,0},{8,12},{12,8},{16,20},{20,16},{24,28},{28,24},{1,5},{5... | collective-permute-start | bytes 786440 | tf_op jit(solution)/shard_map/ppermute | solution.py:58
  83.5 11.0 %collective-permute-start.24 = (bf16[512,256]{1,0:T(8,128)(2,1)S(1)}, bf16[512,256]{1,0:T(8,128)(2,1)S(1)}, u32[]{:S(2)}, u32[]{:S(2)}) collective-permute-start(bf16[512,256]{1,0:T(8,128)(2,1)S(1)} %get-tuple-element.73), channel_id=1, source_target_pairs={{0,1},{1,0},{2,3},{3,2},{4,5},{5,4},{6,7},{7,6},{8,9},{9,8},{10,11... | collective-permute-start | bytes 786440 | tf_op jit(solution)/shard_map/ppermute | solution.py:58
  83.5 10.9 %collective-permute-start.25 = (bf16[512,256]{1,0:T(8,128)(2,1)S(1)}, bf16[512,256]{1,0:T(8,128)(2,1)S(1)}, u32[]{:S(2)}, u32[]{:S(2)}) collective-permute-start(bf16[512,256]{1,0:T(8,128)(2,1)S(1)} %get-tuple-element.74), channel_id=1, source_target_pairs={{0,1},{1,0},{2,3},{3,2},{4,5},{5,4},{6,7},{7,6},{8,9},{9,8},{10,11... | collective-permute-start | bytes 786440 | tf_op jit(solution)/shard_map/ppermute | solution.py:58
  88.4 8.3 %collective-permute-start.30 = (bf16[1,3,128,256]{3,2,1,0:T(8,128)(2,1)S(1)}, bf16[1,3,128,256]{3,2,1,0:T(8,128)(2,1)S(1)}, u32[]{:S(2)}, u32[]{:S(2)}) collective-permute-start(bf16[1,3,128,256]{3,2,1,0:T(8,128)(2,1)S(1)} %get-tuple-element.82), channel_id=1, source_target_pairs={{0,1},{1,0},{2,3},{3,2},{4,5},{5,4},{6,7},{7,6},{8,9},{9,8},{10,11... | collective-permute-start | bytes 589832 | tf_op jit(solution)/shard_map/ppermute | solution.py:58
  90.6 14.0 %collective-permute-start.29 = (bf16[4,128,256]{2,1,0:T(8,128)(2,1)S(1)}, bf16[4,128,256]{2,1,0:T(8,128)(2,1)S(1)}, u32[]{:S(2)}, u32[]{:S(2)}) collective-permute-start(bf16[4,128,256]{2,1,0:T(8,128)(2,1)S(1)} %get-tuple-element.80), channel_id=1, source_target_pairs={{0,16},{4,20},{8,24},{12,28},{16,0},{20,4},{24,8},{28,12},{1,17},{... | collective-permute-start | bytes 786440 | tf_op jit(solution)/shard_map/ppermute | solution.py:63
  92.9 6.8 %collective-permute-start.31 = (bf16[1,3,128,256]{3,2,1,0:T(8,128)(2,1)S(1)}, bf16[1,3,128,256]{3,2,1,0:T(8,128)(2,1)S(1)}, u32[]{:S(2)}, u32[]{:S(2)}) collective-permute-start(bf16[1,3,128,256]{3,2,1,0:T(8,128)(2,1)S(1)} %get-tuple-element.83), channel_id=1, source_target_pairs={{0,2},{1,3},{2,0},{3,1},{4,6},{5,7},{6,4},{7,5},{8,10},{9,11},{10,... | collective-permute-start | bytes 589832 | tf_op jit(solution)/shard_map/ppermute | solution.py:58
  94.4 7.2 %collective-permute-start.32 = (bf16[1,3,128,256]{3,2,1,0:T(8,128)(2,1)S(1)}, bf16[1,3,128,256]{3,2,1,0:T(8,128)(2,1)S(1)}, u32[]{:S(2)}, u32[]{:S(2)}) collective-permute-start(bf16[1,3,128,256]{3,2,1,0:T(8,128)(2,1)S(1)} %get-tuple-element.84), channel_id=1, source_target_pairs={{0,3},{1,2},{2,1},{3,0},{4,7},{5,6},{6,5},{7,4},{8,11},{9,10},{10,... | collective-permute-start | bytes 589832 | tf_op jit(solution)/shard_map/ppermute | solution.py:58
  94.4 14.0 %collective-permute-start.21 = (bf16[2,4,128,128]{3,2,1,0:T(8,128)(2,1)S(1)}, bf16[2,4,128,128]{3,2,1,0:T(8,128)(2,1)S(1)}, u32[]{:S(2)}, u32[]{:S(2)}) collective-permute-start(bf16[2,4,128,128]{3,2,1,0:T(8,128)(2,1)S(1)} %get-tuple-element.68), channel_id=1, source_target_pairs={{0,8},{4,12},{8,0},{12,4},{16,24},{20,28},{24,16},{28,20},{1,9},{5... | collective-permute-start | bytes 786440 | tf_op jit(solution)/shard_map/ppermute | solution.py:58
  96.7 12.9 %collective-permute-start.26 = (bf16[512,256]{1,0:T(8,128)(2,1)S(1)}, bf16[512,256]{1,0:T(8,128)(2,1)S(1)}, u32[]{:S(2)}, u32[]{:S(2)}) collective-permute-start(bf16[512,256]{1,0:T(8,128)(2,1)S(1)} %get-tuple-element.76), channel_id=1, source_target_pairs={{0,2},{1,3},{2,0},{3,1},{4,6},{5,7},{6,4},{7,5},{8,10},{9,11},{10,... | collective-permute-start | bytes 786440 | tf_op jit(solution)/shard_map/ppermute | solution.py:58
  104.7 5.7 %collective-permute-start.33 = (bf16[1,1,128,256]{3,2,1,0:T(8,128)(2,1)S(1)}, bf16[1,1,128,256]{3,2,1,0:T(8,128)(2,1)S(1)}, u32[]{:S(2)}, u32[]{:S(2)}) collective-permute-start(bf16[1,1,128,256]{3,2,1,0:T(8,128)(2,1)S(1)} %get-tuple-element.87), channel_id=1, source_target_pairs={{0,1},{1,0},{2,3},{3,2},{4,5},{5,4},{6,7},{7,6},{8,9},{9,8},{10,11... | collective-permute-start | bytes 196616 | tf_op jit(solution)/shard_map/ppermute | solution.py:58
  105.4 4.9 %collective-permute-start.34 = (bf16[1,1,128,256]{3,2,1,0:T(8,128)(2,1)S(1)}, bf16[1,1,128,256]{3,2,1,0:T(8,128)(2,1)S(1)}, u32[]{:S(2)}, u32[]{:S(2)}) collective-permute-start(bf16[1,1,128,256]{3,2,1,0:T(8,128)(2,1)S(1)} %get-tuple-element.88), channel_id=1, source_target_pairs={{0,2},{1,3},{2,0},{3,1},{4,6},{5,7},{6,4},{7,5},{8,10},{9,11},{10,... | collective-permute-start | bytes 196616 | tf_op jit(solution)/shard_map/ppermute | solution.py:58
  105.8 4.7 %collective-permute-start.35 = (bf16[1,1,128,256]{3,2,1,0:T(8,128)(2,1)S(1)}, bf16[1,1,128,256]{3,2,1,0:T(8,128)(2,1)S(1)}, u32[]{:S(2)}, u32[]{:S(2)}) collective-permute-start(bf16[1,1,128,256]{3,2,1,0:T(8,128)(2,1)S(1)} %get-tuple-element.89), channel_id=1, source_target_pairs={{0,3},{1,2},{2,1},{3,0},{4,7},{5,6},{6,5},{7,4},{8,11},{9,10},{10,... | collective-permute-start | bytes 196616 | tf_op jit(solution)/shard_map/ppermute | solution.py:58

commit v6 on v5

--- a/solution.py
+++ b/solution.py
@@ -645,7 +645,7 @@
             total, sent = add_both(other_state, came, [owns[2], others[1][0]])
             earlier = [swap(sent, "seq", 1)]
             keep, *send = input_products(pieces, expert_weight, gate, [owns[2]])
-            fillers = [touch(others[2])]
+            fillers = []
         own, other = weight_product(
             weighted, [own_heads[number], near[number], across[number], relayed[number]], groups, fillers
         )

time: 113 us -> 113 us (level)
    pallas_call x33 -> x32, Pallas kernels: 26.1 us -> 26 us  [call(): pl.pallas_call(body, out_shape=out_shape, grid_spec=pltpu.PrefetchScalarG...]
  transfers between devices with their start and end apart: 36 -> 36, of which waited for: 20 -> 19; matrix products, arithmetic and copies ran while one was open for 0% -> 0% of each run, Pallas kernels for 19% -> 19%
where the time goes in v6:
time: 113 us; the launch traced here: 112 us
  waiting for transfers between devices  41.8 us (37%)
  starting transfers between devices  40 us (35%)
  Pallas kernels  26 us (23%)
  local copies, waits for them, and re-layouts  3.02 us (3%)
  between operations  1.18 us (1%)
    ppermute x32, starting transfers between devices, swap(): lax.ppermute(array, axis, [(place, place ^ mask) for place in range(count)])  31 us
    ppermute x32, waiting for transfers between devices, swap(): lax.ppermute(array, axis, [(place, place ^ mask) for place in range(count)])  29.5 us
    pallas_call x32, Pallas kernels, call(): pl.pallas_call(body, out_shape=out_shape, grid_spec=pltpu.PrefetchScalarG...  26 us
    ppermute x4, waiting for transfers between devices, shift(): lax.ppermute(array, axis, [(place, (place + step) % count) for place in r...  12.3 us
    ppermute x4, starting transfers between devices, shift(): lax.ppermute(array, axis, [(place, (place + step) % count) for place in r...  9.02 us
    unnamed x22, local copies, waits for them, and re-layouts  3.02 us
  transfers between devices with their start and end apart: 36, of which 19 were waited for; matrix products, arithmetic and copies ran while one was open for 0% of the time, Pallas kernels for 19%

profile of v6, /device:TPU:0, one launch (start us, length us, event | category | flops | bytes accessed | tf_op | source)
XLA Modules:
  0.0 112.1 jit_solution(3558393309018921609)
XLA Ops:
  0.7 3.0 %shard_map.119 = (bf16[4,128,128]{2,1,0:T(8,128)(2,1)}, bf16[272,512]{1,0:T(8,128)(2,1)}, bf16[272,256]{1,0:T(8,128)(2,1)}, bf16[272,256]{1,0:T(8,128)(2,1)}, bf...) custom-call(bf16[512,512]{1,0:T(8,128)(2,1)} %refs_0_.11, bf16[512,512]{1,0:T(8,128)(2,1)} %refs_1_.15, ...), custom_call_target="tpu_custom_call" | custom-call | flops 402653184 | tf_op jit(solution)/shard_map/pallas_call | solution.py:40
  3.7 3.0 %collective-permute-start.7 = (bf16[4,128,128]{2,1,0:T(8,128)(2,1)}, bf16[4,128,128]{2,1,0:T(8,128)(2,1)S(1)}, u32[]{:S(2)}, u32[]{:S(2)}) collective-permute-start(bf16[4,128,128]{2,1,0:T(8,128)(2,1)} %get-tuple-element.53.refs_0_), channel_id=1, source_target_pairs={{0,4},{4,0},{8,12},{12,8},{16,20},{20,16},{24,28},{28,24},{1,5},{5... | collective-permute-start | bytes 393224 | tf_op jit(solution)/shard_map/ppermute | solution.py:58
  6.8 1.6 %collective-permute-start.4 = (bf16[272,256]{1,0:T(8,128)(2,1)}, bf16[272,256]{1,0:T(8,128)(2,1)S(1)}, u32[]{:S(2)}, u32[]{:S(2)}) collective-permute-start(bf16[272,256]{1,0:T(8,128)(2,1)} %get-tuple-element.52), channel_id=1, source_target_pairs={{0,8},{4,12},{8,0},{12,4},{16,24},{20,28},{24,16},{28,20},{1,9},{5... | collective-permute-start | bytes 417800 | tf_op jit(solution)/shard_map/ppermute | solution.py:58
  8.3 0.5 collective-permute-start
  8.9 1.0 copy-done
  9.9 1.0 copy-done.2
  11.3 0.9 copy-done.7
  12.3 2.2 %collective-permute-start.8 = (bf16[4,128,128]{2,1,0:T(8,128)(2,1)S(1)}, bf16[4,128,128]{2,1,0:T(8,128)(2,1)S(1)}, u32[]{:S(2)}, u32[]{:S(2)}) collective-permute-start(bf16[4,128,128]{2,1,0:T(8,128)(2,1)S(1)} %get-tuple-element.54), channel_id=1, source_target_pairs={{0,8},{4,12},{8,0},{12,4},{16,24},{20,28},{24,16},{28,20},{1,9},{5... | collective-permute-start | bytes 393224 | tf_op jit(solution)/shard_map/ppermute | solution.py:58
  14.4 1.5 %collective-permute-start.5 = (bf16[272,256]{1,0:T(8,128)(2,1)S(1)}, bf16[272,256]{1,0:T(8,128)(2,1)S(1)}, u32[]{:S(2)}, u32[]{:S(2)}) collective-permute-start(bf16[272,256]{1,0:T(8,128)(2,1)S(1)} %collective-permute-done.4.refs_3_), channel_id=1, source_target_pairs={{0,4},{4,0},{8,12},{12,8},{16,20},{20,16},{24,28},{28,24},{1,5},{5... | collective-permute-start | bytes 417800 | tf_op jit(solution)/shard_map/ppermute | solution.py:58
  16.5 1.4 %collective-permute-done.8.refs_1_.refs_3_ = bf16[4,128,128]{2,1,0:T(8,128)(2,1)S(1)} collective-permute-done((bf16[4,128,128]{2,1,0:T(8,128)(2,1)S(1)}, bf16[4,128,128]{2,1,0:T(8,128)(2,1)S(1)}, u32[]{:S(2)}, u32[]{:S(2)}) %collective-permute-start.8) | collective-permute-done | bytes 131104 | tf_op jit(solution)/shard_map/ppermute | solution.py:58
  17.9 2.7 %collective-permute-start.9 = (bf16[4,128,128]{2,1,0:T(8,128)(2,1)S(1)}, bf16[4,128,128]{2,1,0:T(8,128)(2,1)S(1)}, u32[]{:S(2)}, u32[]{:S(2)}) collective-permute-start(bf16[4,128,128]{2,1,0:T(8,128)(2,1)S(1)} %shard_map.123.refs_4_), channel_id=1, source_target_pairs={{0,16},{4,20},{8,24},{12,28},{16,0},{20,4},{24,8},{28,12},{1,17},{... | collective-permute-start | bytes 393224 | tf_op jit(solution)/shard_map/ppermute | solution.py:58
  20.6 1.3 %shard_map.124.refs_4_.refs_5_ = f32[2,512,256]{2,1,0:T(8,128)S(1)} custom-call(bf16[512,512]{1,0:T(8,128)(2,1)S(1)} %copy-done.5, bf16[512,512]{1,0:T(8,128)(2,1)S(1)} %copy-done.1, bf16[512,512]{1,0:T(8,128)(2,1)S(1)} %copy-done.3, bf16[512,512]{1,0:T(8,128)(2,1)S(1)} %copy-done.4, bf16[4,128,128]{2,1,0:T(8,128)(2,1)S(1)} %shard_map.123.refs_4_), custom_call_target="tpu_custom_call" | custom-call | flops 1610612736 | tf_op jit(solution)/shard_map/pallas_call | solution.py:40
  22.1 1.3 %shard_map.125.refs_6_.refs_7_ = f32[2,512,256]{2,1,0:T(8,128)S(1)} custom-call(bf16[512,512]{1,0:T(8,128)(2,1)S(1)} %copy-done.5, bf16[512,512]{1,0:T(8,128)(2,1)S(1)} %copy-done.1, bf16[512,512]{1,0:T(8,128)(2,1)S(1)} %copy-done.3, bf16[512,512]{1,0:T(8,128)(2,1)S(1)} %copy-done.4, f32[2,512,256]{2,1,0:T(8,128)S(1)} %shard_map.124.refs_4_.refs_5_), custom_call_target="tpu_custom_call" | custom-call | flops 1610612736 | tf_op jit(solution)/shard_map/pallas_call | solution.py:40
  23.4 2.7 %collective-permute-done.9.refs_4_.refs_1_.refs_2_ = bf16[4,128,128]{2,1,0:T(8,128)(2,1)S(1)} collective-permute-done((bf16[4,128,128]{2,1,0:T(8,128)(2,1)S(1)}, bf16[4,128,128]{2,1,0:T(8,128)(2,1)S(1)}, u32[]{:S(2)}, u32[]{:S(2)}) %collective-permute-start.9) | collective-permute-done | bytes 131104 | tf_op jit(solution)/shard_map/ppermute | solution.py:58
  26.5 0.6 shard_map.128
  27.1 1.4 %collective-permute-start.22 = (bf16[4,512,256]{2,1,0:T(8,128)(2,1)S(1)}, bf16[4,512,256]{2,1,0:T(8,128)(2,1)S(1)}, u32[]{:S(2)}, u32[]{:S(2)}) collective-permute-start(bf16[4,512,256]{2,1,0:T(8,128)(2,1)S(1)} %get-tuple-element.56.refs_0_.refs_1_.refs_2_), channel_id=1, source_target_pairs={{0,2},{1,3},{2,0},{3,1},{4,6},{5,7},{6,4},{7,5},{8,10},{9,11},{10,... | collective-permute-start | bytes 3145736 | tf_op jit(solution)/shard_map/ppermute | solution.py:58
  28.4 0.8 collective-permute-start.10
  29.2 0.7 collective-permute-start.11
  29.9 0.7 shard_map.120.refs_1_.refs_0_
  30.6 4.2 %collective-permute-done.10.refs_2_ = bf16[512,256]{1,0:T(8,128)(2,1)S(1)} collective-permute-done((bf16[512,256]{1,0:T(8,128)(2,1)S(1)}, bf16[512,256]{1,0:T(8,128)(2,1)S(1)}, u32[]{:S(2)}, u32[]{:S(2)}) %collective-permute-start.10) | collective-permute-done | bytes 262176 | tf_op jit(solution)/shard_map/ppermute | solution.py:58
  34.8 0.8 collective-permute-done.11.refs_3_
  35.6 1.2 %collective-permute-start.12 = (bf16[512,256]{1,0:T(8,128)(2,1)S(1)}, bf16[512,256]{1,0:T(8,128)(2,1)S(1)}, u32[]{:S(2)}, u32[]{:S(2)}) collective-permute-start(bf16[512,256]{1,0:T(8,128)(2,1)S(1)} %collective-permute-done.11.refs_3_), channel_id=1, source_target_pairs={{0,4},{4,0},{8,12},{12,8},{16,20},{20,16},{24,28},{28,24},{1,5},{5... | collective-permute-start | bytes 786440 | tf_op jit(solution)/shard_map/ppermute | solution.py:58
  36.8 1.2 %collective-permute-start.14 = (bf16[512,256]{1,0:T(8,128)(2,1)S(1)}, bf16[512,256]{1,0:T(8,128)(2,1)S(1)}, u32[]{:S(2)}, u32[]{:S(2)}) collective-permute-start(bf16[512,256]{1,0:T(8,128)(2,1)S(1)} %get-tuple-element.61), channel_id=1, source_target_pairs={{0,8},{4,12},{8,0},{12,4},{16,24},{20,28},{24,16},{28,20},{1,9},{5... | collective-permute-start | bytes 786440 | tf_op jit(solution)/shard_map/ppermute | solution.py:58
  38.0 1.0 shard_map.129
  39.0 2.9 %collective-permute-done.12.refs_4_ = bf16[512,256]{1,0:T(8,128)(2,1)S(1)} collective-permute-done((bf16[512,256]{1,0:T(8,128)(2,1)S(1)}, bf16[512,256]{1,0:T(8,128)(2,1)S(1)}, u32[]{:S(2)}, u32[]{:S(2)}) %collective-permute-start.12) | collective-permute-done | bytes 262176 | tf_op jit(solution)/shard_map/ppermute | solution.py:58
  42.0 1.3 %shard_map.130 = (f32[4,128,256]{2,1,0:T(8,128)S(1)}, bf16[4,128,256]{2,1,0:T(8,128)(2,1)S(1)}) custom-call(bf16[4,256,2048]{2,1,0:T(8,128)(2,1)S(1)} %shard_map.120.refs_1_.refs_0_, bf16[4,512,256]{2,1,0:T(8,128)(2,1)S(1)} %get-tuple-element.56.refs_0_.refs_1_.refs_2_, bf16[512,256]{1,0:T(8,128)(2,1)S(1)} %collective-permute-done.10.refs_2_, ...), custom_call_target="tpu_custom_call" | custom-call | flops 1073741824 | tf_op jit(solution)/shard_map/pallas_call | solution.py:40
  43.3 1.3 %collective-permute-start.15 = (bf16[2,512,256]{2,1,0:T(8,128)(2,1)S(1)}, bf16[2,512,256]{2,1,0:T(8,128)(2,1)S(1)}, u32[]{:S(2)}, u32[]{:S(2)}) collective-permute-start(bf16[2,512,256]{2,1,0:T(8,128)(2,1)S(1)} %shard_map.132), channel_id=1, source_target_pairs={{0,4},{4,0},{8,12},{12,8},{16,20},{20,16},{24,28},{28,24},{1,5},{5... | collective-permute-start | bytes 1572872 | tf_op jit(solution)/shard_map/ppermute | solution.py:58
  44.6 1.2 %collective-permute-start.13 = (bf16[2,512,256]{2,1,0:T(8,128)(2,1)S(1)}, bf16[2,512,256]{2,1,0:T(8,128)(2,1)S(1)}, u32[]{:S(2)}, u32[]{:S(2)}) collective-permute-start(bf16[2,512,256]{2,1,0:T(8,128)(2,1)S(1)} %get-tuple-element.60), channel_id=1, source_target_pairs={{0,8},{4,12},{8,0},{12,4},{16,24},{20,28},{24,16},{28,20},{1,9},{5... | collective-permute-start | bytes 1572872 | tf_op jit(solution)/shard_map/ppermute | solution.py:58
  45.8 3.4 %collective-permute-start.16 = (bf16[4,128,256]{2,1,0:T(8,128)(2,1)S(1)}, bf16[4,128,256]{2,1,0:T(8,128)(2,1)S(1)}, u32[]{:S(2)}, u32[]{:S(2)}) collective-permute-start(bf16[4,128,256]{2,1,0:T(8,128)(2,1)S(1)} %get-tuple-element.63), channel_id=1, source_target_pairs={{0,16},{4,20},{8,24},{12,28},{16,0},{20,4},{24,8},{28,12},{1,17},{... | collective-permute-start | bytes 786440 | tf_op jit(solution)/shard_map/ppermute | solution.py:63
  49.1 2.3 %collective-permute-done.22.refs_4_ = bf16[4,512,256]{2,1,0:T(8,128)(2,1)S(1)} collective-permute-done((bf16[4,512,256]{2,1,0:T(8,128)(2,1)S(1)}, bf16[4,512,256]{2,1,0:T(8,128)(2,1)S(1)}, u32[]{:S(2)}, u32[]{:S(2)}) %collective-permute-start.22) | collective-permute-done | bytes 1048608 | tf_op jit(solution)/shard_map/ppermute | solution.py:58
  51.4 1.4 %shard_map.131.refs_5_.refs_0_ = f32[512,512]{1,0:T(8,128)S(1)} custom-call(bf16[512,512]{1,0:T(8,128)(2,1)S(1)} %copy-done.1, bf16[512,512]{1,0:T(8,128)(2,1)S(1)} %copy-done.3, bf16[512,512]{1,0:T(8,128)(2,1)S(1)} %copy-done.4, f32[4,128,256]{2,1,0:T(8,128)S(1)} %get-tuple-element.59.refs_3_.refs_2_.refs_0_), custom_call_target="tpu_custom_call" | custom-call | flops 3221225472 | tf_op jit(solution)/shard_map/pallas_call | solution.py:40
  52.8 0.7 collective-permute-done.15.refs_2_.refs_4_
  53.6 1.2 %shard_map.133 = (f32[4,128,256]{2,1,0:T(8,128)S(1)}, bf16[4,128,256]{2,1,0:T(8,128)(2,1)S(1)}) custom-call(bf16[4,256,2048]{2,1,0:T(8,128)(2,1)S(1)} %shard_map.120.refs_1_.refs_0_, bf16[4,512,256]{2,1,0:T(8,128)(2,1)S(1)} %get-tuple-element.56.refs_0_.refs_1_.refs_2_, bf16[2,512,256]{2,1,0:T(8,128)(2,1)S(1)} %collective-permute-done.15.refs_2_.refs_4_, ...), custom_call_target="tpu_custom_call" | custom-call | flops 1073741824 | tf_op jit(solution)/shard_map/pallas_call | solution.py:40
  54.9 4.5 %collective-permute-done.16.refs_0_.refs_1_ = bf16[4,128,256]{2,1,0:T(8,128)(2,1)S(1)} collective-permute-done((bf16[4,128,256]{2,1,0:T(8,128)(2,1)S(1)}, bf16[4,128,256]{2,1,0:T(8,128)(2,1)S(1)}, u32[]{:S(2)}, u32[]{:S(2)}) %collective-permute-start.16) | collective-permute-done | bytes 262176 | tf_op jit(solution)/shard_map/ppermute | solution.py:63
  59.4 0.7 collective-permute-done.13.refs_1_.refs_3_
  60.1 1.5 %collective-permute-start.18 = (bf16[2,512,256]{2,1,0:T(8,128)(2,1)S(1)}, bf16[2,512,256]{2,1,0:T(8,128)(2,1)S(1)}, u32[]{:S(2)}, u32[]{:S(2)}) collective-permute-start(bf16[2,512,256]{2,1,0:T(8,128)(2,1)S(1)} %shard_map.136), channel_id=1, source_target_pairs={{0,4},{4,0},{8,12},{12,8},{16,20},{20,16},{24,28},{28,24},{1,5},{5... | collective-permute-start | bytes 1572872 | tf_op jit(solution)/shard_map/ppermute | solution.py:58
  61.7 2.6 %collective-permute-start.19 = (bf16[4,128,256]{2,1,0:T(8,128)(2,1)S(1)}, bf16[4,128,256]{2,1,0:T(8,128)(2,1)S(1)}, u32[]{:S(2)}, u32[]{:S(2)}) collective-permute-start(bf16[4,128,256]{2,1,0:T(8,128)(2,1)S(1)} %get-tuple-element.65), channel_id=1, source_target_pairs={{0,16},{4,20},{8,24},{12,28},{16,0},{20,4},{24,8},{28,12},{1,17},{... | collective-permute-start | bytes 786440 | tf_op jit(solution)/shard_map/ppermute | solution.py:63
  64.3 7.0 %collective-permute-done.18.refs_2_.refs_4_ = bf16[2,512,256]{2,1,0:T(8,128)(2,1)S(1)} collective-permute-done((bf16[2,512,256]{2,1,0:T(8,128)(2,1)S(1)}, bf16[2,512,256]{2,1,0:T(8,128)(2,1)S(1)}, u32[]{:S(2)}, u32[]{:S(2)}) %collective-permute-start.18) | collective-permute-done | bytes 524320 | tf_op jit(solution)/shard_map/ppermute | solution.py:58
  71.3 1.2 %shard_map.137 = (f32[4,128,256]{2,1,0:T(8,128)S(1)}, bf16[4,128,256]{2,1,0:T(8,128)(2,1)S(1)}) custom-call(bf16[4,256,2048]{2,1,0:T(8,128)(2,1)S(1)} %shard_map.120.refs_1_.refs_0_, bf16[4,512,256]{2,1,0:T(8,128)(2,1)S(1)} %get-tuple-element.56.refs_0_.refs_1_.refs_2_, bf16[2,512,256]{2,1,0:T(8,128)(2,1)S(1)} %collective-permute-done.18.refs_2_.refs_4_, ...), custom_call_target="tpu_custom_call" | custom-call | flops 1073741824 | tf_op jit(solution)/shard_map/pallas_call | solution.py:40
  72.6 1.8 %collective-permute-done.19.refs_3_.refs_0_ = bf16[4,128,256]{2,1,0:T(8,128)(2,1)S(1)} collective-permute-done((bf16[4,128,256]{2,1,0:T(8,128)(2,1)S(1)}, bf16[4,128,256]{2,1,0:T(8,128)(2,1)S(1)}, u32[]{:S(2)}, u32[]{:S(2)}) %collective-permute-start.19) | collective-permute-done | bytes 262176 | tf_op jit(solution)/shard_map/ppermute | solution.py:63
  74.4 0.8 collective-permute-start.27
  75.2 1.7 %collective-permute-start.29 = (bf16[4,128,256]{2,1,0:T(8,128)(2,1)S(1)}, bf16[4,128,256]{2,1,0:T(8,128)(2,1)S(1)}, u32[]{:S(2)}, u32[]{:S(2)}) collective-permute-start(bf16[4,128,256]{2,1,0:T(8,128)(2,1)S(1)} %get-tuple-element.80), channel_id=1, source_target_pairs={{0,16},{4,20},{8,24},{12,28},{16,0},{20,4},{24,8},{28,12},{1,17},{... | collective-permute-start | bytes 786440 | tf_op jit(solution)/shard_map/ppermute | solution.py:63
  76.9 1.7 %collective-permute-start.20 = (bf16[2,4,128,128]{3,2,1,0:T(8,128)(2,1)S(1)}, bf16[2,4,128,128]{3,2,1,0:T(8,128)(2,1)S(1)}, u32[]{:S(2)}, u32[]{:S(2)}) collective-permute-start(bf16[2,4,128,128]{3,2,1,0:T(8,128)(2,1)S(1)} %get-tuple-element.66), channel_id=1, source_target_pairs={{0,4},{4,0},{8,12},{12,8},{16,20},{20,16},{24,28},{28,24},{1,5},{5... | collective-permute-start | bytes 786440 | tf_op jit(solution)/shard_map/ppermute | solution.py:58
  78.7 4.8 %shard_map.141 = (f32[2,512,256]{2,1,0:T(8,128)S(1)}, bf16[512,256]{1,0:T(8,128)(2,1)S(1)}, bf16[512,256]{1,0:T(8,128)(2,1)S(1)}) custom-call(bf16[1,1024,4096]{2,1,0:T(8,128)(2,1)S(1)} %bitcast.3, f32[512,1]{1,0:T(8,128)S(1)} %copy-done.8, bf16[4,512,256]{2,1,0:T(8,128)(2,1)S(1)} %get-tuple-element.56.refs_0_.refs_1_.refs_2_, ...), custom_call_target="tpu_custom_call" | custom-call | flops 4294967296 | tf_op jit(solution)/shard_map/pallas_call | solution.py:40
  83.6 0.5 collective-permute-start.25
  84.1 4.2 %collective-permute-done.29.refs_5_ = bf16[4,128,256]{2,1,0:T(8,128)(2,1)S(1)} collective-permute-done((bf16[4,128,256]{2,1,0:T(8,128)(2,1)S(1)}, bf16[4,128,256]{2,1,0:T(8,128)(2,1)S(1)}, u32[]{:S(2)}, u32[]{:S(2)}) %collective-permute-start.29) | collective-permute-done | bytes 262176 | tf_op jit(solution)/shard_map/ppermute | solution.py:63
  88.4 0.9 collective-permute-done.27.refs_2_.refs_4_
  89.3 1.2 %shard_map.146 = (f32[4,128,256]{2,1,0:T(8,128)S(1)}, bf16[4,128,256]{2,1,0:T(8,128)(2,1)S(1)}) custom-call(bf16[4,256,2048]{2,1,0:T(8,128)(2,1)S(1)} %shard_map.120.refs_1_.refs_0_, bf16[4,512,256]{2,1,0:T(8,128)(2,1)S(1)} %get-tuple-element.56.refs_0_.refs_1_.refs_2_, bf16[2,512,256]{2,1,0:T(8,128)(2,1)S(1)} %collective-permute-done.27.refs_2_.refs_4_, ...), custom_call_target="tpu_custom_call" | custom-call | flops 1073741824 | tf_op jit(solution)/shard_map/pallas_call | solution.py:40
  90.6 1.3 %collective-permute-start.28 = (bf16[4,128,256]{2,1,0:T(8,128)(2,1)S(1)}, bf16[4,128,256]{2,1,0:T(8,128)(2,1)S(1)}, u32[]{:S(2)}, u32[]{:S(2)}) collective-permute-start(bf16[4,128,256]{2,1,0:T(8,128)(2,1)S(1)} %get-tuple-element.79), channel_id=1, source_target_pairs={{0,16},{4,20},{8,24},{12,28},{16,0},{20,4},{24,8},{28,12},{1,17},{... | collective-permute-start | bytes 786440 | tf_op jit(solution)/shard_map/ppermute | solution.py:63
  91.9 0.9 collective-permute-done.20.refs_1_.refs_3_
  92.9 0.5 collective-permute-start.31
  93.4 0.9 shard_map.139
  94.3 2.3 %collective-permute-start.21 = (bf16[2,4,128,128]{3,2,1,0:T(8,128)(2,1)S(1)}, bf16[2,4,128,128]{3,2,1,0:T(8,128)(2,1)S(1)}, u32[]{:S(2)}, u32[]{:S(2)}) collective-permute-start(bf16[2,4,128,128]{3,2,1,0:T(8,128)(2,1)S(1)} %get-tuple-element.68), channel_id=1, source_target_pairs={{0,8},{4,12},{8,0},{12,4},{16,24},{20,28},{24,16},{28,20},{1,9},{5... | collective-permute-start | bytes 786440 | tf_op jit(solution)/shard_map/ppermute | solution.py:58
  96.7 1.6 %collective-permute-start.26 = (bf16[512,256]{1,0:T(8,128)(2,1)S(1)}, bf16[512,256]{1,0:T(8,128)(2,1)S(1)}, u32[]{:S(2)}, u32[]{:S(2)}) collective-permute-start(bf16[512,256]{1,0:T(8,128)(2,1)S(1)} %get-tuple-element.76), channel_id=1, source_target_pairs={{0,2},{1,3},{2,0},{3,1},{4,6},{5,7},{6,4},{7,5},{8,10},{9,11},{10,... | collective-permute-start | bytes 786440 | tf_op jit(solution)/shard_map/ppermute | solution.py:58
  98.3 1.6 %collective-permute-done.31.refs_2_ = bf16[1,3,128,256]{3,2,1,0:T(8,128)(2,1)S(1)} collective-permute-done((bf16[1,3,128,256]{3,2,1,0:T(8,128)(2,1)S(1)}, bf16[1,3,128,256]{3,2,1,0:T(8,128)(2,1)S(1)}, u32[]{:S(2)}, u32[]{:S(2)}) %collective-permute-start.31) | collective-permute-done | bytes 196640 | tf_op jit(solution)/shard_map/ppermute | solution.py:58
  99.9 1.6 %collective-permute-done.32.refs_3_ = bf16[1,3,128,256]{3,2,1,0:T(8,128)(2,1)S(1)} collective-permute-done((bf16[1,3,128,256]{3,2,1,0:T(8,128)(2,1)S(1)}, bf16[1,3,128,256]{3,2,1,0:T(8,128)(2,1)S(1)}, u32[]{:S(2)}, u32[]{:S(2)}) %collective-permute-start.32) | collective-permute-done | bytes 196640 | tf_op jit(solution)/shard_map/ppermute | solution.py:58
  101.4 1.3 %shard_map.148 = (f32[1,128,4096]{2,1,0:T(8,128)}, f32[8,128]{1,0:T(8,128)S(1)}) custom-call(f32[1,3,128,256]{3,2,1,0:T(8,128)S(1)} %get-tuple-element.81.refs_0_, bf16[1,3,128,256]{3,2,1,0:T(8,128)(2,1)S(1)} %collective-permute-done.30.refs_1_, bf16[1,3,128,256]{3,2,1,0:T(8,128)(2,1)S(1)} %collective-permute-done.31.refs_2_, ...), custom_call_target="tpu_custom_call" | custom-call | tf_op jit(solution)/shard_map/pallas_call | solution.py:40
  102.8 1.8 %collective-permute-done.28.refs_1_ = bf16[4,128,256]{2,1,0:T(8,128)(2,1)S(1)} collective-permute-done((bf16[4,128,256]{2,1,0:T(8,128)(2,1)S(1)}, bf16[4,128,256]{2,1,0:T(8,128)(2,1)S(1)}, u32[]{:S(2)}, u32[]{:S(2)}) %collective-permute-start.28) | collective-permute-done | bytes 262176 | tf_op jit(solution)/shard_map/ppermute | solution.py:63
  104.7 1.0 collective-permute-start.33
  105.7 1.4 %collective-permute-start.35 = (bf16[1,1,128,256]{3,2,1,0:T(8,128)(2,1)S(1)}, bf16[1,1,128,256]{3,2,1,0:T(8,128)(2,1)S(1)}, u32[]{:S(2)}, u32[]{:S(2)}) collective-permute-start(bf16[1,1,128,256]{3,2,1,0:T(8,128)(2,1)S(1)} %get-tuple-element.89), channel_id=1, source_target_pairs={{0,3},{1,2},{2,1},{3,0},{4,7},{5,6},{6,5},{7,4},{8,11},{9,10},{10,... | collective-permute-start | bytes 196616 | tf_op jit(solution)/shard_map/ppermute | solution.py:58
  107.1 1.4 %collective-permute-done.21.refs_4_ = bf16[2,4,128,128]{3,2,1,0:T(8,128)(2,1)S(1)} collective-permute-done((bf16[2,4,128,128]{3,2,1,0:T(8,128)(2,1)S(1)}, bf16[2,4,128,128]{3,2,1,0:T(8,128)(2,1)S(1)}, u32[]{:S(2)}, u32[]{:S(2)}) %collective-permute-start.21) | collective-permute-done | bytes 262176 | tf_op jit(solution)/shard_map/ppermute | solution.py:58
  108.5 1.2 %shard_map.140 = bf16[512,512]{1,0:T(8,128)(2,1)} custom-call(f32[512,512]{1,0:T(8,128)S(1)} %shard_map.131.refs_5_.refs_0_, bf16[512,512]{1,0:T(8,128)(2,1)S(1)} %copy-done.4, bf16[4,128,128]{2,1,0:T(8,128)(2,1)S(1)} %collective-permute-done.9.refs_4_.refs_1_.refs_2_, bf16[2,4,128,128]{3,2,1,0:T(8,128)(2,1)S(1)} %collective-permute-done.20.refs_1_.refs_3_, ...), custom_call_target="tpu_custom_call" | custom-call | tf_op jit(solution)/shard_map/pallas_call | solution.py:40
  109.7 0.7 shard_map.143
  110.5 1.4 %shard_map.150 = (f32[1,128,4096]{2,1,0:T(8,128)}, f32[8,128]{1,0:T(8,128)}) custom-call(f32[1,1,128,256]{3,2,1,0:T(8,128)S(1)} %get-tuple-element.86.refs_0_, bf16[1,1,128,256]{3,2,1,0:T(8,128)(2,1)S(1)} %collective-permute-done.33.refs_1_, bf16[1,1,128,256]{3,2,1,0:T(8,128)(2,1)S(1)} %collective-permute-done.34.refs_2_, ...), custom_call_target="tpu_custom_call", output_to_operand_aliasing={{0}: (4, {})} | custom-call | tf_op jit(solution)/shard_map/pallas_call | solution.py:40
  (63 shorter events, 2.0 us)
Async XLA Ops:
  0.6 20.0 %copy-start.4 = (bf16[512,512]{1,0:T(8,128)(2,1)S(1)}, bf16[512,512]{1,0:T(8,128)(2,1)}, u32[]{:S(2)}) copy-start(bf16[512,512]{1,0:T(8,128)(2,1)} %refs_1_.15) | copy-start | bytes 1572868
  0.6 20.0 %copy-start.5 = (bf16[512,512]{1,0:T(8,128)(2,1)S(1)}, bf16[512,512]{1,0:T(8,128)(2,1)}, u32[]{:S(2)}) copy-start(bf16[512,512]{1,0:T(8,128)(2,1)} %refs_0_.11) | copy-start | bytes 1572868
  0.7 20.0 %copy-start.3 = (bf16[512,512]{1,0:T(8,128)(2,1)S(1)}, bf16[512,512]{1,0:T(8,128)(2,1)}, u32[]{:S(2)}) copy-start(bf16[512,512]{1,0:T(8,128)(2,1)} %refs_1_.14) | copy-start | bytes 1572868
  0.7 19.9 %copy-start.1 = (bf16[512,512]{1,0:T(8,128)(2,1)S(1)}, bf16[512,512]{1,0:T(8,128)(2,1)}, u32[]{:S(2)}) copy-start(bf16[512,512]{1,0:T(8,128)(2,1)} %refs_0_.14) | copy-start | bytes 1572868
  3.7 7.6 %collective-permute-start.7 = (bf16[4,128,128]{2,1,0:T(8,128)(2,1)}, bf16[4,128,128]{2,1,0:T(8,128)(2,1)S(1)}, u32[]{:S(2)}, u32[]{:S(2)}) collective-permute-start(bf16[4,128,128]{2,1,0:T(8,128)(2,1)} %get-tuple-element.53.refs_0_), channel_id=1, source_target_pairs={{0,4},{4,0},{8,12},{12,8},{16,20},{20,16},{24,28},{28,24},{1,5},{5... | collective-permute-start | bytes 393224 | tf_op jit(solution)/shard_map/ppermute | solution.py:58
  6.8 7.7 %collective-permute-start.4 = (bf16[272,256]{1,0:T(8,128)(2,1)}, bf16[272,256]{1,0:T(8,128)(2,1)S(1)}, u32[]{:S(2)}, u32[]{:S(2)}) collective-permute-start(bf16[272,256]{1,0:T(8,128)(2,1)} %get-tuple-element.52), channel_id=1, source_target_pairs={{0,8},{4,12},{8,0},{12,4},{16,24},{20,28},{24,16},{28,20},{1,9},{5... | collective-permute-start | bytes 417800 | tf_op jit(solution)/shard_map/ppermute | solution.py:58
  8.3 7.6 %collective-permute-start = (bf16[272,256]{1,0:T(8,128)(2,1)}, bf16[272,256]{1,0:T(8,128)(2,1)S(1)}, u32[]{:S(2)}, u32[]{:S(2)}) collective-permute-start(bf16[272,256]{1,0:T(8,128)(2,1)} %get-tuple-element.50), channel_id=1, source_target_pairs={{0,4},{4,0},{8,12},{12,8},{16,20},{20,16},{24,28},{28,24},{1,5},{5... | collective-permute-start | bytes 417800 | tf_op jit(solution)/shard_map/ppermute | solution.py:58
  8.8 7.4 %collective-permute-start.2 = (bf16[272,256]{1,0:T(8,128)(2,1)}, bf16[272,256]{1,0:T(8,128)(2,1)S(1)}, u32[]{:S(2)}, u32[]{:S(2)}) collective-permute-start(bf16[272,256]{1,0:T(8,128)(2,1)} %get-tuple-element.51), channel_id=1, source_target_pairs={{0,8},{4,12},{8,0},{12,4},{16,24},{20,28},{24,16},{28,20},{1,9},{5... | collective-permute-start | bytes 417800 | tf_op jit(solution)/shard_map/ppermute | solution.py:58
  8.9 1.0 copy-start
  9.9 1.0 copy-start.2
  11.3 0.9 copy-start.7
  12.3 5.6 %collective-permute-start.8 = (bf16[4,128,128]{2,1,0:T(8,128)(2,1)S(1)}, bf16[4,128,128]{2,1,0:T(8,128)(2,1)S(1)}, u32[]{:S(2)}, u32[]{:S(2)}) collective-permute-start(bf16[4,128,128]{2,1,0:T(8,128)(2,1)S(1)} %get-tuple-element.54), channel_id=1, source_target_pairs={{0,8},{4,12},{8,0},{12,4},{16,24},{20,28},{24,16},{28,20},{1,9},{5... | collective-permute-start | bytes 393224 | tf_op jit(solution)/shard_map/ppermute | solution.py:58
  14.4 7.5 %collective-permute-start.5 = (bf16[272,256]{1,0:T(8,128)(2,1)S(1)}, bf16[272,256]{1,0:T(8,128)(2,1)S(1)}, u32[]{:S(2)}, u32[]{:S(2)}) collective-permute-start(bf16[272,256]{1,0:T(8,128)(2,1)S(1)} %collective-permute-done.4.refs_3_), channel_id=1, source_target_pairs={{0,4},{4,0},{8,12},{12,8},{16,20},{20,16},{24,28},{28,24},{1,5},{5... | collective-permute-start | bytes 417800 | tf_op jit(solution)/shard_map/ppermute | solution.py:58
  15.9 10.5 %collective-permute-start.1 = (bf16[272,256]{1,0:T(8,128)(2,1)S(1)}, bf16[272,256]{1,0:T(8,128)(2,1)S(1)}, u32[]{:S(2)}, u32[]{:S(2)}) collective-permute-start(bf16[272,256]{1,0:T(8,128)(2,1)S(1)} %collective-permute-done.refs_1_.refs_0_), channel_id=1, source_target_pairs={{0,1},{1,0},{2,3},{3,2},{4,5},{5,4},{6,7},{7,6},{8,9},{9,8},{10,11... | collective-permute-start | bytes 417800 | tf_op jit(solution)/shard_map/ppermute | solution.py:58
  16.2 10.3 %collective-permute-start.3 = (bf16[272,256]{1,0:T(8,128)(2,1)S(1)}, bf16[272,256]{1,0:T(8,128)(2,1)S(1)}, u32[]{:S(2)}, u32[]{:S(2)}) collective-permute-start(bf16[272,256]{1,0:T(8,128)(2,1)S(1)} %collective-permute-done.2.refs_3_.refs_1_), channel_id=1, source_target_pairs={{0,1},{1,0},{2,3},{3,2},{4,5},{5,4},{6,7},{7,6},{8,9},{9,8},{10,11... | collective-permute-start | bytes 417800 | tf_op jit(solution)/shard_map/ppermute | solution.py:58
  17.9 8.2 %collective-permute-start.9 = (bf16[4,128,128]{2,1,0:T(8,128)(2,1)S(1)}, bf16[4,128,128]{2,1,0:T(8,128)(2,1)S(1)}, u32[]{:S(2)}, u32[]{:S(2)}) collective-permute-start(bf16[4,128,128]{2,1,0:T(8,128)(2,1)S(1)} %shard_map.123.refs_4_), channel_id=1, source_target_pairs={{0,16},{4,20},{8,24},{12,28},{16,0},{20,4},{24,8},{28,12},{1,17},{... | collective-permute-start | bytes 393224 | tf_op jit(solution)/shard_map/ppermute | solution.py:58
  22.0 4.5 %collective-permute-start.6 = (bf16[272,256]{1,0:T(8,128)(2,1)S(1)}, bf16[272,256]{1,0:T(8,128)(2,1)S(1)}, u32[]{:S(2)}, u32[]{:S(2)}) collective-permute-start(bf16[272,256]{1,0:T(8,128)(2,1)S(1)} %collective-permute-done.5.refs_5_.refs_2_), channel_id=1, source_target_pairs={{0,1},{1,0},{2,3},{3,2},{4,5},{5,4},{6,7},{7,6},{8,9},{9,8},{10,11... | collective-permute-start | bytes 417800 | tf_op jit(solution)/shard_map/ppermute | solution.py:58
  23.4 6.5 %copy-start.6 = (bf16[272,512]{1,0:T(8,128)(2,1)S(1)}, bf16[272,512]{1,0:T(8,128)(2,1)}, u32[]{:S(2)}) copy-start(bf16[272,512]{1,0:T(8,128)(2,1)} %get-tuple-element.49.refs_0_) | copy-start | bytes 835588
  27.1 24.3 %collective-permute-start.22 = (bf16[4,512,256]{2,1,0:T(8,128)(2,1)S(1)}, bf16[4,512,256]{2,1,0:T(8,128)(2,1)S(1)}, u32[]{:S(2)}, u32[]{:S(2)}) collective-permute-start(bf16[4,512,256]{2,1,0:T(8,128)(2,1)S(1)} %get-tuple-element.56.refs_0_.refs_1_.refs_2_), channel_id=1, source_target_pairs={{0,2},{1,3},{2,0},{3,1},{4,6},{5,7},{6,4},{7,5},{8,10},{9,11},{10,... | collective-permute-start | bytes 3145736 | tf_op jit(solution)/shard_map/ppermute | solution.py:58
  28.4 6.4 %collective-permute-start.10 = (bf16[512,256]{1,0:T(8,128)(2,1)S(1)}, bf16[512,256]{1,0:T(8,128)(2,1)S(1)}, u32[]{:S(2)}, u32[]{:S(2)}) collective-permute-start(bf16[512,256]{1,0:T(8,128)(2,1)S(1)} %shard_map.127.refs_7_), channel_id=1, source_target_pairs={{0,4},{4,0},{8,12},{12,8},{16,20},{20,16},{24,28},{28,24},{1,5},{5... | collective-permute-start | bytes 786440 | tf_op jit(solution)/shard_map/ppermute | solution.py:58
  29.2 6.4 %collective-permute-start.11 = (bf16[512,256]{1,0:T(8,128)(2,1)S(1)}, bf16[512,256]{1,0:T(8,128)(2,1)S(1)}, u32[]{:S(2)}, u32[]{:S(2)}) collective-permute-start(bf16[512,256]{1,0:T(8,128)(2,1)S(1)} %shard_map.127.refs_7_), channel_id=1, source_target_pairs={{0,8},{4,12},{8,0},{12,4},{16,24},{20,28},{24,16},{28,20},{1,9},{5... | collective-permute-start | bytes 786440 | tf_op jit(solution)/shard_map/ppermute | solution.py:58
  29.9 24.9 %collective-permute-start.17 = (bf16[4,512,256]{2,1,0:T(8,128)(2,1)S(1)}, bf16[4,512,256]{2,1,0:T(8,128)(2,1)S(1)}, u32[]{:S(2)}, u32[]{:S(2)}) collective-permute-start(bf16[4,512,256]{2,1,0:T(8,128)(2,1)S(1)} %get-tuple-element.56.refs_0_.refs_1_.refs_2_), channel_id=1, source_target_pairs={{0,1},{1,0},{2,3},{3,2},{4,5},{5,4},{6,7},{7,6},{8,9},{9,8},{10,11... | collective-permute-start | bytes 3145736 | tf_op jit(solution)/shard_map/ppermute | solution.py:58
  35.6 6.4 %collective-permute-start.12 = (bf16[512,256]{1,0:T(8,128)(2,1)S(1)}, bf16[512,256]{1,0:T(8,128)(2,1)S(1)}, u32[]{:S(2)}, u32[]{:S(2)}) collective-permute-start(bf16[512,256]{1,0:T(8,128)(2,1)S(1)} %collective-permute-done.11.refs_3_), channel_id=1, source_target_pairs={{0,4},{4,0},{8,12},{12,8},{16,20},{20,16},{24,28},{28,24},{1,5},{5... | collective-permute-start | bytes 786440 | tf_op jit(solution)/shard_map/ppermute | solution.py:58
  36.8 6.4 %collective-permute-start.14 = (bf16[512,256]{1,0:T(8,128)(2,1)S(1)}, bf16[512,256]{1,0:T(8,128)(2,1)S(1)}, u32[]{:S(2)}, u32[]{:S(2)}) collective-permute-start(bf16[512,256]{1,0:T(8,128)(2,1)S(1)} %get-tuple-element.61), channel_id=1, source_target_pairs={{0,8},{4,12},{8,0},{12,4},{16,24},{20,28},{24,16},{28,20},{1,9},{5... | collective-permute-start | bytes 786440 | tf_op jit(solution)/shard_map/ppermute | solution.py:58
  43.3 10.3 %collective-permute-start.15 = (bf16[2,512,256]{2,1,0:T(8,128)(2,1)S(1)}, bf16[2,512,256]{2,1,0:T(8,128)(2,1)S(1)}, u32[]{:S(2)}, u32[]{:S(2)}) collective-permute-start(bf16[2,512,256]{2,1,0:T(8,128)(2,1)S(1)} %shard_map.132), channel_id=1, source_target_pairs={{0,4},{4,0},{8,12},{12,8},{16,20},{20,16},{24,28},{28,24},{1,5},{5... | collective-permute-start | bytes 1572872 | tf_op jit(solution)/shard_map/ppermute | solution.py:58
  44.6 15.5 %collective-permute-start.13 = (bf16[2,512,256]{2,1,0:T(8,128)(2,1)S(1)}, bf16[2,512,256]{2,1,0:T(8,128)(2,1)S(1)}, u32[]{:S(2)}, u32[]{:S(2)}) collective-permute-start(bf16[2,512,256]{2,1,0:T(8,128)(2,1)S(1)} %get-tuple-element.60), channel_id=1, source_target_pairs={{0,8},{4,12},{8,0},{12,4},{16,24},{20,28},{24,16},{28,20},{1,9},{5... | collective-permute-start | bytes 1572872 | tf_op jit(solution)/shard_map/ppermute | solution.py:58
  45.8 13.6 %collective-permute-start.16 = (bf16[4,128,256]{2,1,0:T(8,128)(2,1)S(1)}, bf16[4,128,256]{2,1,0:T(8,128)(2,1)S(1)}, u32[]{:S(2)}, u32[]{:S(2)}) collective-permute-start(bf16[4,128,256]{2,1,0:T(8,128)(2,1)S(1)} %get-tuple-element.63), channel_id=1, source_target_pairs={{0,16},{4,20},{8,24},{12,28},{16,0},{20,4},{24,8},{28,12},{1,17},{... | collective-permute-start | bytes 786440 | tf_op jit(solution)/shard_map/ppermute | solution.py:63
  51.4 27.2 %collective-permute-start.23 = (bf16[4,512,256]{2,1,0:T(8,128)(2,1)S(1)}, bf16[4,512,256]{2,1,0:T(8,128)(2,1)S(1)}, u32[]{:S(2)}, u32[]{:S(2)}) collective-permute-start(bf16[4,512,256]{2,1,0:T(8,128)(2,1)S(1)} %collective-permute-done.22.refs_4_), channel_id=1, source_target_pairs={{0,1},{1,0},{2,3},{3,2},{4,5},{5,4},{6,7},{7,6},{8,9},{9,8},{10,11... | collective-permute-start | bytes 3145736 | tf_op jit(solution)/shard_map/ppermute | solution.py:58
  54.8 23.8 %slice-start = ((s8[8388608]{0:T(1024)(128)(4,1)}), s8[4194304]{0:T(1024)(128)(4,1)S(1)}, s32[]{:S(2)}) async-start(s8[8388608]{0:T(1024)(128)(4,1)} %bitcast.2), calls=%async_computation | async-start | bytes 8388608
  60.1 11.2 %collective-permute-start.18 = (bf16[2,512,256]{2,1,0:T(8,128)(2,1)S(1)}, bf16[2,512,256]{2,1,0:T(8,128)(2,1)S(1)}, u32[]{:S(2)}, u32[]{:S(2)}) collective-permute-start(bf16[2,512,256]{2,1,0:T(8,128)(2,1)S(1)} %shard_map.136), channel_id=1, source_target_pairs={{0,4},{4,0},{8,12},{12,8},{16,20},{20,16},{24,28},{28,24},{1,5},{5... | collective-permute-start | bytes 1572872 | tf_op jit(solution)/shard_map/ppermute | solution.py:58
  61.7 17.0 %slice-start.1 = ((s8[8388608]{0:T(1024)(128)(4,1)}), s8[4194304]{0:T(1024)(128)(4,1)S(1)}, s32[]{:S(2)}) async-start(s8[8388608]{0:T(1024)(128)(4,1)} %bitcast.2), calls=%async_computation.1 | async-start | bytes 8388608
  61.7 17.0 %copy-start.8 = (f32[512,1]{1,0:T(8,128)S(1)}, f32[512,1]{1,0:T(8,128)}, u32[]{:S(2)}) copy-start(f32[512,1]{1,0:T(8,128)} %get-tuple-element.71.refs_1_) | copy-start | bytes 6148
  61.7 12.7 %collective-permute-start.19 = (bf16[4,128,256]{2,1,0:T(8,128)(2,1)S(1)}, bf16[4,128,256]{2,1,0:T(8,128)(2,1)S(1)}, u32[]{:S(2)}, u32[]{:S(2)}) collective-permute-start(bf16[4,128,256]{2,1,0:T(8,128)(2,1)S(1)} %get-tuple-element.65), channel_id=1, source_target_pairs={{0,16},{4,20},{8,24},{12,28},{16,0},{20,4},{24,8},{28,12},{1,17},{... | collective-permute-start | bytes 786440 | tf_op jit(solution)/shard_map/ppermute | solution.py:63
  74.4 14.9 %collective-permute-start.27 = (bf16[2,512,256]{2,1,0:T(8,128)(2,1)S(1)}, bf16[2,512,256]{2,1,0:T(8,128)(2,1)S(1)}, u32[]{:S(2)}, u32[]{:S(2)}) collective-permute-start(bf16[2,512,256]{2,1,0:T(8,128)(2,1)S(1)} %shard_map.145), channel_id=1, source_target_pairs={{0,4},{4,0},{8,12},{12,8},{16,20},{20,16},{24,28},{28,24},{1,5},{5... | collective-permute-start | bytes 1572872 | tf_op jit(solution)/shard_map/ppermute | solution.py:58
  75.2 13.0 %collective-permute-start.29 = (bf16[4,128,256]{2,1,0:T(8,128)(2,1)S(1)}, bf16[4,128,256]{2,1,0:T(8,128)(2,1)S(1)}, u32[]{:S(2)}, u32[]{:S(2)}) collective-permute-start(bf16[4,128,256]{2,1,0:T(8,128)(2,1)S(1)} %get-tuple-element.80), channel_id=1, source_target_pairs={{0,16},{4,20},{8,24},{12,28},{16,0},{20,4},{24,8},{28,12},{1,17},{... | collective-permute-start | bytes 786440 | tf_op jit(solution)/shard_map/ppermute | solution.py:63
  76.9 16.0 %collective-permute-start.20 = (bf16[2,4,128,128]{3,2,1,0:T(8,128)(2,1)S(1)}, bf16[2,4,128,128]{3,2,1,0:T(8,128)(2,1)S(1)}, u32[]{:S(2)}, u32[]{:S(2)}) collective-permute-start(bf16[2,4,128,128]{3,2,1,0:T(8,128)(2,1)S(1)} %get-tuple-element.66), channel_id=1, source_target_pairs={{0,4},{4,0},{8,12},{12,8},{16,20},{20,16},{24,28},{28,24},{1,5},{5... | collective-permute-start | bytes 786440 | tf_op jit(solution)/shard_map/ppermute | solution.py:58
  83.5 10.8 %collective-permute-start.24 = (bf16[512,256]{1,0:T(8,128)(2,1)S(1)}, bf16[512,256]{1,0:T(8,128)(2,1)S(1)}, u32[]{:S(2)}, u32[]{:S(2)}) collective-permute-start(bf16[512,256]{1,0:T(8,128)(2,1)S(1)} %get-tuple-element.73), channel_id=1, source_target_pairs={{0,1},{1,0},{2,3},{3,2},{4,5},{5,4},{6,7},{7,6},{8,9},{9,8},{10,11... | collective-permute-start | bytes 786440 | tf_op jit(solution)/shard_map/ppermute | solution.py:58
  83.6 10.7 %collective-permute-start.25 = (bf16[512,256]{1,0:T(8,128)(2,1)S(1)}, bf16[512,256]{1,0:T(8,128)(2,1)S(1)}, u32[]{:S(2)}, u32[]{:S(2)}) collective-permute-start(bf16[512,256]{1,0:T(8,128)(2,1)S(1)} %get-tuple-element.74), channel_id=1, source_target_pairs={{0,1},{1,0},{2,3},{3,2},{4,5},{5,4},{6,7},{7,6},{8,9},{9,8},{10,11... | collective-permute-start | bytes 786440 | tf_op jit(solution)/shard_map/ppermute | solution.py:58
  88.4 8.3 %collective-permute-start.30 = (bf16[1,3,128,256]{3,2,1,0:T(8,128)(2,1)S(1)}, bf16[1,3,128,256]{3,2,1,0:T(8,128)(2,1)S(1)}, u32[]{:S(2)}, u32[]{:S(2)}) collective-permute-start(bf16[1,3,128,256]{3,2,1,0:T(8,128)(2,1)S(1)} %get-tuple-element.82), channel_id=1, source_target_pairs={{0,1},{1,0},{2,3},{3,2},{4,5},{5,4},{6,7},{7,6},{8,9},{9,8},{10,11... | collective-permute-start | bytes 589832 | tf_op jit(solution)/shard_map/ppermute | solution.py:58
  90.6 14.0 %collective-permute-start.28 = (bf16[4,128,256]{2,1,0:T(8,128)(2,1)S(1)}, bf16[4,128,256]{2,1,0:T(8,128)(2,1)S(1)}, u32[]{:S(2)}, u32[]{:S(2)}) collective-permute-start(bf16[4,128,256]{2,1,0:T(8,128)(2,1)S(1)} %get-tuple-element.79), channel_id=1, source_target_pairs={{0,16},{4,20},{8,24},{12,28},{16,0},{20,4},{24,8},{28,12},{1,17},{... | collective-permute-start | bytes 786440 | tf_op jit(solution)/shard_map/ppermute | solution.py:63
  92.9 7.0 %collective-permute-start.31 = (bf16[1,3,128,256]{3,2,1,0:T(8,128)(2,1)S(1)}, bf16[1,3,128,256]{3,2,1,0:T(8,128)(2,1)S(1)}, u32[]{:S(2)}, u32[]{:S(2)}) collective-permute-start(bf16[1,3,128,256]{3,2,1,0:T(8,128)(2,1)S(1)} %get-tuple-element.83), channel_id=1, source_target_pairs={{0,2},{1,3},{2,0},{3,1},{4,6},{5,7},{6,4},{7,5},{8,10},{9,11},{10,... | collective-permute-start | bytes 589832 | tf_op jit(solution)/shard_map/ppermute | solution.py:58
  94.3 7.2 %collective-permute-start.32 = (bf16[1,3,128,256]{3,2,1,0:T(8,128)(2,1)S(1)}, bf16[1,3,128,256]{3,2,1,0:T(8,128)(2,1)S(1)}, u32[]{:S(2)}, u32[]{:S(2)}) collective-permute-start(bf16[1,3,128,256]{3,2,1,0:T(8,128)(2,1)S(1)} %get-tuple-element.84), channel_id=1, source_target_pairs={{0,3},{1,2},{2,1},{3,0},{4,7},{5,6},{6,5},{7,4},{8,11},{9,10},{10,... | collective-permute-start | bytes 589832 | tf_op jit(solution)/shard_map/ppermute | solution.py:58
  94.3 14.2 %collective-permute-start.21 = (bf16[2,4,128,128]{3,2,1,0:T(8,128)(2,1)S(1)}, bf16[2,4,128,128]{3,2,1,0:T(8,128)(2,1)S(1)}, u32[]{:S(2)}, u32[]{:S(2)}) collective-permute-start(bf16[2,4,128,128]{3,2,1,0:T(8,128)(2,1)S(1)} %get-tuple-element.68), channel_id=1, source_target_pairs={{0,8},{4,12},{8,0},{12,4},{16,24},{20,28},{24,16},{28,20},{1,9},{5... | collective-permute-start | bytes 786440 | tf_op jit(solution)/shard_map/ppermute | solution.py:58
  96.7 13.0 %collective-permute-start.26 = (bf16[512,256]{1,0:T(8,128)(2,1)S(1)}, bf16[512,256]{1,0:T(8,128)(2,1)S(1)}, u32[]{:S(2)}, u32[]{:S(2)}) collective-permute-start(bf16[512,256]{1,0:T(8,128)(2,1)S(1)} %get-tuple-element.76), channel_id=1, source_target_pairs={{0,2},{1,3},{2,0},{3,1},{4,6},{5,7},{6,4},{7,5},{8,10},{9,11},{10,... | collective-permute-start | bytes 786440 | tf_op jit(solution)/shard_map/ppermute | solution.py:58
  104.7 5.8 %collective-permute-start.33 = (bf16[1,1,128,256]{3,2,1,0:T(8,128)(2,1)S(1)}, bf16[1,1,128,256]{3,2,1,0:T(8,128)(2,1)S(1)}, u32[]{:S(2)}, u32[]{:S(2)}) collective-permute-start(bf16[1,1,128,256]{3,2,1,0:T(8,128)(2,1)S(1)} %get-tuple-element.87), channel_id=1, source_target_pairs={{0,1},{1,0},{2,3},{3,2},{4,5},{5,4},{6,7},{7,6},{8,9},{9,8},{10,11... | collective-permute-start | bytes 196616 | tf_op jit(solution)/shard_map/ppermute | solution.py:58
  105.7 4.8 %collective-permute-start.34 = (bf16[1,1,128,256]{3,2,1,0:T(8,128)(2,1)S(1)}, bf16[1,1,128,256]{3,2,1,0:T(8,128)(2,1)S(1)}, u32[]{:S(2)}, u32[]{:S(2)}) collective-permute-start(bf16[1,1,128,256]{3,2,1,0:T(8,128)(2,1)S(1)} %get-tuple-element.88), channel_id=1, source_target_pairs={{0,2},{1,3},{2,0},{3,1},{4,6},{5,7},{6,4},{7,5},{8,10},{9,11},{10,... | collective-permute-start | bytes 196616 | tf_op jit(solution)/shard_map/ppermute | solution.py:58
  105.7 4.8 %collective-permute-start.35 = (bf16[1,1,128,256]{3,2,1,0:T(8,128)(2,1)S(1)}, bf16[1,1,128,256]{3,2,1,0:T(8,128)(2,1)S(1)}, u32[]{:S(2)}, u32[]{:S(2)}) collective-permute-start(bf16[1,1,128,256]{3,2,1,0:T(8,128)(2,1)S(1)} %get-tuple-element.89), channel_id=1, source_target_pairs={{0,3},{1,2},{2,1},{3,0},{4,7},{5,6},{6,5},{7,4},{8,11},{9,10},{10,... | collective-permute-start | bytes 196616 | tf_op jit(solution)/shard_map/ppermute | solution.py:58
